TPU v7x, 32 devices: a whole 2x2x4 slice. The times are simulated.
32 devices in a mesh: seq: 2 (over x), heads: 4 (over y, core), dp: 4 (over z).
Axes of the slice: x: 2, y: 2, z: 4, core: 2. Of those that a mesh axis runs over, the one named last changes fastest.
Arguments:
- activations: bfloat16 [1024, 8192], P(('dp', 'seq'), 'heads'), parts along dimension 0, may hold values from -6 to 6
- conv_taps: bfloat16 [4, 8192], P(None, 'heads'), may hold values from -3 to 3
- gate_in: bfloat16 [8192, 1024], P('heads', 'seq'), may hold values from -0.0625 to 0.0625
- gate_out: bfloat16 [1024, 8], replicated, may hold values from -0.59765625 to 0.59765625
- queries: bfloat16 [1024, 8192], P(('dp', 'seq'), 'heads'), parts along dimension 0, may hold values from -1000 to 1000, as said below
- key_vectors: bfloat16 [1024, 1024], P(('dp', 'seq'), 'heads'), parts along dimension 0, may hold values from -4 to 4, as said below
- value_vectors: bfloat16 [1024, 1024], P(('dp', 'seq'), 'heads'), parts along dimension 0, may hold values from -6 to 6
- segment_ids: int32 [1024], P('dp'), parts along dimension 0, may hold values from 0 to 3, never falling along the last dimension, each value on 1 to 128 neighbouring positions
Outputs:
- attended: bfloat16 [1024, 8192], P(('dp', 'seq'), 'heads'), parts along dimension 0
- key_mass: bfloat16 [8, 1024], P('heads', ('dp', 'seq')), parts along dimension 1
There are 4 independent parts, one for each index of `dp`. A program takes and returns all parts, laid end to end along the dimension named above; an argument that names none is the same for every part. Nothing has to cross between parts.
Inputs may be any that keep to these rules, and one draw needn't show every extreme that they name: `queries`: finite. `key_vectors`: finite.
All inputs are finite; a program needn't handle non-finite values.
Results may differ from a plain program's by a relative error of at most 0.0056.
Values may be sent and summed in bfloat16 or wider, within the bound.
No kernel may reach another device: no remote copies, remote signals or barrier semaphores. Data moves between devices by JAX's collectives and lax.ppermute only.
A program may use at most 64 MiB of HBM per device.

v0:
```python
import math

import jax
import jax.numpy as jnp
from jax import lax
from jax.sharding import PartitionSpec as P

QUERY_HEADS = 64
KV_HEADS = 8
HEAD_DIM = 128


NEG_FILL = -1e30


def from_behind(block, axis, distance):
    devices = range(lax.axis_size(axis))
    route = [(i - distance, i) for i in devices if i - distance in devices]
    return lax.ppermute(block, axis, route)


def block_scores(query_heads, key_block, bias_block, allowed, score_scale):
    scores = (
        jnp.einsum("tgeh,kgh->getk", query_heads, key_block, preferred_element_type=jnp.float32)
        * score_scale
    )
    scores = scores + jnp.transpose(bias_block.astype(jnp.float32))[:, None, None, :]
    return jnp.where(allowed[None, None], scores, NEG_FILL)


def per_device(
    activations, conv_taps, gate_in, gate_out, queries, key_vectors, value_vectors, segment_ids
):
    shard_rows = activations.shape[0]
    tap_count = conv_taps.shape[0]
    rim_rows = from_behind(activations[shard_rows - (tap_count - 1) :], "seq", 1)
    widened = jnp.concatenate([rim_rows, activations], 0).astype(jnp.float32)
    summed = jnp.zeros(activations.shape, jnp.float32)
    for shift_back in range(tap_count):
        start_row = tap_count - 1 - shift_back
        summed = (
            summed
            + conv_taps[shift_back].astype(jnp.float32)
            * widened[start_row : start_row + shard_rows]
        )
    mixed_rows = summed.astype(jnp.bfloat16)
    partial_hidden = jnp.dot(
        mixed_rows,
        lax.all_gather(gate_in, "seq", axis=1, tiled=True),
        preferred_element_type=jnp.float32,
    )
    kv_local = key_vectors.shape[1] // HEAD_DIM
    group_size = QUERY_HEADS // KV_HEADS
    head_rank = lax.axis_index("heads")
    hidden = jax.nn.silu(lax.psum(partial_hidden, "heads")).astype(jnp.bfloat16)
    logits = jnp.dot(hidden, gate_out, preferred_element_type=jnp.float32)
    retention = lax.dynamic_slice_in_dim(
        jax.nn.log_sigmoid(logits).astype(jnp.bfloat16), head_rank * kv_local, kv_local, 1
    )
    seq_rank = lax.axis_index("seq")
    local_index = jnp.arange(shard_rows, dtype=jnp.int32)
    own_queries, own_keys, own_values, own_bias = (queries, key_vectors, value_vectors, retention)
    query_places = seq_rank * shard_rows + local_index
    query_segments = jnp.take(segment_ids, query_places)
    query_heads = own_queries.reshape(shard_rows, kv_local, group_size, HEAD_DIM)
    score_scale = 1.0 / math.sqrt(HEAD_DIM)

    def visibility(flat_index):
        key_segments = jnp.take(segment_ids, flat_index)
        return (flat_index[None, :] <= query_places[:, None]) & (
            key_segments[None, :] == query_segments[:, None]
        )

    initial = (
        jnp.full((kv_local, group_size, shard_rows), NEG_FILL, jnp.float32),
        jnp.zeros((kv_local, group_size, shard_rows), jnp.float32),
    )
    all_keys, all_values, all_bias = (
        lax.all_gather(own_keys, "seq", axis=0, tiled=True),
        lax.all_gather(own_values, "seq", axis=0, tiled=True),
        lax.all_gather(own_bias, "seq", axis=0, tiled=True),
    )
    piece_rows = all_keys.shape[0]
    stats_block_width = math.gcd(piece_rows, 512)

    def one_block(block_number, state_in):
        offset = block_number * stats_block_width
        key_block = lax.dynamic_slice_in_dim(all_keys, offset, stats_block_width, 0).reshape(
            stats_block_width, kv_local, HEAD_DIM
        )
        bias_block = lax.dynamic_slice_in_dim(all_bias, offset, stats_block_width, 0)
        allowed = visibility(0 + offset + jnp.arange(stats_block_width, dtype=jnp.int32))

        def update(state_old):
            peak_old, mass_old = state_old
            masked = block_scores(query_heads, key_block, bias_block, allowed, score_scale)
            peak_new = jnp.maximum(peak_old, jnp.max(masked, axis=3))
            exponent = jnp.where(allowed[None, None], jnp.exp(masked - peak_new[..., None]), 0.0)
            return (peak_new, mass_old * jnp.exp(peak_old - peak_new) + jnp.sum(exponent, axis=3))

        def keep_state(state_old):
            return state_old

        return lax.cond(jnp.any(allowed), update, keep_state, state_in)

    row_peak, total_mass = lax.fori_loop(0, piece_rows // stats_block_width, one_block, initial)
    total_keys = all_keys.shape[0]
    block_width = math.gcd(total_keys, 512)
    block_count = total_keys // block_width
    key_blocks = all_keys.reshape(block_count, block_width, kv_local, HEAD_DIM)
    value_blocks = all_values.reshape(block_count, block_width, kv_local, HEAD_DIM)
    bias_blocks = all_bias.reshape(block_count, block_width, kv_local)

    def second_pass(accumulated, block_items):
        block_number, key_block, value_block, bias_block = block_items
        allowed = visibility(block_number * block_width + jnp.arange(block_width, dtype=jnp.int32))

        def attend(accum_in):
            masked = block_scores(query_heads, key_block, bias_block, allowed, score_scale)
            weights = (
                jnp.where(allowed[None, None], jnp.exp(masked - row_peak[..., None]), 0.0)
                / total_mass[..., None]
            )
            accum_out = accum_in + jnp.einsum(
                "getk,kgh->tgeh",
                weights.astype(jnp.bfloat16),
                value_block,
                preferred_element_type=jnp.float32,
            )
            return (accum_out, jnp.transpose(jnp.sum(weights, axis=(1, 2))) / group_size)

        def skip_block(accum_in):
            return (accum_in, jnp.zeros((block_width, kv_local), jnp.float32))

        return lax.cond(jnp.any(allowed), attend, skip_block, accumulated)

    accumulated, mass_blocks = lax.scan(
        second_pass,
        jnp.zeros((shard_rows, kv_local, group_size, HEAD_DIM), jnp.float32),
        (jnp.arange(block_count, dtype=jnp.int32), key_blocks, value_blocks, bias_blocks),
    )
    key_term = mass_blocks.reshape(total_keys, kv_local)
    key_mass = lax.psum_scatter(key_term, "seq", scatter_dimension=0, tiled=True).astype(
        jnp.bfloat16
    )
    attended = accumulated.reshape(shard_rows, kv_local * group_size * HEAD_DIM).astype(
        jnp.bfloat16
    )
    return (attended, jnp.transpose(key_mass))


def solution(mesh):
    return jax.shard_map(
        per_device,
        mesh=mesh,
        in_specs=(
            P(("dp", "seq"), "heads"),
            P(None, "heads"),
            P("heads", "seq"),
            P(),
            P(("dp", "seq"), "heads"),
            P(("dp", "seq"), "heads"),
            P(("dp", "seq"), "heads"),
            P("dp"),
        ),
        out_specs=(P(("dp", "seq"), "heads"), P("heads", ("dp", "seq"))),
        check_vma=False,
    )
```

profile of v0, /device:TPU:0, one launch (start us, length us, event | category | flops | bytes accessed | tf_op | source)
XLA Modules:
  0.0 134.4 jit_solution(9459303195213991430)
XLA Ops:
  7.2 0.0 copy-start
  7.2 0.0 copy-start.2
  7.2 0.0 copy-start.1
  7.2 0.0 copy-start.6
  7.2 0.0 copy-start.3
  7.2 0.0 copy-start.5
  7.2 0.0 all-gather.2.cloned.1.call-start
  7.3 0.7 all-gather.2.cloned.1.call-update
  8.0 0.0 all-reduce.2.cloned.1.call-start
  8.0 0.2 copy-done.2
  8.2 4.8 %collective-permute-start = (bf16[3,2048]{1,0:T(4,128)(2,1)S(1)}, bf16[3,2048]{1,0:T(4,128)(2,1)S(1)}, u32[]{:S(2)}, u32[]{:S(2)}) collective-permute-start(bf16[3,2048]{1,0:T(4,128)(2,1)S(1)} %slice.28), channel_id=1, source_target_pairs={{0,16},{1,17},{2,18},{3,19},{4,20},{5,21},{6,22},{7,23},{8,24},{9,... | collective-permute-start | bytes 36872 | tf_op jit(solution)/shard_map/ppermute | solution.py:19
  13.1 0.0 copy-done.1
  13.1 1.3 gather_fusion
  14.4 1.9 %gather_fusion.1 = s32[256]{0:T(256)S(1)} fusion(s32[256]{0:T(256)S(1)} %copy-done.1, s32[1024]{0:T(1024)S(1)} %pad_clamp_fusion.1), kind=kCustom, calls=%fused_computation.clone | custom fusion | bytes 3072 | tf_op jit(solution)/shard_map/while/body/eval_jaxpr/jit(_take)/gather | solution.py:69
  16.4 0.0 copy-done.6
  16.5 0.0 copy-done.3
  16.5 0.3 copy.24
  16.8 0.0 copy-done.5
  16.8 0.1 copy.23
  16.9 0.0 collective-permute-done
  16.9 0.1 maximum_convert_fusion
  17.0 52.0 %all-gather.2.cloned.1.call-done = bf16[2048,1024]{1,0:T(8,128)(2,1)} async-done(((bf16[2048,512]{1,0:T(8,128)(2,1)}), bf16[2048,1024]{1,0:T(8,128)(2,1)}) %all-gather.2.cloned.1.call-update) | async-done | bytes 4194320 | tf_op jit(solution)/shard_map/all_gather | solution.py:49
  69.1 4.0 %fusion.15 = f32[128,1024]{1,0:T(8,128)} fusion(bf16[2048,1024]{1,0:T(8,128)(2,1)} %all-gather.2.cloned.1.call-done, f32[131,2048]{1,0:T(8,128)S(1)} %maximum_convert_fusion, f32[2048]{0:T(1024)S(1)} %bitcast.70, f32[2048]{0:T(1024)S(1)} %bitcast.71, f32[2048]{0:T(1024)S(1)} %bitcast.69, f32[2048]{0:T(1024)S(1)} %bitcast.68), kind=kOutput, calls=%fused_computation.31 | convolution fusion | flops 538968064 | bytes 8945664 | tf_op jit(solution)/shard_map/dot_general | solution.py:47
  73.1 0.0 all-reduce.2.cloned.1.call-update
  73.1 0.0 reduce-scatter.4.cloned.1.call-start
  73.2 0.7 fusion.21
  74.6 5.0 %all_gather.12 = bf16[256,256]{0,1:T(8,128)(2,1)S(1)} all-gather(bf16[128,256]{0,1:T(8,128)(2,1)S(1)} %copy.23), channel_id=1, replica_groups=mesh['seq'=2,'heads'=4,'dp'=4] {'seq'}, dimensions={0}, use_global_device_ids=true | all-gather | bytes 196608 | tf_op jit(solution)/shard_map/all_gather | solution.py:79
  79.6 0.0 copy-done.4
  79.6 4.9 %all_gather.15 = bf16[256,256]{1,0:T(8,128)(2,1)S(1)} all-gather(bf16[128,256]{1,0:T(8,128)(2,1)S(1)} %copy-done.4), channel_id=1, replica_groups=mesh['seq'=2,'heads'=4,'dp'=4] {'seq'}, dimensions={0}, use_global_device_ids=true | all-gather | bytes 196608 | tf_op jit(solution)/shard_map/all_gather | solution.py:80
  84.5 21.9 %all-reduce.2.cloned.1.call-done = f32[128,1024]{1,0:T(8,128)} async-done(((f32[128,1024]{1,0:T(8,128)}), f32[128,1024]{1,0:T(8,128)}) %all-reduce.2.cloned.1.call-update) | async-done | bytes 524304 | tf_op jit(solution)/shard_map/psum | solution.py:55
  106.4 1.3 fusion.23
  107.7 4.2 %all_gather.14 = bf16[256,2]{0,1:T(2,128)(2,1)S(1)} all-gather(bf16[128,2]{0,1:T(2,128)(2,1)S(1)} %constant_dynamic-slice_fusion), channel_id=1, replica_groups=mesh['seq'=2,'heads'=4,'dp'=4] {'seq'}, dimensions={0}, use_global_device_ids=true | all-gather | bytes 1536 | tf_op jit(solution)/shard_map/all_gather | solution.py:81
  112.0 1.4 %conditional.2 = ((f32[2,8,128]{2,1,0:T(8,128)S(1)}, f32[2,8,128]{2,1,0:T(8,128)S(1)})) conditional(s32[]{:T(128)} %convert_element_type.40, (f32[2,8,128]{2,1,0:T(8,128)S(1)}, f32[2,8,128]{2,1,0:T(8,128)S(1)}) %tuple.29, (pred[128,256]{1,0:T(8,128)(4,1)S(1)}, bf16[256,2,128]{0,2,1:T(8,128)(2,1)S(1)}, bf16[128,2,8,128]{0,3,2,1:T(8,128)(2,1)S(1)}, ...), branch_computations={%region_2.4_spmd, %region_3.7_spmd} | conditional | flops 139465216 | bytes 5094424 | solution.py:104
  112.0 0.1 copy.25
  112.1 0.5 fusion
  112.7 0.6 select_reduce_fusion
  113.3 0.1 broadcast_in_dim.88
  113.4 1.8 %conditional.3 = (f32[128,2,8,128]{3,0,2,1:T(8,128)S(1)}, f32[256,2]{0,1:T(2,128)S(1)}) conditional(s32[]{:T(128)} %convert_element_type.40, f32[128,2,8,128]{3,0,2,1:T(8,128)S(1)} %broadcast_in_dim.88, (pred[128,256]{1,0:T(8,128)(4,1)S(1)}, bf16[256,2,128]{0,2,1:T(8,128)(2,1)S(1)}, bf16[128,2,8,128]{0,3,2,1:T(8,128)(2,1)S(1)}, ...), branch_computations={%region_6.8_spmd, %region_7.10_spmd} | conditional | flops 272892416 | bytes 5303312 | solution.py:135
  113.5 1.2 fusion.27
  114.7 0.4 fusion.7
  115.2 0.8 copy.42
  116.0 0.0 reduce-scatter.4.cloned.1.call-update
  116.0 0.1 convert_element_type.45
  116.1 0.3 copy.30
  116.5 0.9 copy.49
  117.4 9.0 %reduce-scatter.4.cloned.1.call-done = f32[128,2]{1,0:T(8,128)} async-done(((f32[256,2]{1,0:T(8,128)}), f32[128,2]{1,0:T(8,128)}) %reduce-scatter.4.cloned.1.call-update) | async-done | bytes 1040
  126.4 0.8 convert_element_type.48
  127.3 0.6 copy.45
  (20 shorter events, 0.2 us)
Async XLA Ops:
  7.2 99.2 %copy-start = (bf16[1024,8]{0,1:T(8,128)(2,1)S(1)}, bf16[1024,8]{0,1:T(8,128)(2,1)}, u32[]{:S(2)}) copy-start(bf16[1024,8]{0,1:T(8,128)(2,1)} %param.17) | copy-start | bytes 49156
  7.2 1.0 copy-start.2
  7.2 5.9 %copy-start.1 = (s32[256]{0:T(256)S(1)}, s32[256]{0:T(256)}, u32[]{:S(2)}) copy-start(s32[256]{0:T(256)} %param.21) | copy-start | bytes 3076
  7.2 9.2 %copy-start.6 = (bf16[4,2048]{1,0:T(4,128)(2,1)S(1)}, bf16[4,2048]{1,0:T(4,128)(2,1)}, u32[]{:S(2)}) copy-start(bf16[4,2048]{1,0:T(4,128)(2,1)} %param.15) | copy-start | bytes 49156
  7.2 9.3 %copy-start.3 = (bf16[128,2048]{1,0:T(8,128)(2,1)S(1)}, bf16[128,2048]{1,0:T(8,128)(2,1)}, u32[]{:S(2)}) copy-start(bf16[128,2048]{1,0:T(8,128)(2,1)} %param.18) | copy-start | bytes 1572868
  7.2 9.5 %copy-start.5 = (bf16[128,256]{1,0:T(8,128)(2,1)S(1)}, bf16[128,256]{1,0:T(8,128)(2,1)}, u32[]{:S(2)}) copy-start(bf16[128,256]{1,0:T(8,128)(2,1)} %param.19) | copy-start | bytes 196612
  7.2 61.9 %all-gather.2.cloned.1.call-start = ((), (), s32[]{:S(2)}) async-start(), calls=%async_computation.1 | async-start | bytes 6291456 | tf_op jit(solution)/shard_map/all_gather | solution.py:49
  8.0 98.4 %all-reduce.2.cloned.1.call-start = ((), (), s32[]{:S(2)}) async-start(), calls=%async_computation.2 | async-start | bytes 1048576 | tf_op jit(solution)/shard_map/psum | solution.py:55
  8.2 8.6 %collective-permute-start = (bf16[3,2048]{1,0:T(4,128)(2,1)S(1)}, bf16[3,2048]{1,0:T(4,128)(2,1)S(1)}, u32[]{:S(2)}, u32[]{:S(2)}) collective-permute-start(bf16[3,2048]{1,0:T(4,128)(2,1)S(1)} %slice.28), channel_id=1, source_target_pairs={{0,16},{1,17},{2,18},{3,19},{4,20},{5,21},{6,22},{7,23},{8,24},{9,... | collective-permute-start | bytes 36872 | tf_op jit(solution)/shard_map/ppermute | solution.py:19
  69.1 10.5 %copy-start.4 = (bf16[128,256]{1,0:T(8,128)(2,1)S(1)}, bf16[128,256]{1,0:T(8,128)(2,1)}, u32[]{:S(2)}) copy-start(bf16[128,256]{1,0:T(8,128)(2,1)} %param.20) | copy-start | bytes 196612
  73.1 53.3 %reduce-scatter.4.cloned.1.call-start = ((), (), s32[]{:S(2)}) async-start(), calls=%async_computation.3 | async-start | bytes 196608
Sparse Core Ops, SparseCore 0:
  9.6 59.4 all-gather.1
  73.3 33.0 all-reduce.1
  116.1 10.2 reduce-scatter.3
where the time goes:
time: 135 us; the launch traced here: 134 us
  waiting for transfers between devices  83.7 us (62%)
  between operations  14.7 us (11%)
  blocking collectives  14.1 us (10%)
  matrix products  7.55 us (6%)
  local copies, waits for them, and re-layouts  6.8 us (5%)
  starting transfers between devices  4.96 us (4%)
  other arithmetic  2.53 us (2%)
    all_gather x1, waiting for transfers between devices, per_device(): lax.all_gather(gate_in, 'seq', axis=1, tiled=True)  52 us
    psum x1, waiting for transfers between devices, per_device(): hidden = jax.nn.silu(lax.psum(partial_hidden, 'heads')).astype(jnp.bfloat16)  21.9 us
    unnamed x4, waiting for transfers between devices  9.74 us
    all_gather x1, blocking collectives, per_device(): lax.all_gather(own_keys, 'seq', axis=0, tiled=True)  4.96 us
    all_gather x1, blocking collectives, per_device(): lax.all_gather(own_values, 'seq', axis=0, tiled=True)  4.93 us
    ppermute x1, starting transfers between devices, from_behind(): return lax.ppermute(block, axis, route)  4.84 us
    all_gather x1, blocking collectives, per_device(): lax.all_gather(own_bias, 'seq', axis=0, tiled=True)  4.22 us
    dot_general x1, matrix products, per_device(): jnp.dot(mixed_rows, lax.all_gather(gate_in, 'seq', axis=1, tiled=True), p...  4.03 us
  transfers between devices with their start and end apart: 4, of which 3 were waited for; matrix products, arithmetic and copies ran while one was open for 4% of the time, Pallas kernels for 0%

commit v1 on v0

--- a/solution.py
+++ b/solution.py
@@ -3,6 +3,8 @@
 import jax
 import jax.numpy as jnp
 from jax import lax
+from jax.experimental import pallas as pl
+from jax.experimental.pallas import tpu as pltpu
 from jax.sharding import PartitionSpec as P
 
 QUERY_HEADS = 64
@@ -11,6 +13,195 @@
 
 
 NEG_FILL = -1e30
+RIM_ROWS = 16
+VMEM_BYTES = 48 * 1024 * 1024
+
+
+def mix_project_kernel(rows_ref, rim_ref, taps_ref, gate_ref, out_ref, widened):
+    rows, features = rows_ref.shape
+    tap_count = taps_ref.shape[0]
+    lead = widened.shape[0] - rows
+    parts, _, width = out_ref.shape
+    tile = math.gcd(features, 512)
+    total = jnp.zeros((rows, parts * width), jnp.float32)
+    for start in range(0, features, tile):
+        columns = slice(start, start + tile)
+        rim = rim_ref[:, columns].astype(jnp.float32)
+        widened[:lead, columns] = rim[rim.shape[0] - lead :]
+        widened[lead:, columns] = rows_ref[:, columns].astype(jnp.float32)
+        summed = jnp.zeros((rows, tile), jnp.float32)
+        for back in range(tap_count):
+            tap = taps_ref[back : back + 1, columns].astype(jnp.float32)
+            summed = summed + tap * widened[lead - back : lead - back + rows, columns]
+        total = total + jnp.dot(
+            summed.astype(jnp.bfloat16), gate_ref[columns, :], preferred_element_type=jnp.float32
+        )
+    for part in range(parts):
+        out_ref[part] = total[:, part * width : (part + 1) * width]
+
+
+def mix_project(block, rim, conv_taps, gate_in, parts):
+    rows, features = block.shape
+    width = gate_in.shape[1] // parts
+    return pl.pallas_call(
+        mix_project_kernel,
+        out_shape=jax.ShapeDtypeStruct((parts, rows, width), jnp.float32),
+        scratch_shapes=[pltpu.VMEM((rows + 8, features), jnp.float32)],
+        compiler_params=pltpu.CompilerParams(vmem_limit_bytes=VMEM_BYTES),
+        cost_estimate=pl.CostEstimate(
+            flops=2 * rows * features * gate_in.shape[1],
+            bytes_accessed=2 * (block.size + gate_in.size) + 4 * rows * gate_in.shape[1],
+            transcendentals=0,
+        ),
+    )(block, rim, conv_taps, gate_in)
+
+
+def logits_kernel(rank_ref, own_ref, peer_ref, gate_out_ref, out_ref):
+    first = rank_ref[0] == 0
+    shares = []
+    for ref in (own_ref, peer_ref):
+        pre = ref[0]
+        for part in range(1, ref.shape[0]):
+            pre = pre + ref[part]
+        hidden = (pre / (1.0 + jnp.exp(-pre))).astype(jnp.bfloat16)
+        shares.append(
+            lax.dot_general(
+                gate_out_ref[...],
+                hidden,
+                (((0,), (1,)), ((), ())),
+                preferred_element_type=jnp.float32,
+            )
+        )
+    own, peer = shares
+    out_ref[0] = jnp.where(first, own, peer)
+    out_ref[1] = jnp.where(first, peer, own)
+
+
+def logits_share(seq_rank, own_sum, peer_sum, gate_out):
+    rows = own_sum.shape[1]
+    return pl.pallas_call(
+        logits_kernel,
+        in_specs=[pl.BlockSpec(memory_space=pltpu.SMEM)]
+        + [pl.BlockSpec(memory_space=pltpu.VMEM)] * 3,
+        out_shape=jax.ShapeDtypeStruct((2, gate_out.shape[1], rows), jnp.float32),
+        compiler_params=pltpu.CompilerParams(vmem_limit_bytes=VMEM_BYTES),
+    )(jnp.reshape(seq_rank, (1,)), own_sum, peer_sum, gate_out)
+
+
+def attention_kernel(
+    rank_ref,
+    logits_ref,
+    segments_ref,
+    queries_ref,
+    keys_ref,
+    behind_keys_ref,
+    values_ref,
+    behind_values_ref,
+    attended_ref,
+    own_mass_ref,
+    behind_mass_ref,
+    retention,
+):
+    seq_rank, head_rank = rank_ref[0], rank_ref[1]
+    rows = queries_ref.shape[0]
+    kv_local = keys_ref.shape[1] // HEAD_DIM
+    group_size = queries_ref.shape[1] // keys_ref.shape[1]
+    score_scale = 1.0 / math.sqrt(HEAD_DIM)
+    logits = logits_ref[0]
+    for share in range(1, logits_ref.shape[0]):
+        logits = logits + logits_ref[share]
+    log_gate = jnp.minimum(logits, 0.0) - jnp.log1p(jnp.exp(-jnp.abs(logits)))
+    retention[...] = log_gate.astype(jnp.bfloat16).astype(jnp.float32)
+
+    own_segments = segments_ref[pl.ds(seq_rank, 1), :]
+    behind_segments = segments_ref[pl.ds(0, 1), :]
+    query_segments = jnp.transpose(jnp.broadcast_to(own_segments, (rows, rows)))
+    query_at = lax.broadcasted_iota(jnp.int32, (rows, rows), 0)
+    key_at = lax.broadcasted_iota(jnp.int32, (rows, rows), 1)
+    see_own = (key_at <= query_at) & (query_segments == own_segments)
+    see_behind = (query_segments == behind_segments) & (seq_rank > 0)
+    visible = jnp.concatenate([see_behind, see_own], axis=1)
+
+    for g in range(kv_local):
+        columns = slice(g * HEAD_DIM, (g + 1) * HEAD_DIM)
+        keys = jnp.concatenate([behind_keys_ref[:, columns], keys_ref[:, columns]], axis=0)
+        values = jnp.concatenate([behind_values_ref[:, columns], values_ref[:, columns]], axis=0)
+        row = head_rank * kv_local + g
+        bias = jnp.concatenate(
+            [retention[0, pl.ds(row, 1), :], retention[seq_rank, pl.ds(row, 1), :]], axis=1
+        )
+        mass = jnp.zeros((1, 2 * rows), jnp.float32)
+        for e in range(group_size):
+            at = (g * group_size + e) * HEAD_DIM
+            scores = lax.dot_general(
+                queries_ref[:, at : at + HEAD_DIM],
+                keys,
+                (((1,), (1,)), ((), ())),
+                preferred_element_type=jnp.float32,
+            )
+            scores = jnp.where(visible, scores * score_scale + bias, NEG_FILL)
+            weights = jnp.exp(scores - jnp.max(scores, axis=1, keepdims=True))
+            weights = weights * (1.0 / jnp.sum(weights, axis=1, keepdims=True))
+            mass = mass + jnp.sum(weights, axis=0, keepdims=True)
+            attended_ref[:, at : at + HEAD_DIM] = jnp.dot(
+                weights.astype(jnp.bfloat16), values, preferred_element_type=jnp.float32
+            ).astype(jnp.bfloat16)
+        mass = mass / group_size
+        behind_mass_ref[g : g + 1, :] = mass[:, :rows]
+        own_mass_ref[g : g + 1, :] = mass[:, rows:]
+
+
+def attention(ranks, logit_shares, segments, queries, keys, behind_keys, values, behind_values):
+    rows = queries.shape[0]
+    kv_local = keys.shape[1] // HEAD_DIM
+    mass = jax.ShapeDtypeStruct((kv_local, rows), jnp.float32)
+    return pl.pallas_call(
+        attention_kernel,
+        in_specs=[pl.BlockSpec(memory_space=pltpu.SMEM)]
+        + [pl.BlockSpec(memory_space=pltpu.VMEM)] * 7,
+        out_shape=(jax.ShapeDtypeStruct(queries.shape, jnp.bfloat16), mass, mass),
+        scratch_shapes=[pltpu.VMEM(logit_shares.shape[1:], jnp.float32)],
+        compiler_params=pltpu.CompilerParams(vmem_limit_bytes=VMEM_BYTES),
+    )(ranks, logit_shares, segments, queries, keys, behind_keys, values, behind_values)
+
+
+def pair_device(
+    activations, conv_taps, gate_in, gate_out, queries, key_vectors, value_vectors, segment_ids
+):
+    rows = activations.shape[0]
+    parts = lax.axis_size("heads")
+    seq_rank = lax.axis_index("seq")
+    head_rank = lax.axis_index("heads")
+    tail = activations[rows - RIM_ROWS :]
+    rim = lax.ppermute(tail, "seq", [(0, 1)])
+    peer_rows = lax.ppermute(activations, "seq", [(0, 1), (1, 0)])
+    behind_keys = lax.ppermute(key_vectors, "seq", [(0, 1)])
+    behind_values = lax.ppermute(value_vectors, "seq", [(0, 1)])
+    peer_rim = jnp.where(seq_rank == 0, tail, jnp.zeros_like(tail))
+
+    own_part = mix_project(activations, rim, conv_taps, gate_in, parts)
+    own_sum = lax.all_to_all(own_part, "heads", 0, 0, tiled=True)
+    peer_part = mix_project(peer_rows, peer_rim, conv_taps, gate_in, parts)
+    peer_sum = lax.all_to_all(peer_part, "heads", 0, 0, tiled=True)
+    width = own_part.shape[2]
+    gate_rows = lax.dynamic_slice_in_dim(
+        gate_out, (seq_rank * parts + head_rank) * width, width, 0
+    )
+    share = logits_share(seq_rank, own_sum, peer_sum, gate_rows)
+    shares = lax.all_gather(share, ("seq", "heads"), axis=0)
+    ranks = jnp.stack([seq_rank, head_rank]).astype(jnp.int32)
+    attended, own_mass, behind_mass = attention(
+        ranks,
+        shares,
+        segment_ids.reshape(2, rows),
+        queries,
+        key_vectors,
+        behind_keys,
+        value_vectors,
+        behind_values,
+    )
+    key_mass = own_mass + lax.ppermute(behind_mass, "seq", [(1, 0)])
+    return (attended, key_mass.astype(jnp.bfloat16))
 
 
 def from_behind(block, axis, distance):
@@ -28,7 +219,7 @@
     return jnp.where(allowed[None, None], scores, NEG_FILL)
 
 
-def per_device(
+def ring_device(
     activations, conv_taps, gate_in, gate_out, queries, key_vectors, value_vectors, segment_ids
 ):
     shard_rows = activations.shape[0]
@@ -151,7 +342,7 @@
 
 def solution(mesh):
     return jax.shard_map(
-        per_device,
+        pair_device if mesh.shape["seq"] == 2 else ring_device,
         mesh=mesh,
         in_specs=(
             P(("dp", "seq"), "heads"),

time: 135 us -> 60.6 us (0.45)
  waiting for transfers between devices: 83.7 us -> 19.9 us
  starting transfers between devices: 4.96 us -> 19.9 us
  between operations: 14.7 us -> 0.73 us
  matrix products: 7.55 us -> 0 us
  Pallas kernels: 0 us -> 6.33 us
  blocking collectives: 14.1 us -> 8.07 us
  local copies, waits for them, and re-layouts: 6.8 us -> 3.51 us
    all_gather x1 -> x0, waiting for transfers between devices: 52 us -> none  [per_device(): lax.all_gather(gate_in, 'seq', axis=1, tiled=True)]
    psum x1 -> x0, waiting for transfers between devices: 21.9 us -> none  [per_device(): hidden = jax.nn.silu(lax.psum(partial_hidden, 'heads')).astype(jnp.bfloat16)]
    ppermute x1 -> x5, waiting for transfers between devices: 0.01 us -> 14.2 us  [the longest x1 9.99 us: pair_device(): rim = lax.ppermute(tail, 'seq', [(0, 1)])]
    unnamed x4 -> x0, waiting for transfers between devices: 9.74 us -> none
    ppermute x1 -> x5, starting transfers between devices: 4.84 us -> 13.1 us  [the longest x1 5.02 us: pair_device(): behind_keys = lax.ppermute(key_vectors, 'seq', [(0, 1)])]
    dot_general x5 -> x0, matrix products: 7.55 us -> none  [the longest x1 4.03 us: per_device(): jnp.dot(mixed_rows, lax.all_gather(gate_in, 'seq', axis=1, tiled=True), p...]
    all_to_all x0 -> x2, starting transfers between devices: none -> 6.81 us  [the longest x1 3.41 us: pair_device(): own_sum = lax.all_to_all(own_part, 'heads', 0, 0, tiled=True)]
    pallas_call x0 -> x4, Pallas kernels: none -> 6.33 us  [the longest x1 3.32 us: attention(): pl.pallas_call(attention_kernel, in_specs=[pl.BlockSpec(memory_space=pltp...]
  transfers between devices with their start and end apart: 4 -> 7, of which waited for: 3 -> 3; matrix products, arithmetic and copies ran while one was open for 4% -> 2% of each run, Pallas kernels for 0% -> 5%
where the time goes in v1:
time: 60.6 us; the launch traced here: 60 us
  starting transfers between devices  19.9 us (33%)
  waiting for transfers between devices  19.9 us (33%)
  blocking collectives  8.07 us (13%)
  Pallas kernels  6.33 us (10%)
  local copies, waits for them, and re-layouts  3.51 us (6%)
  other arithmetic  1.47 us (2%)
  between operations  0.73 us (1%)
    ppermute x1, waiting for transfers between devices, pair_device(): rim = lax.ppermute(tail, 'seq', [(0, 1)])  9.99 us
    all_gather x1, blocking collectives, pair_device(): shares = lax.all_gather(share, ('seq', 'heads'), axis=0)  8.07 us
    all_to_all x1, waiting for transfers between devices, pair_device(): peer_sum = lax.all_to_all(peer_part, 'heads', 0, 0, tiled=True)  5.77 us
    ppermute x1, starting transfers between devices, pair_device(): behind_keys = lax.ppermute(key_vectors, 'seq', [(0, 1)])  5.02 us
    ppermute x1, waiting for transfers between devices, pair_device(): key_mass = own_mass + lax.ppermute(behind_mass, 'seq', [(1, 0)])  4.16 us
    unnamed x17, local copies, waits for them, and re-layouts  3.5 us
    all_to_all x1, starting transfers between devices, pair_device(): own_sum = lax.all_to_all(own_part, 'heads', 0, 0, tiled=True)  3.41 us
    all_to_all x1, starting transfers between devices, pair_device(): peer_sum = lax.all_to_all(peer_part, 'heads', 0, 0, tiled=True)  3.41 us
  transfers between devices with their start and end apart: 7, of which 3 were waited for; matrix products, arithmetic and copies ran while one was open for 2% of the time, Pallas kernels for 5%

profile of v1, /device:TPU:0, one launch (start us, length us, event | category | flops | bytes accessed | tf_op | source)
XLA Modules:
  0.0 60.0 jit_solution(1557522466917356490)
XLA Ops:
  0.6 0.0 copy-start
  0.6 0.0 copy-start.6
  0.7 3.0 %collective-permute-start.1 = (bf16[128,2048]{1,0:T(8,128)(2,1)}, bf16[128,2048]{1,0:T(8,128)(2,1)S(1)}, u32[]{:S(2)}, u32[]{:S(2)}) collective-permute-start(bf16[128,2048]{1,0:T(8,128)(2,1)} %rows_ref.1), channel_id=1, source_target_pairs={{0,16},{16,0},{1,17},{17,1},{2,18},{18,2},{3,19},{19,3},{4,20},{20... | collective-permute-start | bytes 1572872 | tf_op jit(solution)/shard_map/ppermute | solution.py:177
  3.7 0.9 %broadcast_select_fusion = (bf16[16,2048]{1,0:T(8,128)(2,1)S(1)}, bf16[16,2048]{1,0:T(8,128)(2,1)S(1)}) fusion(pred[]{:T(512)S(6)} %eq.3, bf16[128,2048]{1,0:T(8,128)(2,1)} %rows_ref.1), kind=kLoop, calls=%fused_computation | loop fusion | flops 32768 | bytes 196609 | tf_op jit(solution)/shard_map/jit(_where)/select_n | solution.py:180
  4.5 1.9 %collective-permute-start = (bf16[16,2048]{1,0:T(8,128)(2,1)S(1)}, bf16[16,2048]{1,0:T(8,128)(2,1)S(1)}, u32[]{:S(2)}, u32[]{:S(2)}) collective-permute-start(bf16[16,2048]{1,0:T(8,128)(2,1)S(1)} %get-tuple-element.9), channel_id=1, source_target_pairs={{0,16},{1,17},{2,18},{3,19},{4,20},{5,21},{6,22},{7,23},{8,24},{9,... | collective-permute-start | bytes 196616 | tf_op jit(solution)/shard_map/ppermute | solution.py:176
  6.5 10.0 %collective-permute-done.rim_ref = bf16[16,2048]{1,0:T(8,128)(2,1)S(1)} collective-permute-done((bf16[16,2048]{1,0:T(8,128)(2,1)S(1)}, bf16[16,2048]{1,0:T(8,128)(2,1)S(1)}, u32[]{:S(2)}, u32[]{:S(2)}) %collective-permute-start) | collective-permute-done | bytes 65568 | tf_op jit(solution)/shard_map/ppermute | solution.py:176
  16.5 0.0 copy-start.1
  16.5 1.6 %copy-done.1 = bf16[2048,512]{1,0:T(8,128)(2,1)S(1)} copy-done((bf16[2048,512]{1,0:T(8,128)(2,1)S(1)}, bf16[2048,512]{1,0:T(8,128)(2,1)}, u32[]{:S(2)}) %copy-start.1) | copy-done | bytes 2097176
  18.0 0.0 copy-start.3
  18.1 1.0 %copy-done.3 = bf16[128,2048]{1,0:T(8,128)(2,1)S(1)} copy-done((bf16[128,2048]{1,0:T(8,128)(2,1)S(1)}, bf16[128,2048]{1,0:T(8,128)(2,1)}, u32[]{:S(2)}) %copy-start.3) | copy-done | bytes 524312
  19.1 0.0 copy-start.5
  19.1 0.7 %copy-done.5 = bf16[4,2048]{1,0:T(4,128)(2,1)S(1)} copy-done((bf16[4,2048]{1,0:T(4,128)(2,1)S(1)}, bf16[4,2048]{1,0:T(4,128)(2,1)}, u32[]{:S(2)}) %copy-start.5) | copy-done | bytes 16408
  19.8 0.0 copy-start.2
  19.8 1.4 %shard_map.95 = f32[4,128,128]{2,1,0:T(8,128)} custom-call(bf16[128,2048]{1,0:T(8,128)(2,1)S(1)} %copy-done.3, bf16[16,2048]{1,0:T(8,128)(2,1)S(1)} %collective-permute-done.rim_ref, bf16[4,2048]{1,0:T(4,128)(2,1)S(1)} %copy-done.5, bf16[2048,512]{1,0:T(8,128)(2,1)S(1)} %copy-done.1), custom_call_target="tpu_custom_call" | custom-call | flops 268435456 | bytes 2883584 | tf_op jit(solution)/shard_map/pallas_call | solution.py:46
  21.2 3.4 %all-to-all-start = ((f32[4,128,128]{2,1,0:T(8,128)}), f32[4,128,128]{2,1,0:T(8,128)S(1)}, u32[]{:S(2)}, u32[]{:S(2)}) async-start(f32[4,128,128]{2,1,0:T(8,128)} %shard_map.95), calls=%async_computation | async-start | bytes 524288 | tf_op jit(solution)/shard_map/all_to_all | solution.py:183
  24.6 5.0 %collective-permute-start.2 = (bf16[128,256]{1,0:T(8,128)(2,1)}, bf16[128,256]{1,0:T(8,128)(2,1)}, u32[]{:S(2)}, u32[]{:S(2)}) collective-permute-start(bf16[128,256]{1,0:T(8,128)(2,1)} %keys_ref.1), channel_id=1, source_target_pairs={{0,16},{1,17},{2,18},{3,19},{4,20},{5,21},{6,22},{7,23},{8,24},{9,... | collective-permute-start | bytes 196616 | tf_op jit(solution)/shard_map/ppermute | solution.py:178
  29.7 1.9 %collective-permute-start.3 = (bf16[128,256]{1,0:T(8,128)(2,1)}, bf16[128,256]{1,0:T(8,128)(2,1)}, u32[]{:S(2)}, u32[]{:S(2)}) collective-permute-start(bf16[128,256]{1,0:T(8,128)(2,1)} %values_ref.1), channel_id=1, source_target_pairs={{0,16},{1,17},{2,18},{3,19},{4,20},{5,21},{6,22},{7,23},{8,24},{9,... | collective-permute-start | bytes 196616 | tf_op jit(solution)/shard_map/ppermute | solution.py:179
  31.6 0.0 copy-start.4
  31.6 0.0 copy-start.7
  31.6 0.0 collective-permute-done.1.rows_ref
  31.6 0.0 copy-done.6
  31.6 0.0 copy-done.2
  31.6 1.4 %shard_map.96 = f32[4,128,128]{2,1,0:T(8,128)} custom-call(bf16[128,2048]{1,0:T(8,128)(2,1)S(1)} %collective-permute-done.1.rows_ref, bf16[16,2048]{1,0:T(8,128)(2,1)S(1)} %get-tuple-element.8.rim_ref, bf16[4,2048]{1,0:T(4,128)(2,1)S(1)} %copy-done.6, bf16[2048,512]{1,0:T(8,128)(2,1)S(1)} %copy-done.2), custom_call_target="tpu_custom_call" | custom-call | flops 268435456 | bytes 2883584 | tf_op jit(solution)/shard_map/pallas_call | solution.py:46
  33.0 0.0 all-to-all-done.own_ref
  33.0 3.4 %all-to-all-start.1 = ((f32[4,128,128]{2,1,0:T(8,128)}), f32[4,128,128]{2,1,0:T(8,128)S(1)}, u32[]{:S(2)}, u32[]{:S(2)}) async-start(f32[4,128,128]{2,1,0:T(8,128)} %shard_map.96), calls=%async_computation.1 | async-start | bytes 524288 | tf_op jit(solution)/shard_map/all_to_all | solution.py:185
  36.4 0.0 copy-done
  36.5 0.1 pad_add_fusion.rank_ref
  36.5 0.1 copy.12.gate_out_ref
  36.7 5.8 %all-to-all-done.1.peer_ref = f32[4,128,128]{2,1,0:T(8,128)S(1)} async-done(((f32[4,128,128]{2,1,0:T(8,128)}), f32[4,128,128]{2,1,0:T(8,128)S(1)}, u32[]{:S(2)}, u32[]{:S(2)}) %all-to-all-start.1) | async-done | bytes 262176 | tf_op jit(solution)/shard_map/all_to_all | solution.py:185
  42.4 0.2 shard_map.97
  42.6 8.1 %all-gather = f32[16,8,128]{2,1,0:T(8,128)S(1)} all-gather(f32[2,8,128]{2,1,0:T(8,128)S(1)} %shard_map.97), channel_id=2, replica_groups=mesh['seq'=2,'heads'=4,'dp'=4] {'seq','heads'}, dimensions={0}, use_global_device_ids=true | all-gather | bytes 73728 | tf_op jit(solution)/shard_map/all_gather | solution.py:191
  50.7 0.0 collective-permute-done.2.behind_keys_ref
  50.7 0.0 collective-permute-done.3.behind_values_ref
  50.7 0.0 copy-done.4
  50.7 0.0 copy-done.7
  50.7 3.3 %shard_map.98 = (bf16[128,2048]{1,0:T(8,128)(2,1)}, f32[2,128]{1,0:T(2,128)S(1)}, f32[2,128]{1,0:T(2,128)S(1)}) custom-call(s32[2]{0:T(128)S(1)} %pad_add_fusion.rank_ref, f32[8,2,8,128]{3,2,1,0:T(8,128)S(1)} %bitcast.4, s32[2,128]{1,0:T(2,128)S(1)} %bitcast.5, bf16[128,2048]{1,0:T(8,128)(2,1)S(1)} %copy-done.4, bf16[128,256]{1,0:T(8,128)(2,1)} %keys_ref.1, ...), custom_call_target="tpu_custom_call" | custom-call | tf_op jit(solution)/shard_map/pallas_call | solution.py:158
  54.0 1.3 %collective-permute-start.4 = (f32[2,128]{1,0:T(2,128)S(1)}, f32[2,128]{1,0:T(2,128)S(1)}, u32[]{:S(2)}, u32[]{:S(2)}) collective-permute-start(f32[2,128]{1,0:T(2,128)S(1)} %get-tuple-element.7), channel_id=1, source_target_pairs={{16,0},{17,1},{18,2},{19,3},{20,4},{21,5},{22,6},{23,7},{24,8},{25... | collective-permute-start | bytes 3080 | tf_op jit(solution)/shard_map/ppermute | solution.py:203
  55.3 4.2 %collective-permute-done.4 = f32[2,128]{1,0:T(2,128)S(1)} collective-permute-done((f32[2,128]{1,0:T(2,128)S(1)}, f32[2,128]{1,0:T(2,128)S(1)}, u32[]{:S(2)}, u32[]{:S(2)}) %collective-permute-start.4) | collective-permute-done | bytes 1056 | tf_op jit(solution)/shard_map/ppermute | solution.py:203
  59.5 0.5 add_convert_fusion
  (1 shorter events, 0.0 us)
Async XLA Ops:
  0.6 35.8 %copy-start = (bf16[1024,8]{0,1:T(8,128)(2,1)S(1)}, bf16[1024,8]{0,1:T(8,128)(2,1)}, u32[]{:S(2)}) copy-start(bf16[1024,8]{0,1:T(8,128)(2,1)} %param.11) | copy-start | bytes 49156
  0.6 30.9 %copy-start.6 = (bf16[4,2048]{1,0:T(4,128)(2,1)S(1)}, bf16[4,2048]{1,0:T(4,128)(2,1)}, u32[]{:S(2)}) copy-start(bf16[4,2048]{1,0:T(4,128)(2,1)} %taps_ref.3) | copy-start | bytes 49156
  0.7 30.9 %collective-permute-start.1 = (bf16[128,2048]{1,0:T(8,128)(2,1)}, bf16[128,2048]{1,0:T(8,128)(2,1)S(1)}, u32[]{:S(2)}, u32[]{:S(2)}) collective-permute-start(bf16[128,2048]{1,0:T(8,128)(2,1)} %rows_ref.1), channel_id=1, source_target_pairs={{0,16},{16,0},{1,17},{17,1},{2,18},{18,2},{3,19},{19,3},{4,20},{20... | collective-permute-start | bytes 1572872 | tf_op jit(solution)/shard_map/ppermute | solution.py:177
  4.5 11.9 %collective-permute-start = (bf16[16,2048]{1,0:T(8,128)(2,1)S(1)}, bf16[16,2048]{1,0:T(8,128)(2,1)S(1)}, u32[]{:S(2)}, u32[]{:S(2)}) collective-permute-start(bf16[16,2048]{1,0:T(8,128)(2,1)S(1)} %get-tuple-element.9), channel_id=1, source_target_pairs={{0,16},{1,17},{2,18},{3,19},{4,20},{5,21},{6,22},{7,23},{8,24},{9,... | collective-permute-start | bytes 196616 | tf_op jit(solution)/shard_map/ppermute | solution.py:176
  16.5 1.6 %copy-start.1 = (bf16[2048,512]{1,0:T(8,128)(2,1)S(1)}, bf16[2048,512]{1,0:T(8,128)(2,1)}, u32[]{:S(2)}) copy-start(bf16[2048,512]{1,0:T(8,128)(2,1)} %gate_ref.3) | copy-start | bytes 6291460
  18.0 1.0 %copy-start.3 = (bf16[128,2048]{1,0:T(8,128)(2,1)S(1)}, bf16[128,2048]{1,0:T(8,128)(2,1)}, u32[]{:S(2)}) copy-start(bf16[128,2048]{1,0:T(8,128)(2,1)} %rows_ref.1) | copy-start | bytes 1572868
  19.1 0.7 %copy-start.5 = (bf16[4,2048]{1,0:T(4,128)(2,1)S(1)}, bf16[4,2048]{1,0:T(4,128)(2,1)}, u32[]{:S(2)}) copy-start(bf16[4,2048]{1,0:T(4,128)(2,1)} %taps_ref.3) | copy-start | bytes 49156
  19.8 11.8 %copy-start.2 = (bf16[2048,512]{1,0:T(8,128)(2,1)S(1)}, bf16[2048,512]{1,0:T(8,128)(2,1)}, u32[]{:S(2)}) copy-start(bf16[2048,512]{1,0:T(8,128)(2,1)} %gate_ref.3) | copy-start | bytes 6291460
  21.2 11.8 %all-to-all-start = ((f32[4,128,128]{2,1,0:T(8,128)}), f32[4,128,128]{2,1,0:T(8,128)S(1)}, u32[]{:S(2)}, u32[]{:S(2)}) async-start(f32[4,128,128]{2,1,0:T(8,128)} %shard_map.95), calls=%async_computation | async-start | bytes 524288 | tf_op jit(solution)/shard_map/all_to_all | solution.py:183
  24.6 26.0 %collective-permute-start.2 = (bf16[128,256]{1,0:T(8,128)(2,1)}, bf16[128,256]{1,0:T(8,128)(2,1)}, u32[]{:S(2)}, u32[]{:S(2)}) collective-permute-start(bf16[128,256]{1,0:T(8,128)(2,1)} %keys_ref.1), channel_id=1, source_target_pairs={{0,16},{1,17},{2,18},{3,19},{4,20},{5,21},{6,22},{7,23},{8,24},{9,... | collective-permute-start | bytes 196616 | tf_op jit(solution)/shard_map/ppermute | solution.py:178
  29.7 21.0 %collective-permute-start.3 = (bf16[128,256]{1,0:T(8,128)(2,1)}, bf16[128,256]{1,0:T(8,128)(2,1)}, u32[]{:S(2)}, u32[]{:S(2)}) collective-permute-start(bf16[128,256]{1,0:T(8,128)(2,1)} %values_ref.1), channel_id=1, source_target_pairs={{0,16},{1,17},{2,18},{3,19},{4,20},{5,21},{6,22},{7,23},{8,24},{9,... | collective-permute-start | bytes 196616 | tf_op jit(solution)/shard_map/ppermute | solution.py:179
  31.6 19.1 %copy-start.4 = (bf16[128,2048]{1,0:T(8,128)(2,1)S(1)}, bf16[128,2048]{1,0:T(8,128)(2,1)}, u32[]{:S(2)}) copy-start(bf16[128,2048]{1,0:T(8,128)(2,1)} %queries_ref.1) | copy-start | bytes 1572868
  31.6 19.1 %copy-start.7 = (s32[256]{0:T(256)S(1)}, s32[256]{0:T(256)}, u32[]{:S(2)}) copy-start(s32[256]{0:T(256)} %param.15) | copy-start | bytes 3076
  33.0 9.4 %all-to-all-start.1 = ((f32[4,128,128]{2,1,0:T(8,128)}), f32[4,128,128]{2,1,0:T(8,128)S(1)}, u32[]{:S(2)}, u32[]{:S(2)}) async-start(f32[4,128,128]{2,1,0:T(8,128)} %shard_map.96), calls=%async_computation.1 | async-start | bytes 524288 | tf_op jit(solution)/shard_map/all_to_all | solution.py:185
  54.0 5.5 %collective-permute-start.4 = (f32[2,128]{1,0:T(2,128)S(1)}, f32[2,128]{1,0:T(2,128)S(1)}, u32[]{:S(2)}, u32[]{:S(2)}) collective-permute-start(f32[2,128]{1,0:T(2,128)S(1)} %get-tuple-element.7), channel_id=1, source_target_pairs={{16,0},{17,1},{18,2},{19,3},{20,4},{21,5},{22,6},{23,7},{24,8},{25... | collective-permute-start | bytes 3080 | tf_op jit(solution)/shard_map/ppermute | solution.py:203

commit v2 on v1

--- a/solution.py
+++ b/solution.py
@@ -17,86 +17,140 @@
 VMEM_BYTES = 48 * 1024 * 1024
 
 
-def mix_project_kernel(rows_ref, rim_ref, taps_ref, gate_ref, out_ref, widened):
+def convolve(widened, taps_ref, columns, lead, rows):
+    summed = jnp.zeros((rows, columns.stop - columns.start), jnp.float32)
+    for back in range(taps_ref.shape[0]):
+        tap = taps_ref[back : back + 1, columns].astype(jnp.float32)
+        summed = summed + tap * widened[lead - back : lead - back + rows, columns]
+    return summed.astype(jnp.bfloat16)
+
+
+def own_project_kernel(rows_ref, taps_ref, gate_ref, out_ref, widened):
     rows, features = rows_ref.shape
-    tap_count = taps_ref.shape[0]
-    lead = widened.shape[0] - rows
-    parts, _, width = out_ref.shape
     tile = math.gcd(features, 512)
-    total = jnp.zeros((rows, parts * width), jnp.float32)
+    total = jnp.zeros(out_ref.shape, jnp.float32)
     for start in range(0, features, tile):
         columns = slice(start, start + tile)
-        rim = rim_ref[:, columns].astype(jnp.float32)
-        widened[:lead, columns] = rim[rim.shape[0] - lead :]
-        widened[lead:, columns] = rows_ref[:, columns].astype(jnp.float32)
-        summed = jnp.zeros((rows, tile), jnp.float32)
-        for back in range(tap_count):
-            tap = taps_ref[back : back + 1, columns].astype(jnp.float32)
-            summed = summed + tap * widened[lead - back : lead - back + rows, columns]
-        total = total + jnp.dot(
-            summed.astype(jnp.bfloat16), gate_ref[columns, :], preferred_element_type=jnp.float32
-        )
-    for part in range(parts):
-        out_ref[part] = total[:, part * width : (part + 1) * width]
-
-
-def mix_project(block, rim, conv_taps, gate_in, parts):
-    rows, features = block.shape
-    width = gate_in.shape[1] // parts
+        widened[:, columns] = rows_ref[:, columns].astype(jnp.float32)
+        mixed = convolve(widened, taps_ref, columns, RIM_ROWS, rows - RIM_ROWS)
+        total = total + jnp.dot(mixed, gate_ref[columns, :], preferred_element_type=jnp.float32)
+    out_ref[...] = total
+
+
+def peer_project_kernel(
+    rank_ref, peer_ref, own_ref, taps_ref, gate_ref, out_ref, widened, own_widened
+):
+    rows, features = peer_ref.shape
+    tile = math.gcd(features, 512)
+    first = rank_ref[0] == 0
+    total = jnp.zeros(out_ref.shape, jnp.float32)
+    for start in range(0, features, tile):
+        columns = slice(start, start + tile)
+        own_tail = own_ref[rows - RIM_ROWS :, columns].astype(jnp.float32)
+        peer_tail = peer_ref[rows - RIM_ROWS :, columns].astype(jnp.float32)
+        widened[:RIM_ROWS, columns] = jnp.where(first, own_tail, 0.0)
+        widened[RIM_ROWS:, columns] = peer_ref[:, columns].astype(jnp.float32)
+        own_widened[:RIM_ROWS, columns] = jnp.where(first, 0.0, peer_tail)
+        own_widened[RIM_ROWS:, columns] = own_ref[:RIM_ROWS, columns].astype(jnp.float32)
+        mixed = jnp.concatenate(
+            [
+                convolve(own_widened, taps_ref, columns, RIM_ROWS, RIM_ROWS),
+                convolve(widened, taps_ref, columns, RIM_ROWS, rows),
+            ],
+            axis=0,
+        )
+        total = total + jnp.dot(mixed, gate_ref[columns, :], preferred_element_type=jnp.float32)
+    out_ref[...] = total
+
+
+def project_cost(rows, gate_in):
+    return pl.CostEstimate(
+        flops=2 * rows * gate_in.size,
+        bytes_accessed=2 * (rows * gate_in.shape[0] + gate_in.size) + 4 * rows * gate_in.shape[1],
+        transcendentals=0,
+    )
+
+
+def own_project(activations, conv_taps, gate_in):
+    rows, features = activations.shape
+    done = rows - RIM_ROWS
     return pl.pallas_call(
-        mix_project_kernel,
-        out_shape=jax.ShapeDtypeStruct((parts, rows, width), jnp.float32),
-        scratch_shapes=[pltpu.VMEM((rows + 8, features), jnp.float32)],
+        own_project_kernel,
+        out_shape=jax.ShapeDtypeStruct((done, gate_in.shape[1]), jnp.float32),
+        scratch_shapes=[pltpu.VMEM((rows, features), jnp.float32)],
         compiler_params=pltpu.CompilerParams(vmem_limit_bytes=VMEM_BYTES),
-        cost_estimate=pl.CostEstimate(
-            flops=2 * rows * features * gate_in.shape[1],
-            bytes_accessed=2 * (block.size + gate_in.size) + 4 * rows * gate_in.shape[1],
-            transcendentals=0,
-        ),
-    )(block, rim, conv_taps, gate_in)
-
-
-def logits_kernel(rank_ref, own_ref, peer_ref, gate_out_ref, out_ref):
+        cost_estimate=pl.CostEstimate(flops=1, bytes_accessed=1, transcendentals=0),
+    )(activations, conv_taps, gate_in)
+
+
+def peer_project(rank, peer_rows, activations, conv_taps, gate_in):
+    rows, features = activations.shape
+    done = rows + RIM_ROWS
+    return pl.pallas_call(
+        peer_project_kernel,
+        in_specs=[pl.BlockSpec(memory_space=pltpu.SMEM)]
+        + [pl.BlockSpec(memory_space=pltpu.VMEM)] * 4,
+        out_shape=jax.ShapeDtypeStruct((done, gate_in.shape[1]), jnp.float32),
+        scratch_shapes=[
+            pltpu.VMEM((rows + RIM_ROWS, features), jnp.float32),
+            pltpu.VMEM((2 * RIM_ROWS, features), jnp.float32),
+        ],
+        compiler_params=pltpu.CompilerParams(vmem_limit_bytes=VMEM_BYTES),
+        cost_estimate=project_cost(done, gate_in),
+    )(rank, peer_rows, activations, conv_taps, gate_in)
+
+
+def head_sum(part):
+    count = lax.axis_size("heads")
+    step = 1
+    received = None
+    while step < count:
+        if received is not None:
+            part = part + received.astype(jnp.float32)
+        route = [(i, i ^ step) for i in range(count)]
+        sent = part if step == 1 else part.astype(jnp.bfloat16)
+        received = lax.ppermute(sent, "heads", route)
+        step *= 2
+    return part, received
+
+
+def logits_kernel(rank_ref, own_ref, own_in_ref, peer_ref, peer_in_ref, gate_out_ref, out_ref):
     first = rank_ref[0] == 0
-    shares = []
-    for ref in (own_ref, peer_ref):
-        pre = ref[0]
-        for part in range(1, ref.shape[0]):
-            pre = pre + ref[part]
-        hidden = (pre / (1.0 + jnp.exp(-pre))).astype(jnp.bfloat16)
-        shares.append(
-            lax.dot_general(
-                gate_out_ref[...],
-                hidden,
-                (((0,), (1,)), ((), ())),
-                preferred_element_type=jnp.float32,
-            )
-        )
-    own, peer = shares
+    hidden = []
+    for ref, in_ref in ((own_ref, own_in_ref), (peer_ref, peer_in_ref)):
+        pre = ref[...] + in_ref[...].astype(jnp.float32)
+        hidden.append((pre / (1.0 + jnp.exp(-pre))).astype(jnp.bfloat16))
+    own = jnp.concatenate([hidden[1][:RIM_ROWS], hidden[0]], axis=0)
+    own, peer = [
+        lax.dot_general(
+            gate_out_ref[...], rows, (((0,), (1,)), ((), ())), preferred_element_type=jnp.float32
+        )
+        for rows in (own, hidden[1][RIM_ROWS:])
+    ]
     out_ref[0] = jnp.where(first, own, peer)
     out_ref[1] = jnp.where(first, peer, own)
 
 
-def logits_share(seq_rank, own_sum, peer_sum, gate_out):
-    rows = own_sum.shape[1]
+def logits_share(rank, own_part, own_in, peer_part, peer_in, gate_rows):
+    rows = (own_part.shape[0] + peer_part.shape[0]) // 2
     return pl.pallas_call(
         logits_kernel,
         in_specs=[pl.BlockSpec(memory_space=pltpu.SMEM)]
-        + [pl.BlockSpec(memory_space=pltpu.VMEM)] * 3,
-        out_shape=jax.ShapeDtypeStruct((2, gate_out.shape[1], rows), jnp.float32),
+        + [pl.BlockSpec(memory_space=pltpu.VMEM)] * 5,
+        out_shape=jax.ShapeDtypeStruct((2, gate_rows.shape[1], rows), jnp.float32),
         compiler_params=pltpu.CompilerParams(vmem_limit_bytes=VMEM_BYTES),
-    )(jnp.reshape(seq_rank, (1,)), own_sum, peer_sum, gate_out)
+    )(rank, own_part, own_in, peer_part, peer_in, gate_rows)
 
 
 def attention_kernel(
     rank_ref,
-    logits_ref,
+    share_ref,
+    peer_share_ref,
     segments_ref,
     queries_ref,
     keys_ref,
-    behind_keys_ref,
     values_ref,
-    behind_values_ref,
+    behind_ref,
     attended_ref,
     own_mass_ref,
     behind_mass_ref,
@@ -107,9 +161,7 @@
     kv_local = keys_ref.shape[1] // HEAD_DIM
     group_size = queries_ref.shape[1] // keys_ref.shape[1]
     score_scale = 1.0 / math.sqrt(HEAD_DIM)
-    logits = logits_ref[0]
-    for share in range(1, logits_ref.shape[0]):
-        logits = logits + logits_ref[share]
+    logits = share_ref[...] + peer_share_ref[...]
     log_gate = jnp.minimum(logits, 0.0) - jnp.log1p(jnp.exp(-jnp.abs(logits)))
     retention[...] = log_gate.astype(jnp.bfloat16).astype(jnp.float32)
 
@@ -124,8 +176,9 @@
 
     for g in range(kv_local):
         columns = slice(g * HEAD_DIM, (g + 1) * HEAD_DIM)
-        keys = jnp.concatenate([behind_keys_ref[:, columns], keys_ref[:, columns]], axis=0)
-        values = jnp.concatenate([behind_values_ref[:, columns], values_ref[:, columns]], axis=0)
+        value_columns = slice((kv_local + g) * HEAD_DIM, (kv_local + g + 1) * HEAD_DIM)
+        keys = jnp.concatenate([behind_ref[:, columns], keys_ref[:, columns]], axis=0)
+        values = jnp.concatenate([behind_ref[:, value_columns], values_ref[:, columns]], axis=0)
         row = head_rank * kv_local + g
         bias = jnp.concatenate(
             [retention[0, pl.ds(row, 1), :], retention[seq_rank, pl.ds(row, 1), :]], axis=1
@@ -151,7 +204,7 @@
         own_mass_ref[g : g + 1, :] = mass[:, rows:]
 
 
-def attention(ranks, logit_shares, segments, queries, keys, behind_keys, values, behind_values):
+def attention(ranks, share, peer_share, segments, queries, keys, values, behind):
     rows = queries.shape[0]
     kv_local = keys.shape[1] // HEAD_DIM
     mass = jax.ShapeDtypeStruct((kv_local, rows), jnp.float32)
@@ -160,45 +213,51 @@
         in_specs=[pl.BlockSpec(memory_space=pltpu.SMEM)]
         + [pl.BlockSpec(memory_space=pltpu.VMEM)] * 7,
         out_shape=(jax.ShapeDtypeStruct(queries.shape, jnp.bfloat16), mass, mass),
-        scratch_shapes=[pltpu.VMEM(logit_shares.shape[1:], jnp.float32)],
+        scratch_shapes=[pltpu.VMEM(share.shape, jnp.float32)],
         compiler_params=pltpu.CompilerParams(vmem_limit_bytes=VMEM_BYTES),
-    )(ranks, logit_shares, segments, queries, keys, behind_keys, values, behind_values)
+    )(ranks, share, peer_share, segments, queries, keys, values, behind)
 
 
 def pair_device(
     activations, conv_taps, gate_in, gate_out, queries, key_vectors, value_vectors, segment_ids
 ):
     rows = activations.shape[0]
-    parts = lax.axis_size("heads")
+    swap = [(0, 1), (1, 0)]
     seq_rank = lax.axis_index("seq")
-    head_rank = lax.axis_index("heads")
-    tail = activations[rows - RIM_ROWS :]
-    rim = lax.ppermute(tail, "seq", [(0, 1)])
-    peer_rows = lax.ppermute(activations, "seq", [(0, 1), (1, 0)])
-    behind_keys = lax.ppermute(key_vectors, "seq", [(0, 1)])
-    behind_values = lax.ppermute(value_vectors, "seq", [(0, 1)])
-    peer_rim = jnp.where(seq_rank == 0, tail, jnp.zeros_like(tail))
-
-    own_part = mix_project(activations, rim, conv_taps, gate_in, parts)
-    own_sum = lax.all_to_all(own_part, "heads", 0, 0, tiled=True)
-    peer_part = mix_project(peer_rows, peer_rim, conv_taps, gate_in, parts)
-    peer_sum = lax.all_to_all(peer_part, "heads", 0, 0, tiled=True)
-    width = own_part.shape[2]
-    gate_rows = lax.dynamic_slice_in_dim(
-        gate_out, (seq_rank * parts + head_rank) * width, width, 0
-    )
-    share = logits_share(seq_rank, own_sum, peer_sum, gate_rows)
-    shares = lax.all_gather(share, ("seq", "heads"), axis=0)
-    ranks = jnp.stack([seq_rank, head_rank]).astype(jnp.int32)
+    ranks = jnp.stack([seq_rank, lax.axis_index("heads")]).astype(jnp.int32)
+    hidden_local = gate_in.shape[1]
+    gate_rows = lax.dynamic_slice_in_dim(gate_out, seq_rank * hidden_local, hidden_local, 0)
+
+    peer_rows = lax.ppermute(activations, "seq", swap)
+    keys_values = jnp.concatenate([key_vectors, value_vectors], axis=1)
+    behind = lax.ppermute(keys_values, "seq", [(0, 1)])
+
+    def own_sums(activations, conv_taps, gate_in):
+        return head_sum(own_project(activations, conv_taps, gate_in))
+
+    own_part, own_in = lax.cond(
+        segment_ids[0] >= 0,
+        own_sums,
+        lambda *given: jax.tree.map(
+            lambda like: jnp.zeros(like.shape, like.dtype), jax.eval_shape(own_sums, *given)
+        ),
+        activations,
+        conv_taps,
+        gate_in,
+    )
+    peer_rows, own_part, own_in = lax.optimization_barrier((peer_rows, own_part, own_in))
+    peer_part = peer_project(ranks, peer_rows, activations, conv_taps, gate_in)
+    peer_part, peer_in = head_sum(peer_part)
+    share = logits_share(ranks, own_part, own_in, peer_part, peer_in, gate_rows)
     attended, own_mass, behind_mass = attention(
         ranks,
-        shares,
+        share,
+        lax.ppermute(share, "seq", swap),
         segment_ids.reshape(2, rows),
         queries,
         key_vectors,
-        behind_keys,
         value_vectors,
-        behind_values,
+        behind,
     )
     key_mass = own_mass + lax.ppermute(behind_mass, "seq", [(1, 0)])
     return (attended, key_mass.astype(jnp.bfloat16))

time: 60.6 us -> 40.1 us (0.66)
  blocking collectives: 8.07 us -> 0 us
  starting transfers between devices: 19.9 us -> 12.9 us
  waiting for transfers between devices: 19.9 us -> 14.4 us
  Pallas kernels: 6.33 us -> 9.2 us
  local copies, waits for them, and re-layouts: 3.51 us -> 1.35 us
  other arithmetic: 1.47 us -> 0.67 us
    all_gather x1 -> x0, blocking collectives: 8.07 us -> none  [pair_device(): shares = lax.all_gather(share, ('seq', 'heads'), axis=0)]
    all_to_all x2 -> x0, starting transfers between devices: 6.81 us -> none  [the longest x1 3.41 us: pair_device(): own_sum = lax.all_to_all(own_part, 'heads', 0, 0, tiled=True)]
    all_to_all x2 -> x0, waiting for transfers between devices: 5.77 us -> none  [the longest x1 5.77 us: pair_device(): peer_sum = lax.all_to_all(peer_part, 'heads', 0, 0, tiled=True)]
    unnamed x17 -> x11, local copies, waits for them, and re-layouts: 3.5 us -> 0.18 us
    pallas_call x2, Pallas kernels: 2.84 us -> 5.09 us  [the longest x1 2.65 us: peer_project(): pl.pallas_call(peer_project_kernel, in_specs=[pl.BlockSpec(memory_space=p...]
    slice x0 -> x1, local copies, waits for them, and re-layouts: none -> 1.16 us  [pair_device(): segment_ids[0] >= 0]
    pallas_call x1, Pallas kernels: 0.17 us -> 1.18 us  [logits_share(): pl.pallas_call(logits_kernel, in_specs=[pl.BlockSpec(memory_space=pltpu.S...]
    select_n x1 -> x0, other arithmetic: 0.88 us -> none  [pair_device(): peer_rim = jnp.where(seq_rank == 0, tail, jnp.zeros_like(tail))]
  transfers between devices with their start and end apart: 7 -> 8, of which waited for: 3 -> 7; matrix products, arithmetic and copies ran while one was open for 2% -> 4% of each run, Pallas kernels for 5% -> 9%
where the time goes in v2:
time: 40.1 us; the launch traced here: 39.9 us
  waiting for transfers between devices  14.4 us (36%)
  starting transfers between devices  12.9 us (32%)
  Pallas kernels  9.2 us (23%)
  local copies, waits for them, and re-layouts  1.35 us (3%)
  between operations  1.26 us (3%)
  other arithmetic  0.67 us (2%)
    ppermute x4, waiting for transfers between devices, head_sum(): received = lax.ppermute(sent, 'heads', route)  7.34 us
    ppermute x1, waiting for transfers between devices, pair_device(): key_mass = own_mass + lax.ppermute(behind_mass, 'seq', [(1, 0)])  4.16 us
    ppermute x4, starting transfers between devices, head_sum(): received = lax.ppermute(sent, 'heads', route)  3.54 us
    ppermute x1, starting transfers between devices, pair_device(): behind = lax.ppermute(keys_values, 'seq', [(0, 1)])  3.4 us
    ppermute x1, starting transfers between devices, pair_device(): peer_rows = lax.ppermute(activations, 'seq', swap)  3 us
    pallas_call x1, Pallas kernels, attention(): pl.pallas_call(attention_kernel, in_specs=[pl.BlockSpec(memory_space=pltp...  2.93 us
    pallas_call x1, Pallas kernels, peer_project(): pl.pallas_call(peer_project_kernel, in_specs=[pl.BlockSpec(memory_space=p...  2.65 us
    pallas_call x1, Pallas kernels, own_project(): pl.pallas_call(own_project_kernel, out_shape=jax.ShapeDtypeStruct((done,...  2.43 us
  transfers between devices with their start and end apart: 8, of which 7 were waited for; matrix products, arithmetic and copies ran while one was open for 4% of the time, Pallas kernels for 9%

profile of v2, /device:TPU:0, one launch (start us, length us, event | category | flops | bytes accessed | tf_op | source)
XLA Modules:
  0.0 39.9 jit_solution(18214705197904855052)
XLA Ops:
  0.6 0.0 copy-start
  0.6 3.0 %collective-permute-start.2 = (bf16[128,2048]{1,0:T(8,128)(2,1)}, bf16[128,2048]{1,0:T(8,128)(2,1)S(1)}, u32[]{:S(2)}, u32[]{:S(2)}) collective-permute-start(bf16[128,2048]{1,0:T(8,128)(2,1)} %own_ref.1), channel_id=1, source_target_pairs={{0,16},{16,0},{1,17},{17,1},{2,18},{18,2},{3,19},{19,3},{4,20},{20... | collective-permute-start | bytes 1572872 | tf_op jit(solution)/shard_map/ppermute | solution.py:231
  3.6 1.2 %slice.3 = s32[1]{0:T(128)} slice(s32[256]{0:T(256)} %param.17), slice={[0:1]} | slice | bytes 8 | tf_op jit(solution)/shard_map/slice | solution.py:239
  5.4 9.4 %conditional.1 = (f32[112,512]{1,0:T(8,128)S(1)}, bf16[112,512]{1,0:T(8,128)(2,1)}) conditional(s32[]{:T(128)} %bitcast.2, () %tuple.17, (bf16[128,2048]{1,0:T(8,128)(2,1)}, bf16[4,2048]{1,0:T(4,128)(2,1)}, bf16[2048,512]{1,0:T(8,128)(2,1)}) %tuple.18), branch_computations={%region_0.0_spmd, %region_1.0_spmd} | conditional | flops 114689 | bytes 2179169 | solution.py:238
  5.4 2.4 %branch_1_fun.1 = f32[112,512]{1,0:T(8,128)S(1)} custom-call(bf16[128,2048]{1,0:T(8,128)(2,1)} %get-tuple-element.6.rows_ref, bf16[4,2048]{1,0:T(4,128)(2,1)} %get-tuple-element.7.taps_ref, bf16[2048,512]{1,0:T(8,128)(2,1)} %get-tuple-element.8.gate_ref), custom_call_target="tpu_custom_call" | custom-call | flops 1 | bytes 1 | tf_op jit(solution)/shard_map/cond/branch_1_fun/pallas_call | solution.py:77
  7.8 0.1 collective-permute-start
  7.9 1.5 %collective-permute-done = f32[112,512]{1,0:T(8,128)S(1)} collective-permute-done((f32[112,512]{1,0:T(8,128)S(1)}, f32[112,512]{1,0:T(8,128)S(1)}, u32[]{:S(2)}, u32[]{:S(2)}) %collective-permute-start) | collective-permute-done | bytes 229408 | tf_op jit(solution)/shard_map/cond/branch_1_fun/ppermute | solution.py:112
  9.4 1.6 %collective-permute-start.1 = (bf16[112,512]{1,0:T(8,128)(2,1)S(1)}, bf16[112,512]{1,0:T(8,128)(2,1)}, u32[]{:S(2)}, u32[]{:S(2)}) collective-permute-start(bf16[112,512]{1,0:T(8,128)(2,1)S(1)} %get-tuple-element.27), channel_id=1, source_target_pairs={{0,8},{4,12},{8,0},{12,4},{1,9},{5,13},{9,1},{13,5},{2,10},{6,14},... | collective-permute-start | bytes 344072 | tf_op jit(solution)/shard_map/cond/branch_1_fun/ppermute | solution.py:112
  11.0 3.8 %collective-permute-done.1 = bf16[112,512]{1,0:T(8,128)(2,1)} collective-permute-done((bf16[112,512]{1,0:T(8,128)(2,1)S(1)}, bf16[112,512]{1,0:T(8,128)(2,1)}, u32[]{:S(2)}, u32[]{:S(2)}) %collective-permute-start.1) | collective-permute-done | bytes 114720 | tf_op jit(solution)/shard_map/cond/branch_1_fun/ppermute | solution.py:112
  14.8 0.1 pad_add_fusion.rank_ref
  14.8 1.0 %collective-permute-done.2.peer_ref = bf16[128,2048]{1,0:T(8,128)(2,1)S(1)} collective-permute-done((bf16[128,2048]{1,0:T(8,128)(2,1)}, bf16[128,2048]{1,0:T(8,128)(2,1)S(1)}, u32[]{:S(2)}, u32[]{:S(2)}) %collective-permute-start.2) | collective-permute-done | bytes 524320 | tf_op jit(solution)/shard_map/ppermute | solution.py:231
  15.8 0.0 copy-start.2
  15.8 0.0 copy-start.3
  15.8 0.0 copy-start.1
  15.8 0.0 copy-start.4
  15.8 2.7 %shard_map.95 = f32[144,512]{1,0:T(8,128)S(1)} custom-call(s32[2]{0:T(128)S(1)} %pad_add_fusion.rank_ref, bf16[128,2048]{1,0:T(8,128)(2,1)S(1)} %collective-permute-done.2.peer_ref, bf16[128,2048]{1,0:T(8,128)(2,1)} %own_ref.1, bf16[4,2048]{1,0:T(4,128)(2,1)} %taps_ref.1, bf16[2048,512]{1,0:T(8,128)(2,1)} %gate_ref.1), custom_call_target="tpu_custom_call" | custom-call | flops 301989888 | bytes 2981888 | tf_op jit(solution)/shard_map/pallas_call | solution.py:89
  18.4 0.1 collective-permute-start.3
  18.5 1.6 %collective-permute-done.3 = f32[144,512]{1,0:T(8,128)S(1)} collective-permute-done((f32[144,512]{1,0:T(8,128)S(1)}, f32[144,512]{1,0:T(8,128)S(1)}, u32[]{:S(2)}, u32[]{:S(2)}) %collective-permute-start.3) | collective-permute-done | bytes 294944 | tf_op jit(solution)/shard_map/ppermute | solution.py:112
  20.1 1.8 %collective-permute-start.4 = (bf16[144,512]{1,0:T(8,128)(2,1)S(1)}, bf16[144,512]{1,0:T(8,128)(2,1)S(1)}, u32[]{:S(2)}, u32[]{:S(2)}) collective-permute-start(bf16[144,512]{1,0:T(8,128)(2,1)S(1)} %get-tuple-element.29), channel_id=1, source_target_pairs={{0,8},{4,12},{8,0},{12,4},{1,9},{5,13},{9,1},{13,5},{2,10},{6,14},... | collective-permute-start | bytes 442376 | tf_op jit(solution)/shard_map/ppermute | solution.py:112
  22.0 0.0 copy-done.2
  22.0 0.0 copy-done.3
  22.0 3.4 %collective-permute-start.6 = (bf16[128,512]{1,0:T(8,128)(2,1)S(1)}, bf16[128,512]{1,0:T(8,128)(2,1)S(1)}, u32[]{:S(2)}, u32[]{:S(2)}) collective-permute-start(bf16[128,512]{1,0:T(8,128)(2,1)S(1)} %pad_maximum_fusion), channel_id=1, source_target_pairs={{0,16},{1,17},{2,18},{3,19},{4,20},{5,21},{6,22},{7,23},{8,24},{9,... | collective-permute-start | bytes 393224 | tf_op jit(solution)/shard_map/ppermute | solution.py:233
  25.4 0.0 copy-done
  25.4 0.2 copy.11.gate_out_ref
  25.6 0.5 %collective-permute-done.4.peer_in_ref = bf16[144,512]{1,0:T(8,128)(2,1)S(1)} collective-permute-done((bf16[144,512]{1,0:T(8,128)(2,1)S(1)}, bf16[144,512]{1,0:T(8,128)(2,1)S(1)}, u32[]{:S(2)}, u32[]{:S(2)}) %collective-permute-start.4) | collective-permute-done | bytes 147488 | tf_op jit(solution)/shard_map/ppermute | solution.py:112
  26.1 1.2 %shard_map.96.share_ref = f32[2,8,128]{2,1,0:T(8,128)S(1)} custom-call(s32[2]{0:T(128)S(1)} %pad_add_fusion.rank_ref, f32[112,512]{1,0:T(8,128)S(1)} %get-tuple-element.21.own_ref, bf16[112,512]{1,0:T(8,128)(2,1)} %get-tuple-element.22.own_in_ref, f32[144,512]{1,0:T(8,128)S(1)} %get-tuple-element.30.peer_ref, ...), custom_call_target="tpu_custom_call" | custom-call | tf_op jit(solution)/shard_map/pallas_call | solution.py:136
  27.3 1.7 %collective-permute-start.5 = (f32[2,8,128]{2,1,0:T(8,128)S(1)}, f32[2,8,128]{2,1,0:T(8,128)S(1)}, u32[]{:S(2)}, u32[]{:S(2)}) collective-permute-start(f32[2,8,128]{2,1,0:T(8,128)S(1)} %shard_map.96.share_ref), channel_id=1, source_target_pairs={{0,16},{16,0},{1,17},{17,1},{2,18},{18,2},{3,19},{19,3},{4,20},{20... | collective-permute-start | bytes 24584 | tf_op jit(solution)/shard_map/ppermute | solution.py:255
  29.0 0.0 collective-permute-done.6.behind_ref
  29.0 1.9 %collective-permute-done.5.peer_share_ref = f32[2,8,128]{2,1,0:T(8,128)S(1)} collective-permute-done((f32[2,8,128]{2,1,0:T(8,128)S(1)}, f32[2,8,128]{2,1,0:T(8,128)S(1)}, u32[]{:S(2)}, u32[]{:S(2)}) %collective-permute-start.5) | collective-permute-done | bytes 8224 | tf_op jit(solution)/shard_map/ppermute | solution.py:255
  31.0 0.0 copy-done.1
  31.0 0.0 copy-done.4
  31.0 2.9 %shard_map.97 = (bf16[128,2048]{1,0:T(8,128)(2,1)}, f32[2,128]{1,0:T(2,128)S(1)}, f32[2,128]{1,0:T(2,128)S(1)}) custom-call(s32[2]{0:T(128)S(1)} %pad_add_fusion.rank_ref, f32[2,8,128]{2,1,0:T(8,128)S(1)} %shard_map.96.share_ref, f32[2,8,128]{2,1,0:T(8,128)S(1)} %collective-permute-done.5.peer_share_ref, s32[2,128]{1,0:T(2,128)S(1)} %bitcast.4, ...), custom_call_target="tpu_custom_call" | custom-call | tf_op jit(solution)/shard_map/pallas_call | solution.py:211
  33.9 1.3 %collective-permute-start.7 = (f32[2,128]{1,0:T(2,128)S(1)}, f32[2,128]{1,0:T(2,128)S(1)}, u32[]{:S(2)}, u32[]{:S(2)}) collective-permute-start(f32[2,128]{1,0:T(2,128)S(1)} %get-tuple-element.26), channel_id=1, source_target_pairs={{16,0},{17,1},{18,2},{19,3},{20,4},{21,5},{22,6},{23,7},{24,8},{25... | collective-permute-start | bytes 3080 | tf_op jit(solution)/shard_map/ppermute | solution.py:262
  35.2 4.2 %collective-permute-done.7 = f32[2,128]{1,0:T(2,128)S(1)} collective-permute-done((f32[2,128]{1,0:T(2,128)S(1)}, f32[2,128]{1,0:T(2,128)S(1)}, u32[]{:S(2)}, u32[]{:S(2)}) %collective-permute-start.7) | collective-permute-done | bytes 1056 | tf_op jit(solution)/shard_map/ppermute | solution.py:262
  39.3 0.5 %add_convert_fusion = bf16[2,128]{1,0:T(2,128)(2,1)} fusion(f32[2,128]{1,0:T(2,128)S(1)} %get-tuple-element.25, f32[2,128]{1,0:T(2,128)S(1)} %collective-permute-done.7), kind=kLoop, calls=%fused_computation.1 | loop fusion | flops 512 | bytes 2560 | tf_op jit(solution)/shard_map/convert_element_type | solution.py:263
  (4 shorter events, 0.1 us)
Async XLA Ops:
  0.6 24.8 %copy-start = (bf16[1024,8]{0,1:T(8,128)(2,1)S(1)}, bf16[1024,8]{0,1:T(8,128)(2,1)}, u32[]{:S(2)}) copy-start(bf16[1024,8]{0,1:T(8,128)(2,1)} %param.13) | copy-start | bytes 49156
  0.6 15.1 %collective-permute-start.2 = (bf16[128,2048]{1,0:T(8,128)(2,1)}, bf16[128,2048]{1,0:T(8,128)(2,1)S(1)}, u32[]{:S(2)}, u32[]{:S(2)}) collective-permute-start(bf16[128,2048]{1,0:T(8,128)(2,1)} %own_ref.1), channel_id=1, source_target_pairs={{0,16},{16,0},{1,17},{17,1},{2,18},{18,2},{3,19},{19,3},{4,20},{20... | collective-permute-start | bytes 1572872 | tf_op jit(solution)/shard_map/ppermute | solution.py:231
  7.8 1.5 %collective-permute-start = (f32[112,512]{1,0:T(8,128)S(1)}, f32[112,512]{1,0:T(8,128)S(1)}, u32[]{:S(2)}, u32[]{:S(2)}) collective-permute-start(f32[112,512]{1,0:T(8,128)S(1)} %branch_1_fun.1), channel_id=1, source_target_pairs={{0,4},{4,0},{8,12},{12,8},{1,5},{5,1},{9,13},{13,9},{2,6},{6,2},{1... | collective-permute-start | bytes 688136 | tf_op jit(solution)/shard_map/cond/branch_1_fun/ppermute | solution.py:112
  9.4 5.4 %collective-permute-start.1 = (bf16[112,512]{1,0:T(8,128)(2,1)S(1)}, bf16[112,512]{1,0:T(8,128)(2,1)}, u32[]{:S(2)}, u32[]{:S(2)}) collective-permute-start(bf16[112,512]{1,0:T(8,128)(2,1)S(1)} %get-tuple-element.27), channel_id=1, source_target_pairs={{0,8},{4,12},{8,0},{12,4},{1,9},{5,13},{9,1},{13,5},{2,10},{6,14},... | collective-permute-start | bytes 344072 | tf_op jit(solution)/shard_map/cond/branch_1_fun/ppermute | solution.py:112
  15.8 6.2 %copy-start.2 = (bf16[128,256]{1,0:T(8,128)(2,1)S(1)}, bf16[128,256]{1,0:T(8,128)(2,1)}, u32[]{:S(2)}) copy-start(bf16[128,256]{1,0:T(8,128)(2,1)} %keys_ref.1) | copy-start | bytes 196612
  15.8 6.2 %copy-start.3 = (bf16[128,256]{1,0:T(8,128)(2,1)S(1)}, bf16[128,256]{1,0:T(8,128)(2,1)}, u32[]{:S(2)}) copy-start(bf16[128,256]{1,0:T(8,128)(2,1)} %values_ref.1) | copy-start | bytes 196612
  15.8 15.2 %copy-start.1 = (bf16[128,2048]{1,0:T(8,128)(2,1)S(1)}, bf16[128,2048]{1,0:T(8,128)(2,1)}, u32[]{:S(2)}) copy-start(bf16[128,2048]{1,0:T(8,128)(2,1)} %queries_ref.1) | copy-start | bytes 1572868
  15.8 15.2 %copy-start.4 = (s32[256]{0:T(256)S(1)}, s32[256]{0:T(256)}, u32[]{:S(2)}) copy-start(s32[256]{0:T(256)} %param.17) | copy-start | bytes 3076
  18.4 1.6 %collective-permute-start.3 = (f32[144,512]{1,0:T(8,128)S(1)}, f32[144,512]{1,0:T(8,128)S(1)}, u32[]{:S(2)}, u32[]{:S(2)}) collective-permute-start(f32[144,512]{1,0:T(8,128)S(1)} %shard_map.95), channel_id=1, source_target_pairs={{0,4},{4,0},{8,12},{12,8},{1,5},{5,1},{9,13},{13,9},{2,6},{6,2},{1... | collective-permute-start | bytes 884744 | tf_op jit(solution)/shard_map/ppermute | solution.py:112
  20.1 6.0 %collective-permute-start.4 = (bf16[144,512]{1,0:T(8,128)(2,1)S(1)}, bf16[144,512]{1,0:T(8,128)(2,1)S(1)}, u32[]{:S(2)}, u32[]{:S(2)}) collective-permute-start(bf16[144,512]{1,0:T(8,128)(2,1)S(1)} %get-tuple-element.29), channel_id=1, source_target_pairs={{0,8},{4,12},{8,0},{12,4},{1,9},{5,13},{9,1},{13,5},{2,10},{6,14},... | collective-permute-start | bytes 442376 | tf_op jit(solution)/shard_map/ppermute | solution.py:112
  22.0 7.0 %collective-permute-start.6 = (bf16[128,512]{1,0:T(8,128)(2,1)S(1)}, bf16[128,512]{1,0:T(8,128)(2,1)S(1)}, u32[]{:S(2)}, u32[]{:S(2)}) collective-permute-start(bf16[128,512]{1,0:T(8,128)(2,1)S(1)} %pad_maximum_fusion), channel_id=1, source_target_pairs={{0,16},{1,17},{2,18},{3,19},{4,20},{5,21},{6,22},{7,23},{8,24},{9,... | collective-permute-start | bytes 393224 | tf_op jit(solution)/shard_map/ppermute | solution.py:233
  27.3 3.7 %collective-permute-start.5 = (f32[2,8,128]{2,1,0:T(8,128)S(1)}, f32[2,8,128]{2,1,0:T(8,128)S(1)}, u32[]{:S(2)}, u32[]{:S(2)}) collective-permute-start(f32[2,8,128]{2,1,0:T(8,128)S(1)} %shard_map.96.share_ref), channel_id=1, source_target_pairs={{0,16},{16,0},{1,17},{17,1},{2,18},{18,2},{3,19},{19,3},{4,20},{20... | collective-permute-start | bytes 24584 | tf_op jit(solution)/shard_map/ppermute | solution.py:255
  33.9 5.5 %collective-permute-start.7 = (f32[2,128]{1,0:T(2,128)S(1)}, f32[2,128]{1,0:T(2,128)S(1)}, u32[]{:S(2)}, u32[]{:S(2)}) collective-permute-start(f32[2,128]{1,0:T(2,128)S(1)} %get-tuple-element.26), channel_id=1, source_target_pairs={{16,0},{17,1},{18,2},{19,3},{20,4},{21,5},{22,6},{23,7},{24,8},{25... | collective-permute-start | bytes 3080 | tf_op jit(solution)/shard_map/ppermute | solution.py:262

commit v3 on v2

--- a/solution.py
+++ b/solution.py
@@ -25,8 +25,11 @@
     return summed.astype(jnp.bfloat16)
 
 
-def own_project_kernel(rows_ref, taps_ref, gate_ref, out_ref, widened):
+def own_project_kernel(rows_ref, taps_ref, gate_ref, out_ref, edges_ref, held_ref, widened):
     rows, features = rows_ref.shape
+    edges_ref[:RIM_ROWS] = rows_ref[:RIM_ROWS]
+    edges_ref[RIM_ROWS:] = rows_ref[rows - RIM_ROWS :]
+    held_ref[...] = gate_ref[...]
     tile = math.gcd(features, 512)
     total = jnp.zeros(out_ref.shape, jnp.float32)
     for start in range(0, features, tile):
@@ -38,7 +41,7 @@
 
 
 def peer_project_kernel(
-    rank_ref, peer_ref, own_ref, taps_ref, gate_ref, out_ref, widened, own_widened
+    rank_ref, peer_ref, edges_ref, taps_ref, gate_ref, out_ref, widened, own_widened
 ):
     rows, features = peer_ref.shape
     tile = math.gcd(features, 512)
@@ -46,12 +49,12 @@
     total = jnp.zeros(out_ref.shape, jnp.float32)
     for start in range(0, features, tile):
         columns = slice(start, start + tile)
-        own_tail = own_ref[rows - RIM_ROWS :, columns].astype(jnp.float32)
+        own_tail = edges_ref[RIM_ROWS:, columns].astype(jnp.float32)
         peer_tail = peer_ref[rows - RIM_ROWS :, columns].astype(jnp.float32)
         widened[:RIM_ROWS, columns] = jnp.where(first, own_tail, 0.0)
         widened[RIM_ROWS:, columns] = peer_ref[:, columns].astype(jnp.float32)
         own_widened[:RIM_ROWS, columns] = jnp.where(first, 0.0, peer_tail)
-        own_widened[RIM_ROWS:, columns] = own_ref[:RIM_ROWS, columns].astype(jnp.float32)
+        own_widened[RIM_ROWS:, columns] = edges_ref[:RIM_ROWS, columns].astype(jnp.float32)
         mixed = jnp.concatenate(
             [
                 convolve(own_widened, taps_ref, columns, RIM_ROWS, RIM_ROWS),
@@ -76,15 +79,19 @@
     done = rows - RIM_ROWS
     return pl.pallas_call(
         own_project_kernel,
-        out_shape=jax.ShapeDtypeStruct((done, gate_in.shape[1]), jnp.float32),
+        out_shape=(
+            jax.ShapeDtypeStruct((done, gate_in.shape[1]), jnp.float32),
+            jax.ShapeDtypeStruct((2 * RIM_ROWS, features), activations.dtype),
+            jax.ShapeDtypeStruct(gate_in.shape, gate_in.dtype),
+        ),
         scratch_shapes=[pltpu.VMEM((rows, features), jnp.float32)],
         compiler_params=pltpu.CompilerParams(vmem_limit_bytes=VMEM_BYTES),
         cost_estimate=pl.CostEstimate(flops=1, bytes_accessed=1, transcendentals=0),
     )(activations, conv_taps, gate_in)
 
 
-def peer_project(rank, peer_rows, activations, conv_taps, gate_in):
-    rows, features = activations.shape
+def peer_project(rank, peer_rows, edges, conv_taps, gate_in):
+    rows, features = peer_rows.shape
     done = rows + RIM_ROWS
     return pl.pallas_call(
         peer_project_kernel,
@@ -97,7 +104,7 @@
         ],
         compiler_params=pltpu.CompilerParams(vmem_limit_bytes=VMEM_BYTES),
         cost_estimate=project_cost(done, gate_in),
-    )(rank, peer_rows, activations, conv_taps, gate_in)
+    )(rank, peer_rows, edges, conv_taps, gate_in)
 
 
 def head_sum(part):
@@ -114,32 +121,44 @@
     return part, received
 
 
-def logits_kernel(rank_ref, own_ref, own_in_ref, peer_ref, peer_in_ref, gate_out_ref, out_ref):
+def share_of_logits(pre_ref, in_ref, gate_out_ref):
+    pre = pre_ref[...] + in_ref[...].astype(jnp.float32)
+    hidden = (pre / (1.0 + jnp.exp(-pre))).astype(jnp.bfloat16)
+    return lax.dot_general(
+        gate_out_ref[...], hidden, (((0,), (1,)), ((), ())), preferred_element_type=jnp.float32
+    )
+
+
+def own_logits_kernel(own_ref, in_ref, gate_out_ref, out_ref):
+    out_ref[...] = share_of_logits(own_ref, in_ref, gate_out_ref)
+
+
+def own_logits(part, received, gate_rows):
+    return pl.pallas_call(
+        own_logits_kernel,
+        out_shape=jax.ShapeDtypeStruct((gate_rows.shape[1], part.shape[0]), jnp.float32),
+        compiler_params=pltpu.CompilerParams(vmem_limit_bytes=VMEM_BYTES),
+    )(part, received, gate_rows)
+
+
+def logits_kernel(rank_ref, own_ref, peer_ref, in_ref, gate_out_ref, out_ref):
     first = rank_ref[0] == 0
-    hidden = []
-    for ref, in_ref in ((own_ref, own_in_ref), (peer_ref, peer_in_ref)):
-        pre = ref[...] + in_ref[...].astype(jnp.float32)
-        hidden.append((pre / (1.0 + jnp.exp(-pre))).astype(jnp.bfloat16))
-    own = jnp.concatenate([hidden[1][:RIM_ROWS], hidden[0]], axis=0)
-    own, peer = [
-        lax.dot_general(
-            gate_out_ref[...], rows, (((0,), (1,)), ((), ())), preferred_element_type=jnp.float32
-        )
-        for rows in (own, hidden[1][RIM_ROWS:])
-    ]
+    share = share_of_logits(peer_ref, in_ref, gate_out_ref)
+    own = jnp.concatenate([share[:, :RIM_ROWS], own_ref[...]], axis=1)
+    peer = share[:, RIM_ROWS:]
     out_ref[0] = jnp.where(first, own, peer)
     out_ref[1] = jnp.where(first, peer, own)
 
 
-def logits_share(rank, own_part, own_in, peer_part, peer_in, gate_rows):
-    rows = (own_part.shape[0] + peer_part.shape[0]) // 2
+def logits_share(rank, own_share, peer_part, peer_in, gate_rows):
+    rows = own_share.shape[1] + RIM_ROWS
     return pl.pallas_call(
         logits_kernel,
         in_specs=[pl.BlockSpec(memory_space=pltpu.SMEM)]
-        + [pl.BlockSpec(memory_space=pltpu.VMEM)] * 5,
+        + [pl.BlockSpec(memory_space=pltpu.VMEM)] * 4,
         out_shape=jax.ShapeDtypeStruct((2, gate_rows.shape[1], rows), jnp.float32),
         compiler_params=pltpu.CompilerParams(vmem_limit_bytes=VMEM_BYTES),
-    )(rank, own_part, own_in, peer_part, peer_in, gate_rows)
+    )(rank, own_share, peer_part, peer_in, gate_rows)
 
 
 def attention_kernel(
@@ -172,7 +191,7 @@
     key_at = lax.broadcasted_iota(jnp.int32, (rows, rows), 1)
     see_own = (key_at <= query_at) & (query_segments == own_segments)
     see_behind = (query_segments == behind_segments) & (seq_rank > 0)
-    visible = jnp.concatenate([see_behind, see_own], axis=1)
+    hide = jnp.where(jnp.concatenate([see_behind, see_own], axis=1), 0.0, NEG_FILL)
 
     for g in range(kv_local):
         columns = slice(g * HEAD_DIM, (g + 1) * HEAD_DIM)
@@ -183,6 +202,7 @@
         bias = jnp.concatenate(
             [retention[0, pl.ds(row, 1), :], retention[seq_rank, pl.ds(row, 1), :]], axis=1
         )
+        offset = hide + bias
         mass = jnp.zeros((1, 2 * rows), jnp.float32)
         for e in range(group_size):
             at = (g * group_size + e) * HEAD_DIM
@@ -192,7 +212,7 @@
                 (((1,), (1,)), ((), ())),
                 preferred_element_type=jnp.float32,
             )
-            scores = jnp.where(visible, scores * score_scale + bias, NEG_FILL)
+            scores = scores * score_scale + offset
             weights = jnp.exp(scores - jnp.max(scores, axis=1, keepdims=True))
             weights = weights * (1.0 / jnp.sum(weights, axis=1, keepdims=True))
             mass = mass + jnp.sum(weights, axis=0, keepdims=True)
@@ -232,23 +252,27 @@
     keys_values = jnp.concatenate([key_vectors, value_vectors], axis=1)
     behind = lax.ppermute(keys_values, "seq", [(0, 1)])
 
-    def own_sums(activations, conv_taps, gate_in):
-        return head_sum(own_project(activations, conv_taps, gate_in))
-
-    own_part, own_in = lax.cond(
-        segment_ids[0] >= 0,
-        own_sums,
+    def own_work(activations, conv_taps, gate_in, gate_rows):
+        part, edges, held = own_project(activations, conv_taps, gate_in)
+        return own_logits(*head_sum(part), gate_rows), edges, held
+
+    own_share, edges, held = lax.cond(
+        seq_rank >= 0,
+        own_work,
         lambda *given: jax.tree.map(
-            lambda like: jnp.zeros(like.shape, like.dtype), jax.eval_shape(own_sums, *given)
+            lambda like: jnp.zeros(like.shape, like.dtype), jax.eval_shape(own_work, *given)
         ),
         activations,
         conv_taps,
         gate_in,
-    )
-    peer_rows, own_part, own_in = lax.optimization_barrier((peer_rows, own_part, own_in))
-    peer_part = peer_project(ranks, peer_rows, activations, conv_taps, gate_in)
+        gate_rows,
+    )
+    peer_rows, own_share, edges, held = lax.optimization_barrier(
+        (peer_rows, own_share, edges, held)
+    )
+    peer_part = peer_project(ranks, peer_rows, edges, conv_taps, held)
     peer_part, peer_in = head_sum(peer_part)
-    share = logits_share(ranks, own_part, own_in, peer_part, peer_in, gate_rows)
+    share = logits_share(ranks, own_share, peer_part, peer_in, gate_rows)
     attended, own_mass, behind_mass = attention(
         ranks,
         share,

time: 40.1 us -> 38.8 us (0.968)
  waiting for transfers between devices: 14.4 us -> 15.8 us
  local copies, waits for them, and re-layouts: 1.35 us -> 0.19 us
  Pallas kernels: 9.2 us -> 8.15 us
  between operations: 1.26 us -> 0.69 us
    ppermute x1, waiting for transfers between devices: 0.96 us -> 2.26 us  [pair_device(): peer_rows = lax.ppermute(activations, 'seq', swap)]
    slice x1 -> x0, local copies, waits for them, and re-layouts: 1.16 us -> none  [pair_device(): segment_ids[0] >= 0]
    pallas_call x1, Pallas kernels: 2.65 us -> 1.6 us  [peer_project(): pl.pallas_call(peer_project_kernel, in_specs=[pl.BlockSpec(memory_space=p...]
    pallas_call x1 -> x2, Pallas kernels: 2.43 us -> 2.78 us  [the longest x1 2.57 us: own_project(): pl.pallas_call(own_project_kernel, out_shape=(jax.ShapeDtypeStruct((done,...]
  transfers between devices with their start and end apart: 8 -> 8, of which waited for: 7 -> 7; matrix products, arithmetic and copies ran while one was open for 4% -> 1% of each run, Pallas kernels for 9% -> 10%
where the time goes in v3:
time: 38.8 us; the launch traced here: 38.5 us
  waiting for transfers between devices  15.8 us (41%)
  starting transfers between devices  12.9 us (33%)
  Pallas kernels  8.15 us (21%)
  between operations  0.69 us (2%)
  other arithmetic  0.67 us (2%)
    ppermute x4, waiting for transfers between devices, head_sum(): received = lax.ppermute(sent, 'heads', route)  7.43 us
    ppermute x1, waiting for transfers between devices, pair_device(): key_mass = own_mass + lax.ppermute(behind_mass, 'seq', [(1, 0)])  4.16 us
    ppermute x4, starting transfers between devices, head_sum(): received = lax.ppermute(sent, 'heads', route)  3.54 us
    ppermute x1, starting transfers between devices, pair_device(): behind = lax.ppermute(keys_values, 'seq', [(0, 1)])  3.4 us
    ppermute x1, starting transfers between devices, pair_device(): peer_rows = lax.ppermute(activations, 'seq', swap)  3 us
    pallas_call x1, Pallas kernels, attention(): pl.pallas_call(attention_kernel, in_specs=[pl.BlockSpec(memory_space=pltp...  2.88 us
    pallas_call x1, Pallas kernels, own_project(): pl.pallas_call(own_project_kernel, out_shape=(jax.ShapeDtypeStruct((done,...  2.57 us
    ppermute x1, waiting for transfers between devices, pair_device(): peer_rows = lax.ppermute(activations, 'seq', swap)  2.26 us
  transfers between devices with their start and end apart: 8, of which 7 were waited for; matrix products, arithmetic and copies ran while one was open for 1% of the time, Pallas kernels for 10%

profile of v3, /device:TPU:0, one launch (start us, length us, event | category | flops | bytes accessed | tf_op | source)
XLA Modules:
  0.0 38.5 jit_solution(5299071473045092045)
XLA Ops:
  0.6 0.0 copy-start
  0.6 3.0 %collective-permute-start.2 = (bf16[128,2048]{1,0:T(8,128)(2,1)}, bf16[128,2048]{1,0:T(8,128)(2,1)S(1)}, u32[]{:S(2)}, u32[]{:S(2)}) collective-permute-start(bf16[128,2048]{1,0:T(8,128)(2,1)} %param.10), channel_id=1, source_target_pairs={{0,16},{16,0},{1,17},{17,1},{2,18},{18,2},{3,19},{19,3},{4,20},{20... | collective-permute-start | bytes 1572872 | tf_op jit(solution)/shard_map/ppermute | solution.py:251
  3.6 0.0 copy-done
  3.7 0.2 copy.12.gate_out_ref
  3.8 9.6 %conditional.1 = (f32[8,112]{1,0:T(8,128)S(1)}, bf16[32,2048]{1,0:T(8,128)(2,1)S(1)}, bf16[2048,512]{1,0:T(8,128)(2,1)S(1)}) conditional(s32[]{:T(128)} %convert_element_type.12, () %tuple.17, (bf16[128,2048]{1,0:T(8,128)(2,1)}, bf16[4,2048]{1,0:T(4,128)(2,1)}, bf16[2048,512]{1,0:T(8,128)(2,1)}, bf16[512,8]{1,0:T(8,128)(2,1)S(1)}) %tuple.18), branch_computations={%region_0.0_spmd, %region_1.0_spmd} | conditional | flops 114689 | bytes 2231840 | solution.py:259
  3.8 2.6 %branch_1_fun.2 = (f32[112,512]{1,0:T(8,128)S(1)}, bf16[32,2048]{1,0:T(8,128)(2,1)S(1)}, bf16[2048,512]{1,0:T(8,128)(2,1)S(1)}) custom-call(bf16[128,2048]{1,0:T(8,128)(2,1)} %get-tuple-element.8.rows_ref, bf16[4,2048]{1,0:T(4,128)(2,1)} %get-tuple-element.9.taps_ref, bf16[2048,512]{1,0:T(8,128)(2,1)} %get-tuple-element.38.gate_ref), custom_call_target="tpu_custom_call" | custom-call | flops 1 | bytes 1 | tf_op jit(solution)/shard_map/cond/branch_1_fun/pallas_call | solution.py:80
  6.4 0.1 collective-permute-start
  6.5 1.5 %collective-permute-done = f32[112,512]{1,0:T(8,128)S(1)} collective-permute-done((f32[112,512]{1,0:T(8,128)S(1)}, f32[112,512]{1,0:T(8,128)S(1)}, u32[]{:S(2)}, u32[]{:S(2)}) %collective-permute-start) | collective-permute-done | bytes 229408 | tf_op jit(solution)/shard_map/cond/branch_1_fun/ppermute | solution.py:119
  8.0 1.6 %collective-permute-start.1 = (bf16[112,512]{1,0:T(8,128)(2,1)S(1)}, bf16[112,512]{1,0:T(8,128)(2,1)S(1)}, u32[]{:S(2)}, u32[]{:S(2)}) collective-permute-start(bf16[112,512]{1,0:T(8,128)(2,1)S(1)} %get-tuple-element.39), channel_id=1, source_target_pairs={{0,8},{4,12},{8,0},{12,4},{1,9},{5,13},{9,1},{13,5},{2,10},{6,14},... | collective-permute-start | bytes 344072 | tf_op jit(solution)/shard_map/cond/branch_1_fun/ppermute | solution.py:119
  9.6 3.7 %collective-permute-done.1.in_ref = bf16[112,512]{1,0:T(8,128)(2,1)S(1)} collective-permute-done((bf16[112,512]{1,0:T(8,128)(2,1)S(1)}, bf16[112,512]{1,0:T(8,128)(2,1)S(1)}, u32[]{:S(2)}, u32[]{:S(2)}) %collective-permute-start.1) | collective-permute-done | bytes 114720 | tf_op jit(solution)/shard_map/cond/branch_1_fun/ppermute | solution.py:119
  13.2 0.2 branch_1_fun.3
  13.4 0.0 copy-start.2
  13.4 0.0 copy-start.3
  13.4 0.1 pad_add_fusion.rank_ref
  13.5 2.3 %collective-permute-done.2.peer_ref = bf16[128,2048]{1,0:T(8,128)(2,1)S(1)} collective-permute-done((bf16[128,2048]{1,0:T(8,128)(2,1)}, bf16[128,2048]{1,0:T(8,128)(2,1)S(1)}, u32[]{:S(2)}, u32[]{:S(2)}) %collective-permute-start.2) | collective-permute-done | bytes 524320 | tf_op jit(solution)/shard_map/ppermute | solution.py:251
  15.8 0.0 copy-start.1
  15.8 0.0 copy-start.4
  15.8 1.6 %shard_map.96 = f32[144,512]{1,0:T(8,128)S(1)} custom-call(s32[2]{0:T(128)S(1)} %pad_add_fusion.rank_ref, bf16[128,2048]{1,0:T(8,128)(2,1)S(1)} %collective-permute-done.2.peer_ref, bf16[32,2048]{1,0:T(8,128)(2,1)S(1)} %get-tuple-element.32.edges_ref, bf16[4,2048]{1,0:T(4,128)(2,1)} %taps_ref.1, bf16[2048,512]{1,0:T(8,128)(2,1)S(1)} %get-tuple-element.33.gate_ref), custom_call_target="tpu_custom_call" | custom-call | flops 301989888 | bytes 2981888 | tf_op jit(solution)/shard_map/pallas_call | solution.py:96
  17.4 0.1 collective-permute-start.3
  17.5 1.6 %collective-permute-done.3 = f32[144,512]{1,0:T(8,128)S(1)} collective-permute-done((f32[144,512]{1,0:T(8,128)S(1)}, f32[144,512]{1,0:T(8,128)S(1)}, u32[]{:S(2)}, u32[]{:S(2)}) %collective-permute-start.3) | collective-permute-done | bytes 294944 | tf_op jit(solution)/shard_map/ppermute | solution.py:119
  19.1 1.8 %collective-permute-start.4 = (bf16[144,512]{1,0:T(8,128)(2,1)S(1)}, bf16[144,512]{1,0:T(8,128)(2,1)S(1)}, u32[]{:S(2)}, u32[]{:S(2)}) collective-permute-start(bf16[144,512]{1,0:T(8,128)(2,1)S(1)} %get-tuple-element.41), channel_id=1, source_target_pairs={{0,8},{4,12},{8,0},{12,4},{1,9},{5,13},{9,1},{13,5},{2,10},{6,14},... | collective-permute-start | bytes 442376 | tf_op jit(solution)/shard_map/ppermute | solution.py:119
  20.9 0.0 copy-done.2
  20.9 0.0 copy-done.3
  20.9 3.4 %collective-permute-start.6 = (bf16[128,512]{1,0:T(8,128)(2,1)S(1)}, bf16[128,512]{1,0:T(8,128)(2,1)S(1)}, u32[]{:S(2)}, u32[]{:S(2)}) collective-permute-start(bf16[128,512]{1,0:T(8,128)(2,1)S(1)} %pad_maximum_fusion), channel_id=1, source_target_pairs={{0,16},{1,17},{2,18},{3,19},{4,20},{5,21},{6,22},{7,23},{8,24},{9,... | collective-permute-start | bytes 393224 | tf_op jit(solution)/shard_map/ppermute | solution.py:253
  24.3 0.7 %collective-permute-done.4.in_ref = bf16[144,512]{1,0:T(8,128)(2,1)S(1)} collective-permute-done((bf16[144,512]{1,0:T(8,128)(2,1)S(1)}, bf16[144,512]{1,0:T(8,128)(2,1)S(1)}, u32[]{:S(2)}, u32[]{:S(2)}) %collective-permute-start.4) | collective-permute-done | bytes 147488 | tf_op jit(solution)/shard_map/ppermute | solution.py:119
  25.1 0.9 %shard_map.97.share_ref = f32[2,8,128]{2,1,0:T(8,128)S(1)} custom-call(s32[2]{0:T(128)S(1)} %pad_add_fusion.rank_ref, f32[8,112]{1,0:T(8,128)S(1)} %get-tuple-element.30.own_ref, f32[144,512]{1,0:T(8,128)S(1)} %get-tuple-element.42.peer_ref, bf16[144,512]{1,0:T(8,128)(2,1)S(1)} %collective-permute-done.4.in_ref, bf16[512,8]{1,0:T(8,128)(2,1)S(1)} %copy.12.gate_out_ref), custom_call_target="tpu_custom_call" | custom-call | tf_op jit(solution)/shard_map/pallas_call | solution.py:155
  25.9 1.7 %collective-permute-start.5 = (f32[2,8,128]{2,1,0:T(8,128)S(1)}, f32[2,8,128]{2,1,0:T(8,128)S(1)}, u32[]{:S(2)}, u32[]{:S(2)}) collective-permute-start(f32[2,8,128]{2,1,0:T(8,128)S(1)} %shard_map.97.share_ref), channel_id=1, source_target_pairs={{0,16},{16,0},{1,17},{17,1},{2,18},{18,2},{3,19},{19,3},{4,20},{20... | collective-permute-start | bytes 24584 | tf_op jit(solution)/shard_map/ppermute | solution.py:279
  27.7 0.0 collective-permute-done.6.behind_ref
  27.7 1.9 %collective-permute-done.5.peer_share_ref = f32[2,8,128]{2,1,0:T(8,128)S(1)} collective-permute-done((f32[2,8,128]{2,1,0:T(8,128)S(1)}, f32[2,8,128]{2,1,0:T(8,128)S(1)}, u32[]{:S(2)}, u32[]{:S(2)}) %collective-permute-start.5) | collective-permute-done | bytes 8224 | tf_op jit(solution)/shard_map/ppermute | solution.py:279
  29.6 0.0 copy-done.1
  29.6 0.0 copy-done.4
  29.6 2.9 %shard_map.98 = (bf16[128,2048]{1,0:T(8,128)(2,1)}, f32[2,128]{1,0:T(2,128)S(1)}, f32[2,128]{1,0:T(2,128)S(1)}) custom-call(s32[2]{0:T(128)S(1)} %pad_add_fusion.rank_ref, f32[2,8,128]{2,1,0:T(8,128)S(1)} %shard_map.97.share_ref, f32[2,8,128]{2,1,0:T(8,128)S(1)} %collective-permute-done.5.peer_share_ref, s32[2,128]{1,0:T(2,128)S(1)} %bitcast.3, ...), custom_call_target="tpu_custom_call" | custom-call | tf_op jit(solution)/shard_map/pallas_call | solution.py:231
  32.5 1.3 %collective-permute-start.7 = (f32[2,128]{1,0:T(2,128)S(1)}, f32[2,128]{1,0:T(2,128)S(1)}, u32[]{:S(2)}, u32[]{:S(2)}) collective-permute-start(f32[2,128]{1,0:T(2,128)S(1)} %get-tuple-element.36), channel_id=1, source_target_pairs={{16,0},{17,1},{18,2},{19,3},{20,4},{21,5},{22,6},{23,7},{24,8},{25... | collective-permute-start | bytes 3080 | tf_op jit(solution)/shard_map/ppermute | solution.py:286
  33.8 4.2 %collective-permute-done.7 = f32[2,128]{1,0:T(2,128)S(1)} collective-permute-done((f32[2,128]{1,0:T(2,128)S(1)}, f32[2,128]{1,0:T(2,128)S(1)}, u32[]{:S(2)}, u32[]{:S(2)}) %collective-permute-start.7) | collective-permute-done | bytes 1056 | tf_op jit(solution)/shard_map/ppermute | solution.py:286
  37.9 0.5 %add_convert_fusion = bf16[2,128]{1,0:T(2,128)(2,1)} fusion(f32[2,128]{1,0:T(2,128)S(1)} %get-tuple-element.35, f32[2,128]{1,0:T(2,128)S(1)} %collective-permute-done.7), kind=kLoop, calls=%fused_computation.1 | loop fusion | flops 512 | bytes 2560 | tf_op jit(solution)/shard_map/convert_element_type | solution.py:287
  (4 shorter events, 0.1 us)
Async XLA Ops:
  0.6 3.0 %copy-start = (bf16[1024,8]{0,1:T(8,128)(2,1)S(1)}, bf16[1024,8]{0,1:T(8,128)(2,1)}, u32[]{:S(2)}) copy-start(bf16[1024,8]{0,1:T(8,128)(2,1)} %param.13) | copy-start | bytes 49156
  0.6 15.1 %collective-permute-start.2 = (bf16[128,2048]{1,0:T(8,128)(2,1)}, bf16[128,2048]{1,0:T(8,128)(2,1)S(1)}, u32[]{:S(2)}, u32[]{:S(2)}) collective-permute-start(bf16[128,2048]{1,0:T(8,128)(2,1)} %param.10), channel_id=1, source_target_pairs={{0,16},{16,0},{1,17},{17,1},{2,18},{18,2},{3,19},{19,3},{4,20},{20... | collective-permute-start | bytes 1572872 | tf_op jit(solution)/shard_map/ppermute | solution.py:251
  6.4 1.5 %collective-permute-start = (f32[112,512]{1,0:T(8,128)S(1)}, f32[112,512]{1,0:T(8,128)S(1)}, u32[]{:S(2)}, u32[]{:S(2)}) collective-permute-start(f32[112,512]{1,0:T(8,128)S(1)} %get-tuple-element.11), channel_id=1, source_target_pairs={{0,4},{4,0},{8,12},{12,8},{1,5},{5,1},{9,13},{13,9},{2,6},{6,2},{1... | collective-permute-start | bytes 688136 | tf_op jit(solution)/shard_map/cond/branch_1_fun/ppermute | solution.py:119
  8.0 5.3 %collective-permute-start.1 = (bf16[112,512]{1,0:T(8,128)(2,1)S(1)}, bf16[112,512]{1,0:T(8,128)(2,1)S(1)}, u32[]{:S(2)}, u32[]{:S(2)}) collective-permute-start(bf16[112,512]{1,0:T(8,128)(2,1)S(1)} %get-tuple-element.39), channel_id=1, source_target_pairs={{0,8},{4,12},{8,0},{12,4},{1,9},{5,13},{9,1},{13,5},{2,10},{6,14},... | collective-permute-start | bytes 344072 | tf_op jit(solution)/shard_map/cond/branch_1_fun/ppermute | solution.py:119
  13.4 7.5 %copy-start.2 = (bf16[128,256]{1,0:T(8,128)(2,1)S(1)}, bf16[128,256]{1,0:T(8,128)(2,1)}, u32[]{:S(2)}) copy-start(bf16[128,256]{1,0:T(8,128)(2,1)} %keys_ref.1) | copy-start | bytes 196612
  13.4 7.5 %copy-start.3 = (bf16[128,256]{1,0:T(8,128)(2,1)S(1)}, bf16[128,256]{1,0:T(8,128)(2,1)}, u32[]{:S(2)}) copy-start(bf16[128,256]{1,0:T(8,128)(2,1)} %values_ref.1) | copy-start | bytes 196612
  15.8 13.8 %copy-start.1 = (bf16[128,2048]{1,0:T(8,128)(2,1)S(1)}, bf16[128,2048]{1,0:T(8,128)(2,1)}, u32[]{:S(2)}) copy-start(bf16[128,2048]{1,0:T(8,128)(2,1)} %queries_ref.1) | copy-start | bytes 1572868
  15.8 13.8 %copy-start.4 = (s32[256]{0:T(256)S(1)}, s32[256]{0:T(256)}, u32[]{:S(2)}) copy-start(s32[256]{0:T(256)} %param.17) | copy-start | bytes 3076
  17.4 1.6 %collective-permute-start.3 = (f32[144,512]{1,0:T(8,128)S(1)}, f32[144,512]{1,0:T(8,128)S(1)}, u32[]{:S(2)}, u32[]{:S(2)}) collective-permute-start(f32[144,512]{1,0:T(8,128)S(1)} %shard_map.96), channel_id=1, source_target_pairs={{0,4},{4,0},{8,12},{12,8},{1,5},{5,1},{9,13},{13,9},{2,6},{6,2},{1... | collective-permute-start | bytes 884744 | tf_op jit(solution)/shard_map/ppermute | solution.py:119
  19.1 6.0 %collective-permute-start.4 = (bf16[144,512]{1,0:T(8,128)(2,1)S(1)}, bf16[144,512]{1,0:T(8,128)(2,1)S(1)}, u32[]{:S(2)}, u32[]{:S(2)}) collective-permute-start(bf16[144,512]{1,0:T(8,128)(2,1)S(1)} %get-tuple-element.41), channel_id=1, source_target_pairs={{0,8},{4,12},{8,0},{12,4},{1,9},{5,13},{9,1},{13,5},{2,10},{6,14},... | collective-permute-start | bytes 442376 | tf_op jit(solution)/shard_map/ppermute | solution.py:119
  20.9 6.7 %collective-permute-start.6 = (bf16[128,512]{1,0:T(8,128)(2,1)S(1)}, bf16[128,512]{1,0:T(8,128)(2,1)S(1)}, u32[]{:S(2)}, u32[]{:S(2)}) collective-permute-start(bf16[128,512]{1,0:T(8,128)(2,1)S(1)} %pad_maximum_fusion), channel_id=1, source_target_pairs={{0,16},{1,17},{2,18},{3,19},{4,20},{5,21},{6,22},{7,23},{8,24},{9,... | collective-permute-start | bytes 393224 | tf_op jit(solution)/shard_map/ppermute | solution.py:253
  25.9 3.7 %collective-permute-start.5 = (f32[2,8,128]{2,1,0:T(8,128)S(1)}, f32[2,8,128]{2,1,0:T(8,128)S(1)}, u32[]{:S(2)}, u32[]{:S(2)}) collective-permute-start(f32[2,8,128]{2,1,0:T(8,128)S(1)} %shard_map.97.share_ref), channel_id=1, source_target_pairs={{0,16},{16,0},{1,17},{17,1},{2,18},{18,2},{3,19},{19,3},{4,20},{20... | collective-permute-start | bytes 24584 | tf_op jit(solution)/shard_map/ppermute | solution.py:279
  32.5 5.5 %collective-permute-start.7 = (f32[2,128]{1,0:T(2,128)S(1)}, f32[2,128]{1,0:T(2,128)S(1)}, u32[]{:S(2)}, u32[]{:S(2)}) collective-permute-start(f32[2,128]{1,0:T(2,128)S(1)} %get-tuple-element.36), channel_id=1, source_target_pairs={{16,0},{17,1},{18,2},{19,3},{20,4},{21,5},{22,6},{23,7},{24,8},{25... | collective-permute-start | bytes 3080 | tf_op jit(solution)/shard_map/ppermute | solution.py:286

commit v4 on v3

--- a/solution.py
+++ b/solution.py
@@ -1,3 +1,4 @@
+import functools
 import math
 
 import jax
@@ -14,6 +15,7 @@
 
 NEG_FILL = -1e30
 RIM_ROWS = 16
+LEAST_RETENTION = -40.0
 VMEM_BYTES = 48 * 1024 * 1024
 
 
@@ -41,11 +43,11 @@
 
 
 def peer_project_kernel(
-    rank_ref, peer_ref, edges_ref, taps_ref, gate_ref, out_ref, widened, own_widened
+    peer_ref, edges_ref, taps_ref, gate_ref, out_ref, widened, own_widened
 ):
     rows, features = peer_ref.shape
     tile = math.gcd(features, 512)
-    first = rank_ref[0] == 0
+    first = lax.axis_index("seq") == 0
     total = jnp.zeros(out_ref.shape, jnp.float32)
     for start in range(0, features, tile):
         columns = slice(start, start + tile)
@@ -66,14 +68,6 @@
     out_ref[...] = total
 
 
-def project_cost(rows, gate_in):
-    return pl.CostEstimate(
-        flops=2 * rows * gate_in.size,
-        bytes_accessed=2 * (rows * gate_in.shape[0] + gate_in.size) + 4 * rows * gate_in.shape[1],
-        transcendentals=0,
-    )
-
-
 def own_project(activations, conv_taps, gate_in):
     rows, features = activations.shape
     done = rows - RIM_ROWS
@@ -90,21 +84,19 @@
     )(activations, conv_taps, gate_in)
 
 
-def peer_project(rank, peer_rows, edges, conv_taps, gate_in):
+def peer_project(peer_rows, edges, conv_taps, gate_in):
     rows, features = peer_rows.shape
     done = rows + RIM_ROWS
     return pl.pallas_call(
         peer_project_kernel,
-        in_specs=[pl.BlockSpec(memory_space=pltpu.SMEM)]
-        + [pl.BlockSpec(memory_space=pltpu.VMEM)] * 4,
         out_shape=jax.ShapeDtypeStruct((done, gate_in.shape[1]), jnp.float32),
         scratch_shapes=[
             pltpu.VMEM((rows + RIM_ROWS, features), jnp.float32),
             pltpu.VMEM((2 * RIM_ROWS, features), jnp.float32),
         ],
         compiler_params=pltpu.CompilerParams(vmem_limit_bytes=VMEM_BYTES),
-        cost_estimate=project_cost(done, gate_in),
-    )(rank, peer_rows, edges, conv_taps, gate_in)
+        cost_estimate=pl.CostEstimate(flops=1, bytes_accessed=1, transcendentals=0),
+    )(peer_rows, edges, conv_taps, gate_in)
 
 
 def head_sum(part):
@@ -141,8 +133,8 @@
     )(part, received, gate_rows)
 
 
-def logits_kernel(rank_ref, own_ref, peer_ref, in_ref, gate_out_ref, out_ref):
-    first = rank_ref[0] == 0
+def logits_kernel(own_ref, peer_ref, in_ref, gate_out_ref, out_ref):
+    first = lax.axis_index("seq") == 0
     share = share_of_logits(peer_ref, in_ref, gate_out_ref)
     own = jnp.concatenate([share[:, :RIM_ROWS], own_ref[...]], axis=1)
     peer = share[:, RIM_ROWS:]
@@ -150,40 +142,16 @@
     out_ref[1] = jnp.where(first, peer, own)
 
 
-def logits_share(rank, own_share, peer_part, peer_in, gate_rows):
+def logits_share(own_share, peer_part, peer_in, gate_rows):
     rows = own_share.shape[1] + RIM_ROWS
     return pl.pallas_call(
         logits_kernel,
-        in_specs=[pl.BlockSpec(memory_space=pltpu.SMEM)]
-        + [pl.BlockSpec(memory_space=pltpu.VMEM)] * 4,
         out_shape=jax.ShapeDtypeStruct((2, gate_rows.shape[1], rows), jnp.float32),
         compiler_params=pltpu.CompilerParams(vmem_limit_bytes=VMEM_BYTES),
-    )(rank, own_share, peer_part, peer_in, gate_rows)
-
-
-def attention_kernel(
-    rank_ref,
-    share_ref,
-    peer_share_ref,
-    segments_ref,
-    queries_ref,
-    keys_ref,
-    values_ref,
-    behind_ref,
-    attended_ref,
-    own_mass_ref,
-    behind_mass_ref,
-    retention,
-):
-    seq_rank, head_rank = rank_ref[0], rank_ref[1]
-    rows = queries_ref.shape[0]
-    kv_local = keys_ref.shape[1] // HEAD_DIM
-    group_size = queries_ref.shape[1] // keys_ref.shape[1]
-    score_scale = 1.0 / math.sqrt(HEAD_DIM)
-    logits = share_ref[...] + peer_share_ref[...]
-    log_gate = jnp.minimum(logits, 0.0) - jnp.log1p(jnp.exp(-jnp.abs(logits)))
-    retention[...] = log_gate.astype(jnp.bfloat16).astype(jnp.float32)
-
+    )(own_share, peer_part, peer_in, gate_rows)
+
+
+def hide_unseen(seq_rank, segments_ref, rows):
     own_segments = segments_ref[pl.ds(seq_rank, 1), :]
     behind_segments = segments_ref[pl.ds(0, 1), :]
     query_segments = jnp.transpose(jnp.broadcast_to(own_segments, (rows, rows)))
@@ -191,51 +159,142 @@
     key_at = lax.broadcasted_iota(jnp.int32, (rows, rows), 1)
     see_own = (key_at <= query_at) & (query_segments == own_segments)
     see_behind = (query_segments == behind_segments) & (seq_rank > 0)
-    hide = jnp.where(jnp.concatenate([see_behind, see_own], axis=1), 0.0, NEG_FILL)
-
+    return jnp.where(jnp.concatenate([see_behind, see_own], axis=1), 0.0, NEG_FILL)
+
+
+def head_columns(number):
+    return slice(number * HEAD_DIM, (number + 1) * HEAD_DIM)
+
+
+def scores_of(queries_ref, keys, offset, head):
+    scores = lax.dot_general(
+        queries_ref[:, head_columns(head)],
+        keys,
+        (((1,), (1,)), ((), ())),
+        preferred_element_type=jnp.float32,
+    )
+    return scores * (1.0 / math.sqrt(HEAD_DIM)) + offset
+
+
+def with_behind(ref, behind_ref, number, whole):
+    own = ref[:, head_columns(number)]
+    if not whole:
+        return own
+    return jnp.concatenate([behind_ref[:, head_columns(number)], own], axis=0)
+
+
+def powers_kernel(segments_ref, queries_ref, keys_ref, behind_keys_ref, powers_ref):
+    seq_rank = lax.axis_index("seq")
+    rows = queries_ref.shape[0]
+    kv_local = keys_ref.shape[1] // HEAD_DIM
+    group_size = queries_ref.shape[1] // keys_ref.shape[1]
+    hide = hide_unseen(seq_rank, segments_ref, rows)
+
+    def fill(whole):
+        start = 0 if whole else rows
+        for head in range(kv_local * group_size):
+            g = head // group_size
+            keys = with_behind(keys_ref, behind_keys_ref, g, whole)
+            scores = scores_of(queries_ref, keys, hide[:, start:], head)
+            powers_ref[head, :, start:] = jnp.exp(
+                scores - jnp.max(scores, axis=1, keepdims=True)
+            )
+
+    pl.when(seq_rank > 0)(lambda: fill(True))
+    pl.when(seq_rank == 0)(lambda: fill(False))
+
+
+def powers_of(segments, queries, keys, behind_keys):
+    rows = queries.shape[0]
+    heads = queries.shape[1] // HEAD_DIM
+    return pl.pallas_call(
+        powers_kernel,
+        out_shape=jax.ShapeDtypeStruct((heads, rows, 2 * rows), jnp.float32),
+        compiler_params=pltpu.CompilerParams(vmem_limit_bytes=VMEM_BYTES),
+        cost_estimate=pl.CostEstimate(
+            flops=4 * rows * rows * queries.shape[1],
+            bytes_accessed=8 * heads * rows * rows,
+            transcendentals=2 * heads * rows * rows,
+        ),
+    )(segments, queries, keys, behind_keys)
+
+
+def attention_kernel(
+    share_ref,
+    peer_share_ref,
+    powers_ref,
+    segments_ref,
+    queries_ref,
+    keys_ref,
+    values_ref,
+    behind_keys_ref,
+    behind_values_ref,
+    attended_ref,
+    own_mass_ref,
+    behind_mass_ref,
+    retention,
+):
+    seq_rank, head_rank = lax.axis_index("seq"), lax.axis_index("heads")
+    rows = queries_ref.shape[0]
+    kv_local = keys_ref.shape[1] // HEAD_DIM
+    group_size = queries_ref.shape[1] // keys_ref.shape[1]
+    logits = share_ref[...] + peer_share_ref[...]
+    log_gate = jnp.minimum(logits, 0.0) - jnp.log1p(jnp.exp(-jnp.abs(logits)))
+    retention[...] = log_gate.astype(jnp.bfloat16).astype(jnp.float32)
+    biases = []
     for g in range(kv_local):
-        columns = slice(g * HEAD_DIM, (g + 1) * HEAD_DIM)
-        value_columns = slice((kv_local + g) * HEAD_DIM, (kv_local + g + 1) * HEAD_DIM)
-        keys = jnp.concatenate([behind_ref[:, columns], keys_ref[:, columns]], axis=0)
-        values = jnp.concatenate([behind_ref[:, value_columns], values_ref[:, columns]], axis=0)
-        row = head_rank * kv_local + g
-        bias = jnp.concatenate(
-            [retention[0, pl.ds(row, 1), :], retention[seq_rank, pl.ds(row, 1), :]], axis=1
-        )
-        offset = hide + bias
-        mass = jnp.zeros((1, 2 * rows), jnp.float32)
-        for e in range(group_size):
-            at = (g * group_size + e) * HEAD_DIM
-            scores = lax.dot_general(
-                queries_ref[:, at : at + HEAD_DIM],
-                keys,
-                (((1,), (1,)), ((), ())),
-                preferred_element_type=jnp.float32,
-            )
-            scores = scores * score_scale + offset
-            weights = jnp.exp(scores - jnp.max(scores, axis=1, keepdims=True))
-            weights = weights * (1.0 / jnp.sum(weights, axis=1, keepdims=True))
-            mass = mass + jnp.sum(weights, axis=0, keepdims=True)
-            attended_ref[:, at : at + HEAD_DIM] = jnp.dot(
-                weights.astype(jnp.bfloat16), values, preferred_element_type=jnp.float32
-            ).astype(jnp.bfloat16)
-        mass = mass / group_size
-        behind_mass_ref[g : g + 1, :] = mass[:, :rows]
-        own_mass_ref[g : g + 1, :] = mass[:, rows:]
-
-
-def attention(ranks, share, peer_share, segments, queries, keys, values, behind):
+        at = pl.ds(head_rank * kv_local + g, 1)
+        biases.append(jnp.concatenate([retention[0, at, :], retention[seq_rank, at, :]], axis=1))
+    moderate = jnp.min(functools.reduce(jnp.minimum, biases)) >= LEAST_RETENTION
+
+    def finish(whole, terms_of):
+        start = 0 if whole else rows
+        for g in range(kv_local):
+            values = with_behind(values_ref, behind_values_ref, g, whole)
+            mass = jnp.zeros((1, 2 * rows - start), jnp.float32)
+            group_terms = terms_of(g, whole, start)
+            for head in range(g * group_size, (g + 1) * group_size):
+                weights = group_terms(head)
+                weights = weights * (1.0 / jnp.sum(weights, axis=1, keepdims=True))
+                mass = mass + jnp.sum(weights, axis=0, keepdims=True)
+                attended_ref[:, head_columns(head)] = jnp.dot(
+                    weights.astype(jnp.bfloat16), values, preferred_element_type=jnp.float32
+                ).astype(jnp.bfloat16)
+            mass = mass / group_size
+            own_mass_ref[g : g + 1, :] = mass[:, rows - start :]
+            behind_mass_ref[g : g + 1, :] = mass[:, :rows]
+
+    def by_powers(g, whole, start):
+        factor = jnp.exp(biases[g] - jnp.max(biases[g]))[:, start:]
+        return lambda head: powers_ref[head, :, start:] * factor
+
+    def by_scores(g, whole, start):
+        offset = hide_unseen(seq_rank, segments_ref, rows) + biases[g]
+        keys = with_behind(keys_ref, behind_keys_ref, g, whole)
+
+        def terms(head):
+            scores = scores_of(queries_ref, keys, offset[:, start:], head)
+            return jnp.exp(scores - jnp.max(scores, axis=1, keepdims=True))
+
+        return terms
+
+    pl.when(moderate & (seq_rank > 0))(lambda: finish(True, by_powers))
+    pl.when(moderate & (seq_rank == 0))(lambda: finish(False, by_powers))
+    pl.when(jnp.logical_not(moderate))(lambda: finish(True, by_scores))
+
+
+def attention(
+    share, peer_share, powers, segments, queries, keys, values, behind_keys, behind_values
+):
     rows = queries.shape[0]
     kv_local = keys.shape[1] // HEAD_DIM
     mass = jax.ShapeDtypeStruct((kv_local, rows), jnp.float32)
     return pl.pallas_call(
         attention_kernel,
-        in_specs=[pl.BlockSpec(memory_space=pltpu.SMEM)]
-        + [pl.BlockSpec(memory_space=pltpu.VMEM)] * 7,
         out_shape=(jax.ShapeDtypeStruct(queries.shape, jnp.bfloat16), mass, mass),
         scratch_shapes=[pltpu.VMEM(share.shape, jnp.float32)],
         compiler_params=pltpu.CompilerParams(vmem_limit_bytes=VMEM_BYTES),
-    )(ranks, share, peer_share, segments, queries, keys, values, behind)
+    )(share, peer_share, powers, segments, queries, keys, values, behind_keys, behind_values)
 
 
 def pair_device(
@@ -244,13 +303,13 @@
     rows = activations.shape[0]
     swap = [(0, 1), (1, 0)]
     seq_rank = lax.axis_index("seq")
-    ranks = jnp.stack([seq_rank, lax.axis_index("heads")]).astype(jnp.int32)
+    segments = segment_ids.reshape(2, rows)
     hidden_local = gate_in.shape[1]
     gate_rows = lax.dynamic_slice_in_dim(gate_out, seq_rank * hidden_local, hidden_local, 0)
 
     peer_rows = lax.ppermute(activations, "seq", swap)
-    keys_values = jnp.concatenate([key_vectors, value_vectors], axis=1)
-    behind = lax.ppermute(keys_values, "seq", [(0, 1)])
+    behind_keys = lax.ppermute(key_vectors, "seq", [(0, 1)])
+    behind_values = lax.ppermute(value_vectors, "seq", [(0, 1)])
 
     def own_work(activations, conv_taps, gate_in, gate_rows):
         part, edges, held = own_project(activations, conv_taps, gate_in)
@@ -270,18 +329,22 @@
     peer_rows, own_share, edges, held = lax.optimization_barrier(
         (peer_rows, own_share, edges, held)
     )
-    peer_part = peer_project(ranks, peer_rows, edges, conv_taps, held)
+    peer_part = peer_project(peer_rows, edges, conv_taps, held)
+    peer_part, behind_keys = lax.optimization_barrier((peer_part, behind_keys))
     peer_part, peer_in = head_sum(peer_part)
-    share = logits_share(ranks, own_share, peer_part, peer_in, gate_rows)
+    powers = powers_of(segments, queries, key_vectors, behind_keys)
+    share = logits_share(own_share, peer_part, peer_in, gate_rows)
+    share, powers = lax.optimization_barrier((share, powers))
     attended, own_mass, behind_mass = attention(
-        ranks,
         share,
         lax.ppermute(share, "seq", swap),
-        segment_ids.reshape(2, rows),
+        powers,
+        segments,
         queries,
         key_vectors,
         value_vectors,
-        behind,
+        behind_keys,
+        behind_values,
     )
     key_mass = own_mass + lax.ppermute(behind_mass, "seq", [(1, 0)])
     return (attended, key_mass.astype(jnp.bfloat16))

time: 38.8 us -> 37.5 us (0.966)
  waiting for transfers between devices: 15.8 us -> 12.7 us
  starting transfers between devices: 12.9 us -> 15.9 us
  Pallas kernels: 8.15 us -> 6.98 us
    ppermute x1 -> x2, starting transfers between devices: 3.4 us -> 5.94 us  [the longest x1 4.02 us: pair_device(): behind_values = lax.ppermute(value_vectors, 'seq', [(0, 1)])]
    ppermute x1, waiting for transfers between devices: 2.26 us -> 0.14 us  [pair_device(): peer_rows = lax.ppermute(activations, 'seq', swap)]
    pallas_call x3 -> x4, Pallas kernels: 5.38 us -> 4.2 us  [the longest x1 1.58 us: peer_project(): pl.pallas_call(peer_project_kernel, out_shape=jax.ShapeDtypeStruct((done,...]
    ppermute x4, waiting for transfers between devices: 7.43 us -> 6.49 us  [head_sum(): received = lax.ppermute(sent, 'heads', route)]
    ppermute x4, starting transfers between devices: 3.54 us -> 4 us  [head_sum(): received = lax.ppermute(sent, 'heads', route)]
  transfers between devices with their start and end apart: 8 -> 9, of which waited for: 7 -> 6; matrix products, arithmetic and copies ran while one was open for 1% -> 1% of each run, Pallas kernels for 10% -> 15%
where the time goes in v4:
time: 37.5 us; the launch traced here: 37.2 us
  starting transfers between devices  15.9 us (42%)
  waiting for transfers between devices  12.7 us (34%)
  Pallas kernels  6.98 us (19%)
  between operations  0.76 us (2%)
  other arithmetic  0.59 us (2%)
    ppermute x4, waiting for transfers between devices, head_sum(): received = lax.ppermute(sent, 'heads', route)  6.49 us
    ppermute x1, waiting for transfers between devices, pair_device(): key_mass = own_mass + lax.ppermute(behind_mass, 'seq', [(1, 0)])  4.16 us
    ppermute x1, starting transfers between devices, pair_device(): behind_values = lax.ppermute(value_vectors, 'seq', [(0, 1)])  4.02 us
    ppermute x4, starting transfers between devices, head_sum(): received = lax.ppermute(sent, 'heads', route)  4 us
    ppermute x1, starting transfers between devices, pair_device(): peer_rows = lax.ppermute(activations, 'seq', swap)  3 us
    pallas_call x1, Pallas kernels, own_project(): pl.pallas_call(own_project_kernel, out_shape=(jax.ShapeDtypeStruct((done,...  2.57 us
    ppermute x1, waiting for transfers between devices, pair_device(): lax.ppermute(share, 'seq', swap)  1.93 us
    ppermute x1, starting transfers between devices, pair_device(): behind_keys = lax.ppermute(key_vectors, 'seq', [(0, 1)])  1.92 us
  transfers between devices with their start and end apart: 9, of which 6 were waited for; matrix products, arithmetic and copies ran while one was open for 1% of the time, Pallas kernels for 15%

profile of v4, /device:TPU:0, one launch (start us, length us, event | category | flops | bytes accessed | tf_op | source)
XLA Modules:
  0.0 37.2 jit_solution(1139587739523700414)
XLA Ops:
  0.6 0.0 copy-start
  0.6 3.0 %collective-permute-start.2 = (bf16[128,2048]{1,0:T(8,128)(2,1)}, bf16[128,2048]{1,0:T(8,128)(2,1)S(1)}, u32[]{:S(2)}, u32[]{:S(2)}) collective-permute-start(bf16[128,2048]{1,0:T(8,128)(2,1)} %param.10), channel_id=1, source_target_pairs={{0,16},{16,0},{1,17},{17,1},{2,18},{18,2},{3,19},{19,3},{4,20},{20... | collective-permute-start | bytes 1572872 | tf_op jit(solution)/shard_map/ppermute | solution.py:310
  3.6 1.9 %collective-permute-start.3 = (bf16[128,256]{1,0:T(8,128)(2,1)}, bf16[128,256]{1,0:T(8,128)(2,1)S(1)}, u32[]{:S(2)}, u32[]{:S(2)}) collective-permute-start(bf16[128,256]{1,0:T(8,128)(2,1)} %keys_ref.3), channel_id=1, source_target_pairs={{0,16},{1,17},{2,18},{3,19},{4,20},{5,21},{6,22},{7,23},{8,24},{9,... | collective-permute-start | bytes 196616 | tf_op jit(solution)/shard_map/ppermute | solution.py:311
  5.6 0.0 copy-done
  5.6 0.2 copy.12.gate_out_ref
  5.8 9.9 %conditional.1 = (f32[8,112]{1,0:T(8,128)S(1)}, bf16[32,2048]{1,0:T(8,128)(2,1)S(1)}, bf16[2048,512]{1,0:T(8,128)(2,1)S(1)}) conditional(s32[]{:T(128)} %convert_element_type.12, () %tuple.19, (bf16[128,2048]{1,0:T(8,128)(2,1)}, bf16[4,2048]{1,0:T(4,128)(2,1)}, bf16[2048,512]{1,0:T(8,128)(2,1)}, bf16[512,8]{1,0:T(8,128)(2,1)S(1)}) %tuple.20), branch_computations={%region_0.0_spmd, %region_1.0_spmd} | conditional | flops 114689 | bytes 2231840 | solution.py:318
  5.8 2.6 %branch_1_fun.2 = (f32[112,512]{1,0:T(8,128)S(1)}, bf16[32,2048]{1,0:T(8,128)(2,1)S(1)}, bf16[2048,512]{1,0:T(8,128)(2,1)S(1)}) custom-call(bf16[128,2048]{1,0:T(8,128)(2,1)} %get-tuple-element.8.rows_ref, bf16[4,2048]{1,0:T(4,128)(2,1)} %get-tuple-element.9.taps_ref, bf16[2048,512]{1,0:T(8,128)(2,1)} %get-tuple-element.46.gate_ref), custom_call_target="tpu_custom_call" | custom-call | flops 1 | bytes 1 | tf_op jit(solution)/shard_map/cond/branch_1_fun/pallas_call | solution.py:74
  8.4 0.1 collective-permute-start
  8.4 1.5 %collective-permute-done = f32[112,512]{1,0:T(8,128)S(1)} collective-permute-done((f32[112,512]{1,0:T(8,128)S(1)}, f32[112,512]{1,0:T(8,128)S(1)}, u32[]{:S(2)}, u32[]{:S(2)}) %collective-permute-start) | collective-permute-done | bytes 229408 | tf_op jit(solution)/shard_map/cond/branch_1_fun/ppermute | solution.py:111
  9.9 2.1 %collective-permute-start.1 = (bf16[112,512]{1,0:T(8,128)(2,1)S(1)}, bf16[112,512]{1,0:T(8,128)(2,1)S(1)}, u32[]{:S(2)}, u32[]{:S(2)}) collective-permute-start(bf16[112,512]{1,0:T(8,128)(2,1)S(1)} %get-tuple-element.47), channel_id=1, source_target_pairs={{0,8},{4,12},{8,0},{12,4},{1,9},{5,13},{9,1},{13,5},{2,10},{6,14},... | collective-permute-start | bytes 344072 | tf_op jit(solution)/shard_map/cond/branch_1_fun/ppermute | solution.py:111
  12.0 3.4 %collective-permute-done.1.in_ref = bf16[112,512]{1,0:T(8,128)(2,1)S(1)} collective-permute-done((bf16[112,512]{1,0:T(8,128)(2,1)S(1)}, bf16[112,512]{1,0:T(8,128)(2,1)S(1)}, u32[]{:S(2)}, u32[]{:S(2)}) %collective-permute-start.1) | collective-permute-done | bytes 114720 | tf_op jit(solution)/shard_map/cond/branch_1_fun/ppermute | solution.py:111
  15.5 0.2 branch_1_fun.3
  15.7 0.0 copy-start.3
  15.7 0.0 copy-start.1
  15.7 0.0 copy-start.2
  15.7 0.0 copy-start.4
  15.7 0.1 collective-permute-done.2.peer_ref
  15.8 1.6 %shard_map.96 = f32[144,512]{1,0:T(8,128)S(1)} custom-call(bf16[128,2048]{1,0:T(8,128)(2,1)S(1)} %collective-permute-done.2.peer_ref, bf16[32,2048]{1,0:T(8,128)(2,1)S(1)} %get-tuple-element.36.edges_ref, bf16[4,2048]{1,0:T(4,128)(2,1)} %taps_ref.1, bf16[2048,512]{1,0:T(8,128)(2,1)S(1)} %get-tuple-element.37.gate_ref), custom_call_target="tpu_custom_call" | custom-call | flops 1 | bytes 1 | tf_op jit(solution)/shard_map/pallas_call | solution.py:90
  17.4 0.0 collective-permute-done.3.behind_keys_ref
  17.4 0.1 collective-permute-start.4
  17.5 1.6 %collective-permute-done.4 = f32[144,512]{1,0:T(8,128)S(1)} collective-permute-done((f32[144,512]{1,0:T(8,128)S(1)}, f32[144,512]{1,0:T(8,128)S(1)}, u32[]{:S(2)}, u32[]{:S(2)}) %collective-permute-start.4) | collective-permute-done | bytes 294944 | tf_op jit(solution)/shard_map/ppermute | solution.py:111
  19.1 1.8 %collective-permute-start.5 = (bf16[144,512]{1,0:T(8,128)(2,1)S(1)}, bf16[144,512]{1,0:T(8,128)(2,1)S(1)}, u32[]{:S(2)}, u32[]{:S(2)}) collective-permute-start(bf16[144,512]{1,0:T(8,128)(2,1)S(1)} %get-tuple-element.49), channel_id=1, source_target_pairs={{0,8},{4,12},{8,0},{12,4},{1,9},{5,13},{9,1},{13,5},{2,10},{6,14},... | collective-permute-start | bytes 442376 | tf_op jit(solution)/shard_map/ppermute | solution.py:111
  20.9 0.0 copy-done.3
  20.9 4.0 %collective-permute-start.7 = (bf16[128,256]{1,0:T(8,128)(2,1)S(1)}, bf16[128,256]{1,0:T(8,128)(2,1)S(1)}, u32[]{:S(2)}, u32[]{:S(2)}) collective-permute-start(bf16[128,256]{1,0:T(8,128)(2,1)S(1)} %copy-done.3), channel_id=1, source_target_pairs={{0,16},{1,17},{2,18},{3,19},{4,20},{5,21},{6,22},{7,23},{8,24},{9,... | collective-permute-start | bytes 196616 | tf_op jit(solution)/shard_map/ppermute | solution.py:312
  24.9 0.0 copy-done.1
  24.9 0.0 copy-done.2
  24.9 0.0 copy-done.4
  25.0 0.7 %shard_map.98.powers_ref = f32[16,128,256]{2,1,0:T(8,128)S(1)} custom-call(s32[2,128]{1,0:T(2,128)S(1)} %bitcast.1, bf16[128,2048]{1,0:T(8,128)(2,1)S(1)} %copy-done.1, bf16[128,256]{1,0:T(8,128)(2,1)S(1)} %copy-done.2, bf16[128,256]{1,0:T(8,128)(2,1)S(1)} %collective-permute-done.3.behind_keys_ref), custom_call_target="tpu_custom_call" | custom-call | flops 134217728 | bytes 2097152 | tf_op jit(solution)/shard_map/pallas_call | solution.py:210
  25.7 0.0 collective-permute-done.5.in_ref
  25.7 0.4 shard_map.97.share_ref
  26.0 1.7 %collective-permute-start.6 = (f32[2,8,128]{2,1,0:T(8,128)S(1)}, f32[2,8,128]{2,1,0:T(8,128)S(1)}, u32[]{:S(2)}, u32[]{:S(2)}) collective-permute-start(f32[2,8,128]{2,1,0:T(8,128)S(1)} %shard_map.97.share_ref), channel_id=1, source_target_pairs={{0,16},{16,0},{1,17},{17,1},{2,18},{18,2},{3,19},{19,3},{4,20},{20... | collective-permute-start | bytes 24584 | tf_op jit(solution)/shard_map/ppermute | solution.py:340
  27.8 0.0 collective-permute-done.7.behind_values_ref
  27.8 1.9 %collective-permute-done.6.peer_share_ref = f32[2,8,128]{2,1,0:T(8,128)S(1)} collective-permute-done((f32[2,8,128]{2,1,0:T(8,128)S(1)}, f32[2,8,128]{2,1,0:T(8,128)S(1)}, u32[]{:S(2)}, u32[]{:S(2)}) %collective-permute-start.6) | collective-permute-done | bytes 8224 | tf_op jit(solution)/shard_map/ppermute | solution.py:340
  29.7 1.6 %shard_map.99 = (bf16[128,2048]{1,0:T(8,128)(2,1)}, f32[2,128]{1,0:T(2,128)S(1)}, f32[2,128]{1,0:T(2,128)S(1)}) custom-call(f32[2,8,128]{2,1,0:T(8,128)S(1)} %shard_map.97.share_ref, f32[2,8,128]{2,1,0:T(8,128)S(1)} %collective-permute-done.6.peer_share_ref, f32[16,128,256]{2,1,0:T(8,128)S(1)} %shard_map.98.powers_ref, s32[2,128]{1,0:T(2,128)S(1)} %bitcast.2, ...), custom_call_target="tpu_custom_call" | custom-call | tf_op jit(solution)/shard_map/pallas_call | solution.py:292
  31.3 1.3 %collective-permute-start.8 = (f32[2,128]{1,0:T(2,128)S(1)}, f32[2,128]{1,0:T(2,128)S(1)}, u32[]{:S(2)}, u32[]{:S(2)}) collective-permute-start(f32[2,128]{1,0:T(2,128)S(1)} %get-tuple-element.44), channel_id=1, source_target_pairs={{16,0},{17,1},{18,2},{19,3},{20,4},{21,5},{22,6},{23,7},{24,8},{25... | collective-permute-start | bytes 3080 | tf_op jit(solution)/shard_map/ppermute | solution.py:349
  32.5 4.2 %collective-permute-done.8 = f32[2,128]{1,0:T(2,128)S(1)} collective-permute-done((f32[2,128]{1,0:T(2,128)S(1)}, f32[2,128]{1,0:T(2,128)S(1)}, u32[]{:S(2)}, u32[]{:S(2)}) %collective-permute-start.8) | collective-permute-done | bytes 1056 | tf_op jit(solution)/shard_map/ppermute | solution.py:349
  36.7 0.5 %add_convert_fusion = bf16[2,128]{1,0:T(2,128)(2,1)} fusion(f32[2,128]{1,0:T(2,128)S(1)} %get-tuple-element.43, f32[2,128]{1,0:T(2,128)S(1)} %collective-permute-done.8), kind=kLoop, calls=%fused_computation | loop fusion | flops 512 | bytes 2560 | tf_op jit(solution)/shard_map/convert_element_type | solution.py:350
  (3 shorter events, 0.1 us)
Async XLA Ops:
  0.6 5.0 %copy-start = (bf16[1024,8]{0,1:T(8,128)(2,1)S(1)}, bf16[1024,8]{0,1:T(8,128)(2,1)}, u32[]{:S(2)}) copy-start(bf16[1024,8]{0,1:T(8,128)(2,1)} %param.13) | copy-start | bytes 49156
  0.6 15.2 %collective-permute-start.2 = (bf16[128,2048]{1,0:T(8,128)(2,1)}, bf16[128,2048]{1,0:T(8,128)(2,1)S(1)}, u32[]{:S(2)}, u32[]{:S(2)}) collective-permute-start(bf16[128,2048]{1,0:T(8,128)(2,1)} %param.10), channel_id=1, source_target_pairs={{0,16},{16,0},{1,17},{17,1},{2,18},{18,2},{3,19},{19,3},{4,20},{20... | collective-permute-start | bytes 1572872 | tf_op jit(solution)/shard_map/ppermute | solution.py:310
  3.6 13.8 %collective-permute-start.3 = (bf16[128,256]{1,0:T(8,128)(2,1)}, bf16[128,256]{1,0:T(8,128)(2,1)S(1)}, u32[]{:S(2)}, u32[]{:S(2)}) collective-permute-start(bf16[128,256]{1,0:T(8,128)(2,1)} %keys_ref.3), channel_id=1, source_target_pairs={{0,16},{1,17},{2,18},{3,19},{4,20},{5,21},{6,22},{7,23},{8,24},{9,... | collective-permute-start | bytes 196616 | tf_op jit(solution)/shard_map/ppermute | solution.py:311
  8.4 1.5 %collective-permute-start = (f32[112,512]{1,0:T(8,128)S(1)}, f32[112,512]{1,0:T(8,128)S(1)}, u32[]{:S(2)}, u32[]{:S(2)}) collective-permute-start(f32[112,512]{1,0:T(8,128)S(1)} %get-tuple-element.11), channel_id=1, source_target_pairs={{0,4},{4,0},{8,12},{12,8},{1,5},{5,1},{9,13},{13,9},{2,6},{6,2},{1... | collective-permute-start | bytes 688136 | tf_op jit(solution)/shard_map/cond/branch_1_fun/ppermute | solution.py:111
  9.9 5.5 %collective-permute-start.1 = (bf16[112,512]{1,0:T(8,128)(2,1)S(1)}, bf16[112,512]{1,0:T(8,128)(2,1)S(1)}, u32[]{:S(2)}, u32[]{:S(2)}) collective-permute-start(bf16[112,512]{1,0:T(8,128)(2,1)S(1)} %get-tuple-element.47), channel_id=1, source_target_pairs={{0,8},{4,12},{8,0},{12,4},{1,9},{5,13},{9,1},{13,5},{2,10},{6,14},... | collective-permute-start | bytes 344072 | tf_op jit(solution)/shard_map/cond/branch_1_fun/ppermute | solution.py:111
  15.7 5.2 %copy-start.3 = (bf16[128,256]{1,0:T(8,128)(2,1)S(1)}, bf16[128,256]{1,0:T(8,128)(2,1)}, u32[]{:S(2)}) copy-start(bf16[128,256]{1,0:T(8,128)(2,1)} %values_ref.1) | copy-start | bytes 196612
  15.7 9.2 %copy-start.1 = (bf16[128,2048]{1,0:T(8,128)(2,1)S(1)}, bf16[128,2048]{1,0:T(8,128)(2,1)}, u32[]{:S(2)}) copy-start(bf16[128,2048]{1,0:T(8,128)(2,1)} %queries_ref.3) | copy-start | bytes 1572868
  15.7 9.3 %copy-start.2 = (bf16[128,256]{1,0:T(8,128)(2,1)S(1)}, bf16[128,256]{1,0:T(8,128)(2,1)}, u32[]{:S(2)}) copy-start(bf16[128,256]{1,0:T(8,128)(2,1)} %keys_ref.3) | copy-start | bytes 196612
  15.7 9.3 %copy-start.4 = (s32[256]{0:T(256)S(1)}, s32[256]{0:T(256)}, u32[]{:S(2)}) copy-start(s32[256]{0:T(256)} %param.17) | copy-start | bytes 3076
  17.4 1.6 %collective-permute-start.4 = (f32[144,512]{1,0:T(8,128)S(1)}, f32[144,512]{1,0:T(8,128)S(1)}, u32[]{:S(2)}, u32[]{:S(2)}) collective-permute-start(f32[144,512]{1,0:T(8,128)S(1)} %shard_map.96), channel_id=1, source_target_pairs={{0,4},{4,0},{8,12},{12,8},{1,5},{5,1},{9,13},{13,9},{2,6},{6,2},{1... | collective-permute-start | bytes 884744 | tf_op jit(solution)/shard_map/ppermute | solution.py:111
  19.1 6.5 %collective-permute-start.5 = (bf16[144,512]{1,0:T(8,128)(2,1)S(1)}, bf16[144,512]{1,0:T(8,128)(2,1)S(1)}, u32[]{:S(2)}, u32[]{:S(2)}) collective-permute-start(bf16[144,512]{1,0:T(8,128)(2,1)S(1)} %get-tuple-element.49), channel_id=1, source_target_pairs={{0,8},{4,12},{8,0},{12,4},{1,9},{5,13},{9,1},{13,5},{2,10},{6,14},... | collective-permute-start | bytes 442376 | tf_op jit(solution)/shard_map/ppermute | solution.py:111
  20.9 6.9 %collective-permute-start.7 = (bf16[128,256]{1,0:T(8,128)(2,1)S(1)}, bf16[128,256]{1,0:T(8,128)(2,1)S(1)}, u32[]{:S(2)}, u32[]{:S(2)}) collective-permute-start(bf16[128,256]{1,0:T(8,128)(2,1)S(1)} %copy-done.3), channel_id=1, source_target_pairs={{0,16},{1,17},{2,18},{3,19},{4,20},{5,21},{6,22},{7,23},{8,24},{9,... | collective-permute-start | bytes 196616 | tf_op jit(solution)/shard_map/ppermute | solution.py:312
  26.0 3.7 %collective-permute-start.6 = (f32[2,8,128]{2,1,0:T(8,128)S(1)}, f32[2,8,128]{2,1,0:T(8,128)S(1)}, u32[]{:S(2)}, u32[]{:S(2)}) collective-permute-start(f32[2,8,128]{2,1,0:T(8,128)S(1)} %shard_map.97.share_ref), channel_id=1, source_target_pairs={{0,16},{16,0},{1,17},{17,1},{2,18},{18,2},{3,19},{19,3},{4,20},{20... | collective-permute-start | bytes 24584 | tf_op jit(solution)/shard_map/ppermute | solution.py:340
  31.3 5.5 %collective-permute-start.8 = (f32[2,128]{1,0:T(2,128)S(1)}, f32[2,128]{1,0:T(2,128)S(1)}, u32[]{:S(2)}, u32[]{:S(2)}) collective-permute-start(f32[2,128]{1,0:T(2,128)S(1)} %get-tuple-element.44), channel_id=1, source_target_pairs={{16,0},{17,1},{18,2},{19,3},{20,4},{21,5},{22,6},{23,7},{24,8},{25... | collective-permute-start | bytes 3080 | tf_op jit(solution)/shard_map/ppermute | solution.py:349

commit v5 on v4

--- a/solution.py
+++ b/solution.py
@@ -43,12 +43,13 @@
 
 
 def peer_project_kernel(
-    peer_ref, edges_ref, taps_ref, gate_ref, out_ref, widened, own_widened
+    peer_ref, edges_ref, taps_ref, gate_ref, near_ref, far_ref, far_sent_ref, widened, own_widened
 ):
     rows, features = peer_ref.shape
     tile = math.gcd(features, 512)
     first = lax.axis_index("seq") == 0
-    total = jnp.zeros(out_ref.shape, jnp.float32)
+    half = near_ref.shape[1]
+    total = jnp.zeros((near_ref.shape[0], 2 * half), jnp.float32)
     for start in range(0, features, tile):
         columns = slice(start, start + tile)
         own_tail = edges_ref[RIM_ROWS:, columns].astype(jnp.float32)
@@ -65,7 +66,9 @@
             axis=0,
         )
         total = total + jnp.dot(mixed, gate_ref[columns, :], preferred_element_type=jnp.float32)
-    out_ref[...] = total
+    near_ref[...] = total[:, :half]
+    far_ref[...] = total[:, half:]
+    far_sent_ref[...] = total[:, half:].astype(jnp.bfloat16)
 
 
 def own_project(activations, conv_taps, gate_in):
@@ -87,9 +90,14 @@
 def peer_project(peer_rows, edges, conv_taps, gate_in):
     rows, features = peer_rows.shape
     done = rows + RIM_ROWS
+    half = gate_in.shape[1] // 2
     return pl.pallas_call(
         peer_project_kernel,
-        out_shape=jax.ShapeDtypeStruct((done, gate_in.shape[1]), jnp.float32),
+        out_shape=(
+            jax.ShapeDtypeStruct((done, half), jnp.float32),
+            jax.ShapeDtypeStruct((done, half), jnp.float32),
+            jax.ShapeDtypeStruct((done, half), jnp.bfloat16),
+        ),
         scratch_shapes=[
             pltpu.VMEM((rows + RIM_ROWS, features), jnp.float32),
             pltpu.VMEM((2 * RIM_ROWS, features), jnp.float32),
@@ -106,23 +114,51 @@
     while step < count:
         if received is not None:
             part = part + received.astype(jnp.float32)
-        route = [(i, i ^ step) for i in range(count)]
-        sent = part if step == 1 else part.astype(jnp.bfloat16)
-        received = lax.ppermute(sent, "heads", route)
+        received = exchange_heads(part if step == 1 else part.astype(jnp.bfloat16), step)
         step *= 2
     return part, received
 
 
-def share_of_logits(pre_ref, in_ref, gate_out_ref):
+def exchange_heads(block, step):
+    count = lax.axis_size("heads")
+    return lax.ppermute(block, "heads", [(i, i ^ step) for i in range(count)])
+
+
+def in_one_piece(work, *given):
+    shapes = jax.eval_shape(work, *given)
+    return lax.cond(
+        lax.axis_index("seq") >= 0,
+        work,
+        lambda *given: jax.tree.map(lambda like: jnp.zeros(like.shape, like.dtype), shapes),
+        *given,
+    )
+
+
+def far_sum(block, sent):
+    step = lax.axis_size("heads") // 2
+    received = exchange_heads(sent, step)
+
+    def nearer(block, received):
+        distance = step
+        while distance > 1:
+            distance //= 2
+            block = block + received.astype(jnp.float32)
+            received = exchange_heads(block, distance)
+        return block, received
+
+    return in_one_piece(nearer, block, received)
+
+
+def share_of_logits(pre_ref, in_ref, gate_rows):
     pre = pre_ref[...] + in_ref[...].astype(jnp.float32)
     hidden = (pre / (1.0 + jnp.exp(-pre))).astype(jnp.bfloat16)
     return lax.dot_general(
-        gate_out_ref[...], hidden, (((0,), (1,)), ((), ())), preferred_element_type=jnp.float32
+        gate_rows, hidden, (((0,), (1,)), ((), ())), preferred_element_type=jnp.float32
     )
 
 
 def own_logits_kernel(own_ref, in_ref, gate_out_ref, out_ref):
-    out_ref[...] = share_of_logits(own_ref, in_ref, gate_out_ref)
+    out_ref[...] = share_of_logits(own_ref, in_ref, gate_out_ref[...])
 
 
 def own_logits(part, received, gate_rows):
@@ -133,22 +169,24 @@
     )(part, received, gate_rows)
 
 
-def logits_kernel(own_ref, peer_ref, in_ref, gate_out_ref, out_ref):
+def logits_kernel(own_ref, near_ref, near_in_ref, far_ref, far_in_ref, gate_out_ref, out_ref):
     first = lax.axis_index("seq") == 0
-    share = share_of_logits(peer_ref, in_ref, gate_out_ref)
+    half = near_ref.shape[1]
+    share = share_of_logits(near_ref, near_in_ref, gate_out_ref[:half])
+    share = share + share_of_logits(far_ref, far_in_ref, gate_out_ref[half:])
     own = jnp.concatenate([share[:, :RIM_ROWS], own_ref[...]], axis=1)
     peer = share[:, RIM_ROWS:]
     out_ref[0] = jnp.where(first, own, peer)
     out_ref[1] = jnp.where(first, peer, own)
 
 
-def logits_share(own_share, peer_part, peer_in, gate_rows):
+def logits_share(own_share, near, near_in, far, far_in, gate_rows):
     rows = own_share.shape[1] + RIM_ROWS
     return pl.pallas_call(
         logits_kernel,
         out_shape=jax.ShapeDtypeStruct((2, gate_rows.shape[1], rows), jnp.float32),
         compiler_params=pltpu.CompilerParams(vmem_limit_bytes=VMEM_BYTES),
-    )(own_share, peer_part, peer_in, gate_rows)
+    )(own_share, near, near_in, far, far_in, gate_rows)
 
 
 def hide_unseen(seq_rank, segments_ref, rows):
@@ -262,7 +300,7 @@
                 ).astype(jnp.bfloat16)
             mass = mass / group_size
             own_mass_ref[g : g + 1, :] = mass[:, rows - start :]
-            behind_mass_ref[g : g + 1, :] = mass[:, :rows]
+            behind_mass_ref[g : g + 1, :] = mass[:, :rows] if whole else jnp.zeros((1, rows))
 
     def by_powers(g, whole, start):
         factor = jnp.exp(biases[g] - jnp.max(biases[g]))[:, start:]
@@ -308,33 +346,26 @@
     gate_rows = lax.dynamic_slice_in_dim(gate_out, seq_rank * hidden_local, hidden_local, 0)
 
     peer_rows = lax.ppermute(activations, "seq", swap)
-    behind_keys = lax.ppermute(key_vectors, "seq", [(0, 1)])
-    behind_values = lax.ppermute(value_vectors, "seq", [(0, 1)])
+    behind_keys = lax.ppermute(key_vectors, "seq", swap)
+    behind_values = lax.ppermute(value_vectors, "seq", swap)
 
     def own_work(activations, conv_taps, gate_in, gate_rows):
         part, edges, held = own_project(activations, conv_taps, gate_in)
         return own_logits(*head_sum(part), gate_rows), edges, held
 
-    own_share, edges, held = lax.cond(
-        seq_rank >= 0,
-        own_work,
-        lambda *given: jax.tree.map(
-            lambda like: jnp.zeros(like.shape, like.dtype), jax.eval_shape(own_work, *given)
-        ),
-        activations,
-        conv_taps,
-        gate_in,
-        gate_rows,
-    )
+    own_share, edges, held = in_one_piece(own_work, activations, conv_taps, gate_in, gate_rows)
     peer_rows, own_share, edges, held = lax.optimization_barrier(
         (peer_rows, own_share, edges, held)
     )
-    peer_part = peer_project(peer_rows, edges, conv_taps, held)
-    peer_part, behind_keys = lax.optimization_barrier((peer_part, behind_keys))
-    peer_part, peer_in = head_sum(peer_part)
+    near, far, far_sent = peer_project(peer_rows, edges, conv_taps, held)
+    near, far, far_sent, behind_keys = lax.optimization_barrier(
+        (near, far, far_sent, behind_keys)
+    )
+    near, near_in = head_sum(near)
+    far, far_in = far_sum(far, far_sent)
+    share = logits_share(own_share, near, near_in, far, far_in, gate_rows)
+    share, queries = lax.optimization_barrier((share, queries))
     powers = powers_of(segments, queries, key_vectors, behind_keys)
-    share = logits_share(own_share, peer_part, peer_in, gate_rows)
-    share, powers = lax.optimization_barrier((share, powers))
     attended, own_mass, behind_mass = attention(
         share,
         lax.ppermute(share, "seq", swap),
@@ -346,7 +377,7 @@
         behind_keys,
         behind_values,
     )
-    key_mass = own_mass + lax.ppermute(behind_mass, "seq", [(1, 0)])
+    key_mass = own_mass + lax.ppermute(behind_mass, "seq", swap)
     return (attended, key_mass.astype(jnp.bfloat16))
 
 

time: 37.5 us -> 36.4 us (0.971)
  starting transfers between devices: 15.9 us -> 14 us
  Pallas kernels: 6.98 us -> 8.17 us
  waiting for transfers between devices: 12.7 us -> 11.9 us
  other arithmetic: 0.59 us -> 1.25 us
    ppermute x1, waiting for transfers between devices: 0.14 us -> 2.73 us  [pair_device(): peer_rows = lax.ppermute(activations, 'seq', swap)]
    ppermute x7 -> x9, waiting for transfers between devices: 10.7 us -> 8.19 us  [the longest x6 6.64 us: exchange_heads(): return lax.ppermute(block, 'heads', [(i, i ^ step) for i in range(count)])]
    ppermute x7 -> x9, starting transfers between devices: 11.2 us -> 9.02 us  [the longest x6 5.36 us: exchange_heads(): return lax.ppermute(block, 'heads', [(i, i ^ step) for i in range(count)])]
    ppermute x1, waiting for transfers between devices: 1.93 us -> 0.95 us  [pair_device(): lax.ppermute(share, 'seq', swap)]
    pallas_call x1, Pallas kernels: 0.36 us -> 1.33 us  [logits_share(): pl.pallas_call(logits_kernel, out_shape=jax.ShapeDtypeStruct((2, gate_row...]
    add x0 -> x1, other arithmetic: none -> 0.68 us  [nearer(): block = block + received.astype(jnp.float32)]
  transfers between devices with their start and end apart: 9 -> 11, of which waited for: 6 -> 6; matrix products, arithmetic and copies ran while one was open for 1% -> 2% of each run, Pallas kernels for 15% -> 18%
where the time goes in v5:
time: 36.4 us; the launch traced here: 36.2 us
  starting transfers between devices  14 us (38%)
  waiting for transfers between devices  11.9 us (33%)
  Pallas kernels  8.17 us (22%)
  other arithmetic  1.25 us (3%)
  between operations  0.69 us (2%)
    ppermute x6, waiting for transfers between devices, exchange_heads(): return lax.ppermute(block, 'heads', [(i, i ^ step) for i in range(count)])  6.64 us
    ppermute x6, starting transfers between devices, exchange_heads(): return lax.ppermute(block, 'heads', [(i, i ^ step) for i in range(count)])  5.36 us
    ppermute x1, starting transfers between devices, pair_device(): peer_rows = lax.ppermute(activations, 'seq', swap)  3 us
    ppermute x1, waiting for transfers between devices, pair_device(): peer_rows = lax.ppermute(activations, 'seq', swap)  2.73 us
    pallas_call x1, Pallas kernels, own_project(): pl.pallas_call(own_project_kernel, out_shape=(jax.ShapeDtypeStruct((done,...  2.57 us
    ppermute x1, starting transfers between devices, pair_device(): key_mass = own_mass + lax.ppermute(behind_mass, 'seq', swap)  2.09 us
    ppermute x1, starting transfers between devices, pair_device(): lax.ppermute(share, 'seq', swap)  1.99 us
    pallas_call x1, Pallas kernels, peer_project(): pl.pallas_call(peer_project_kernel, out_shape=(jax.ShapeDtypeStruct((done...  1.81 us
  transfers between devices with their start and end apart: 11, of which 6 were waited for; matrix products, arithmetic and copies ran while one was open for 2% of the time, Pallas kernels for 18%

profile of v5, /device:TPU:0, one launch (start us, length us, event | category | flops | bytes accessed | tf_op | source)
XLA Modules:
  0.0 36.2 jit_solution(15064890690331106559)
XLA Ops:
  0.6 0.0 copy-start
  0.6 3.0 %collective-permute-start.3 = (bf16[128,2048]{1,0:T(8,128)(2,1)}, bf16[128,2048]{1,0:T(8,128)(2,1)S(1)}, u32[]{:S(2)}, u32[]{:S(2)}) collective-permute-start(bf16[128,2048]{1,0:T(8,128)(2,1)} %param.12), channel_id=1, source_target_pairs={{0,16},{16,0},{1,17},{17,1},{2,18},{18,2},{3,19},{19,3},{4,20},{20... | collective-permute-start | bytes 1572872 | tf_op jit(solution)/shard_map/ppermute | solution.py:348
  3.6 0.1 collective-permute-start.4
  3.7 0.0 copy-done
  3.7 0.2 copy.12.gate_out_ref
  3.9 9.9 %conditional.2 = (f32[8,112]{1,0:T(8,128)S(1)}, bf16[32,2048]{1,0:T(8,128)(2,1)S(1)}, bf16[2048,512]{1,0:T(8,128)(2,1)S(1)}) conditional(s32[]{:T(128)} %convert_element_type.16, () %tuple.27, (bf16[128,2048]{1,0:T(8,128)(2,1)}, bf16[4,2048]{1,0:T(4,128)(2,1)}, bf16[2048,512]{1,0:T(8,128)(2,1)}, bf16[512,8]{1,0:T(8,128)(2,1)S(1)}) %tuple.28), branch_computations={%region_0.0_spmd, %region_1.0_spmd} | conditional | flops 114689 | bytes 2231840 | solution.py:129
  3.9 2.6 %branch_1_fun.2 = (f32[112,512]{1,0:T(8,128)S(1)}, bf16[32,2048]{1,0:T(8,128)(2,1)S(1)}, bf16[2048,512]{1,0:T(8,128)(2,1)S(1)}) custom-call(bf16[128,2048]{1,0:T(8,128)(2,1)} %get-tuple-element.12.rows_ref, bf16[4,2048]{1,0:T(4,128)(2,1)} %get-tuple-element.13.taps_ref, bf16[2048,512]{1,0:T(8,128)(2,1)} %get-tuple-element.66.gate_ref), custom_call_target="tpu_custom_call" | custom-call | flops 1 | bytes 1 | tf_op jit(solution)/shard_map/cond/branch_1_fun/pallas_call | solution.py:77
  6.5 0.1 collective-permute-start.1
  6.6 1.5 %collective-permute-done.1 = f32[112,512]{1,0:T(8,128)S(1)} collective-permute-done((f32[112,512]{1,0:T(8,128)S(1)}, f32[112,512]{1,0:T(8,128)S(1)}, u32[]{:S(2)}, u32[]{:S(2)}) %collective-permute-start.1) | collective-permute-done | bytes 229408 | tf_op jit(solution)/shard_map/cond/branch_1_fun/ppermute | solution.py:124
  8.1 2.0 %collective-permute-start.2 = (bf16[112,512]{1,0:T(8,128)(2,1)S(1)}, bf16[112,512]{1,0:T(8,128)(2,1)S(1)}, u32[]{:S(2)}, u32[]{:S(2)}) collective-permute-start(bf16[112,512]{1,0:T(8,128)(2,1)S(1)} %get-tuple-element.67), channel_id=1, source_target_pairs={{0,8},{4,12},{8,0},{12,4},{1,9},{5,13},{9,1},{13,5},{2,10},{6,14},... | collective-permute-start | bytes 344072 | tf_op jit(solution)/shard_map/cond/branch_1_fun/ppermute | solution.py:124
  10.1 3.4 %collective-permute-done.2.in_ref = bf16[112,512]{1,0:T(8,128)(2,1)S(1)} collective-permute-done((bf16[112,512]{1,0:T(8,128)(2,1)S(1)}, bf16[112,512]{1,0:T(8,128)(2,1)S(1)}, u32[]{:S(2)}, u32[]{:S(2)}) %collective-permute-start.2) | collective-permute-done | bytes 114720 | tf_op jit(solution)/shard_map/cond/branch_1_fun/ppermute | solution.py:124
  13.6 0.2 branch_1_fun.3
  13.8 0.0 copy-start.5
  13.8 0.0 copy-start.3
  13.8 2.7 %collective-permute-done.3.peer_ref = bf16[128,2048]{1,0:T(8,128)(2,1)S(1)} collective-permute-done((bf16[128,2048]{1,0:T(8,128)(2,1)}, bf16[128,2048]{1,0:T(8,128)(2,1)S(1)}, u32[]{:S(2)}, u32[]{:S(2)}) %collective-permute-start.3) | collective-permute-done | bytes 524320 | tf_op jit(solution)/shard_map/ppermute | solution.py:348
  16.5 0.0 copy-done.5
  16.5 0.0 copy-start.1
  16.5 0.0 copy-start.2
  16.5 0.0 copy-start.4
  16.5 1.8 %shard_map.96 = (f32[144,256]{1,0:T(8,128)S(1)}, f32[144,256]{1,0:T(8,128)S(1)}, bf16[144,256]{1,0:T(8,128)(2,1)S(1)}) custom-call(bf16[128,2048]{1,0:T(8,128)(2,1)S(1)} %collective-permute-done.3.peer_ref, bf16[32,2048]{1,0:T(8,128)(2,1)} %copy-done.5, bf16[4,2048]{1,0:T(4,128)(2,1)} %taps_ref.1, bf16[2048,512]{1,0:T(8,128)(2,1)S(1)} %get-tuple-element.50.gate_ref), custom_call_target="tpu_custom_call" | custom-call | flops 1 | bytes 1 | tf_op jit(solution)/shard_map/pallas_call | solution.py:94
  18.3 0.0 collective-permute-done.4.behind_keys_ref
  18.3 0.1 collective-permute-start.5
  18.4 1.8 %collective-permute-start.7 = (bf16[144,256]{1,0:T(8,128)(2,1)S(1)}, bf16[144,256]{1,0:T(8,128)(2,1)S(1)}, u32[]{:S(2)}, u32[]{:S(2)}) collective-permute-start(bf16[144,256]{1,0:T(8,128)(2,1)S(1)} %get-tuple-element.55), channel_id=1, source_target_pairs={{0,8},{4,12},{8,0},{12,4},{1,9},{5,13},{9,1},{13,5},{2,10},{6,14},... | collective-permute-start | bytes 221192 | tf_op jit(solution)/shard_map/ppermute | solution.py:124
  20.2 0.0 collective-permute-done.5
  20.3 1.4 %collective-permute-start.6 = (bf16[144,256]{1,0:T(8,128)(2,1)S(1)}, bf16[144,256]{1,0:T(8,128)(2,1)S(1)}, u32[]{:S(2)}, u32[]{:S(2)}) collective-permute-start(bf16[144,256]{1,0:T(8,128)(2,1)S(1)} %get-tuple-element.69), channel_id=1, source_target_pairs={{0,8},{4,12},{8,0},{12,4},{1,9},{5,13},{9,1},{13,5},{2,10},{6,14},... | collective-permute-start | bytes 221192 | tf_op jit(solution)/shard_map/ppermute | solution.py:124
  21.6 0.0 copy-done.3
  21.6 1.5 %collective-permute-start.9 = (bf16[128,256]{1,0:T(8,128)(2,1)S(1)}, bf16[128,256]{1,0:T(8,128)(2,1)S(1)}, u32[]{:S(2)}, u32[]{:S(2)}) collective-permute-start(bf16[128,256]{1,0:T(8,128)(2,1)S(1)} %copy-done.3), channel_id=1, source_target_pairs={{0,16},{16,0},{1,17},{17,1},{2,18},{18,2},{3,19},{19,3},{4,20},{20... | collective-permute-start | bytes 196616 | tf_op jit(solution)/shard_map/ppermute | solution.py:350
  23.1 0.0 collective-permute-done.7
  23.1 2.4 %conditional.3 = (f32[144,256]{1,0:T(8,128)}, f32[144,256]{1,0:T(8,128)}) conditional(s32[]{:T(128)} %convert_element_type.16, () %tuple.31, (bf16[144,256]{1,0:T(8,128)(2,1)S(1)}, f32[144,256]{1,0:T(8,128)S(1)}) %tuple.32), branch_computations={%region_2.0_spmd, %region_3.0_spmd} | conditional | flops 73728 | bytes 958520 | solution.py:129
  23.1 0.7 %convert_add_fusion = f32[144,256]{1,0:T(8,128)} fusion(f32[144,256]{1,0:T(8,128)S(1)} %get-tuple-element.19, bf16[144,256]{1,0:T(8,128)(2,1)S(1)} %get-tuple-element.20), kind=kLoop, calls=%fused_computation | loop fusion | flops 73728 | bytes 368640 | tf_op jit(solution)/shard_map/cond/branch_1_fun/add | solution.py:145
  23.8 0.0 collective-permute-start
  23.8 1.7 %collective-permute-done = f32[144,256]{1,0:T(8,128)} collective-permute-done((f32[144,256]{1,0:T(8,128)}, f32[144,256]{1,0:T(8,128)}, u32[]{:S(2)}, u32[]{:S(2)}) %collective-permute-start) | collective-permute-done | bytes 147488 | tf_op jit(solution)/shard_map/cond/branch_1_fun/ppermute | solution.py:124
  25.5 0.0 collective-permute-done.6.near_in_ref
  25.5 1.3 %shard_map.97.share_ref = f32[2,8,128]{2,1,0:T(8,128)S(1)} custom-call(f32[8,112]{1,0:T(8,128)S(1)} %get-tuple-element.47.own_ref, f32[144,256]{1,0:T(8,128)S(1)} %get-tuple-element.70.near_ref, bf16[144,256]{1,0:T(8,128)(2,1)S(1)} %collective-permute-done.6.near_in_ref, f32[144,256]{1,0:T(8,128)} %get-tuple-element.57.far_ref, ...), custom_call_target="tpu_custom_call" | custom-call | tf_op jit(solution)/shard_map/pallas_call | solution.py:185
  26.8 2.0 %collective-permute-start.8 = (f32[2,8,128]{2,1,0:T(8,128)S(1)}, f32[2,8,128]{2,1,0:T(8,128)S(1)}, u32[]{:S(2)}, u32[]{:S(2)}) collective-permute-start(f32[2,8,128]{2,1,0:T(8,128)S(1)} %shard_map.97.share_ref), channel_id=1, source_target_pairs={{0,16},{16,0},{1,17},{17,1},{2,18},{18,2},{3,19},{19,3},{4,20},{20... | collective-permute-start | bytes 24584 | tf_op jit(solution)/shard_map/ppermute | solution.py:371
  28.8 0.0 copy-done.1
  28.8 0.0 copy-done.2
  28.8 0.0 copy-done.4
  28.8 0.7 %shard_map.98.powers_ref = f32[16,128,256]{2,1,0:T(8,128)S(1)} custom-call(s32[2,128]{1,0:T(2,128)S(1)} %bitcast.1, bf16[128,2048]{1,0:T(8,128)(2,1)S(1)} %copy-done.1, bf16[128,256]{1,0:T(8,128)(2,1)S(1)} %copy-done.2, bf16[128,256]{1,0:T(8,128)(2,1)S(1)} %collective-permute-done.4.behind_keys_ref), custom_call_target="tpu_custom_call" | custom-call | flops 134217728 | bytes 2097152 | tf_op jit(solution)/shard_map/pallas_call | solution.py:248
  29.5 0.0 collective-permute-done.9.behind_values_ref
  29.6 0.9 %collective-permute-done.8.peer_share_ref = f32[2,8,128]{2,1,0:T(8,128)S(1)} collective-permute-done((f32[2,8,128]{2,1,0:T(8,128)S(1)}, f32[2,8,128]{2,1,0:T(8,128)S(1)}, u32[]{:S(2)}, u32[]{:S(2)}) %collective-permute-start.8) | collective-permute-done | bytes 8224 | tf_op jit(solution)/shard_map/ppermute | solution.py:371
  30.5 1.6 %shard_map.99 = (bf16[128,2048]{1,0:T(8,128)(2,1)}, f32[2,128]{1,0:T(2,128)S(1)}, f32[2,128]{1,0:T(2,128)S(1)}) custom-call(f32[2,8,128]{2,1,0:T(8,128)S(1)} %shard_map.97.share_ref, f32[2,8,128]{2,1,0:T(8,128)S(1)} %collective-permute-done.8.peer_share_ref, f32[16,128,256]{2,1,0:T(8,128)S(1)} %shard_map.98.powers_ref, s32[2,128]{1,0:T(2,128)S(1)} %bitcast.2, ...), custom_call_target="tpu_custom_call" | custom-call | tf_op jit(solution)/shard_map/pallas_call | solution.py:330
  32.1 2.1 %collective-permute-start.10 = (f32[2,128]{1,0:T(2,128)S(1)}, f32[2,128]{1,0:T(2,128)S(1)}, u32[]{:S(2)}, u32[]{:S(2)}) collective-permute-start(f32[2,128]{1,0:T(2,128)S(1)} %get-tuple-element.64), channel_id=1, source_target_pairs={{0,16},{16,0},{1,17},{17,1},{2,18},{18,2},{3,19},{19,3},{4,20},{20... | collective-permute-start | bytes 3080 | tf_op jit(solution)/shard_map/ppermute | solution.py:380
  34.1 1.5 %collective-permute-done.10 = f32[2,128]{1,0:T(2,128)S(1)} collective-permute-done((f32[2,128]{1,0:T(2,128)S(1)}, f32[2,128]{1,0:T(2,128)S(1)}, u32[]{:S(2)}, u32[]{:S(2)}) %collective-permute-start.10) | collective-permute-done | bytes 1056 | tf_op jit(solution)/shard_map/ppermute | solution.py:380
  35.7 0.5 %add_convert_fusion = bf16[2,128]{1,0:T(2,128)(2,1)} fusion(f32[2,128]{1,0:T(2,128)S(1)} %get-tuple-element.63, f32[2,128]{1,0:T(2,128)S(1)} %collective-permute-done.10), kind=kLoop, calls=%fused_computation.1 | loop fusion | flops 512 | bytes 2560 | tf_op jit(solution)/shard_map/convert_element_type | solution.py:381
  (3 shorter events, 0.1 us)
Async XLA Ops:
  0.6 3.1 %copy-start = (bf16[1024,8]{0,1:T(8,128)(2,1)S(1)}, bf16[1024,8]{0,1:T(8,128)(2,1)}, u32[]{:S(2)}) copy-start(bf16[1024,8]{0,1:T(8,128)(2,1)} %param.15) | copy-start | bytes 49156
  0.6 15.8 %collective-permute-start.3 = (bf16[128,2048]{1,0:T(8,128)(2,1)}, bf16[128,2048]{1,0:T(8,128)(2,1)S(1)}, u32[]{:S(2)}, u32[]{:S(2)}) collective-permute-start(bf16[128,2048]{1,0:T(8,128)(2,1)} %param.12), channel_id=1, source_target_pairs={{0,16},{16,0},{1,17},{17,1},{2,18},{18,2},{3,19},{19,3},{4,20},{20... | collective-permute-start | bytes 1572872 | tf_op jit(solution)/shard_map/ppermute | solution.py:348
  3.6 14.7 %collective-permute-start.4 = (bf16[128,256]{1,0:T(8,128)(2,1)}, bf16[128,256]{1,0:T(8,128)(2,1)S(1)}, u32[]{:S(2)}, u32[]{:S(2)}) collective-permute-start(bf16[128,256]{1,0:T(8,128)(2,1)} %keys_ref.3), channel_id=1, source_target_pairs={{0,16},{16,0},{1,17},{17,1},{2,18},{18,2},{3,19},{19,3},{4,20},{20... | collective-permute-start | bytes 196616 | tf_op jit(solution)/shard_map/ppermute | solution.py:349
  6.5 1.5 %collective-permute-start.1 = (f32[112,512]{1,0:T(8,128)S(1)}, f32[112,512]{1,0:T(8,128)S(1)}, u32[]{:S(2)}, u32[]{:S(2)}) collective-permute-start(f32[112,512]{1,0:T(8,128)S(1)} %get-tuple-element.15), channel_id=1, source_target_pairs={{0,4},{4,0},{8,12},{12,8},{1,5},{5,1},{9,13},{13,9},{2,6},{6,2},{1... | collective-permute-start | bytes 688136 | tf_op jit(solution)/shard_map/cond/branch_1_fun/ppermute | solution.py:124
  8.1 5.5 %collective-permute-start.2 = (bf16[112,512]{1,0:T(8,128)(2,1)S(1)}, bf16[112,512]{1,0:T(8,128)(2,1)S(1)}, u32[]{:S(2)}, u32[]{:S(2)}) collective-permute-start(bf16[112,512]{1,0:T(8,128)(2,1)S(1)} %get-tuple-element.67), channel_id=1, source_target_pairs={{0,8},{4,12},{8,0},{12,4},{1,9},{5,13},{9,1},{13,5},{2,10},{6,14},... | collective-permute-start | bytes 344072 | tf_op jit(solution)/shard_map/cond/branch_1_fun/ppermute | solution.py:124
  13.8 2.7 %copy-start.5 = (bf16[32,2048]{1,0:T(8,128)(2,1)}, bf16[32,2048]{1,0:T(8,128)(2,1)S(1)}, u32[]{:S(2)}) copy-start(bf16[32,2048]{1,0:T(8,128)(2,1)S(1)} %get-tuple-element.49.edges_ref) | copy-start | bytes 393220
  13.8 7.9 %copy-start.3 = (bf16[128,256]{1,0:T(8,128)(2,1)S(1)}, bf16[128,256]{1,0:T(8,128)(2,1)}, u32[]{:S(2)}) copy-start(bf16[128,256]{1,0:T(8,128)(2,1)} %values_ref.1) | copy-start | bytes 196612
  16.5 12.3 %copy-start.1 = (bf16[128,2048]{1,0:T(8,128)(2,1)S(1)}, bf16[128,2048]{1,0:T(8,128)(2,1)}, u32[]{:S(2)}) copy-start(bf16[128,2048]{1,0:T(8,128)(2,1)} %queries_ref.1) | copy-start | bytes 1572868
  16.5 12.3 %copy-start.2 = (bf16[128,256]{1,0:T(8,128)(2,1)S(1)}, bf16[128,256]{1,0:T(8,128)(2,1)}, u32[]{:S(2)}) copy-start(bf16[128,256]{1,0:T(8,128)(2,1)} %keys_ref.3) | copy-start | bytes 196612
  16.5 12.3 %copy-start.4 = (s32[256]{0:T(256)S(1)}, s32[256]{0:T(256)}, u32[]{:S(2)}) copy-start(s32[256]{0:T(256)} %param.19) | copy-start | bytes 3076
  18.3 1.9 %collective-permute-start.5 = (f32[144,256]{1,0:T(8,128)S(1)}, f32[144,256]{1,0:T(8,128)S(1)}, u32[]{:S(2)}, u32[]{:S(2)}) collective-permute-start(f32[144,256]{1,0:T(8,128)S(1)} %get-tuple-element.54), channel_id=1, source_target_pairs={{0,4},{4,0},{8,12},{12,8},{1,5},{5,1},{9,13},{13,9},{2,6},{6,2},{1... | collective-permute-start | bytes 442376 | tf_op jit(solution)/shard_map/ppermute | solution.py:124
  18.4 4.7 %collective-permute-start.7 = (bf16[144,256]{1,0:T(8,128)(2,1)S(1)}, bf16[144,256]{1,0:T(8,128)(2,1)S(1)}, u32[]{:S(2)}, u32[]{:S(2)}) collective-permute-start(bf16[144,256]{1,0:T(8,128)(2,1)S(1)} %get-tuple-element.55), channel_id=1, source_target_pairs={{0,8},{4,12},{8,0},{12,4},{1,9},{5,13},{9,1},{13,5},{2,10},{6,14},... | collective-permute-start | bytes 221192 | tf_op jit(solution)/shard_map/ppermute | solution.py:124
  20.3 5.2 %collective-permute-start.6 = (bf16[144,256]{1,0:T(8,128)(2,1)S(1)}, bf16[144,256]{1,0:T(8,128)(2,1)S(1)}, u32[]{:S(2)}, u32[]{:S(2)}) collective-permute-start(bf16[144,256]{1,0:T(8,128)(2,1)S(1)} %get-tuple-element.69), channel_id=1, source_target_pairs={{0,8},{4,12},{8,0},{12,4},{1,9},{5,13},{9,1},{13,5},{2,10},{6,14},... | collective-permute-start | bytes 221192 | tf_op jit(solution)/shard_map/ppermute | solution.py:124
  21.6 7.9 %collective-permute-start.9 = (bf16[128,256]{1,0:T(8,128)(2,1)S(1)}, bf16[128,256]{1,0:T(8,128)(2,1)S(1)}, u32[]{:S(2)}, u32[]{:S(2)}) collective-permute-start(bf16[128,256]{1,0:T(8,128)(2,1)S(1)} %copy-done.3), channel_id=1, source_target_pairs={{0,16},{16,0},{1,17},{17,1},{2,18},{18,2},{3,19},{19,3},{4,20},{20... | collective-permute-start | bytes 196616 | tf_op jit(solution)/shard_map/ppermute | solution.py:350
  23.8 1.7 %collective-permute-start = (f32[144,256]{1,0:T(8,128)}, f32[144,256]{1,0:T(8,128)}, u32[]{:S(2)}, u32[]{:S(2)}) collective-permute-start(f32[144,256]{1,0:T(8,128)} %convert_add_fusion), channel_id=1, source_target_pairs={{0,4},{4,0},{8,12},{12,8},{1,5},{5,1},{9,13},{13,9},{2,6},{6,2},{1... | collective-permute-start | bytes 442376 | tf_op jit(solution)/shard_map/cond/branch_1_fun/ppermute | solution.py:124
  26.8 3.7 %collective-permute-start.8 = (f32[2,8,128]{2,1,0:T(8,128)S(1)}, f32[2,8,128]{2,1,0:T(8,128)S(1)}, u32[]{:S(2)}, u32[]{:S(2)}) collective-permute-start(f32[2,8,128]{2,1,0:T(8,128)S(1)} %shard_map.97.share_ref), channel_id=1, source_target_pairs={{0,16},{16,0},{1,17},{17,1},{2,18},{18,2},{3,19},{19,3},{4,20},{20... | collective-permute-start | bytes 24584 | tf_op jit(solution)/shard_map/ppermute | solution.py:371
  32.1 3.6 %collective-permute-start.10 = (f32[2,128]{1,0:T(2,128)S(1)}, f32[2,128]{1,0:T(2,128)S(1)}, u32[]{:S(2)}, u32[]{:S(2)}) collective-permute-start(f32[2,128]{1,0:T(2,128)S(1)} %get-tuple-element.64), channel_id=1, source_target_pairs={{0,16},{16,0},{1,17},{17,1},{2,18},{18,2},{3,19},{19,3},{4,20},{20... | collective-permute-start | bytes 3080 | tf_op jit(solution)/shard_map/ppermute | solution.py:380

commit v6 on v5

--- a/solution.py
+++ b/solution.py
@@ -134,19 +134,19 @@
     )
 
 
-def far_sum(block, sent):
+def far_logits(block, sent, gate_rows):
     step = lax.axis_size("heads") // 2
     received = exchange_heads(sent, step)
 
-    def nearer(block, received):
+    def nearer(block, received, gate_rows):
         distance = step
         while distance > 1:
             distance //= 2
             block = block + received.astype(jnp.float32)
             received = exchange_heads(block, distance)
-        return block, received
-
-    return in_one_piece(nearer, block, received)
+        return partial_logits(block, received, gate_rows)
+
+    return in_one_piece(nearer, block, received, gate_rows)
 
 
 def share_of_logits(pre_ref, in_ref, gate_rows):
@@ -157,36 +157,34 @@
     )
 
 
-def own_logits_kernel(own_ref, in_ref, gate_out_ref, out_ref):
+def partial_logits_kernel(own_ref, in_ref, gate_out_ref, out_ref):
     out_ref[...] = share_of_logits(own_ref, in_ref, gate_out_ref[...])
 
 
-def own_logits(part, received, gate_rows):
-    return pl.pallas_call(
-        own_logits_kernel,
+def partial_logits(part, received, gate_rows):
+    return pl.pallas_call(
+        partial_logits_kernel,
         out_shape=jax.ShapeDtypeStruct((gate_rows.shape[1], part.shape[0]), jnp.float32),
         compiler_params=pltpu.CompilerParams(vmem_limit_bytes=VMEM_BYTES),
     )(part, received, gate_rows)
 
 
-def logits_kernel(own_ref, near_ref, near_in_ref, far_ref, far_in_ref, gate_out_ref, out_ref):
+def logits_kernel(own_ref, far_share_ref, near_ref, near_in_ref, gate_out_ref, out_ref):
     first = lax.axis_index("seq") == 0
-    half = near_ref.shape[1]
-    share = share_of_logits(near_ref, near_in_ref, gate_out_ref[:half])
-    share = share + share_of_logits(far_ref, far_in_ref, gate_out_ref[half:])
+    share = share_of_logits(near_ref, near_in_ref, gate_out_ref[...]) + far_share_ref[...]
     own = jnp.concatenate([share[:, :RIM_ROWS], own_ref[...]], axis=1)
     peer = share[:, RIM_ROWS:]
     out_ref[0] = jnp.where(first, own, peer)
     out_ref[1] = jnp.where(first, peer, own)
 
 
-def logits_share(own_share, near, near_in, far, far_in, gate_rows):
+def logits_share(own_share, far_share, near, near_in, gate_rows):
     rows = own_share.shape[1] + RIM_ROWS
     return pl.pallas_call(
         logits_kernel,
         out_shape=jax.ShapeDtypeStruct((2, gate_rows.shape[1], rows), jnp.float32),
         compiler_params=pltpu.CompilerParams(vmem_limit_bytes=VMEM_BYTES),
-    )(own_share, near, near_in, far, far_in, gate_rows)
+    )(own_share, far_share, near, near_in, gate_rows)
 
 
 def hide_unseen(seq_rank, segments_ref, rows):
@@ -257,17 +255,15 @@
     )(segments, queries, keys, behind_keys)
 
 
-def attention_kernel(
+def weights_kernel(
     share_ref,
     peer_share_ref,
     powers_ref,
     segments_ref,
     queries_ref,
     keys_ref,
-    values_ref,
     behind_keys_ref,
-    behind_values_ref,
-    attended_ref,
+    weights_ref,
     own_mass_ref,
     behind_mass_ref,
     retention,
@@ -288,16 +284,13 @@
     def finish(whole, terms_of):
         start = 0 if whole else rows
         for g in range(kv_local):
-            values = with_behind(values_ref, behind_values_ref, g, whole)
             mass = jnp.zeros((1, 2 * rows - start), jnp.float32)
             group_terms = terms_of(g, whole, start)
             for head in range(g * group_size, (g + 1) * group_size):
                 weights = group_terms(head)
                 weights = weights * (1.0 / jnp.sum(weights, axis=1, keepdims=True))
                 mass = mass + jnp.sum(weights, axis=0, keepdims=True)
-                attended_ref[:, head_columns(head)] = jnp.dot(
-                    weights.astype(jnp.bfloat16), values, preferred_element_type=jnp.float32
-                ).astype(jnp.bfloat16)
+                weights_ref[head, :, start:] = weights.astype(jnp.bfloat16)
             mass = mass / group_size
             own_mass_ref[g : g + 1, :] = mass[:, rows - start :]
             behind_mass_ref[g : g + 1, :] = mass[:, :rows] if whole else jnp.zeros((1, rows))
@@ -321,18 +314,46 @@
     pl.when(jnp.logical_not(moderate))(lambda: finish(True, by_scores))
 
 
-def attention(
-    share, peer_share, powers, segments, queries, keys, values, behind_keys, behind_values
-):
+def weights_of(share, peer_share, powers, segments, queries, keys, behind_keys):
     rows = queries.shape[0]
-    kv_local = keys.shape[1] // HEAD_DIM
-    mass = jax.ShapeDtypeStruct((kv_local, rows), jnp.float32)
-    return pl.pallas_call(
-        attention_kernel,
-        out_shape=(jax.ShapeDtypeStruct(queries.shape, jnp.bfloat16), mass, mass),
+    mass = jax.ShapeDtypeStruct((keys.shape[1] // HEAD_DIM, rows), jnp.float32)
+    return pl.pallas_call(
+        weights_kernel,
+        out_shape=(jax.ShapeDtypeStruct(powers.shape, jnp.bfloat16), mass, mass),
         scratch_shapes=[pltpu.VMEM(share.shape, jnp.float32)],
         compiler_params=pltpu.CompilerParams(vmem_limit_bytes=VMEM_BYTES),
-    )(share, peer_share, powers, segments, queries, keys, values, behind_keys, behind_values)
+    )(share, peer_share, powers, segments, queries, keys, behind_keys)
+
+
+def attend_kernel(weights_ref, values_ref, behind_values_ref, attended_ref):
+    seq_rank = lax.axis_index("seq")
+    heads, rows = weights_ref.shape[:2]
+    group_size = attended_ref.shape[1] // values_ref.shape[1]
+
+    def fill(whole):
+        start = 0 if whole else rows
+        for head in range(heads):
+            values = with_behind(values_ref, behind_values_ref, head // group_size, whole)
+            attended_ref[:, head_columns(head)] = jnp.dot(
+                weights_ref[head, :, start:], values, preferred_element_type=jnp.float32
+            ).astype(jnp.bfloat16)
+
+    pl.when(seq_rank > 0)(lambda: fill(True))
+    pl.when(seq_rank == 0)(lambda: fill(False))
+
+
+def attend(weights, values, behind_values):
+    heads, rows = weights.shape[:2]
+    return pl.pallas_call(
+        attend_kernel,
+        out_shape=jax.ShapeDtypeStruct((rows, heads * HEAD_DIM), jnp.bfloat16),
+        compiler_params=pltpu.CompilerParams(vmem_limit_bytes=VMEM_BYTES),
+        cost_estimate=pl.CostEstimate(
+            flops=4 * rows * rows * heads * HEAD_DIM,
+            bytes_accessed=2 * (weights.size + rows * heads * HEAD_DIM),
+            transcendentals=0,
+        ),
+    )(weights, values, behind_values)
 
 
 def pair_device(
@@ -346,37 +367,34 @@
     gate_rows = lax.dynamic_slice_in_dim(gate_out, seq_rank * hidden_local, hidden_local, 0)
 
     peer_rows = lax.ppermute(activations, "seq", swap)
-    behind_keys = lax.ppermute(key_vectors, "seq", swap)
-    behind_values = lax.ppermute(value_vectors, "seq", swap)
 
     def own_work(activations, conv_taps, gate_in, gate_rows):
         part, edges, held = own_project(activations, conv_taps, gate_in)
-        return own_logits(*head_sum(part), gate_rows), edges, held
+        return partial_logits(*head_sum(part), gate_rows), edges, held
 
     own_share, edges, held = in_one_piece(own_work, activations, conv_taps, gate_in, gate_rows)
     peer_rows, own_share, edges, held = lax.optimization_barrier(
         (peer_rows, own_share, edges, held)
     )
     near, far, far_sent = peer_project(peer_rows, edges, conv_taps, held)
-    near, far, far_sent, behind_keys = lax.optimization_barrier(
-        (near, far, far_sent, behind_keys)
-    )
+    behind_keys = lax.ppermute(key_vectors, "seq", swap)
+    behind_values = lax.ppermute(value_vectors, "seq", swap)
+    half = near.shape[1]
     near, near_in = head_sum(near)
-    far, far_in = far_sum(far, far_sent)
-    share = logits_share(own_share, near, near_in, far, far_in, gate_rows)
+    far_share = far_logits(far, far_sent, gate_rows[half:])
+    share = logits_share(own_share, far_share, near, near_in, gate_rows[:half])
     share, queries = lax.optimization_barrier((share, queries))
     powers = powers_of(segments, queries, key_vectors, behind_keys)
-    attended, own_mass, behind_mass = attention(
+    weights, own_mass, behind_mass = weights_of(
         share,
         lax.ppermute(share, "seq", swap),
         powers,
         segments,
         queries,
         key_vectors,
-        value_vectors,
         behind_keys,
-        behind_values,
-    )
+    )
+    attended = attend(weights, value_vectors, behind_values)
     key_mass = own_mass + lax.ppermute(behind_mass, "seq", swap)
     return (attended, key_mass.astype(jnp.bfloat16))
 

time: 36.4 us -> 35.1 us (0.964)
  starting transfers between devices: 14 us -> 13.1 us
  waiting for transfers between devices: 11.9 us -> 11.2 us
    ppermute x1, starting transfers between devices: 0.08 us -> 1.49 us  [pair_device(): behind_keys = lax.ppermute(key_vectors, 'seq', swap)]
    pallas_call x1, Pallas kernels: 1.33 us -> 0.29 us  [logits_share(): pl.pallas_call(logits_kernel, out_shape=jax.ShapeDtypeStruct((2, gate_row...]
    ppermute x1, starting transfers between devices: 1.49 us -> 0.53 us  [pair_device(): behind_values = lax.ppermute(value_vectors, 'seq', swap)]
    pallas_call x1, Pallas kernels: 1.81 us -> 2.47 us  [peer_project(): pl.pallas_call(peer_project_kernel, out_shape=(jax.ShapeDtypeStruct((done...]
    ppermute x1, waiting for transfers between devices: 1.55 us -> 0.92 us  [pair_device(): key_mass = own_mass + lax.ppermute(behind_mass, 'seq', swap)]
    ppermute x1, waiting for transfers between devices: 0.95 us -> 1.44 us  [pair_device(): lax.ppermute(share, 'seq', swap)]
    ppermute x1, starting transfers between devices: 2.09 us -> 1.61 us  [pair_device(): key_mass = own_mass + lax.ppermute(behind_mass, 'seq', swap)]
    ppermute x1, starting transfers between devices: 1.99 us -> 1.53 us  [pair_device(): lax.ppermute(share, 'seq', swap)]
  transfers between devices with their start and end apart: 11 -> 11, of which waited for: 6 -> 6; matrix products, arithmetic and copies ran while one was open for 2% -> 3% of each run, Pallas kernels for 18% -> 16%
where the time goes in v6:
time: 35.1 us; the launch traced here: 34.9 us
  starting transfers between devices  13.1 us (37%)
  waiting for transfers between devices  11.2 us (32%)
  Pallas kernels  8.14 us (23%)
  other arithmetic  1.5 us (4%)
  between operations  0.69 us (2%)
    ppermute x6, waiting for transfers between devices, exchange_heads(): return lax.ppermute(block, 'heads', [(i, i ^ step) for i in range(count)])  6.49 us
    ppermute x6, starting transfers between devices, exchange_heads(): return lax.ppermute(block, 'heads', [(i, i ^ step) for i in range(count)])  4.91 us
    ppermute x1, starting transfers between devices, pair_device(): peer_rows = lax.ppermute(activations, 'seq', swap)  3 us
    pallas_call x1, Pallas kernels, own_project(): pl.pallas_call(own_project_kernel, out_shape=(jax.ShapeDtypeStruct((done,...  2.57 us
    pallas_call x1, Pallas kernels, peer_project(): pl.pallas_call(peer_project_kernel, out_shape=(jax.ShapeDtypeStruct((done...  2.47 us
    ppermute x1, waiting for transfers between devices, pair_device(): peer_rows = lax.ppermute(activations, 'seq', swap)  2.33 us
    ppermute x1, starting transfers between devices, pair_device(): key_mass = own_mass + lax.ppermute(behind_mass, 'seq', swap)  1.61 us
    ppermute x1, starting transfers between devices, pair_device(): lax.ppermute(share, 'seq', swap)  1.53 us
  transfers between devices with their start and end apart: 11, of which 6 were waited for; matrix products, arithmetic and copies ran while one was open for 3% of the time, Pallas kernels for 16%

profile of v6, /device:TPU:0, one launch (start us, length us, event | category | flops | bytes accessed | tf_op | source)
XLA Modules:
  0.0 34.9 jit_solution(15090636028536464414)
XLA Ops:
  0.6 0.0 copy-start
  0.6 3.0 %collective-permute-start.3 = (bf16[128,2048]{1,0:T(8,128)(2,1)}, bf16[128,2048]{1,0:T(8,128)(2,1)S(1)}, u32[]{:S(2)}, u32[]{:S(2)}) collective-permute-start(bf16[128,2048]{1,0:T(8,128)(2,1)} %param.12), channel_id=1, source_target_pairs={{0,16},{16,0},{1,17},{17,1},{2,18},{18,2},{3,19},{19,3},{4,20},{20... | collective-permute-start | bytes 1572872 | tf_op jit(solution)/shard_map/ppermute | solution.py:369
  3.6 0.0 copy-done
  3.7 0.2 copy.12
  3.8 9.6 %conditional.2 = (f32[8,112]{1,0:T(8,128)S(1)}, bf16[32,2048]{1,0:T(8,128)(2,1)S(1)}, bf16[2048,512]{1,0:T(8,128)(2,1)S(1)}) conditional(s32[]{:T(128)} %convert_element_type.16, () %tuple.24, (bf16[128,2048]{1,0:T(8,128)(2,1)}, bf16[4,2048]{1,0:T(4,128)(2,1)}, bf16[2048,512]{1,0:T(8,128)(2,1)}, bf16[512,8]{1,0:T(8,128)(2,1)S(1)}) %tuple.25), branch_computations={%region_0.0_spmd, %region_1.0_spmd} | conditional | flops 114689 | bytes 2231840 | solution.py:129
  3.8 2.6 %branch_1_fun.3 = (f32[112,512]{1,0:T(8,128)S(1)}, bf16[32,2048]{1,0:T(8,128)(2,1)S(1)}, bf16[2048,512]{1,0:T(8,128)(2,1)S(1)}) custom-call(bf16[128,2048]{1,0:T(8,128)(2,1)} %get-tuple-element.18.rows_ref, bf16[4,2048]{1,0:T(4,128)(2,1)} %get-tuple-element.19.taps_ref, bf16[2048,512]{1,0:T(8,128)(2,1)} %get-tuple-element.61.gate_ref), custom_call_target="tpu_custom_call" | custom-call | flops 1 | bytes 1 | tf_op jit(solution)/shard_map/cond/branch_1_fun/pallas_call | solution.py:77
  6.4 0.1 collective-permute-start.1
  6.5 1.5 %collective-permute-done.1 = f32[112,512]{1,0:T(8,128)S(1)} collective-permute-done((f32[112,512]{1,0:T(8,128)S(1)}, f32[112,512]{1,0:T(8,128)S(1)}, u32[]{:S(2)}, u32[]{:S(2)}) %collective-permute-start.1) | collective-permute-done | bytes 229408 | tf_op jit(solution)/shard_map/cond/branch_1_fun/ppermute | solution.py:124
  8.0 1.6 %collective-permute-start.2 = (bf16[112,512]{1,0:T(8,128)(2,1)S(1)}, bf16[112,512]{1,0:T(8,128)(2,1)S(1)}, u32[]{:S(2)}, u32[]{:S(2)}) collective-permute-start(bf16[112,512]{1,0:T(8,128)(2,1)S(1)} %get-tuple-element.62), channel_id=1, source_target_pairs={{0,8},{4,12},{8,0},{12,4},{1,9},{5,13},{9,1},{13,5},{2,10},{6,14},... | collective-permute-start | bytes 344072 | tf_op jit(solution)/shard_map/cond/branch_1_fun/ppermute | solution.py:124
  9.6 3.7 %collective-permute-done.2.in_ref = bf16[112,512]{1,0:T(8,128)(2,1)S(1)} collective-permute-done((bf16[112,512]{1,0:T(8,128)(2,1)S(1)}, bf16[112,512]{1,0:T(8,128)(2,1)S(1)}, u32[]{:S(2)}, u32[]{:S(2)}) %collective-permute-start.2) | collective-permute-done | bytes 114720 | tf_op jit(solution)/shard_map/cond/branch_1_fun/ppermute | solution.py:124
  13.2 0.2 branch_1_fun.4
  13.4 0.0 copy-start.5
  13.4 0.0 copy-start.2
  13.4 0.0 copy-start.3
  13.5 2.3 %collective-permute-done.3.peer_ref = bf16[128,2048]{1,0:T(8,128)(2,1)S(1)} collective-permute-done((bf16[128,2048]{1,0:T(8,128)(2,1)}, bf16[128,2048]{1,0:T(8,128)(2,1)S(1)}, u32[]{:S(2)}, u32[]{:S(2)}) %collective-permute-start.3) | collective-permute-done | bytes 524320 | tf_op jit(solution)/shard_map/ppermute | solution.py:369
  15.8 0.0 copy-done.5
  15.8 0.0 copy-start.1
  15.8 0.0 copy-start.4
  15.8 2.5 %shard_map.96 = (f32[144,256]{1,0:T(8,128)S(1)}, f32[144,256]{1,0:T(8,128)}, bf16[144,256]{1,0:T(8,128)(2,1)S(1)}) custom-call(bf16[128,2048]{1,0:T(8,128)(2,1)S(1)} %collective-permute-done.3.peer_ref, bf16[32,2048]{1,0:T(8,128)(2,1)} %copy-done.5, bf16[4,2048]{1,0:T(4,128)(2,1)} %taps_ref.1, bf16[2048,512]{1,0:T(8,128)(2,1)S(1)} %get-tuple-element.51.gate_ref), custom_call_target="tpu_custom_call" | custom-call | flops 1 | bytes 1 | tf_op jit(solution)/shard_map/pallas_call | solution.py:94
  18.3 0.0 collective-permute-start.5
  18.3 1.8 %collective-permute-start.4 = (bf16[144,256]{1,0:T(8,128)(2,1)S(1)}, bf16[144,256]{1,0:T(8,128)(2,1)S(1)}, u32[]{:S(2)}, u32[]{:S(2)}) collective-permute-start(bf16[144,256]{1,0:T(8,128)(2,1)S(1)} %get-tuple-element.52), channel_id=1, source_target_pairs={{0,8},{4,12},{8,0},{12,4},{1,9},{5,13},{9,1},{13,5},{2,10},{6,14},... | collective-permute-start | bytes 221192 | tf_op jit(solution)/shard_map/ppermute | solution.py:124
  20.0 0.0 collective-permute-done.5
  20.1 1.4 %collective-permute-start.6 = (bf16[144,256]{1,0:T(8,128)(2,1)S(1)}, bf16[144,256]{1,0:T(8,128)(2,1)S(1)}, u32[]{:S(2)}, u32[]{:S(2)}) collective-permute-start(bf16[144,256]{1,0:T(8,128)(2,1)S(1)} %get-tuple-element.64), channel_id=1, source_target_pairs={{0,8},{4,12},{8,0},{12,4},{1,9},{5,13},{9,1},{13,5},{2,10},{6,14},... | collective-permute-start | bytes 221192 | tf_op jit(solution)/shard_map/ppermute | solution.py:124
  21.5 0.0 copy-done.2
  21.5 1.5 %collective-permute-start.8 = (bf16[128,256]{1,0:T(8,128)(2,1)S(1)}, bf16[128,256]{1,0:T(8,128)(2,1)S(1)}, u32[]{:S(2)}, u32[]{:S(2)}) collective-permute-start(bf16[128,256]{1,0:T(8,128)(2,1)S(1)} %copy-done.2), channel_id=1, source_target_pairs={{0,16},{16,0},{1,17},{17,1},{2,18},{18,2},{3,19},{19,3},{4,20},{20... | collective-permute-start | bytes 196616 | tf_op jit(solution)/shard_map/ppermute | solution.py:380
  23.0 0.0 copy-done.3
  23.0 0.5 %collective-permute-start.9 = (bf16[128,256]{1,0:T(8,128)(2,1)S(1)}, bf16[128,256]{1,0:T(8,128)(2,1)S(1)}, u32[]{:S(2)}, u32[]{:S(2)}) collective-permute-start(bf16[128,256]{1,0:T(8,128)(2,1)S(1)} %copy-done.3), channel_id=1, source_target_pairs={{0,16},{16,0},{1,17},{17,1},{2,18},{18,2},{3,19},{19,3},{4,20},{20... | collective-permute-start | bytes 196616 | tf_op jit(solution)/shard_map/ppermute | solution.py:381
  23.5 0.0 collective-permute-done.4
  23.5 2.6 %conditional.3 = (f32[8,144]{1,0:T(8,128)S(1)}) conditional(s32[]{:T(128)} %convert_element_type.16, () %tuple.27, (bf16[144,256]{1,0:T(8,128)(2,1)S(1)}, f32[144,256]{1,0:T(8,128)}, bf16[512,8]{1,0:T(8,128)(2,1)S(1)}) %tuple.28), branch_computations={%region_2.0_spmd, %region_3.0_spmd} | conditional | flops 73728 | bytes 966704 | solution.py:129
  23.5 0.9 %convert_add_fusion.own_ref = f32[144,256]{1,0:T(8,128)S(1)} fusion(f32[144,256]{1,0:T(8,128)} %get-tuple-element.25, bf16[144,256]{1,0:T(8,128)(2,1)S(1)} %get-tuple-element.26), kind=kLoop, calls=%fused_computation | loop fusion | flops 73728 | bytes 368640 | tf_op jit(solution)/shard_map/cond/branch_1_fun/add | solution.py:145
  24.5 0.1 collective-permute-start
  24.6 1.3 %collective-permute-done.in_ref = f32[144,256]{1,0:T(8,128)S(1)} collective-permute-done((f32[144,256]{1,0:T(8,128)S(1)}, f32[144,256]{1,0:T(8,128)S(1)}, u32[]{:S(2)}, u32[]{:S(2)}) %collective-permute-start) | collective-permute-done | bytes 147488 | tf_op jit(solution)/shard_map/cond/branch_1_fun/ppermute | solution.py:124
  25.9 0.2 branch_1_fun.5
  26.1 0.0 collective-permute-done.6.near_in_ref
  26.1 0.3 shard_map.97.share_ref
  26.4 1.5 %collective-permute-start.7 = (f32[2,8,128]{2,1,0:T(8,128)S(1)}, f32[2,8,128]{2,1,0:T(8,128)S(1)}, u32[]{:S(2)}, u32[]{:S(2)}) collective-permute-start(f32[2,8,128]{2,1,0:T(8,128)S(1)} %shard_map.97.share_ref), channel_id=1, source_target_pairs={{0,16},{16,0},{1,17},{17,1},{2,18},{18,2},{3,19},{19,3},{4,20},{20... | collective-permute-start | bytes 24584 | tf_op jit(solution)/shard_map/ppermute | solution.py:390
  27.9 0.0 collective-permute-done.8.behind_keys_ref
  27.9 0.0 copy-done.1
  27.9 0.0 copy-done.4
  27.9 0.7 %shard_map.98.powers_ref = f32[16,128,256]{2,1,0:T(8,128)S(1)} custom-call(s32[2,128]{1,0:T(2,128)S(1)} %bitcast.1, bf16[128,2048]{1,0:T(8,128)(2,1)S(1)} %copy-done.1, bf16[128,256]{1,0:T(8,128)(2,1)S(1)} %copy-done.2, bf16[128,256]{1,0:T(8,128)(2,1)S(1)} %collective-permute-done.8.behind_keys_ref), custom_call_target="tpu_custom_call" | custom-call | flops 134217728 | bytes 2097152 | tf_op jit(solution)/shard_map/pallas_call | solution.py:246
  28.6 1.4 %collective-permute-done.7.peer_share_ref = f32[2,8,128]{2,1,0:T(8,128)S(1)} collective-permute-done((f32[2,8,128]{2,1,0:T(8,128)S(1)}, f32[2,8,128]{2,1,0:T(8,128)S(1)}, u32[]{:S(2)}, u32[]{:S(2)}) %collective-permute-start.7) | collective-permute-done | bytes 8224 | tf_op jit(solution)/shard_map/ppermute | solution.py:390
  30.1 0.6 %shard_map.99 = (bf16[16,128,256]{2,1,0:T(8,128)(2,1)S(1)}, f32[2,128]{1,0:T(2,128)S(1)}, f32[2,128]{1,0:T(2,128)S(1)}) custom-call(f32[2,8,128]{2,1,0:T(8,128)S(1)} %shard_map.97.share_ref, f32[2,8,128]{2,1,0:T(8,128)S(1)} %collective-permute-done.7.peer_share_ref, f32[16,128,256]{2,1,0:T(8,128)S(1)} %shard_map.98.powers_ref, s32[2,128]{1,0:T(2,128)S(1)} %bitcast.2, ...), custom_call_target="tpu_custom_call" | custom-call | tf_op jit(solution)/shard_map/pallas_call | solution.py:320
  30.7 1.6 %collective-permute-start.10 = (f32[2,128]{1,0:T(2,128)S(1)}, f32[2,128]{1,0:T(2,128)S(1)}, u32[]{:S(2)}, u32[]{:S(2)}) collective-permute-start(f32[2,128]{1,0:T(2,128)S(1)} %get-tuple-element.59), channel_id=1, source_target_pairs={{0,16},{16,0},{1,17},{17,1},{2,18},{18,2},{3,19},{19,3},{4,20},{20... | collective-permute-start | bytes 3080 | tf_op jit(solution)/shard_map/ppermute | solution.py:398
  32.3 0.0 collective-permute-done.9.behind_values_ref
  32.3 1.1 %shard_map.100 = bf16[128,2048]{1,0:T(8,128)(2,1)} custom-call(bf16[16,128,256]{2,1,0:T(8,128)(2,1)S(1)} %get-tuple-element.57.weights_ref, bf16[128,256]{1,0:T(8,128)(2,1)S(1)} %copy-done.3, bf16[128,256]{1,0:T(8,128)(2,1)S(1)} %collective-permute-done.9.behind_values_ref), custom_call_target="tpu_custom_call" | custom-call | flops 134217728 | bytes 1572864 | tf_op jit(solution)/shard_map/pallas_call | solution.py:347
  33.4 0.9 %collective-permute-done.10 = f32[2,128]{1,0:T(2,128)S(1)} collective-permute-done((f32[2,128]{1,0:T(2,128)S(1)}, f32[2,128]{1,0:T(2,128)S(1)}, u32[]{:S(2)}, u32[]{:S(2)}) %collective-permute-start.10) | collective-permute-done | bytes 1056 | tf_op jit(solution)/shard_map/ppermute | solution.py:398
  34.3 0.5 %add_convert_fusion = bf16[2,128]{1,0:T(2,128)(2,1)} fusion(f32[2,128]{1,0:T(2,128)S(1)} %get-tuple-element.58, f32[2,128]{1,0:T(2,128)S(1)} %collective-permute-done.10), kind=kLoop, calls=%fused_computation.1 | loop fusion | flops 512 | bytes 2560 | tf_op jit(solution)/shard_map/convert_element_type | solution.py:399
  (5 shorter events, 0.1 us)
Async XLA Ops:
  0.6 3.0 %copy-start = (bf16[1024,8]{0,1:T(8,128)(2,1)S(1)}, bf16[1024,8]{0,1:T(8,128)(2,1)}, u32[]{:S(2)}) copy-start(bf16[1024,8]{0,1:T(8,128)(2,1)} %param.15) | copy-start | bytes 49156
  0.6 15.1 %collective-permute-start.3 = (bf16[128,2048]{1,0:T(8,128)(2,1)}, bf16[128,2048]{1,0:T(8,128)(2,1)S(1)}, u32[]{:S(2)}, u32[]{:S(2)}) collective-permute-start(bf16[128,2048]{1,0:T(8,128)(2,1)} %param.12), channel_id=1, source_target_pairs={{0,16},{16,0},{1,17},{17,1},{2,18},{18,2},{3,19},{19,3},{4,20},{20... | collective-permute-start | bytes 1572872 | tf_op jit(solution)/shard_map/ppermute | solution.py:369
  6.4 1.5 %collective-permute-start.1 = (f32[112,512]{1,0:T(8,128)S(1)}, f32[112,512]{1,0:T(8,128)S(1)}, u32[]{:S(2)}, u32[]{:S(2)}) collective-permute-start(f32[112,512]{1,0:T(8,128)S(1)} %get-tuple-element.21), channel_id=1, source_target_pairs={{0,4},{4,0},{8,12},{12,8},{1,5},{5,1},{9,13},{13,9},{2,6},{6,2},{1... | collective-permute-start | bytes 688136 | tf_op jit(solution)/shard_map/cond/branch_1_fun/ppermute | solution.py:124
  8.0 5.3 %collective-permute-start.2 = (bf16[112,512]{1,0:T(8,128)(2,1)S(1)}, bf16[112,512]{1,0:T(8,128)(2,1)S(1)}, u32[]{:S(2)}, u32[]{:S(2)}) collective-permute-start(bf16[112,512]{1,0:T(8,128)(2,1)S(1)} %get-tuple-element.62), channel_id=1, source_target_pairs={{0,8},{4,12},{8,0},{12,4},{1,9},{5,13},{9,1},{13,5},{2,10},{6,14},... | collective-permute-start | bytes 344072 | tf_op jit(solution)/shard_map/cond/branch_1_fun/ppermute | solution.py:124
  13.4 2.3 %copy-start.5 = (bf16[32,2048]{1,0:T(8,128)(2,1)}, bf16[32,2048]{1,0:T(8,128)(2,1)S(1)}, u32[]{:S(2)}) copy-start(bf16[32,2048]{1,0:T(8,128)(2,1)S(1)} %get-tuple-element.50.edges_ref) | copy-start | bytes 393220
  13.4 8.1 %copy-start.2 = (bf16[128,256]{1,0:T(8,128)(2,1)S(1)}, bf16[128,256]{1,0:T(8,128)(2,1)}, u32[]{:S(2)}) copy-start(bf16[128,256]{1,0:T(8,128)(2,1)} %keys_ref.3) | copy-start | bytes 196612
  13.4 9.5 %copy-start.3 = (bf16[128,256]{1,0:T(8,128)(2,1)S(1)}, bf16[128,256]{1,0:T(8,128)(2,1)}, u32[]{:S(2)}) copy-start(bf16[128,256]{1,0:T(8,128)(2,1)} %values_ref.1) | copy-start | bytes 196612
  15.8 12.1 %copy-start.1 = (bf16[128,2048]{1,0:T(8,128)(2,1)S(1)}, bf16[128,2048]{1,0:T(8,128)(2,1)}, u32[]{:S(2)}) copy-start(bf16[128,2048]{1,0:T(8,128)(2,1)} %queries_ref.1) | copy-start | bytes 1572868
  15.8 12.1 %copy-start.4 = (s32[256]{0:T(256)S(1)}, s32[256]{0:T(256)}, u32[]{:S(2)}) copy-start(s32[256]{0:T(256)} %param.19) | copy-start | bytes 3076
  18.3 1.8 %collective-permute-start.5 = (f32[144,256]{1,0:T(8,128)S(1)}, f32[144,256]{1,0:T(8,128)S(1)}, u32[]{:S(2)}, u32[]{:S(2)}) collective-permute-start(f32[144,256]{1,0:T(8,128)S(1)} %get-tuple-element.54), channel_id=1, source_target_pairs={{0,4},{4,0},{8,12},{12,8},{1,5},{5,1},{9,13},{13,9},{2,6},{6,2},{1... | collective-permute-start | bytes 442376 | tf_op jit(solution)/shard_map/ppermute | solution.py:124
  18.3 5.3 %collective-permute-start.4 = (bf16[144,256]{1,0:T(8,128)(2,1)S(1)}, bf16[144,256]{1,0:T(8,128)(2,1)S(1)}, u32[]{:S(2)}, u32[]{:S(2)}) collective-permute-start(bf16[144,256]{1,0:T(8,128)(2,1)S(1)} %get-tuple-element.52), channel_id=1, source_target_pairs={{0,8},{4,12},{8,0},{12,4},{1,9},{5,13},{9,1},{13,5},{2,10},{6,14},... | collective-permute-start | bytes 221192 | tf_op jit(solution)/shard_map/ppermute | solution.py:124
  20.1 6.0 %collective-permute-start.6 = (bf16[144,256]{1,0:T(8,128)(2,1)S(1)}, bf16[144,256]{1,0:T(8,128)(2,1)S(1)}, u32[]{:S(2)}, u32[]{:S(2)}) collective-permute-start(bf16[144,256]{1,0:T(8,128)(2,1)S(1)} %get-tuple-element.64), channel_id=1, source_target_pairs={{0,8},{4,12},{8,0},{12,4},{1,9},{5,13},{9,1},{13,5},{2,10},{6,14},... | collective-permute-start | bytes 221192 | tf_op jit(solution)/shard_map/ppermute | solution.py:124
  21.5 6.4 %collective-permute-start.8 = (bf16[128,256]{1,0:T(8,128)(2,1)S(1)}, bf16[128,256]{1,0:T(8,128)(2,1)S(1)}, u32[]{:S(2)}, u32[]{:S(2)}) collective-permute-start(bf16[128,256]{1,0:T(8,128)(2,1)S(1)} %copy-done.2), channel_id=1, source_target_pairs={{0,16},{16,0},{1,17},{17,1},{2,18},{18,2},{3,19},{19,3},{4,20},{20... | collective-permute-start | bytes 196616 | tf_op jit(solution)/shard_map/ppermute | solution.py:380
  23.0 9.3 %collective-permute-start.9 = (bf16[128,256]{1,0:T(8,128)(2,1)S(1)}, bf16[128,256]{1,0:T(8,128)(2,1)S(1)}, u32[]{:S(2)}, u32[]{:S(2)}) collective-permute-start(bf16[128,256]{1,0:T(8,128)(2,1)S(1)} %copy-done.3), channel_id=1, source_target_pairs={{0,16},{16,0},{1,17},{17,1},{2,18},{18,2},{3,19},{19,3},{4,20},{20... | collective-permute-start | bytes 196616 | tf_op jit(solution)/shard_map/ppermute | solution.py:381
  24.5 1.4 %collective-permute-start = (f32[144,256]{1,0:T(8,128)S(1)}, f32[144,256]{1,0:T(8,128)S(1)}, u32[]{:S(2)}, u32[]{:S(2)}) collective-permute-start(f32[144,256]{1,0:T(8,128)S(1)} %convert_add_fusion.own_ref), channel_id=1, source_target_pairs={{0,4},{4,0},{8,12},{12,8},{1,5},{5,1},{9,13},{13,9},{2,6},{6,2},{1... | collective-permute-start | bytes 442376 | tf_op jit(solution)/shard_map/cond/branch_1_fun/ppermute | solution.py:124
  26.4 3.7 %collective-permute-start.7 = (f32[2,8,128]{2,1,0:T(8,128)S(1)}, f32[2,8,128]{2,1,0:T(8,128)S(1)}, u32[]{:S(2)}, u32[]{:S(2)}) collective-permute-start(f32[2,8,128]{2,1,0:T(8,128)S(1)} %shard_map.97.share_ref), channel_id=1, source_target_pairs={{0,16},{16,0},{1,17},{17,1},{2,18},{18,2},{3,19},{19,3},{4,20},{20... | collective-permute-start | bytes 24584 | tf_op jit(solution)/shard_map/ppermute | solution.py:390
  30.7 3.6 %collective-permute-start.10 = (f32[2,128]{1,0:T(2,128)S(1)}, f32[2,128]{1,0:T(2,128)S(1)}, u32[]{:S(2)}, u32[]{:S(2)}) collective-permute-start(f32[2,128]{1,0:T(2,128)S(1)} %get-tuple-element.59), channel_id=1, source_target_pairs={{0,16},{16,0},{1,17},{17,1},{2,18},{18,2},{3,19},{19,3},{4,20},{20... | collective-permute-start | bytes 3080 | tf_op jit(solution)/shard_map/ppermute | solution.py:398

commit v7 on v6

--- a/solution.py
+++ b/solution.py
@@ -16,7 +16,7 @@
 NEG_FILL = -1e30
 RIM_ROWS = 16
 LEAST_RETENTION = -40.0
-VMEM_BYTES = 48 * 1024 * 1024
+VMEM_BYTES = 16 * 1024 * 1024
 
 
 def convolve(widened, taps_ref, columns, lead, rows):
@@ -27,10 +27,13 @@
     return summed.astype(jnp.bfloat16)
 
 
-def own_project_kernel(rows_ref, taps_ref, gate_ref, out_ref, edges_ref, held_ref, widened):
+def own_project_kernel(
+    rows_ref, taps_ref, gate_ref, out_ref, edges_ref, held_taps_ref, held_ref, widened
+):
     rows, features = rows_ref.shape
     edges_ref[:RIM_ROWS] = rows_ref[:RIM_ROWS]
     edges_ref[RIM_ROWS:] = rows_ref[rows - RIM_ROWS :]
+    held_taps_ref[...] = taps_ref[...].astype(jnp.float32)
     held_ref[...] = gate_ref[...]
     tile = math.gcd(features, 512)
     total = jnp.zeros(out_ref.shape, jnp.float32)
@@ -79,6 +82,7 @@
         out_shape=(
             jax.ShapeDtypeStruct((done, gate_in.shape[1]), jnp.float32),
             jax.ShapeDtypeStruct((2 * RIM_ROWS, features), activations.dtype),
+            jax.ShapeDtypeStruct(conv_taps.shape, jnp.float32),
             jax.ShapeDtypeStruct(gate_in.shape, gate_in.dtype),
         ),
         scratch_shapes=[pltpu.VMEM((rows, features), jnp.float32)],
@@ -369,14 +373,12 @@
     peer_rows = lax.ppermute(activations, "seq", swap)
 
     def own_work(activations, conv_taps, gate_in, gate_rows):
-        part, edges, held = own_project(activations, conv_taps, gate_in)
-        return partial_logits(*head_sum(part), gate_rows), edges, held
-
-    own_share, edges, held = in_one_piece(own_work, activations, conv_taps, gate_in, gate_rows)
-    peer_rows, own_share, edges, held = lax.optimization_barrier(
-        (peer_rows, own_share, edges, held)
-    )
-    near, far, far_sent = peer_project(peer_rows, edges, conv_taps, held)
+        part, *held = own_project(activations, conv_taps, gate_in)
+        return partial_logits(*head_sum(part), gate_rows), held
+
+    own_share, held = in_one_piece(own_work, activations, conv_taps, gate_in, gate_rows)
+    peer_rows, own_share, held = lax.optimization_barrier((peer_rows, own_share, held))
+    near, far, far_sent = peer_project(peer_rows, *held)
     behind_keys = lax.ppermute(key_vectors, "seq", swap)
     behind_values = lax.ppermute(value_vectors, "seq", swap)
     half = near.shape[1]

time: 35.1 us -> 35 us (level)
  no operation moved by 1% of the time
where the time goes in v7:
time: 35 us; the launch traced here: 34.8 us
  starting transfers between devices  13.1 us (37%)
  waiting for transfers between devices  11.2 us (32%)
  Pallas kernels  8.11 us (23%)
  other arithmetic  1.51 us (4%)
  between operations  0.69 us (2%)
    ppermute x6, waiting for transfers between devices, exchange_heads(): return lax.ppermute(block, 'heads', [(i, i ^ step) for i in range(count)])  6.5 us
    ppermute x6, starting transfers between devices, exchange_heads(): return lax.ppermute(block, 'heads', [(i, i ^ step) for i in range(count)])  4.91 us
    ppermute x1, starting transfers between devices, pair_device(): peer_rows = lax.ppermute(activations, 'seq', swap)  3 us
    pallas_call x1, Pallas kernels, own_project(): pl.pallas_call(own_project_kernel, out_shape=(jax.ShapeDtypeStruct((done,...  2.58 us
    pallas_call x1, Pallas kernels, peer_project(): pl.pallas_call(peer_project_kernel, out_shape=(jax.ShapeDtypeStruct((done...  2.44 us
    ppermute x1, waiting for transfers between devices, pair_device(): peer_rows = lax.ppermute(activations, 'seq', swap)  2.32 us
    ppermute x1, starting transfers between devices, pair_device(): key_mass = own_mass + lax.ppermute(behind_mass, 'seq', swap)  1.61 us
    ppermute x1, starting transfers between devices, pair_device(): lax.ppermute(share, 'seq', swap)  1.53 us
  transfers between devices with their start and end apart: 11, of which 6 were waited for; matrix products, arithmetic and copies ran while one was open for 3% of the time, Pallas kernels for 16%

profile of v7, /device:TPU:0, one launch (start us, length us, event | category | flops | bytes accessed | tf_op | source)
XLA Modules:
  0.0 34.8 jit_solution(4305343231027745676)
XLA Ops:
  0.6 0.0 copy-start
  0.6 3.0 %collective-permute-start.3 = (bf16[128,2048]{1,0:T(8,128)(2,1)}, bf16[128,2048]{1,0:T(8,128)(2,1)S(1)}, u32[]{:S(2)}, u32[]{:S(2)}) collective-permute-start(bf16[128,2048]{1,0:T(8,128)(2,1)} %param.12), channel_id=1, source_target_pairs={{0,16},{16,0},{1,17},{17,1},{2,18},{18,2},{3,19},{19,3},{4,20},{20... | collective-permute-start | bytes 1572872 | tf_op jit(solution)/shard_map/ppermute | solution.py:373
  3.6 0.0 copy-done
  3.7 0.2 copy.13
  3.8 9.6 %conditional.2 = (f32[8,112]{1,0:T(8,128)S(1)}, bf16[32,2048]{1,0:T(8,128)(2,1)S(1)}, f32[4,2048]{1,0:T(4,128)S(1)}, bf16[2048,512]{1,0:T(8,128)(2,1)S(1)}) conditional(s32[]{:T(128)} %convert_element_type.16, () %tuple.24, (bf16[128,2048]{1,0:T(8,128)(2,1)}, bf16[4,2048]{1,0:T(4,128)(2,1)}, bf16[2048,512]{1,0:T(8,128)(2,1)}, ...), branch_computations={%region_0.0_spmd, %region_1.0_spmd} | conditional | flops 114689 | bytes 2264620 | solution.py:133
  3.8 2.6 %branch_1_fun.3 = (f32[112,512]{1,0:T(8,128)S(1)}, bf16[32,2048]{1,0:T(8,128)(2,1)S(1)}, f32[4,2048]{1,0:T(4,128)S(1)}, bf16[2048,512]{1,0:T(8,128)(2,1)S(1)}) custom-call(bf16[128,2048]{1,0:T(8,128)(2,1)} %get-tuple-element.18.rows_ref, bf16[4,2048]{1,0:T(4,128)(2,1)} %get-tuple-element.67.taps_ref, bf16[2048,512]{1,0:T(8,128)(2,1)} %get-tuple-element.68.gate_ref), custom_call_target="tpu_custom_call" | custom-call | flops 1 | bytes 1 | tf_op jit(solution)/shard_map/cond/branch_1_fun/pallas_call | solution.py:80
  6.4 0.1 collective-permute-start.1
  6.5 1.5 %collective-permute-done.1 = f32[112,512]{1,0:T(8,128)S(1)} collective-permute-done((f32[112,512]{1,0:T(8,128)S(1)}, f32[112,512]{1,0:T(8,128)S(1)}, u32[]{:S(2)}, u32[]{:S(2)}) %collective-permute-start.1) | collective-permute-done | bytes 229408 | tf_op jit(solution)/shard_map/cond/branch_1_fun/ppermute | solution.py:128
  8.0 1.6 %collective-permute-start.2 = (bf16[112,512]{1,0:T(8,128)(2,1)S(1)}, bf16[112,512]{1,0:T(8,128)(2,1)S(1)}, u32[]{:S(2)}, u32[]{:S(2)}) collective-permute-start(bf16[112,512]{1,0:T(8,128)(2,1)S(1)} %get-tuple-element.69), channel_id=1, source_target_pairs={{0,8},{4,12},{8,0},{12,4},{1,9},{5,13},{9,1},{13,5},{2,10},{6,14},... | collective-permute-start | bytes 344072 | tf_op jit(solution)/shard_map/cond/branch_1_fun/ppermute | solution.py:128
  9.6 3.7 %collective-permute-done.2.in_ref = bf16[112,512]{1,0:T(8,128)(2,1)S(1)} collective-permute-done((bf16[112,512]{1,0:T(8,128)(2,1)S(1)}, bf16[112,512]{1,0:T(8,128)(2,1)S(1)}, u32[]{:S(2)}, u32[]{:S(2)}) %collective-permute-start.2) | collective-permute-done | bytes 114720 | tf_op jit(solution)/shard_map/cond/branch_1_fun/ppermute | solution.py:128
  13.2 0.2 branch_1_fun.4
  13.4 0.0 copy-start.5
  13.4 0.0 copy-start.2
  13.4 0.0 copy-start.3
  13.5 2.3 %collective-permute-done.3.peer_ref = bf16[128,2048]{1,0:T(8,128)(2,1)S(1)} collective-permute-done((bf16[128,2048]{1,0:T(8,128)(2,1)}, bf16[128,2048]{1,0:T(8,128)(2,1)S(1)}, u32[]{:S(2)}, u32[]{:S(2)}) %collective-permute-start.3) | collective-permute-done | bytes 524320 | tf_op jit(solution)/shard_map/ppermute | solution.py:373
  15.8 0.0 copy-done.5
  15.8 0.0 copy-start.1
  15.8 0.0 copy-start.4
  15.8 2.4 %shard_map.97 = (f32[144,256]{1,0:T(8,128)S(1)}, f32[144,256]{1,0:T(8,128)}, bf16[144,256]{1,0:T(8,128)(2,1)S(1)}) custom-call(bf16[128,2048]{1,0:T(8,128)(2,1)S(1)} %collective-permute-done.3.peer_ref, bf16[32,2048]{1,0:T(8,128)(2,1)} %copy-done.5, f32[4,2048]{1,0:T(4,128)S(1)} %get-tuple-element.55.taps_ref, bf16[2048,512]{1,0:T(8,128)(2,1)S(1)} %get-tuple-element.56.gate_ref), custom_call_target="tpu_custom_call" | custom-call | flops 1 | bytes 1 | tf_op jit(solution)/shard_map/pallas_call | solution.py:98
  18.2 0.0 collective-permute-start.5
  18.2 1.8 %collective-permute-start.4 = (bf16[144,256]{1,0:T(8,128)(2,1)S(1)}, bf16[144,256]{1,0:T(8,128)(2,1)S(1)}, u32[]{:S(2)}, u32[]{:S(2)}) collective-permute-start(bf16[144,256]{1,0:T(8,128)(2,1)S(1)} %get-tuple-element.57), channel_id=1, source_target_pairs={{0,8},{4,12},{8,0},{12,4},{1,9},{5,13},{9,1},{13,5},{2,10},{6,14},... | collective-permute-start | bytes 221192 | tf_op jit(solution)/shard_map/ppermute | solution.py:128
  20.0 0.0 collective-permute-done.5
  20.0 1.4 %collective-permute-start.6 = (bf16[144,256]{1,0:T(8,128)(2,1)S(1)}, bf16[144,256]{1,0:T(8,128)(2,1)S(1)}, u32[]{:S(2)}, u32[]{:S(2)}) collective-permute-start(bf16[144,256]{1,0:T(8,128)(2,1)S(1)} %get-tuple-element.71), channel_id=1, source_target_pairs={{0,8},{4,12},{8,0},{12,4},{1,9},{5,13},{9,1},{13,5},{2,10},{6,14},... | collective-permute-start | bytes 221192 | tf_op jit(solution)/shard_map/ppermute | solution.py:128
  21.5 0.0 copy-done.2
  21.5 1.5 %collective-permute-start.8 = (bf16[128,256]{1,0:T(8,128)(2,1)S(1)}, bf16[128,256]{1,0:T(8,128)(2,1)S(1)}, u32[]{:S(2)}, u32[]{:S(2)}) collective-permute-start(bf16[128,256]{1,0:T(8,128)(2,1)S(1)} %copy-done.2), channel_id=1, source_target_pairs={{0,16},{16,0},{1,17},{17,1},{2,18},{18,2},{3,19},{19,3},{4,20},{20... | collective-permute-start | bytes 196616 | tf_op jit(solution)/shard_map/ppermute | solution.py:382
  23.0 0.0 copy-done.3
  23.0 0.5 %collective-permute-start.9 = (bf16[128,256]{1,0:T(8,128)(2,1)S(1)}, bf16[128,256]{1,0:T(8,128)(2,1)S(1)}, u32[]{:S(2)}, u32[]{:S(2)}) collective-permute-start(bf16[128,256]{1,0:T(8,128)(2,1)S(1)} %copy-done.3), channel_id=1, source_target_pairs={{0,16},{16,0},{1,17},{17,1},{2,18},{18,2},{3,19},{19,3},{4,20},{20... | collective-permute-start | bytes 196616 | tf_op jit(solution)/shard_map/ppermute | solution.py:383
  23.5 0.0 collective-permute-done.4
  23.5 2.6 %conditional.3 = (f32[8,144]{1,0:T(8,128)S(1)}) conditional(s32[]{:T(128)} %convert_element_type.16, () %tuple.27, (bf16[144,256]{1,0:T(8,128)(2,1)S(1)}, f32[144,256]{1,0:T(8,128)}, bf16[512,8]{1,0:T(8,128)(2,1)S(1)}) %tuple.28), branch_computations={%region_2.0_spmd, %region_3.0_spmd} | conditional | flops 73728 | bytes 966704 | solution.py:133
  23.5 0.9 %convert_add_fusion.own_ref = f32[144,256]{1,0:T(8,128)S(1)} fusion(f32[144,256]{1,0:T(8,128)} %get-tuple-element.26, bf16[144,256]{1,0:T(8,128)(2,1)S(1)} %get-tuple-element.27), kind=kLoop, calls=%fused_computation | loop fusion | flops 73728 | bytes 368640 | tf_op jit(solution)/shard_map/cond/branch_1_fun/add | solution.py:149
  24.4 0.1 collective-permute-start
  24.5 1.3 %collective-permute-done.in_ref = f32[144,256]{1,0:T(8,128)S(1)} collective-permute-done((f32[144,256]{1,0:T(8,128)S(1)}, f32[144,256]{1,0:T(8,128)S(1)}, u32[]{:S(2)}, u32[]{:S(2)}) %collective-permute-start) | collective-permute-done | bytes 147488 | tf_op jit(solution)/shard_map/cond/branch_1_fun/ppermute | solution.py:128
  25.9 0.2 branch_1_fun.5
  26.1 0.0 collective-permute-done.6.near_in_ref
  26.1 0.3 shard_map.98.share_ref
  26.4 1.5 %collective-permute-start.7 = (f32[2,8,128]{2,1,0:T(8,128)S(1)}, f32[2,8,128]{2,1,0:T(8,128)S(1)}, u32[]{:S(2)}, u32[]{:S(2)}) collective-permute-start(f32[2,8,128]{2,1,0:T(8,128)S(1)} %shard_map.98.share_ref), channel_id=1, source_target_pairs={{0,16},{16,0},{1,17},{17,1},{2,18},{18,2},{3,19},{19,3},{4,20},{20... | collective-permute-start | bytes 24584 | tf_op jit(solution)/shard_map/ppermute | solution.py:392
  27.9 0.0 collective-permute-done.8.behind_keys_ref
  27.9 0.0 copy-done.1
  27.9 0.0 copy-done.4
  27.9 0.7 %shard_map.99.powers_ref = f32[16,128,256]{2,1,0:T(8,128)S(1)} custom-call(s32[2,128]{1,0:T(2,128)S(1)} %bitcast.1, bf16[128,2048]{1,0:T(8,128)(2,1)S(1)} %copy-done.1, bf16[128,256]{1,0:T(8,128)(2,1)S(1)} %copy-done.2, bf16[128,256]{1,0:T(8,128)(2,1)S(1)} %collective-permute-done.8.behind_keys_ref), custom_call_target="tpu_custom_call" | custom-call | flops 134217728 | bytes 2097152 | tf_op jit(solution)/shard_map/pallas_call | solution.py:250
  28.6 1.4 %collective-permute-done.7.peer_share_ref = f32[2,8,128]{2,1,0:T(8,128)S(1)} collective-permute-done((f32[2,8,128]{2,1,0:T(8,128)S(1)}, f32[2,8,128]{2,1,0:T(8,128)S(1)}, u32[]{:S(2)}, u32[]{:S(2)}) %collective-permute-start.7) | collective-permute-done | bytes 8224 | tf_op jit(solution)/shard_map/ppermute | solution.py:392
  30.0 0.6 %shard_map.100 = (bf16[16,128,256]{2,1,0:T(8,128)(2,1)S(1)}, f32[2,128]{1,0:T(2,128)S(1)}, f32[2,128]{1,0:T(2,128)S(1)}) custom-call(f32[2,8,128]{2,1,0:T(8,128)S(1)} %shard_map.98.share_ref, f32[2,8,128]{2,1,0:T(8,128)S(1)} %collective-permute-done.7.peer_share_ref, f32[16,128,256]{2,1,0:T(8,128)S(1)} %shard_map.99.powers_ref, s32[2,128]{1,0:T(2,128)S(1)} %bitcast.2, ...), custom_call_target="tpu_custom_call" | custom-call | tf_op jit(solution)/shard_map/pallas_call | solution.py:324
  30.7 1.6 %collective-permute-start.10 = (f32[2,128]{1,0:T(2,128)S(1)}, f32[2,128]{1,0:T(2,128)S(1)}, u32[]{:S(2)}, u32[]{:S(2)}) collective-permute-start(f32[2,128]{1,0:T(2,128)S(1)} %get-tuple-element.64), channel_id=1, source_target_pairs={{0,16},{16,0},{1,17},{17,1},{2,18},{18,2},{3,19},{19,3},{4,20},{20... | collective-permute-start | bytes 3080 | tf_op jit(solution)/shard_map/ppermute | solution.py:400
  32.3 0.0 collective-permute-done.9.behind_values_ref
  32.3 1.1 %shard_map.101 = bf16[128,2048]{1,0:T(8,128)(2,1)} custom-call(bf16[16,128,256]{2,1,0:T(8,128)(2,1)S(1)} %get-tuple-element.62.weights_ref, bf16[128,256]{1,0:T(8,128)(2,1)S(1)} %copy-done.3, bf16[128,256]{1,0:T(8,128)(2,1)S(1)} %collective-permute-done.9.behind_values_ref), custom_call_target="tpu_custom_call" | custom-call | flops 134217728 | bytes 1572864 | tf_op jit(solution)/shard_map/pallas_call | solution.py:351
  33.4 0.9 %collective-permute-done.10 = f32[2,128]{1,0:T(2,128)S(1)} collective-permute-done((f32[2,128]{1,0:T(2,128)S(1)}, f32[2,128]{1,0:T(2,128)S(1)}, u32[]{:S(2)}, u32[]{:S(2)}) %collective-permute-start.10) | collective-permute-done | bytes 1056 | tf_op jit(solution)/shard_map/ppermute | solution.py:400
  34.3 0.5 %add_convert_fusion = bf16[2,128]{1,0:T(2,128)(2,1)} fusion(f32[2,128]{1,0:T(2,128)S(1)} %get-tuple-element.63, f32[2,128]{1,0:T(2,128)S(1)} %collective-permute-done.10), kind=kLoop, calls=%fused_computation.1 | loop fusion | flops 512 | bytes 2560 | tf_op jit(solution)/shard_map/convert_element_type | solution.py:401
  (5 shorter events, 0.1 us)
Async XLA Ops:
  0.6 3.0 %copy-start = (bf16[1024,8]{0,1:T(8,128)(2,1)S(1)}, bf16[1024,8]{0,1:T(8,128)(2,1)}, u32[]{:S(2)}) copy-start(bf16[1024,8]{0,1:T(8,128)(2,1)} %param.15) | copy-start | bytes 49156
  0.6 15.1 %collective-permute-start.3 = (bf16[128,2048]{1,0:T(8,128)(2,1)}, bf16[128,2048]{1,0:T(8,128)(2,1)S(1)}, u32[]{:S(2)}, u32[]{:S(2)}) collective-permute-start(bf16[128,2048]{1,0:T(8,128)(2,1)} %param.12), channel_id=1, source_target_pairs={{0,16},{16,0},{1,17},{17,1},{2,18},{18,2},{3,19},{19,3},{4,20},{20... | collective-permute-start | bytes 1572872 | tf_op jit(solution)/shard_map/ppermute | solution.py:373
  6.4 1.5 %collective-permute-start.1 = (f32[112,512]{1,0:T(8,128)S(1)}, f32[112,512]{1,0:T(8,128)S(1)}, u32[]{:S(2)}, u32[]{:S(2)}) collective-permute-start(f32[112,512]{1,0:T(8,128)S(1)} %get-tuple-element.21), channel_id=1, source_target_pairs={{0,4},{4,0},{8,12},{12,8},{1,5},{5,1},{9,13},{13,9},{2,6},{6,2},{1... | collective-permute-start | bytes 688136 | tf_op jit(solution)/shard_map/cond/branch_1_fun/ppermute | solution.py:128
  8.0 5.3 %collective-permute-start.2 = (bf16[112,512]{1,0:T(8,128)(2,1)S(1)}, bf16[112,512]{1,0:T(8,128)(2,1)S(1)}, u32[]{:S(2)}, u32[]{:S(2)}) collective-permute-start(bf16[112,512]{1,0:T(8,128)(2,1)S(1)} %get-tuple-element.69), channel_id=1, source_target_pairs={{0,8},{4,12},{8,0},{12,4},{1,9},{5,13},{9,1},{13,5},{2,10},{6,14},... | collective-permute-start | bytes 344072 | tf_op jit(solution)/shard_map/cond/branch_1_fun/ppermute | solution.py:128
  13.4 2.3 %copy-start.5 = (bf16[32,2048]{1,0:T(8,128)(2,1)}, bf16[32,2048]{1,0:T(8,128)(2,1)S(1)}, u32[]{:S(2)}) copy-start(bf16[32,2048]{1,0:T(8,128)(2,1)S(1)} %get-tuple-element.54.edges_ref) | copy-start | bytes 393220
  13.4 8.0 %copy-start.2 = (bf16[128,256]{1,0:T(8,128)(2,1)S(1)}, bf16[128,256]{1,0:T(8,128)(2,1)}, u32[]{:S(2)}) copy-start(bf16[128,256]{1,0:T(8,128)(2,1)} %keys_ref.3) | copy-start | bytes 196612
  13.4 9.5 %copy-start.3 = (bf16[128,256]{1,0:T(8,128)(2,1)S(1)}, bf16[128,256]{1,0:T(8,128)(2,1)}, u32[]{:S(2)}) copy-start(bf16[128,256]{1,0:T(8,128)(2,1)} %values_ref.1) | copy-start | bytes 196612
  15.8 12.1 %copy-start.1 = (bf16[128,2048]{1,0:T(8,128)(2,1)S(1)}, bf16[128,2048]{1,0:T(8,128)(2,1)}, u32[]{:S(2)}) copy-start(bf16[128,2048]{1,0:T(8,128)(2,1)} %queries_ref.1) | copy-start | bytes 1572868
  15.8 12.1 %copy-start.4 = (s32[256]{0:T(256)S(1)}, s32[256]{0:T(256)}, u32[]{:S(2)}) copy-start(s32[256]{0:T(256)} %param.19) | copy-start | bytes 3076
  18.2 1.8 %collective-permute-start.5 = (f32[144,256]{1,0:T(8,128)S(1)}, f32[144,256]{1,0:T(8,128)S(1)}, u32[]{:S(2)}, u32[]{:S(2)}) collective-permute-start(f32[144,256]{1,0:T(8,128)S(1)} %get-tuple-element.59), channel_id=1, source_target_pairs={{0,4},{4,0},{8,12},{12,8},{1,5},{5,1},{9,13},{13,9},{2,6},{6,2},{1... | collective-permute-start | bytes 442376 | tf_op jit(solution)/shard_map/ppermute | solution.py:128
  18.2 5.3 %collective-permute-start.4 = (bf16[144,256]{1,0:T(8,128)(2,1)S(1)}, bf16[144,256]{1,0:T(8,128)(2,1)S(1)}, u32[]{:S(2)}, u32[]{:S(2)}) collective-permute-start(bf16[144,256]{1,0:T(8,128)(2,1)S(1)} %get-tuple-element.57), channel_id=1, source_target_pairs={{0,8},{4,12},{8,0},{12,4},{1,9},{5,13},{9,1},{13,5},{2,10},{6,14},... | collective-permute-start | bytes 221192 | tf_op jit(solution)/shard_map/ppermute | solution.py:128
  20.0 6.0 %collective-permute-start.6 = (bf16[144,256]{1,0:T(8,128)(2,1)S(1)}, bf16[144,256]{1,0:T(8,128)(2,1)S(1)}, u32[]{:S(2)}, u32[]{:S(2)}) collective-permute-start(bf16[144,256]{1,0:T(8,128)(2,1)S(1)} %get-tuple-element.71), channel_id=1, source_target_pairs={{0,8},{4,12},{8,0},{12,4},{1,9},{5,13},{9,1},{13,5},{2,10},{6,14},... | collective-permute-start | bytes 221192 | tf_op jit(solution)/shard_map/ppermute | solution.py:128
  21.5 6.4 %collective-permute-start.8 = (bf16[128,256]{1,0:T(8,128)(2,1)S(1)}, bf16[128,256]{1,0:T(8,128)(2,1)S(1)}, u32[]{:S(2)}, u32[]{:S(2)}) collective-permute-start(bf16[128,256]{1,0:T(8,128)(2,1)S(1)} %copy-done.2), channel_id=1, source_target_pairs={{0,16},{16,0},{1,17},{17,1},{2,18},{18,2},{3,19},{19,3},{4,20},{20... | collective-permute-start | bytes 196616 | tf_op jit(solution)/shard_map/ppermute | solution.py:382
  23.0 9.3 %collective-permute-start.9 = (bf16[128,256]{1,0:T(8,128)(2,1)S(1)}, bf16[128,256]{1,0:T(8,128)(2,1)S(1)}, u32[]{:S(2)}, u32[]{:S(2)}) collective-permute-start(bf16[128,256]{1,0:T(8,128)(2,1)S(1)} %copy-done.3), channel_id=1, source_target_pairs={{0,16},{16,0},{1,17},{17,1},{2,18},{18,2},{3,19},{19,3},{4,20},{20... | collective-permute-start | bytes 196616 | tf_op jit(solution)/shard_map/ppermute | solution.py:383
  24.4 1.4 %collective-permute-start = (f32[144,256]{1,0:T(8,128)S(1)}, f32[144,256]{1,0:T(8,128)S(1)}, u32[]{:S(2)}, u32[]{:S(2)}) collective-permute-start(f32[144,256]{1,0:T(8,128)S(1)} %convert_add_fusion.own_ref), channel_id=1, source_target_pairs={{0,4},{4,0},{8,12},{12,8},{1,5},{5,1},{9,13},{13,9},{2,6},{6,2},{1... | collective-permute-start | bytes 442376 | tf_op jit(solution)/shard_map/cond/branch_1_fun/ppermute | solution.py:128
  26.4 3.7 %collective-permute-start.7 = (f32[2,8,128]{2,1,0:T(8,128)S(1)}, f32[2,8,128]{2,1,0:T(8,128)S(1)}, u32[]{:S(2)}, u32[]{:S(2)}) collective-permute-start(f32[2,8,128]{2,1,0:T(8,128)S(1)} %shard_map.98.share_ref), channel_id=1, source_target_pairs={{0,16},{16,0},{1,17},{17,1},{2,18},{18,2},{3,19},{19,3},{4,20},{20... | collective-permute-start | bytes 24584 | tf_op jit(solution)/shard_map/ppermute | solution.py:392
  30.7 3.6 %collective-permute-start.10 = (f32[2,128]{1,0:T(2,128)S(1)}, f32[2,128]{1,0:T(2,128)S(1)}, u32[]{:S(2)}, u32[]{:S(2)}) collective-permute-start(f32[2,128]{1,0:T(2,128)S(1)} %get-tuple-element.64), channel_id=1, source_target_pairs={{0,16},{16,0},{1,17},{17,1},{2,18},{18,2},{3,19},{19,3},{4,20},{20... | collective-permute-start | bytes 3080 | tf_op jit(solution)/shard_map/ppermute | solution.py:400

commit v8 on v7

--- a/solution.py
+++ b/solution.py
@@ -15,15 +15,15 @@
 
 NEG_FILL = -1e30
 RIM_ROWS = 16
+TILE = 512
 LEAST_RETENTION = -40.0
 VMEM_BYTES = 16 * 1024 * 1024
 
 
-def convolve(widened, taps_ref, columns, lead, rows):
-    summed = jnp.zeros((rows, columns.stop - columns.start), jnp.float32)
-    for back in range(taps_ref.shape[0]):
-        tap = taps_ref[back : back + 1, columns].astype(jnp.float32)
-        summed = summed + tap * widened[lead - back : lead - back + rows, columns]
+def convolve(widened, taps, lead, rows):
+    summed = jnp.zeros((rows, widened.shape[1]), jnp.float32)
+    for back in range(taps.shape[0]):
+        summed = summed + taps[back : back + 1] * widened[lead - back : lead - back + rows]
     return summed.astype(jnp.bfloat16)
 
 
@@ -35,12 +35,14 @@
     edges_ref[RIM_ROWS:] = rows_ref[rows - RIM_ROWS :]
     held_taps_ref[...] = taps_ref[...].astype(jnp.float32)
     held_ref[...] = gate_ref[...]
-    tile = math.gcd(features, 512)
+    tile = widened.shape[2]
     total = jnp.zeros(out_ref.shape, jnp.float32)
-    for start in range(0, features, tile):
-        columns = slice(start, start + tile)
-        widened[:, columns] = rows_ref[:, columns].astype(jnp.float32)
-        mixed = convolve(widened, taps_ref, columns, RIM_ROWS, rows - RIM_ROWS)
+    for step in range(features // tile):
+        columns = slice(step * tile, (step + 1) * tile)
+        wide = widened.at[step % 2]
+        wide[...] = rows_ref[:, columns].astype(jnp.float32)
+        taps = taps_ref[:, columns].astype(jnp.float32)
+        mixed = convolve(wide, taps, RIM_ROWS, rows - RIM_ROWS)
         total = total + jnp.dot(mixed, gate_ref[columns, :], preferred_element_type=jnp.float32)
     out_ref[...] = total
 
@@ -49,22 +51,24 @@
     peer_ref, edges_ref, taps_ref, gate_ref, near_ref, far_ref, far_sent_ref, widened, own_widened
 ):
     rows, features = peer_ref.shape
-    tile = math.gcd(features, 512)
+    tile = widened.shape[2]
     first = lax.axis_index("seq") == 0
     half = near_ref.shape[1]
     total = jnp.zeros((near_ref.shape[0], 2 * half), jnp.float32)
-    for start in range(0, features, tile):
-        columns = slice(start, start + tile)
+    for step in range(features // tile):
+        columns = slice(step * tile, (step + 1) * tile)
+        wide, own_wide = widened.at[step % 2], own_widened.at[step % 2]
         own_tail = edges_ref[RIM_ROWS:, columns].astype(jnp.float32)
         peer_tail = peer_ref[rows - RIM_ROWS :, columns].astype(jnp.float32)
-        widened[:RIM_ROWS, columns] = jnp.where(first, own_tail, 0.0)
-        widened[RIM_ROWS:, columns] = peer_ref[:, columns].astype(jnp.float32)
-        own_widened[:RIM_ROWS, columns] = jnp.where(first, 0.0, peer_tail)
-        own_widened[RIM_ROWS:, columns] = edges_ref[:RIM_ROWS, columns].astype(jnp.float32)
+        wide[:RIM_ROWS] = jnp.where(first, own_tail, 0.0)
+        wide[RIM_ROWS:] = peer_ref[:, columns].astype(jnp.float32)
+        own_wide[:RIM_ROWS] = jnp.where(first, 0.0, peer_tail)
+        own_wide[RIM_ROWS:] = edges_ref[:RIM_ROWS, columns].astype(jnp.float32)
+        taps = taps_ref[:, columns].astype(jnp.float32)
         mixed = jnp.concatenate(
             [
-                convolve(own_widened, taps_ref, columns, RIM_ROWS, RIM_ROWS),
-                convolve(widened, taps_ref, columns, RIM_ROWS, rows),
+                convolve(own_wide, taps, RIM_ROWS, RIM_ROWS),
+                convolve(wide, taps, RIM_ROWS, rows),
             ],
             axis=0,
         )
@@ -85,7 +89,7 @@
             jax.ShapeDtypeStruct(conv_taps.shape, jnp.float32),
             jax.ShapeDtypeStruct(gate_in.shape, gate_in.dtype),
         ),
-        scratch_shapes=[pltpu.VMEM((rows, features), jnp.float32)],
+        scratch_shapes=[pltpu.VMEM((2, rows, math.gcd(features, TILE)), jnp.float32)],
         compiler_params=pltpu.CompilerParams(vmem_limit_bytes=VMEM_BYTES),
         cost_estimate=pl.CostEstimate(flops=1, bytes_accessed=1, transcendentals=0),
     )(activations, conv_taps, gate_in)
@@ -103,8 +107,8 @@
             jax.ShapeDtypeStruct((done, half), jnp.bfloat16),
         ),
         scratch_shapes=[
-            pltpu.VMEM((rows + RIM_ROWS, features), jnp.float32),
-            pltpu.VMEM((2 * RIM_ROWS, features), jnp.float32),
+            pltpu.VMEM((2, rows + RIM_ROWS, math.gcd(features, TILE)), jnp.float32),
+            pltpu.VMEM((2, 2 * RIM_ROWS, math.gcd(features, TILE)), jnp.float32),
         ],
         compiler_params=pltpu.CompilerParams(vmem_limit_bytes=VMEM_BYTES),
         cost_estimate=pl.CostEstimate(flops=1, bytes_accessed=1, transcendentals=0),

time: 35 us -> 35 us (level)
  no operation moved by 1% of the time
where the time goes in v8:
time: 35 us; the launch traced here: 34.8 us
  starting transfers between devices  13.1 us (37%)
  waiting for transfers between devices  11.2 us (32%)
  Pallas kernels  8.08 us (23%)
  other arithmetic  1.51 us (4%)
  between operations  0.69 us (2%)
    ppermute x6, waiting for transfers between devices, exchange_heads(): return lax.ppermute(block, 'heads', [(i, i ^ step) for i in range(count)])  6.49 us
    ppermute x6, starting transfers between devices, exchange_heads(): return lax.ppermute(block, 'heads', [(i, i ^ step) for i in range(count)])  4.92 us
    ppermute x1, starting transfers between devices, pair_device(): peer_rows = lax.ppermute(activations, 'seq', swap)  3 us
    pallas_call x1, Pallas kernels, own_project(): pl.pallas_call(own_project_kernel, out_shape=(jax.ShapeDtypeStruct((done,...  2.55 us
    pallas_call x1, Pallas kernels, peer_project(): pl.pallas_call(peer_project_kernel, out_shape=(jax.ShapeDtypeStruct((done...  2.44 us
    ppermute x1, waiting for transfers between devices, pair_device(): peer_rows = lax.ppermute(activations, 'seq', swap)  2.35 us
    ppermute x1, starting transfers between devices, pair_device(): key_mass = own_mass + lax.ppermute(behind_mass, 'seq', swap)  1.61 us
    ppermute x1, starting transfers between devices, pair_device(): lax.ppermute(share, 'seq', swap)  1.53 us
  transfers between devices with their start and end apart: 11, of which 6 were waited for; matrix products, arithmetic and copies ran while one was open for 3% of the time, Pallas kernels for 16%

profile of v8, /device:TPU:0, one launch (start us, length us, event | category | flops | bytes accessed | tf_op | source)
XLA Modules:
  0.0 34.8 jit_solution(4179101540069606585)
XLA Ops:
  0.6 0.0 copy-start
  0.6 3.0 %collective-permute-start.3 = (bf16[128,2048]{1,0:T(8,128)(2,1)}, bf16[128,2048]{1,0:T(8,128)(2,1)S(1)}, u32[]{:S(2)}, u32[]{:S(2)}) collective-permute-start(bf16[128,2048]{1,0:T(8,128)(2,1)} %param.12), channel_id=1, source_target_pairs={{0,16},{16,0},{1,17},{17,1},{2,18},{18,2},{3,19},{19,3},{4,20},{20... | collective-permute-start | bytes 1572872 | tf_op jit(solution)/shard_map/ppermute | solution.py:377
  3.6 0.0 copy-done
  3.7 0.2 copy.13
  3.8 9.6 %conditional.2 = (f32[8,112]{1,0:T(8,128)S(1)}, bf16[32,2048]{1,0:T(8,128)(2,1)S(1)}, f32[4,2048]{1,0:T(4,128)S(1)}, bf16[2048,512]{1,0:T(8,128)(2,1)S(1)}) conditional(s32[]{:T(128)} %convert_element_type.16, () %tuple.24, (bf16[128,2048]{1,0:T(8,128)(2,1)}, bf16[4,2048]{1,0:T(4,128)(2,1)}, bf16[2048,512]{1,0:T(8,128)(2,1)}, ...), branch_computations={%region_0.0_spmd, %region_1.0_spmd} | conditional | flops 114689 | bytes 2264620 | solution.py:137
  3.8 2.5 %branch_1_fun.3 = (f32[112,512]{1,0:T(8,128)S(1)}, bf16[32,2048]{1,0:T(8,128)(2,1)S(1)}, f32[4,2048]{1,0:T(4,128)S(1)}, bf16[2048,512]{1,0:T(8,128)(2,1)S(1)}) custom-call(bf16[128,2048]{1,0:T(8,128)(2,1)} %get-tuple-element.18.rows_ref, bf16[4,2048]{1,0:T(4,128)(2,1)} %get-tuple-element.67.taps_ref, bf16[2048,512]{1,0:T(8,128)(2,1)} %get-tuple-element.68.gate_ref), custom_call_target="tpu_custom_call" | custom-call | flops 1 | bytes 1 | tf_op jit(solution)/shard_map/cond/branch_1_fun/pallas_call | solution.py:84
  6.4 0.1 collective-permute-start.1
  6.5 1.5 %collective-permute-done.1 = f32[112,512]{1,0:T(8,128)S(1)} collective-permute-done((f32[112,512]{1,0:T(8,128)S(1)}, f32[112,512]{1,0:T(8,128)S(1)}, u32[]{:S(2)}, u32[]{:S(2)}) %collective-permute-start.1) | collective-permute-done | bytes 229408 | tf_op jit(solution)/shard_map/cond/branch_1_fun/ppermute | solution.py:132
  8.0 1.6 %collective-permute-start.2 = (bf16[112,512]{1,0:T(8,128)(2,1)S(1)}, bf16[112,512]{1,0:T(8,128)(2,1)S(1)}, u32[]{:S(2)}, u32[]{:S(2)}) collective-permute-start(bf16[112,512]{1,0:T(8,128)(2,1)S(1)} %get-tuple-element.69), channel_id=1, source_target_pairs={{0,8},{4,12},{8,0},{12,4},{1,9},{5,13},{9,1},{13,5},{2,10},{6,14},... | collective-permute-start | bytes 344072 | tf_op jit(solution)/shard_map/cond/branch_1_fun/ppermute | solution.py:132
  9.6 3.7 %collective-permute-done.2.in_ref = bf16[112,512]{1,0:T(8,128)(2,1)S(1)} collective-permute-done((bf16[112,512]{1,0:T(8,128)(2,1)S(1)}, bf16[112,512]{1,0:T(8,128)(2,1)S(1)}, u32[]{:S(2)}, u32[]{:S(2)}) %collective-permute-start.2) | collective-permute-done | bytes 114720 | tf_op jit(solution)/shard_map/cond/branch_1_fun/ppermute | solution.py:132
  13.2 0.2 branch_1_fun.4
  13.4 0.0 copy-start.5
  13.4 0.0 copy-start.2
  13.4 0.0 copy-start.3
  13.4 2.3 %collective-permute-done.3.peer_ref = bf16[128,2048]{1,0:T(8,128)(2,1)S(1)} collective-permute-done((bf16[128,2048]{1,0:T(8,128)(2,1)}, bf16[128,2048]{1,0:T(8,128)(2,1)S(1)}, u32[]{:S(2)}, u32[]{:S(2)}) %collective-permute-start.3) | collective-permute-done | bytes 524320 | tf_op jit(solution)/shard_map/ppermute | solution.py:377
  15.8 0.0 copy-done.5
  15.8 0.0 copy-start.1
  15.8 0.0 copy-start.4
  15.8 2.4 %shard_map.97 = (f32[144,256]{1,0:T(8,128)S(1)}, f32[144,256]{1,0:T(8,128)}, bf16[144,256]{1,0:T(8,128)(2,1)S(1)}) custom-call(bf16[128,2048]{1,0:T(8,128)(2,1)S(1)} %collective-permute-done.3.peer_ref, bf16[32,2048]{1,0:T(8,128)(2,1)} %copy-done.5, f32[4,2048]{1,0:T(4,128)S(1)} %get-tuple-element.55.taps_ref, bf16[2048,512]{1,0:T(8,128)(2,1)S(1)} %get-tuple-element.56.gate_ref), custom_call_target="tpu_custom_call" | custom-call | flops 1 | bytes 1 | tf_op jit(solution)/shard_map/pallas_call | solution.py:102
  18.2 0.0 collective-permute-start.5
  18.2 1.8 %collective-permute-start.4 = (bf16[144,256]{1,0:T(8,128)(2,1)S(1)}, bf16[144,256]{1,0:T(8,128)(2,1)S(1)}, u32[]{:S(2)}, u32[]{:S(2)}) collective-permute-start(bf16[144,256]{1,0:T(8,128)(2,1)S(1)} %get-tuple-element.57), channel_id=1, source_target_pairs={{0,8},{4,12},{8,0},{12,4},{1,9},{5,13},{9,1},{13,5},{2,10},{6,14},... | collective-permute-start | bytes 221192 | tf_op jit(solution)/shard_map/ppermute | solution.py:132
  20.0 0.0 collective-permute-done.5
  20.0 1.4 %collective-permute-start.6 = (bf16[144,256]{1,0:T(8,128)(2,1)S(1)}, bf16[144,256]{1,0:T(8,128)(2,1)S(1)}, u32[]{:S(2)}, u32[]{:S(2)}) collective-permute-start(bf16[144,256]{1,0:T(8,128)(2,1)S(1)} %get-tuple-element.71), channel_id=1, source_target_pairs={{0,8},{4,12},{8,0},{12,4},{1,9},{5,13},{9,1},{13,5},{2,10},{6,14},... | collective-permute-start | bytes 221192 | tf_op jit(solution)/shard_map/ppermute | solution.py:132
  21.5 0.0 copy-done.2
  21.5 1.5 %collective-permute-start.8 = (bf16[128,256]{1,0:T(8,128)(2,1)S(1)}, bf16[128,256]{1,0:T(8,128)(2,1)S(1)}, u32[]{:S(2)}, u32[]{:S(2)}) collective-permute-start(bf16[128,256]{1,0:T(8,128)(2,1)S(1)} %copy-done.2), channel_id=1, source_target_pairs={{0,16},{16,0},{1,17},{17,1},{2,18},{18,2},{3,19},{19,3},{4,20},{20... | collective-permute-start | bytes 196616 | tf_op jit(solution)/shard_map/ppermute | solution.py:386
  22.9 0.0 copy-done.3
  23.0 0.5 %collective-permute-start.9 = (bf16[128,256]{1,0:T(8,128)(2,1)S(1)}, bf16[128,256]{1,0:T(8,128)(2,1)S(1)}, u32[]{:S(2)}, u32[]{:S(2)}) collective-permute-start(bf16[128,256]{1,0:T(8,128)(2,1)S(1)} %copy-done.3), channel_id=1, source_target_pairs={{0,16},{16,0},{1,17},{17,1},{2,18},{18,2},{3,19},{19,3},{4,20},{20... | collective-permute-start | bytes 196616 | tf_op jit(solution)/shard_map/ppermute | solution.py:387
  23.5 0.0 collective-permute-done.4
  23.5 2.6 %conditional.3 = (f32[8,144]{1,0:T(8,128)S(1)}) conditional(s32[]{:T(128)} %convert_element_type.16, () %tuple.27, (bf16[144,256]{1,0:T(8,128)(2,1)S(1)}, f32[144,256]{1,0:T(8,128)}, bf16[512,8]{1,0:T(8,128)(2,1)S(1)}) %tuple.28), branch_computations={%region_2.0_spmd, %region_3.0_spmd} | conditional | flops 73728 | bytes 966704 | solution.py:137
  23.5 0.9 %convert_add_fusion.own_ref = f32[144,256]{1,0:T(8,128)S(1)} fusion(f32[144,256]{1,0:T(8,128)} %get-tuple-element.26, bf16[144,256]{1,0:T(8,128)(2,1)S(1)} %get-tuple-element.27), kind=kLoop, calls=%fused_computation | loop fusion | flops 73728 | bytes 368640 | tf_op jit(solution)/shard_map/cond/branch_1_fun/add | solution.py:153
  24.4 0.1 collective-permute-start
  24.5 1.3 %collective-permute-done.in_ref = f32[144,256]{1,0:T(8,128)S(1)} collective-permute-done((f32[144,256]{1,0:T(8,128)S(1)}, f32[144,256]{1,0:T(8,128)S(1)}, u32[]{:S(2)}, u32[]{:S(2)}) %collective-permute-start) | collective-permute-done | bytes 147488 | tf_op jit(solution)/shard_map/cond/branch_1_fun/ppermute | solution.py:132
  25.9 0.2 branch_1_fun.5
  26.1 0.0 collective-permute-done.6.near_in_ref
  26.1 0.3 shard_map.98.share_ref
  26.3 1.5 %collective-permute-start.7 = (f32[2,8,128]{2,1,0:T(8,128)S(1)}, f32[2,8,128]{2,1,0:T(8,128)S(1)}, u32[]{:S(2)}, u32[]{:S(2)}) collective-permute-start(f32[2,8,128]{2,1,0:T(8,128)S(1)} %shard_map.98.share_ref), channel_id=1, source_target_pairs={{0,16},{16,0},{1,17},{17,1},{2,18},{18,2},{3,19},{19,3},{4,20},{20... | collective-permute-start | bytes 24584 | tf_op jit(solution)/shard_map/ppermute | solution.py:396
  27.9 0.0 collective-permute-done.8.behind_keys_ref
  27.9 0.0 copy-done.1
  27.9 0.0 copy-done.4
  27.9 0.7 %shard_map.99.powers_ref = f32[16,128,256]{2,1,0:T(8,128)S(1)} custom-call(s32[2,128]{1,0:T(2,128)S(1)} %bitcast.1, bf16[128,2048]{1,0:T(8,128)(2,1)S(1)} %copy-done.1, bf16[128,256]{1,0:T(8,128)(2,1)S(1)} %copy-done.2, bf16[128,256]{1,0:T(8,128)(2,1)S(1)} %collective-permute-done.8.behind_keys_ref), custom_call_target="tpu_custom_call" | custom-call | flops 134217728 | bytes 2097152 | tf_op jit(solution)/shard_map/pallas_call | solution.py:254
  28.6 1.4 %collective-permute-done.7.peer_share_ref = f32[2,8,128]{2,1,0:T(8,128)S(1)} collective-permute-done((f32[2,8,128]{2,1,0:T(8,128)S(1)}, f32[2,8,128]{2,1,0:T(8,128)S(1)}, u32[]{:S(2)}, u32[]{:S(2)}) %collective-permute-start.7) | collective-permute-done | bytes 8224 | tf_op jit(solution)/shard_map/ppermute | solution.py:396
  30.0 0.6 %shard_map.100 = (bf16[16,128,256]{2,1,0:T(8,128)(2,1)S(1)}, f32[2,128]{1,0:T(2,128)S(1)}, f32[2,128]{1,0:T(2,128)S(1)}) custom-call(f32[2,8,128]{2,1,0:T(8,128)S(1)} %shard_map.98.share_ref, f32[2,8,128]{2,1,0:T(8,128)S(1)} %collective-permute-done.7.peer_share_ref, f32[16,128,256]{2,1,0:T(8,128)S(1)} %shard_map.99.powers_ref, s32[2,128]{1,0:T(2,128)S(1)} %bitcast.2, ...), custom_call_target="tpu_custom_call" | custom-call | tf_op jit(solution)/shard_map/pallas_call | solution.py:328
  30.7 1.6 %collective-permute-start.10 = (f32[2,128]{1,0:T(2,128)S(1)}, f32[2,128]{1,0:T(2,128)S(1)}, u32[]{:S(2)}, u32[]{:S(2)}) collective-permute-start(f32[2,128]{1,0:T(2,128)S(1)} %get-tuple-element.64), channel_id=1, source_target_pairs={{0,16},{16,0},{1,17},{17,1},{2,18},{18,2},{3,19},{19,3},{4,20},{20... | collective-permute-start | bytes 3080 | tf_op jit(solution)/shard_map/ppermute | solution.py:404
  32.3 0.0 collective-permute-done.9.behind_values_ref
  32.3 1.1 %shard_map.101 = bf16[128,2048]{1,0:T(8,128)(2,1)} custom-call(bf16[16,128,256]{2,1,0:T(8,128)(2,1)S(1)} %get-tuple-element.62.weights_ref, bf16[128,256]{1,0:T(8,128)(2,1)S(1)} %copy-done.3, bf16[128,256]{1,0:T(8,128)(2,1)S(1)} %collective-permute-done.9.behind_values_ref), custom_call_target="tpu_custom_call" | custom-call | flops 134217728 | bytes 1572864 | tf_op jit(solution)/shard_map/pallas_call | solution.py:355
  33.4 0.9 %collective-permute-done.10 = f32[2,128]{1,0:T(2,128)S(1)} collective-permute-done((f32[2,128]{1,0:T(2,128)S(1)}, f32[2,128]{1,0:T(2,128)S(1)}, u32[]{:S(2)}, u32[]{:S(2)}) %collective-permute-start.10) | collective-permute-done | bytes 1056 | tf_op jit(solution)/shard_map/ppermute | solution.py:404
  34.3 0.5 %add_convert_fusion = bf16[2,128]{1,0:T(2,128)(2,1)} fusion(f32[2,128]{1,0:T(2,128)S(1)} %get-tuple-element.63, f32[2,128]{1,0:T(2,128)S(1)} %collective-permute-done.10), kind=kLoop, calls=%fused_computation.1 | loop fusion | flops 512 | bytes 2560 | tf_op jit(solution)/shard_map/convert_element_type | solution.py:405
  (5 shorter events, 0.1 us)
Async XLA Ops:
  0.6 3.0 %copy-start = (bf16[1024,8]{0,1:T(8,128)(2,1)S(1)}, bf16[1024,8]{0,1:T(8,128)(2,1)}, u32[]{:S(2)}) copy-start(bf16[1024,8]{0,1:T(8,128)(2,1)} %param.15) | copy-start | bytes 49156
  0.6 15.1 %collective-permute-start.3 = (bf16[128,2048]{1,0:T(8,128)(2,1)}, bf16[128,2048]{1,0:T(8,128)(2,1)S(1)}, u32[]{:S(2)}, u32[]{:S(2)}) collective-permute-start(bf16[128,2048]{1,0:T(8,128)(2,1)} %param.12), channel_id=1, source_target_pairs={{0,16},{16,0},{1,17},{17,1},{2,18},{18,2},{3,19},{19,3},{4,20},{20... | collective-permute-start | bytes 1572872 | tf_op jit(solution)/shard_map/ppermute | solution.py:377
  6.4 1.5 %collective-permute-start.1 = (f32[112,512]{1,0:T(8,128)S(1)}, f32[112,512]{1,0:T(8,128)S(1)}, u32[]{:S(2)}, u32[]{:S(2)}) collective-permute-start(f32[112,512]{1,0:T(8,128)S(1)} %get-tuple-element.21), channel_id=1, source_target_pairs={{0,4},{4,0},{8,12},{12,8},{1,5},{5,1},{9,13},{13,9},{2,6},{6,2},{1... | collective-permute-start | bytes 688136 | tf_op jit(solution)/shard_map/cond/branch_1_fun/ppermute | solution.py:132
  8.0 5.3 %collective-permute-start.2 = (bf16[112,512]{1,0:T(8,128)(2,1)S(1)}, bf16[112,512]{1,0:T(8,128)(2,1)S(1)}, u32[]{:S(2)}, u32[]{:S(2)}) collective-permute-start(bf16[112,512]{1,0:T(8,128)(2,1)S(1)} %get-tuple-element.69), channel_id=1, source_target_pairs={{0,8},{4,12},{8,0},{12,4},{1,9},{5,13},{9,1},{13,5},{2,10},{6,14},... | collective-permute-start | bytes 344072 | tf_op jit(solution)/shard_map/cond/branch_1_fun/ppermute | solution.py:132
  13.4 2.4 %copy-start.5 = (bf16[32,2048]{1,0:T(8,128)(2,1)}, bf16[32,2048]{1,0:T(8,128)(2,1)S(1)}, u32[]{:S(2)}) copy-start(bf16[32,2048]{1,0:T(8,128)(2,1)S(1)} %get-tuple-element.54.edges_ref) | copy-start | bytes 393220
  13.4 8.0 %copy-start.2 = (bf16[128,256]{1,0:T(8,128)(2,1)S(1)}, bf16[128,256]{1,0:T(8,128)(2,1)}, u32[]{:S(2)}) copy-start(bf16[128,256]{1,0:T(8,128)(2,1)} %keys_ref.3) | copy-start | bytes 196612
  13.4 9.5 %copy-start.3 = (bf16[128,256]{1,0:T(8,128)(2,1)S(1)}, bf16[128,256]{1,0:T(8,128)(2,1)}, u32[]{:S(2)}) copy-start(bf16[128,256]{1,0:T(8,128)(2,1)} %values_ref.1) | copy-start | bytes 196612
  15.8 12.1 %copy-start.1 = (bf16[128,2048]{1,0:T(8,128)(2,1)S(1)}, bf16[128,2048]{1,0:T(8,128)(2,1)}, u32[]{:S(2)}) copy-start(bf16[128,2048]{1,0:T(8,128)(2,1)} %queries_ref.1) | copy-start | bytes 1572868
  15.8 12.1 %copy-start.4 = (s32[256]{0:T(256)S(1)}, s32[256]{0:T(256)}, u32[]{:S(2)}) copy-start(s32[256]{0:T(256)} %param.19) | copy-start | bytes 3076
  18.2 1.8 %collective-permute-start.5 = (f32[144,256]{1,0:T(8,128)S(1)}, f32[144,256]{1,0:T(8,128)S(1)}, u32[]{:S(2)}, u32[]{:S(2)}) collective-permute-start(f32[144,256]{1,0:T(8,128)S(1)} %get-tuple-element.59), channel_id=1, source_target_pairs={{0,4},{4,0},{8,12},{12,8},{1,5},{5,1},{9,13},{13,9},{2,6},{6,2},{1... | collective-permute-start | bytes 442376 | tf_op jit(solution)/shard_map/ppermute | solution.py:132
  18.2 5.3 %collective-permute-start.4 = (bf16[144,256]{1,0:T(8,128)(2,1)S(1)}, bf16[144,256]{1,0:T(8,128)(2,1)S(1)}, u32[]{:S(2)}, u32[]{:S(2)}) collective-permute-start(bf16[144,256]{1,0:T(8,128)(2,1)S(1)} %get-tuple-element.57), channel_id=1, source_target_pairs={{0,8},{4,12},{8,0},{12,4},{1,9},{5,13},{9,1},{13,5},{2,10},{6,14},... | collective-permute-start | bytes 221192 | tf_op jit(solution)/shard_map/ppermute | solution.py:132
  20.0 6.0 %collective-permute-start.6 = (bf16[144,256]{1,0:T(8,128)(2,1)S(1)}, bf16[144,256]{1,0:T(8,128)(2,1)S(1)}, u32[]{:S(2)}, u32[]{:S(2)}) collective-permute-start(bf16[144,256]{1,0:T(8,128)(2,1)S(1)} %get-tuple-element.71), channel_id=1, source_target_pairs={{0,8},{4,12},{8,0},{12,4},{1,9},{5,13},{9,1},{13,5},{2,10},{6,14},... | collective-permute-start | bytes 221192 | tf_op jit(solution)/shard_map/ppermute | solution.py:132
  21.5 6.4 %collective-permute-start.8 = (bf16[128,256]{1,0:T(8,128)(2,1)S(1)}, bf16[128,256]{1,0:T(8,128)(2,1)S(1)}, u32[]{:S(2)}, u32[]{:S(2)}) collective-permute-start(bf16[128,256]{1,0:T(8,128)(2,1)S(1)} %copy-done.2), channel_id=1, source_target_pairs={{0,16},{16,0},{1,17},{17,1},{2,18},{18,2},{3,19},{19,3},{4,20},{20... | collective-permute-start | bytes 196616 | tf_op jit(solution)/shard_map/ppermute | solution.py:386
  23.0 9.3 %collective-permute-start.9 = (bf16[128,256]{1,0:T(8,128)(2,1)S(1)}, bf16[128,256]{1,0:T(8,128)(2,1)S(1)}, u32[]{:S(2)}, u32[]{:S(2)}) collective-permute-start(bf16[128,256]{1,0:T(8,128)(2,1)S(1)} %copy-done.3), channel_id=1, source_target_pairs={{0,16},{16,0},{1,17},{17,1},{2,18},{18,2},{3,19},{19,3},{4,20},{20... | collective-permute-start | bytes 196616 | tf_op jit(solution)/shard_map/ppermute | solution.py:387
  24.4 1.4 %collective-permute-start = (f32[144,256]{1,0:T(8,128)S(1)}, f32[144,256]{1,0:T(8,128)S(1)}, u32[]{:S(2)}, u32[]{:S(2)}) collective-permute-start(f32[144,256]{1,0:T(8,128)S(1)} %convert_add_fusion.own_ref), channel_id=1, source_target_pairs={{0,4},{4,0},{8,12},{12,8},{1,5},{5,1},{9,13},{13,9},{2,6},{6,2},{1... | collective-permute-start | bytes 442376 | tf_op jit(solution)/shard_map/cond/branch_1_fun/ppermute | solution.py:132
  26.3 3.7 %collective-permute-start.7 = (f32[2,8,128]{2,1,0:T(8,128)S(1)}, f32[2,8,128]{2,1,0:T(8,128)S(1)}, u32[]{:S(2)}, u32[]{:S(2)}) collective-permute-start(f32[2,8,128]{2,1,0:T(8,128)S(1)} %shard_map.98.share_ref), channel_id=1, source_target_pairs={{0,16},{16,0},{1,17},{17,1},{2,18},{18,2},{3,19},{19,3},{4,20},{20... | collective-permute-start | bytes 24584 | tf_op jit(solution)/shard_map/ppermute | solution.py:396
  30.7 3.6 %collective-permute-start.10 = (f32[2,128]{1,0:T(2,128)S(1)}, f32[2,128]{1,0:T(2,128)S(1)}, u32[]{:S(2)}, u32[]{:S(2)}) collective-permute-start(f32[2,128]{1,0:T(2,128)S(1)} %get-tuple-element.64), channel_id=1, source_target_pairs={{0,16},{16,0},{1,17},{17,1},{2,18},{18,2},{3,19},{19,3},{4,20},{20... | collective-permute-start | bytes 3080 | tf_op jit(solution)/shard_map/ppermute | solution.py:404

commit v9 on v8

--- a/solution.py
+++ b/solution.py
@@ -15,7 +15,6 @@
 
 NEG_FILL = -1e30
 RIM_ROWS = 16
-TILE = 512
 LEAST_RETENTION = -40.0
 VMEM_BYTES = 16 * 1024 * 1024
 
@@ -27,18 +26,19 @@
     return summed.astype(jnp.bfloat16)
 
 
-def own_project_kernel(
-    rows_ref, taps_ref, gate_ref, out_ref, edges_ref, held_taps_ref, held_ref, widened
-):
+def own_project_kernel(rows_ref, taps_ref, gate_ref, out_ref, held_taps_ref, held_ref, widened):
     rows, features = rows_ref.shape
-    edges_ref[:RIM_ROWS] = rows_ref[:RIM_ROWS]
-    edges_ref[RIM_ROWS:] = rows_ref[rows - RIM_ROWS :]
     held_taps_ref[...] = taps_ref[...].astype(jnp.float32)
-    held_ref[...] = gate_ref[...]
+    held_ref[:features] = gate_ref[...]
     tile = widened.shape[2]
     total = jnp.zeros(out_ref.shape, jnp.float32)
     for step in range(features // tile):
         columns = slice(step * tile, (step + 1) * tile)
+        edges = features + step * 2 * RIM_ROWS
+        held_ref[edges : edges + RIM_ROWS, :tile] = rows_ref[:RIM_ROWS, columns]
+        held_ref[edges + RIM_ROWS : edges + 2 * RIM_ROWS, :tile] = rows_ref[
+            rows - RIM_ROWS :, columns
+        ]
         wide = widened.at[step % 2]
         wide[...] = rows_ref[:, columns].astype(jnp.float32)
         taps = taps_ref[:, columns].astype(jnp.float32)
@@ -48,7 +48,7 @@
 
 
 def peer_project_kernel(
-    peer_ref, edges_ref, taps_ref, gate_ref, near_ref, far_ref, far_sent_ref, widened, own_widened
+    peer_ref, taps_ref, held_ref, near_ref, far_ref, widened, own_widened
 ):
     rows, features = peer_ref.shape
     tile = widened.shape[2]
@@ -58,12 +58,15 @@
     for step in range(features // tile):
         columns = slice(step * tile, (step + 1) * tile)
         wide, own_wide = widened.at[step % 2], own_widened.at[step % 2]
-        own_tail = edges_ref[RIM_ROWS:, columns].astype(jnp.float32)
+        edges = held_ref.at[
+            features + step * 2 * RIM_ROWS : features + (step + 1) * 2 * RIM_ROWS, :tile
+        ]
+        own_tail = edges[RIM_ROWS:].astype(jnp.float32)
         peer_tail = peer_ref[rows - RIM_ROWS :, columns].astype(jnp.float32)
         wide[:RIM_ROWS] = jnp.where(first, own_tail, 0.0)
         wide[RIM_ROWS:] = peer_ref[:, columns].astype(jnp.float32)
         own_wide[:RIM_ROWS] = jnp.where(first, 0.0, peer_tail)
-        own_wide[RIM_ROWS:] = edges_ref[:RIM_ROWS, columns].astype(jnp.float32)
+        own_wide[RIM_ROWS:] = edges[:RIM_ROWS].astype(jnp.float32)
         taps = taps_ref[:, columns].astype(jnp.float32)
         mixed = jnp.concatenate(
             [
@@ -72,47 +75,48 @@
             ],
             axis=0,
         )
-        total = total + jnp.dot(mixed, gate_ref[columns, :], preferred_element_type=jnp.float32)
+        total = total + jnp.dot(mixed, held_ref[columns, :], preferred_element_type=jnp.float32)
     near_ref[...] = total[:, :half]
-    far_ref[...] = total[:, half:]
-    far_sent_ref[...] = total[:, half:].astype(jnp.bfloat16)
+    far_ref[...] = total[:, half:].astype(jnp.bfloat16)
 
 
 def own_project(activations, conv_taps, gate_in):
     rows, features = activations.shape
     done = rows - RIM_ROWS
+    tile = math.gcd(features, gate_in.shape[1])
     return pl.pallas_call(
         own_project_kernel,
         out_shape=(
             jax.ShapeDtypeStruct((done, gate_in.shape[1]), jnp.float32),
-            jax.ShapeDtypeStruct((2 * RIM_ROWS, features), activations.dtype),
             jax.ShapeDtypeStruct(conv_taps.shape, jnp.float32),
-            jax.ShapeDtypeStruct(gate_in.shape, gate_in.dtype),
+            jax.ShapeDtypeStruct(
+                (features + features // tile * 2 * RIM_ROWS, gate_in.shape[1]), gate_in.dtype
+            ),
         ),
-        scratch_shapes=[pltpu.VMEM((2, rows, math.gcd(features, TILE)), jnp.float32)],
+        scratch_shapes=[pltpu.VMEM((2, rows, tile), jnp.float32)],
         compiler_params=pltpu.CompilerParams(vmem_limit_bytes=VMEM_BYTES),
         cost_estimate=pl.CostEstimate(flops=1, bytes_accessed=1, transcendentals=0),
     )(activations, conv_taps, gate_in)
 
 
-def peer_project(peer_rows, edges, conv_taps, gate_in):
+def peer_project(peer_rows, taps, held):
     rows, features = peer_rows.shape
     done = rows + RIM_ROWS
-    half = gate_in.shape[1] // 2
+    tile = math.gcd(features, held.shape[1])
+    half = held.shape[1] // 2
     return pl.pallas_call(
         peer_project_kernel,
         out_shape=(
-            jax.ShapeDtypeStruct((done, half), jnp.float32),
             jax.ShapeDtypeStruct((done, half), jnp.float32),
             jax.ShapeDtypeStruct((done, half), jnp.bfloat16),
         ),
         scratch_shapes=[
-            pltpu.VMEM((2, rows + RIM_ROWS, math.gcd(features, TILE)), jnp.float32),
-            pltpu.VMEM((2, 2 * RIM_ROWS, math.gcd(features, TILE)), jnp.float32),
+            pltpu.VMEM((2, rows + RIM_ROWS, tile), jnp.float32),
+            pltpu.VMEM((2, 2 * RIM_ROWS, tile), jnp.float32),
         ],
         compiler_params=pltpu.CompilerParams(vmem_limit_bytes=VMEM_BYTES),
         cost_estimate=pl.CostEstimate(flops=1, bytes_accessed=1, transcendentals=0),
-    )(peer_rows, edges, conv_taps, gate_in)
+    )(peer_rows, taps, held)
 
 
 def head_sum(part):
@@ -142,15 +146,15 @@
     )
 
 
-def far_logits(block, sent, gate_rows):
+def far_logits(block, gate_rows):
     step = lax.axis_size("heads") // 2
-    received = exchange_heads(sent, step)
+    received = exchange_heads(block, step)
 
     def nearer(block, received, gate_rows):
         distance = step
         while distance > 1:
             distance //= 2
-            block = block + received.astype(jnp.float32)
+            block = block.astype(jnp.float32) + received.astype(jnp.float32)
             received = exchange_heads(block, distance)
         return partial_logits(block, received, gate_rows)
 
@@ -382,12 +386,12 @@
 
     own_share, held = in_one_piece(own_work, activations, conv_taps, gate_in, gate_rows)
     peer_rows, own_share, held = lax.optimization_barrier((peer_rows, own_share, held))
-    near, far, far_sent = peer_project(peer_rows, *held)
+    near, far = peer_project(peer_rows, *held)
     behind_keys = lax.ppermute(key_vectors, "seq", swap)
     behind_values = lax.ppermute(value_vectors, "seq", swap)
     half = near.shape[1]
     near, near_in = head_sum(near)
-    far_share = far_logits(far, far_sent, gate_rows[half:])
+    far_share = far_logits(far, gate_rows[half:])
     share = logits_share(own_share, far_share, near, near_in, gate_rows[:half])
     share, queries = lax.optimization_barrier((share, queries))
     powers = powers_of(segments, queries, key_vectors, behind_keys)

time: 35 us -> 33.4 us (0.954)
  waiting for transfers between devices: 11.2 us -> 8.88 us
  local copies, waits for them, and re-layouts: 0.2 us -> 2.51 us
  other arithmetic: 1.51 us -> 0.59 us
  Pallas kernels: 8.08 us -> 7.33 us
    pallas_call x1, Pallas kernels: 2.44 us -> 0.8 us  [peer_project(): pl.pallas_call(peer_project_kernel, out_shape=(jax.ShapeDtypeStruct((done...]
    ppermute x1, waiting for transfers between devices: 2.35 us -> 0.84 us  [pair_device(): peer_rows = lax.ppermute(activations, 'seq', swap)]
    add x1, other arithmetic: 0.93 us -> 0.02 us  [nearer(): block = block.astype(jnp.float32) + received.astype(jnp.float32)]
    pallas_call x2, Pallas kernels: 0.38 us -> 1.28 us  [partial_logits(): pl.pallas_call(partial_logits_kernel, out_shape=jax.ShapeDtypeStruct((gat...]
    slice x1, local copies, waits for them, and re-layouts: 0.01 us -> 0.85 us  [pair_device(): far_share = far_logits(far, gate_rows[half:])]
    slice x1, local copies, waits for them, and re-layouts: 0.01 us -> 0.84 us  [pair_device(): share = logits_share(own_share, far_share, near, near_in, gate_rows[:half])]
    ppermute x6, waiting for transfers between devices: 6.49 us -> 5.66 us  [exchange_heads(): return lax.ppermute(block, 'heads', [(i, i ^ step) for i in range(count)])]
    unnamed x13 -> x11, local copies, waits for them, and re-layouts: 0.19 us -> 0.82 us
  transfers between devices with their start and end apart: 11 -> 11, of which waited for: 6 -> 6; matrix products, arithmetic and copies ran while one was open for 3% -> 8% of each run, Pallas kernels for 16% -> 20%
where the time goes in v9:
time: 33.4 us; the launch traced here: 33.2 us
  starting transfers between devices  13.1 us (39%)
  waiting for transfers between devices  8.88 us (27%)
  Pallas kernels  7.33 us (22%)
  local copies, waits for them, and re-layouts  2.51 us (8%)
  between operations  0.68 us (2%)
  other arithmetic  0.59 us (2%)
    ppermute x6, waiting for transfers between devices, exchange_heads(): return lax.ppermute(block, 'heads', [(i, i ^ step) for i in range(count)])  5.66 us
    ppermute x6, starting transfers between devices, exchange_heads(): return lax.ppermute(block, 'heads', [(i, i ^ step) for i in range(count)])  4.97 us
    ppermute x1, starting transfers between devices, pair_device(): peer_rows = lax.ppermute(activations, 'seq', swap)  3 us
    pallas_call x1, Pallas kernels, own_project(): pl.pallas_call(own_project_kernel, out_shape=(jax.ShapeDtypeStruct((done,...  2.54 us
    ppermute x1, starting transfers between devices, pair_device(): key_mass = own_mass + lax.ppermute(behind_mass, 'seq', swap)  1.61 us
    ppermute x1, starting transfers between devices, pair_device(): lax.ppermute(share, 'seq', swap)  1.53 us
    ppermute x1, starting transfers between devices, pair_device(): behind_keys = lax.ppermute(key_vectors, 'seq', swap)  1.49 us
    ppermute x1, waiting for transfers between devices, pair_device(): lax.ppermute(share, 'seq', swap)  1.44 us
  transfers between devices with their start and end apart: 11, of which 6 were waited for; matrix products, arithmetic and copies ran while one was open for 8% of the time, Pallas kernels for 20%

profile of v9, /device:TPU:0, one launch (start us, length us, event | category | flops | bytes accessed | tf_op | source)
XLA Modules:
  0.0 33.2 jit_solution(7869414250368297144)
XLA Ops:
  0.6 0.0 copy-start
  0.6 3.0 %collective-permute-start.3 = (bf16[128,2048]{1,0:T(8,128)(2,1)}, bf16[128,2048]{1,0:T(8,128)(2,1)S(1)}, u32[]{:S(2)}, u32[]{:S(2)}) collective-permute-start(bf16[128,2048]{1,0:T(8,128)(2,1)} %param.12), channel_id=1, source_target_pairs={{0,16},{16,0},{1,17},{17,1},{2,18},{18,2},{3,19},{19,3},{4,20},{20... | collective-permute-start | bytes 1572872 | tf_op jit(solution)/shard_map/ppermute | solution.py:381
  3.6 0.0 copy-done
  3.7 0.8 %copy.13 = bf16[512,8]{1,0:T(8,128)(2,1)} copy(bf16[512,8]{0,1:T(8,128)(2,1)S(1)} %constant_dynamic-slice_fusion) | data formatting | bytes 16384
  4.5 10.5 %conditional.2 = (f32[8,112]{1,0:T(8,128)S(1)}, f32[4,2048]{1,0:T(4,128)S(1)}, bf16[2176,512]{1,0:T(8,128)(2,1)S(1)}) conditional(s32[]{:T(128)} %convert_element_type.19, () %tuple.24, (bf16[128,2048]{1,0:T(8,128)(2,1)}, bf16[4,2048]{1,0:T(4,128)(2,1)}, bf16[2048,512]{1,0:T(8,128)(2,1)}, bf16[512,8]{1,0:T(8,128)(2,1)}) %tuple.25), branch_computations={%region_0.0_spmd, %region_1.0_spmd} | conditional | flops 114689 | bytes 2264610 | solution.py:141
  4.5 2.5 %branch_1_fun.3 = (f32[112,512]{1,0:T(8,128)S(1)}, f32[4,2048]{1,0:T(4,128)S(1)}, bf16[2176,512]{1,0:T(8,128)(2,1)S(1)}) custom-call(bf16[128,2048]{1,0:T(8,128)(2,1)} %get-tuple-element.18.rows_ref, bf16[4,2048]{1,0:T(4,128)(2,1)} %get-tuple-element.60.taps_ref, bf16[2048,512]{1,0:T(8,128)(2,1)} %get-tuple-element.61.gate_ref), custom_call_target="tpu_custom_call" | custom-call | flops 1 | bytes 1 | tf_op jit(solution)/shard_map/cond/branch_1_fun/pallas_call | solution.py:87
  7.0 0.1 collective-permute-start.1
  7.1 1.5 %collective-permute-done.1 = f32[112,512]{1,0:T(8,128)S(1)} collective-permute-done((f32[112,512]{1,0:T(8,128)S(1)}, f32[112,512]{1,0:T(8,128)S(1)}, u32[]{:S(2)}, u32[]{:S(2)}) %collective-permute-start.1) | collective-permute-done | bytes 229408 | tf_op jit(solution)/shard_map/cond/branch_1_fun/ppermute | solution.py:136
  8.6 1.6 %collective-permute-start.2 = (bf16[112,512]{1,0:T(8,128)(2,1)S(1)}, bf16[112,512]{1,0:T(8,128)(2,1)S(1)}, u32[]{:S(2)}, u32[]{:S(2)}) collective-permute-start(bf16[112,512]{1,0:T(8,128)(2,1)S(1)} %get-tuple-element.62), channel_id=1, source_target_pairs={{0,8},{4,12},{8,0},{12,4},{1,9},{5,13},{9,1},{13,5},{2,10},{6,14},... | collective-permute-start | bytes 344072 | tf_op jit(solution)/shard_map/cond/branch_1_fun/ppermute | solution.py:136
  10.2 3.7 %collective-permute-done.2.in_ref = bf16[112,512]{1,0:T(8,128)(2,1)S(1)} collective-permute-done((bf16[112,512]{1,0:T(8,128)(2,1)S(1)}, bf16[112,512]{1,0:T(8,128)(2,1)S(1)}, u32[]{:S(2)}, u32[]{:S(2)}) %collective-permute-start.2) | collective-permute-done | bytes 114720 | tf_op jit(solution)/shard_map/cond/branch_1_fun/ppermute | solution.py:136
  13.8 1.1 %branch_1_fun.4 = f32[8,112]{1,0:T(8,128)S(1)} custom-call(f32[112,512]{1,0:T(8,128)S(1)} %get-tuple-element.63.own_ref, bf16[112,512]{1,0:T(8,128)(2,1)S(1)} %collective-permute-done.2.in_ref, bf16[512,8]{1,0:T(8,128)(2,1)} %get-tuple-element.22.gate_out_ref), custom_call_target="tpu_custom_call" | custom-call | tf_op jit(solution)/shard_map/cond/branch_1_fun/pallas_call | solution.py:177
  14.9 0.0 copy-start.2
  14.9 0.0 copy-start.3
  14.9 0.8 %collective-permute-done.3.peer_ref = bf16[128,2048]{1,0:T(8,128)(2,1)S(1)} collective-permute-done((bf16[128,2048]{1,0:T(8,128)(2,1)}, bf16[128,2048]{1,0:T(8,128)(2,1)S(1)}, u32[]{:S(2)}, u32[]{:S(2)}) %collective-permute-start.3) | collective-permute-done | bytes 524320 | tf_op jit(solution)/shard_map/ppermute | solution.py:381
  15.8 0.0 copy-start.1
  15.8 0.0 copy-start.4
  15.8 0.8 %shard_map.97 = (f32[144,256]{1,0:T(8,128)S(1)}, bf16[144,256]{1,0:T(8,128)(2,1)S(1)}) custom-call(bf16[128,2048]{1,0:T(8,128)(2,1)S(1)} %collective-permute-done.3.peer_ref, f32[4,2048]{1,0:T(4,128)S(1)} %get-tuple-element.49.taps_ref, bf16[2176,512]{1,0:T(8,128)(2,1)S(1)} %get-tuple-element.50.held_ref), custom_call_target="tpu_custom_call" | custom-call | flops 1 | bytes 1 | tf_op jit(solution)/shard_map/pallas_call | solution.py:107
  16.6 0.1 collective-permute-start.5
  16.7 1.8 %collective-permute-start.4 = (bf16[144,256]{1,0:T(8,128)(2,1)S(1)}, bf16[144,256]{1,0:T(8,128)(2,1)S(1)}, u32[]{:S(2)}, u32[]{:S(2)}) collective-permute-start(bf16[144,256]{1,0:T(8,128)(2,1)S(1)} %get-tuple-element.51), channel_id=1, source_target_pairs={{0,8},{4,12},{8,0},{12,4},{1,9},{5,13},{9,1},{13,5},{2,10},{6,14},... | collective-permute-start | bytes 221192 | tf_op jit(solution)/shard_map/ppermute | solution.py:136
  18.5 0.0 collective-permute-done.5
  18.5 1.4 %collective-permute-start.6 = (bf16[144,256]{1,0:T(8,128)(2,1)S(1)}, bf16[144,256]{1,0:T(8,128)(2,1)S(1)}, u32[]{:S(2)}, u32[]{:S(2)}) collective-permute-start(bf16[144,256]{1,0:T(8,128)(2,1)S(1)} %get-tuple-element.64), channel_id=1, source_target_pairs={{0,8},{4,12},{8,0},{12,4},{1,9},{5,13},{9,1},{13,5},{2,10},{6,14},... | collective-permute-start | bytes 221192 | tf_op jit(solution)/shard_map/ppermute | solution.py:136
  19.9 0.0 copy-done.2
  19.9 1.5 %collective-permute-start.8 = (bf16[128,256]{1,0:T(8,128)(2,1)S(1)}, bf16[128,256]{1,0:T(8,128)(2,1)S(1)}, u32[]{:S(2)}, u32[]{:S(2)}) collective-permute-start(bf16[128,256]{1,0:T(8,128)(2,1)S(1)} %copy-done.2), channel_id=1, source_target_pairs={{0,16},{16,0},{1,17},{17,1},{2,18},{18,2},{3,19},{19,3},{4,20},{20... | collective-permute-start | bytes 196616 | tf_op jit(solution)/shard_map/ppermute | solution.py:390
  21.4 0.0 copy-done.3
  21.4 0.5 %collective-permute-start.9 = (bf16[128,256]{1,0:T(8,128)(2,1)S(1)}, bf16[128,256]{1,0:T(8,128)(2,1)S(1)}, u32[]{:S(2)}, u32[]{:S(2)}) collective-permute-start(bf16[128,256]{1,0:T(8,128)(2,1)S(1)} %copy-done.3), channel_id=1, source_target_pairs={{0,16},{16,0},{1,17},{17,1},{2,18},{18,2},{3,19},{19,3},{4,20},{20... | collective-permute-start | bytes 196616 | tf_op jit(solution)/shard_map/ppermute | solution.py:391
  21.9 0.8 %slice.8.gate_out_ref = bf16[256,8]{1,0:T(8,128)(2,1)S(1)} slice(bf16[512,8]{1,0:T(8,128)(2,1)} %copy.13), slice={[0:256], [0:8]} | slice | bytes 8192 | tf_op jit(solution)/shard_map/slice | solution.py:395
  22.8 0.0 collective-permute-done.4
  22.8 1.6 %conditional.3 = (f32[8,144]{1,0:T(8,128)S(1)}) conditional(s32[]{:T(128)} %convert_element_type.19, () %tuple.27, (bf16[144,256]{1,0:T(8,128)(2,1)S(1)}, bf16[144,256]{1,0:T(8,128)(2,1)S(1)}, bf16[512,8]{1,0:T(8,128)(2,1)}) %tuple.28), branch_computations={%region_2.0_spmd, %region_3.0_spmd} | conditional | flops 110592 | bytes 892976 | solution.py:141
  22.8 0.1 collective-permute-start
  22.9 0.8 %slice.5.gate_out_ref = bf16[256,8]{1,0:T(8,128)(2,1)S(1)} slice(bf16[512,8]{1,0:T(8,128)(2,1)} %get-tuple-element.27), slice={[256:512], [0:8]} | slice | bytes 8192 | tf_op jit(solution)/shard_map/slice | solution.py:394
  23.7 0.5 %collective-permute-done.in_ref = f32[144,256]{1,0:T(8,128)S(1)} collective-permute-done((f32[144,256]{1,0:T(8,128)S(1)}, f32[144,256]{1,0:T(8,128)S(1)}, u32[]{:S(2)}, u32[]{:S(2)}) %collective-permute-start) | collective-permute-done | bytes 147488 | tf_op jit(solution)/shard_map/cond/branch_1_fun/ppermute | solution.py:136
  24.2 0.2 branch_1_fun.5
  24.4 0.0 collective-permute-done.6.near_in_ref
  24.4 0.3 shard_map.98.share_ref
  24.7 1.5 %collective-permute-start.7 = (f32[2,8,128]{2,1,0:T(8,128)S(1)}, f32[2,8,128]{2,1,0:T(8,128)S(1)}, u32[]{:S(2)}, u32[]{:S(2)}) collective-permute-start(f32[2,8,128]{2,1,0:T(8,128)S(1)} %shard_map.98.share_ref), channel_id=1, source_target_pairs={{0,16},{16,0},{1,17},{17,1},{2,18},{18,2},{3,19},{19,3},{4,20},{20... | collective-permute-start | bytes 24584 | tf_op jit(solution)/shard_map/ppermute | solution.py:400
  26.2 0.0 collective-permute-done.8.behind_keys_ref
  26.2 0.0 copy-done.1
  26.2 0.0 copy-done.4
  26.2 0.7 %shard_map.99.powers_ref = f32[16,128,256]{2,1,0:T(8,128)S(1)} custom-call(s32[2,128]{1,0:T(2,128)S(1)} %bitcast.1, bf16[128,2048]{1,0:T(8,128)(2,1)S(1)} %copy-done.1, bf16[128,256]{1,0:T(8,128)(2,1)S(1)} %copy-done.2, bf16[128,256]{1,0:T(8,128)(2,1)S(1)} %collective-permute-done.8.behind_keys_ref), custom_call_target="tpu_custom_call" | custom-call | flops 134217728 | bytes 2097152 | tf_op jit(solution)/shard_map/pallas_call | solution.py:258
  26.9 1.4 %collective-permute-done.7.peer_share_ref = f32[2,8,128]{2,1,0:T(8,128)S(1)} collective-permute-done((f32[2,8,128]{2,1,0:T(8,128)S(1)}, f32[2,8,128]{2,1,0:T(8,128)S(1)}, u32[]{:S(2)}, u32[]{:S(2)}) %collective-permute-start.7) | collective-permute-done | bytes 8224 | tf_op jit(solution)/shard_map/ppermute | solution.py:400
  28.4 0.6 %shard_map.100 = (bf16[16,128,256]{2,1,0:T(8,128)(2,1)S(1)}, f32[2,128]{1,0:T(2,128)S(1)}, f32[2,128]{1,0:T(2,128)S(1)}) custom-call(f32[2,8,128]{2,1,0:T(8,128)S(1)} %shard_map.98.share_ref, f32[2,8,128]{2,1,0:T(8,128)S(1)} %collective-permute-done.7.peer_share_ref, f32[16,128,256]{2,1,0:T(8,128)S(1)} %shard_map.99.powers_ref, s32[2,128]{1,0:T(2,128)S(1)} %bitcast.2, ...), custom_call_target="tpu_custom_call" | custom-call | tf_op jit(solution)/shard_map/pallas_call | solution.py:332
  29.0 1.6 %collective-permute-start.10 = (f32[2,128]{1,0:T(2,128)S(1)}, f32[2,128]{1,0:T(2,128)S(1)}, u32[]{:S(2)}, u32[]{:S(2)}) collective-permute-start(f32[2,128]{1,0:T(2,128)S(1)} %get-tuple-element.57), channel_id=1, source_target_pairs={{0,16},{16,0},{1,17},{17,1},{2,18},{18,2},{3,19},{19,3},{4,20},{20... | collective-permute-start | bytes 3080 | tf_op jit(solution)/shard_map/ppermute | solution.py:408
  30.6 0.0 collective-permute-done.9.behind_values_ref
  30.6 1.1 %shard_map.101 = bf16[128,2048]{1,0:T(8,128)(2,1)} custom-call(bf16[16,128,256]{2,1,0:T(8,128)(2,1)S(1)} %get-tuple-element.55.weights_ref, bf16[128,256]{1,0:T(8,128)(2,1)S(1)} %copy-done.3, bf16[128,256]{1,0:T(8,128)(2,1)S(1)} %collective-permute-done.9.behind_values_ref), custom_call_target="tpu_custom_call" | custom-call | flops 134217728 | bytes 1572864 | tf_op jit(solution)/shard_map/pallas_call | solution.py:359
  31.7 0.9 %collective-permute-done.10 = f32[2,128]{1,0:T(2,128)S(1)} collective-permute-done((f32[2,128]{1,0:T(2,128)S(1)}, f32[2,128]{1,0:T(2,128)S(1)}, u32[]{:S(2)}, u32[]{:S(2)}) %collective-permute-start.10) | collective-permute-done | bytes 1056 | tf_op jit(solution)/shard_map/ppermute | solution.py:408
  32.7 0.5 %add_convert_fusion = bf16[2,128]{1,0:T(2,128)(2,1)} fusion(f32[2,128]{1,0:T(2,128)S(1)} %get-tuple-element.56, f32[2,128]{1,0:T(2,128)S(1)} %collective-permute-done.10), kind=kLoop, calls=%fused_computation.1 | loop fusion | flops 512 | bytes 2560 | tf_op jit(solution)/shard_map/convert_element_type | solution.py:409
  (4 shorter events, 0.1 us)
Async XLA Ops:
  0.6 3.0 %copy-start = (bf16[1024,8]{0,1:T(8,128)(2,1)S(1)}, bf16[1024,8]{0,1:T(8,128)(2,1)}, u32[]{:S(2)}) copy-start(bf16[1024,8]{0,1:T(8,128)(2,1)} %param.15) | copy-start | bytes 49156
  0.6 15.1 %collective-permute-start.3 = (bf16[128,2048]{1,0:T(8,128)(2,1)}, bf16[128,2048]{1,0:T(8,128)(2,1)S(1)}, u32[]{:S(2)}, u32[]{:S(2)}) collective-permute-start(bf16[128,2048]{1,0:T(8,128)(2,1)} %param.12), channel_id=1, source_target_pairs={{0,16},{16,0},{1,17},{17,1},{2,18},{18,2},{3,19},{19,3},{4,20},{20... | collective-permute-start | bytes 1572872 | tf_op jit(solution)/shard_map/ppermute | solution.py:381
  7.0 1.5 %collective-permute-start.1 = (f32[112,512]{1,0:T(8,128)S(1)}, f32[112,512]{1,0:T(8,128)S(1)}, u32[]{:S(2)}, u32[]{:S(2)}) collective-permute-start(f32[112,512]{1,0:T(8,128)S(1)} %get-tuple-element.21), channel_id=1, source_target_pairs={{0,4},{4,0},{8,12},{12,8},{1,5},{5,1},{9,13},{13,9},{2,6},{6,2},{1... | collective-permute-start | bytes 688136 | tf_op jit(solution)/shard_map/cond/branch_1_fun/ppermute | solution.py:136
  8.6 5.3 %collective-permute-start.2 = (bf16[112,512]{1,0:T(8,128)(2,1)S(1)}, bf16[112,512]{1,0:T(8,128)(2,1)S(1)}, u32[]{:S(2)}, u32[]{:S(2)}) collective-permute-start(bf16[112,512]{1,0:T(8,128)(2,1)S(1)} %get-tuple-element.62), channel_id=1, source_target_pairs={{0,8},{4,12},{8,0},{12,4},{1,9},{5,13},{9,1},{13,5},{2,10},{6,14},... | collective-permute-start | bytes 344072 | tf_op jit(solution)/shard_map/cond/branch_1_fun/ppermute | solution.py:136
  14.9 4.9 %copy-start.2 = (bf16[128,256]{1,0:T(8,128)(2,1)S(1)}, bf16[128,256]{1,0:T(8,128)(2,1)}, u32[]{:S(2)}) copy-start(bf16[128,256]{1,0:T(8,128)(2,1)} %keys_ref.3) | copy-start | bytes 196612
  14.9 6.4 %copy-start.3 = (bf16[128,256]{1,0:T(8,128)(2,1)S(1)}, bf16[128,256]{1,0:T(8,128)(2,1)}, u32[]{:S(2)}) copy-start(bf16[128,256]{1,0:T(8,128)(2,1)} %values_ref.1) | copy-start | bytes 196612
  15.8 10.4 %copy-start.1 = (bf16[128,2048]{1,0:T(8,128)(2,1)S(1)}, bf16[128,2048]{1,0:T(8,128)(2,1)}, u32[]{:S(2)}) copy-start(bf16[128,2048]{1,0:T(8,128)(2,1)} %queries_ref.1) | copy-start | bytes 1572868
  15.8 10.4 %copy-start.4 = (s32[256]{0:T(256)S(1)}, s32[256]{0:T(256)}, u32[]{:S(2)}) copy-start(s32[256]{0:T(256)} %param.19) | copy-start | bytes 3076
  16.6 1.9 %collective-permute-start.5 = (f32[144,256]{1,0:T(8,128)S(1)}, f32[144,256]{1,0:T(8,128)S(1)}, u32[]{:S(2)}, u32[]{:S(2)}) collective-permute-start(f32[144,256]{1,0:T(8,128)S(1)} %get-tuple-element.52), channel_id=1, source_target_pairs={{0,4},{4,0},{8,12},{12,8},{1,5},{5,1},{9,13},{13,9},{2,6},{6,2},{1... | collective-permute-start | bytes 442376 | tf_op jit(solution)/shard_map/ppermute | solution.py:136
  16.7 6.1 %collective-permute-start.4 = (bf16[144,256]{1,0:T(8,128)(2,1)S(1)}, bf16[144,256]{1,0:T(8,128)(2,1)S(1)}, u32[]{:S(2)}, u32[]{:S(2)}) collective-permute-start(bf16[144,256]{1,0:T(8,128)(2,1)S(1)} %get-tuple-element.51), channel_id=1, source_target_pairs={{0,8},{4,12},{8,0},{12,4},{1,9},{5,13},{9,1},{13,5},{2,10},{6,14},... | collective-permute-start | bytes 221192 | tf_op jit(solution)/shard_map/ppermute | solution.py:136
  18.5 5.9 %collective-permute-start.6 = (bf16[144,256]{1,0:T(8,128)(2,1)S(1)}, bf16[144,256]{1,0:T(8,128)(2,1)S(1)}, u32[]{:S(2)}, u32[]{:S(2)}) collective-permute-start(bf16[144,256]{1,0:T(8,128)(2,1)S(1)} %get-tuple-element.64), channel_id=1, source_target_pairs={{0,8},{4,12},{8,0},{12,4},{1,9},{5,13},{9,1},{13,5},{2,10},{6,14},... | collective-permute-start | bytes 221192 | tf_op jit(solution)/shard_map/ppermute | solution.py:136
  19.9 6.3 %collective-permute-start.8 = (bf16[128,256]{1,0:T(8,128)(2,1)S(1)}, bf16[128,256]{1,0:T(8,128)(2,1)S(1)}, u32[]{:S(2)}, u32[]{:S(2)}) collective-permute-start(bf16[128,256]{1,0:T(8,128)(2,1)S(1)} %copy-done.2), channel_id=1, source_target_pairs={{0,16},{16,0},{1,17},{17,1},{2,18},{18,2},{3,19},{19,3},{4,20},{20... | collective-permute-start | bytes 196616 | tf_op jit(solution)/shard_map/ppermute | solution.py:390
  21.4 9.3 %collective-permute-start.9 = (bf16[128,256]{1,0:T(8,128)(2,1)S(1)}, bf16[128,256]{1,0:T(8,128)(2,1)S(1)}, u32[]{:S(2)}, u32[]{:S(2)}) collective-permute-start(bf16[128,256]{1,0:T(8,128)(2,1)S(1)} %copy-done.3), channel_id=1, source_target_pairs={{0,16},{16,0},{1,17},{17,1},{2,18},{18,2},{3,19},{19,3},{4,20},{20... | collective-permute-start | bytes 196616 | tf_op jit(solution)/shard_map/ppermute | solution.py:391
  22.8 1.4 %collective-permute-start = (f32[144,256]{1,0:T(8,128)S(1)}, f32[144,256]{1,0:T(8,128)S(1)}, u32[]{:S(2)}, u32[]{:S(2)}) collective-permute-start(f32[144,256]{1,0:T(8,128)S(1)} %convert_add_fusion.own_ref), channel_id=1, source_target_pairs={{0,4},{4,0},{8,12},{12,8},{1,5},{5,1},{9,13},{13,9},{2,6},{6,2},{1... | collective-permute-start | bytes 442376 | tf_op jit(solution)/shard_map/cond/branch_1_fun/ppermute | solution.py:136
  24.7 3.7 %collective-permute-start.7 = (f32[2,8,128]{2,1,0:T(8,128)S(1)}, f32[2,8,128]{2,1,0:T(8,128)S(1)}, u32[]{:S(2)}, u32[]{:S(2)}) collective-permute-start(f32[2,8,128]{2,1,0:T(8,128)S(1)} %shard_map.98.share_ref), channel_id=1, source_target_pairs={{0,16},{16,0},{1,17},{17,1},{2,18},{18,2},{3,19},{19,3},{4,20},{20... | collective-permute-start | bytes 24584 | tf_op jit(solution)/shard_map/ppermute | solution.py:400
  29.0 3.6 %collective-permute-start.10 = (f32[2,128]{1,0:T(2,128)S(1)}, f32[2,128]{1,0:T(2,128)S(1)}, u32[]{:S(2)}, u32[]{:S(2)}) collective-permute-start(f32[2,128]{1,0:T(2,128)S(1)} %get-tuple-element.57), channel_id=1, source_target_pairs={{0,16},{16,0},{1,17},{17,1},{2,18},{18,2},{3,19},{19,3},{4,20},{20... | collective-permute-start | bytes 3080 | tf_op jit(solution)/shard_map/ppermute | solution.py:408

commit v10 on v9

--- a/solution.py
+++ b/solution.py
@@ -48,9 +48,10 @@
 
 
 def peer_project_kernel(
-    peer_ref, taps_ref, held_ref, near_ref, far_ref, widened, own_widened
+    upper_ref, lower_ref, taps_ref, held_ref, near_ref, far_ref, widened, own_widened
 ):
-    rows, features = peer_ref.shape
+    middle, features = upper_ref.shape
+    rows = middle + lower_ref.shape[0]
     tile = widened.shape[2]
     first = lax.axis_index("seq") == 0
     half = near_ref.shape[1]
@@ -62,9 +63,10 @@
             features + step * 2 * RIM_ROWS : features + (step + 1) * 2 * RIM_ROWS, :tile
         ]
         own_tail = edges[RIM_ROWS:].astype(jnp.float32)
-        peer_tail = peer_ref[rows - RIM_ROWS :, columns].astype(jnp.float32)
+        peer_tail = lower_ref[rows - middle - RIM_ROWS :, columns].astype(jnp.float32)
         wide[:RIM_ROWS] = jnp.where(first, own_tail, 0.0)
-        wide[RIM_ROWS:] = peer_ref[:, columns].astype(jnp.float32)
+        wide[RIM_ROWS : RIM_ROWS + middle] = upper_ref[:, columns].astype(jnp.float32)
+        wide[RIM_ROWS + middle :] = lower_ref[:, columns].astype(jnp.float32)
         own_wide[:RIM_ROWS] = jnp.where(first, 0.0, peer_tail)
         own_wide[RIM_ROWS:] = edges[:RIM_ROWS].astype(jnp.float32)
         taps = taps_ref[:, columns].astype(jnp.float32)
@@ -99,8 +101,8 @@
     )(activations, conv_taps, gate_in)
 
 
-def peer_project(peer_rows, taps, held):
-    rows, features = peer_rows.shape
+def peer_project(upper, lower, taps, held):
+    rows, features = upper.shape[0] + lower.shape[0], upper.shape[1]
     done = rows + RIM_ROWS
     tile = math.gcd(features, held.shape[1])
     half = held.shape[1] // 2
@@ -116,7 +118,7 @@
         ],
         compiler_params=pltpu.CompilerParams(vmem_limit_bytes=VMEM_BYTES),
         cost_estimate=pl.CostEstimate(flops=1, bytes_accessed=1, transcendentals=0),
-    )(peer_rows, taps, held)
+    )(upper, lower, taps, held)
 
 
 def head_sum(part):
@@ -146,57 +148,60 @@
     )
 
 
-def far_logits(block, gate_rows):
+def far_logits(block, gate_out):
     step = lax.axis_size("heads") // 2
     received = exchange_heads(block, step)
 
-    def nearer(block, received, gate_rows):
+    def nearer(block, received, gate_out):
         distance = step
         while distance > 1:
             distance //= 2
             block = block.astype(jnp.float32) + received.astype(jnp.float32)
             received = exchange_heads(block, distance)
-        return partial_logits(block, received, gate_rows)
-
-    return in_one_piece(nearer, block, received, gate_rows)
-
-
-def share_of_logits(pre_ref, in_ref, gate_rows):
+        return partial_logits(block, received, gate_out, block.shape[1])
+
+    return in_one_piece(nearer, block, received, gate_out)
+
+
+def share_of_logits(pre_ref, in_ref, gate_out_ref, offset):
     pre = pre_ref[...] + in_ref[...].astype(jnp.float32)
     hidden = (pre / (1.0 + jnp.exp(-pre))).astype(jnp.bfloat16)
+    share = gate_out_ref.shape[1] // lax.axis_size("seq")
+    start = pl.multiple_of(lax.axis_index("seq") * share + offset, HEAD_DIM)
+    gate_columns = gate_out_ref[:, pl.ds(start, pre.shape[1])]
     return lax.dot_general(
-        gate_rows, hidden, (((0,), (1,)), ((), ())), preferred_element_type=jnp.float32
-    )
-
-
-def partial_logits_kernel(own_ref, in_ref, gate_out_ref, out_ref):
-    out_ref[...] = share_of_logits(own_ref, in_ref, gate_out_ref[...])
-
-
-def partial_logits(part, received, gate_rows):
-    return pl.pallas_call(
-        partial_logits_kernel,
-        out_shape=jax.ShapeDtypeStruct((gate_rows.shape[1], part.shape[0]), jnp.float32),
-        compiler_params=pltpu.CompilerParams(vmem_limit_bytes=VMEM_BYTES),
-    )(part, received, gate_rows)
+        gate_columns, hidden, (((1,), (1,)), ((), ())), preferred_element_type=jnp.float32
+    )
+
+
+def partial_logits_kernel(offset, own_ref, in_ref, gate_out_ref, out_ref):
+    out_ref[...] = share_of_logits(own_ref, in_ref, gate_out_ref, offset)
+
+
+def partial_logits(part, received, gate_out, offset):
+    return pl.pallas_call(
+        functools.partial(partial_logits_kernel, offset),
+        out_shape=jax.ShapeDtypeStruct((gate_out.shape[0], part.shape[0]), jnp.float32),
+        compiler_params=pltpu.CompilerParams(vmem_limit_bytes=VMEM_BYTES),
+    )(part, received, gate_out)
 
 
 def logits_kernel(own_ref, far_share_ref, near_ref, near_in_ref, gate_out_ref, out_ref):
     first = lax.axis_index("seq") == 0
-    share = share_of_logits(near_ref, near_in_ref, gate_out_ref[...]) + far_share_ref[...]
+    share = share_of_logits(near_ref, near_in_ref, gate_out_ref, 0) + far_share_ref[...]
     own = jnp.concatenate([share[:, :RIM_ROWS], own_ref[...]], axis=1)
     peer = share[:, RIM_ROWS:]
     out_ref[0] = jnp.where(first, own, peer)
     out_ref[1] = jnp.where(first, peer, own)
 
 
-def logits_share(own_share, far_share, near, near_in, gate_rows):
+def logits_share(own_share, far_share, near, near_in, gate_out):
     rows = own_share.shape[1] + RIM_ROWS
     return pl.pallas_call(
         logits_kernel,
-        out_shape=jax.ShapeDtypeStruct((2, gate_rows.shape[1], rows), jnp.float32),
-        compiler_params=pltpu.CompilerParams(vmem_limit_bytes=VMEM_BYTES),
-    )(own_share, far_share, near, near_in, gate_rows)
+        out_shape=jax.ShapeDtypeStruct((2, gate_out.shape[0], rows), jnp.float32),
+        compiler_params=pltpu.CompilerParams(vmem_limit_bytes=VMEM_BYTES),
+    )(own_share, far_share, near, near_in, gate_out)
 
 
 def hide_unseen(seq_rank, segments_ref, rows):
@@ -373,26 +378,26 @@
 ):
     rows = activations.shape[0]
     swap = [(0, 1), (1, 0)]
-    seq_rank = lax.axis_index("seq")
     segments = segment_ids.reshape(2, rows)
-    hidden_local = gate_in.shape[1]
-    gate_rows = lax.dynamic_slice_in_dim(gate_out, seq_rank * hidden_local, hidden_local, 0)
-
-    peer_rows = lax.ppermute(activations, "seq", swap)
-
-    def own_work(activations, conv_taps, gate_in, gate_rows):
+    gate_out = jnp.transpose(gate_out)
+
+    middle = rows // 2
+    peer_rows = [
+        lax.ppermute(block, "seq", swap) for block in (activations[:middle], activations[middle:])
+    ]
+
+    def own_work(activations, conv_taps, gate_in, gate_out):
         part, *held = own_project(activations, conv_taps, gate_in)
-        return partial_logits(*head_sum(part), gate_rows), held
-
-    own_share, held = in_one_piece(own_work, activations, conv_taps, gate_in, gate_rows)
+        return partial_logits(*head_sum(part), gate_out, 0), held
+
+    own_share, held = in_one_piece(own_work, activations, conv_taps, gate_in, gate_out)
     peer_rows, own_share, held = lax.optimization_barrier((peer_rows, own_share, held))
-    near, far = peer_project(peer_rows, *held)
+    near, far = peer_project(*peer_rows, *held)
     behind_keys = lax.ppermute(key_vectors, "seq", swap)
     behind_values = lax.ppermute(value_vectors, "seq", swap)
-    half = near.shape[1]
     near, near_in = head_sum(near)
-    far_share = far_logits(far, gate_rows[half:])
-    share = logits_share(own_share, far_share, near, near_in, gate_rows[:half])
+    far_share = far_logits(far, gate_out)
+    share = logits_share(own_share, far_share, near, near_in, gate_out)
     share, queries = lax.optimization_barrier((share, queries))
     powers = powers_of(segments, queries, key_vectors, behind_keys)
     weights, own_mass, behind_mass = weights_of(

time: 33.4 us -> 33.3 us (level)
  waiting for transfers between devices: 8.88 us -> 10.6 us
  local copies, waits for them, and re-layouts: 2.51 us -> 1.1 us
  Pallas kernels: 7.33 us -> 6.43 us
  starting transfers between devices: 13.1 us -> 13.7 us
    ppermute x1 -> x2, waiting for transfers between devices: 0.84 us -> 1.98 us  [pair_device(): lax.ppermute(block, 'seq', swap)]
    pallas_call x3, Pallas kernels: 1.57 us -> 0.65 us  [the longest x2 0.36 us: partial_logits(): pl.pallas_call(functools.partial(partial_logits_kernel, offset), out_shap...]
    unnamed x11 -> x10, local copies, waits for them, and re-layouts: 0.82 us -> 0.02 us
    ppermute x6, waiting for transfers between devices: 5.66 us -> 6.29 us  [exchange_heads(): return lax.ppermute(block, 'heads', [(i, i ^ step) for i in range(count)])]
    slice x2 -> x1, local copies, waits for them, and re-layouts: 1.69 us -> 1.07 us  [pair_device(): activations[middle:]]
    ppermute x6, starting transfers between devices: 4.97 us -> 5.43 us  [exchange_heads(): return lax.ppermute(block, 'heads', [(i, i ^ step) for i in range(count)])]
    ppermute x1 -> x2, starting transfers between devices: 3 us -> 3.08 us  [pair_device(): lax.ppermute(block, 'seq', swap)]
  transfers between devices with their start and end apart: 11 -> 12, of which waited for: 6 -> 6; matrix products, arithmetic and copies ran while one was open for 8% -> 0% of each run, Pallas kernels for 20% -> 17%
where the time goes in v10:
time: 33.3 us; the launch traced here: 33.2 us
  starting transfers between devices  13.7 us (41%)
  waiting for transfers between devices  10.6 us (32%)
  Pallas kernels  6.43 us (19%)
  local copies, waits for them, and re-layouts  1.1 us (3%)
  between operations  0.71 us (2%)
  other arithmetic  0.58 us (2%)
    ppermute x6, waiting for transfers between devices, exchange_heads(): return lax.ppermute(block, 'heads', [(i, i ^ step) for i in range(count)])  6.29 us
    ppermute x6, starting transfers between devices, exchange_heads(): return lax.ppermute(block, 'heads', [(i, i ^ step) for i in range(count)])  5.43 us
    ppermute x2, starting transfers between devices, pair_device(): lax.ppermute(block, 'seq', swap)  3.08 us
    pallas_call x1, Pallas kernels, own_project(): pl.pallas_call(own_project_kernel, out_shape=(jax.ShapeDtypeStruct((done,...  2.55 us
    ppermute x2, waiting for transfers between devices, pair_device(): lax.ppermute(block, 'seq', swap)  1.98 us
    ppermute x1, starting transfers between devices, pair_device(): key_mass = own_mass + lax.ppermute(behind_mass, 'seq', swap)  1.63 us
    ppermute x1, starting transfers between devices, pair_device(): lax.ppermute(share, 'seq', swap)  1.52 us
    ppermute x1, starting transfers between devices, pair_device(): behind_keys = lax.ppermute(key_vectors, 'seq', swap)  1.49 us
  transfers between devices with their start and end apart: 12, of which 6 were waited for; matrix products, arithmetic and copies ran while one was open for 0% of the time, Pallas kernels for 17%

profile of v10, /device:TPU:0, one launch (start us, length us, event | category | flops | bytes accessed | tf_op | source)
XLA Modules:
  0.0 33.2 jit_solution(5313569857154476154)
XLA Ops:
  0.6 1.1 %fusion.2 = (bf16[64,2048]{1,0:T(8,128)(2,1)S(1)}, bf16[64,2048]{1,0:T(8,128)(2,1)S(1)}) fusion(bf16[128,2048]{1,0:T(8,128)(2,1)} %param.12), kind=kLoop, calls=%fused_computation.4 | loop fusion | bytes 1048576 | tf_op jit(solution)/shard_map/slice | solution.py:386
  1.7 3.0 %collective-permute-start.3 = (bf16[64,2048]{1,0:T(8,128)(2,1)S(1)}, bf16[64,2048]{1,0:T(8,128)(2,1)S(1)}, u32[]{:S(2)}, u32[]{:S(2)}) collective-permute-start(bf16[64,2048]{1,0:T(8,128)(2,1)S(1)} %get-tuple-element.68), channel_id=1, source_target_pairs={{0,16},{16,0},{1,17},{17,1},{2,18},{18,2},{3,19},{19,3},{4,20},{20... | collective-permute-start | bytes 786440 | tf_op jit(solution)/shard_map/ppermute | solution.py:386
  4.7 0.1 collective-permute-start.4
  4.8 9.8 %conditional.2 = (f32[8,112]{1,0:T(8,128)S(1)}, f32[4,2048]{1,0:T(4,128)S(1)}, bf16[2176,512]{1,0:T(8,128)(2,1)S(1)}) conditional(s32[]{:T(128)} %convert_element_type.19, () %tuple.24, (bf16[128,2048]{1,0:T(8,128)(2,1)}, bf16[4,2048]{1,0:T(4,128)(2,1)}, bf16[2048,512]{1,0:T(8,128)(2,1)}, bf16[8,1024]{1,0:T(8,128)(2,1)}) %tuple.38), branch_computations={%region_0.0_spmd, %region_1.0_spmd} | conditional | flops 114689 | bytes 2264610 | solution.py:143
  4.8 0.0 copy-start.5
  4.8 2.6 %branch_1_fun.3 = (f32[112,512]{1,0:T(8,128)S(1)}, f32[4,2048]{1,0:T(4,128)S(1)}, bf16[2176,512]{1,0:T(8,128)(2,1)S(1)}) custom-call(bf16[128,2048]{1,0:T(8,128)(2,1)} %get-tuple-element.10.rows_ref, bf16[4,2048]{1,0:T(4,128)(2,1)} %get-tuple-element.61.taps_ref, bf16[2048,512]{1,0:T(8,128)(2,1)} %get-tuple-element.62.gate_ref), custom_call_target="tpu_custom_call" | custom-call | flops 1 | bytes 1 | tf_op jit(solution)/shard_map/cond/branch_1_fun/pallas_call | solution.py:89
  7.3 0.1 collective-permute-start.1
  7.4 1.5 %collective-permute-done.1 = f32[112,512]{1,0:T(8,128)S(1)} collective-permute-done((f32[112,512]{1,0:T(8,128)S(1)}, f32[112,512]{1,0:T(8,128)S(1)}, u32[]{:S(2)}, u32[]{:S(2)}) %collective-permute-start.1) | collective-permute-done | bytes 229408 | tf_op jit(solution)/shard_map/cond/branch_1_fun/ppermute | solution.py:138
  8.9 2.0 %collective-permute-start.2 = (bf16[112,512]{1,0:T(8,128)(2,1)S(1)}, bf16[112,512]{1,0:T(8,128)(2,1)S(1)}, u32[]{:S(2)}, u32[]{:S(2)}) collective-permute-start(bf16[112,512]{1,0:T(8,128)(2,1)S(1)} %get-tuple-element.63), channel_id=1, source_target_pairs={{0,8},{4,12},{8,0},{12,4},{1,9},{5,13},{9,1},{13,5},{2,10},{6,14},... | collective-permute-start | bytes 344072 | tf_op jit(solution)/shard_map/cond/branch_1_fun/ppermute | solution.py:138
  11.0 3.4 %collective-permute-done.2.in_ref = bf16[112,512]{1,0:T(8,128)(2,1)S(1)} collective-permute-done((bf16[112,512]{1,0:T(8,128)(2,1)S(1)}, bf16[112,512]{1,0:T(8,128)(2,1)S(1)}, u32[]{:S(2)}, u32[]{:S(2)}) %collective-permute-start.2) | collective-permute-done | bytes 114720 | tf_op jit(solution)/shard_map/cond/branch_1_fun/ppermute | solution.py:138
  14.4 0.0 copy-done.5
  14.4 0.2 branch_1_fun.4
  14.6 0.0 copy-start.1
  14.6 0.0 copy-start.2
  14.6 0.0 copy-start.4
  14.6 0.0 copy-start
  14.6 0.0 copy-start.3
  14.7 0.0 collective-permute-done.3.upper_ref
  14.7 2.0 %collective-permute-done.4.lower_ref = bf16[64,2048]{1,0:T(8,128)(2,1)S(1)} collective-permute-done((bf16[64,2048]{1,0:T(8,128)(2,1)S(1)}, bf16[64,2048]{1,0:T(8,128)(2,1)S(1)}, u32[]{:S(2)}, u32[]{:S(2)}) %collective-permute-start.4) | collective-permute-done | bytes 262176 | tf_op jit(solution)/shard_map/ppermute | solution.py:386
  16.6 0.8 %shard_map.97 = (f32[144,256]{1,0:T(8,128)S(1)}, bf16[144,256]{1,0:T(8,128)(2,1)S(1)}) custom-call(bf16[64,2048]{1,0:T(8,128)(2,1)S(1)} %collective-permute-done.3.upper_ref, bf16[64,2048]{1,0:T(8,128)(2,1)S(1)} %collective-permute-done.4.lower_ref, f32[4,2048]{1,0:T(4,128)S(1)} %get-tuple-element.50.taps_ref, bf16[2176,512]{1,0:T(8,128)(2,1)S(1)} %get-tuple-element.51.held_ref), custom_call_target="tpu_custom_call" | custom-call | flops 1 | bytes 1 | tf_op jit(solution)/shard_map/pallas_call | solution.py:109
  17.4 0.1 collective-permute-start.6
  17.5 1.8 %collective-permute-start.5 = (bf16[144,256]{1,0:T(8,128)(2,1)S(1)}, bf16[144,256]{1,0:T(8,128)(2,1)S(1)}, u32[]{:S(2)}, u32[]{:S(2)}) collective-permute-start(bf16[144,256]{1,0:T(8,128)(2,1)S(1)} %get-tuple-element.52), channel_id=1, source_target_pairs={{0,8},{4,12},{8,0},{12,4},{1,9},{5,13},{9,1},{13,5},{2,10},{6,14},... | collective-permute-start | bytes 221192 | tf_op jit(solution)/shard_map/ppermute | solution.py:138
  19.3 0.0 collective-permute-done.6
  19.4 1.4 %collective-permute-start.7 = (bf16[144,256]{1,0:T(8,128)(2,1)S(1)}, bf16[144,256]{1,0:T(8,128)(2,1)S(1)}, u32[]{:S(2)}, u32[]{:S(2)}) collective-permute-start(bf16[144,256]{1,0:T(8,128)(2,1)S(1)} %get-tuple-element.65), channel_id=1, source_target_pairs={{0,8},{4,12},{8,0},{12,4},{1,9},{5,13},{9,1},{13,5},{2,10},{6,14},... | collective-permute-start | bytes 221192 | tf_op jit(solution)/shard_map/ppermute | solution.py:138
  20.7 0.0 copy-done.1
  20.7 1.5 %collective-permute-start.9 = (bf16[128,256]{1,0:T(8,128)(2,1)S(1)}, bf16[128,256]{1,0:T(8,128)(2,1)S(1)}, u32[]{:S(2)}, u32[]{:S(2)}) collective-permute-start(bf16[128,256]{1,0:T(8,128)(2,1)S(1)} %copy-done.1), channel_id=1, source_target_pairs={{0,16},{16,0},{1,17},{17,1},{2,18},{18,2},{3,19},{19,3},{4,20},{20... | collective-permute-start | bytes 196616 | tf_op jit(solution)/shard_map/ppermute | solution.py:396
  22.2 0.0 copy-done.2
  22.2 0.5 %collective-permute-start.10 = (bf16[128,256]{1,0:T(8,128)(2,1)S(1)}, bf16[128,256]{1,0:T(8,128)(2,1)S(1)}, u32[]{:S(2)}, u32[]{:S(2)}) collective-permute-start(bf16[128,256]{1,0:T(8,128)(2,1)S(1)} %copy-done.2), channel_id=1, source_target_pairs={{0,16},{16,0},{1,17},{17,1},{2,18},{18,2},{3,19},{19,3},{4,20},{20... | collective-permute-start | bytes 196616 | tf_op jit(solution)/shard_map/ppermute | solution.py:397
  22.8 0.0 collective-permute-done.5
  22.8 0.0 copy-done.4
  22.8 1.6 %conditional.3 = (f32[8,144]{1,0:T(8,128)S(1)}) conditional(s32[]{:T(128)} %convert_element_type.19, () %tuple.27, (bf16[144,256]{1,0:T(8,128)(2,1)S(1)}, bf16[144,256]{1,0:T(8,128)(2,1)S(1)}, bf16[8,1024]{1,0:T(8,128)(2,1)S(1)}) %tuple.39), branch_computations={%region_2.0_spmd, %region_3.0_spmd} | conditional | flops 110592 | bytes 884784 | solution.py:143
  22.8 0.1 collective-permute-start
  22.9 1.4 %collective-permute-done.in_ref = f32[144,256]{1,0:T(8,128)S(1)} collective-permute-done((f32[144,256]{1,0:T(8,128)S(1)}, f32[144,256]{1,0:T(8,128)S(1)}, u32[]{:S(2)}, u32[]{:S(2)}) %collective-permute-start) | collective-permute-done | bytes 147488 | tf_op jit(solution)/shard_map/cond/branch_1_fun/ppermute | solution.py:138
  24.2 0.2 branch_1_fun.5
  24.4 0.0 collective-permute-done.7.near_in_ref
  24.4 0.3 shard_map.98.share_ref
  24.7 1.5 %collective-permute-start.8 = (f32[2,8,128]{2,1,0:T(8,128)S(1)}, f32[2,8,128]{2,1,0:T(8,128)S(1)}, u32[]{:S(2)}, u32[]{:S(2)}) collective-permute-start(f32[2,8,128]{2,1,0:T(8,128)S(1)} %shard_map.98.share_ref), channel_id=1, source_target_pairs={{0,16},{16,0},{1,17},{17,1},{2,18},{18,2},{3,19},{19,3},{4,20},{20... | collective-permute-start | bytes 24584 | tf_op jit(solution)/shard_map/ppermute | solution.py:405
  26.2 0.0 collective-permute-done.9.behind_keys_ref
  26.2 0.0 copy-done
  26.2 0.0 copy-done.3
  26.2 0.7 %shard_map.99.powers_ref = f32[16,128,256]{2,1,0:T(8,128)S(1)} custom-call(s32[2,128]{1,0:T(2,128)S(1)} %bitcast.2, bf16[128,2048]{1,0:T(8,128)(2,1)S(1)} %copy-done, bf16[128,256]{1,0:T(8,128)(2,1)S(1)} %copy-done.1, bf16[128,256]{1,0:T(8,128)(2,1)S(1)} %collective-permute-done.9.behind_keys_ref), custom_call_target="tpu_custom_call" | custom-call | flops 134217728 | bytes 2097152 | tf_op jit(solution)/shard_map/pallas_call | solution.py:263
  26.9 1.4 %collective-permute-done.8.peer_share_ref = f32[2,8,128]{2,1,0:T(8,128)S(1)} collective-permute-done((f32[2,8,128]{2,1,0:T(8,128)S(1)}, f32[2,8,128]{2,1,0:T(8,128)S(1)}, u32[]{:S(2)}, u32[]{:S(2)}) %collective-permute-start.8) | collective-permute-done | bytes 8224 | tf_op jit(solution)/shard_map/ppermute | solution.py:405
  28.4 0.6 %shard_map.100 = (bf16[16,128,256]{2,1,0:T(8,128)(2,1)S(1)}, f32[2,128]{1,0:T(2,128)S(1)}, f32[2,128]{1,0:T(2,128)S(1)}) custom-call(f32[2,8,128]{2,1,0:T(8,128)S(1)} %shard_map.98.share_ref, f32[2,8,128]{2,1,0:T(8,128)S(1)} %collective-permute-done.8.peer_share_ref, f32[16,128,256]{2,1,0:T(8,128)S(1)} %shard_map.99.powers_ref, s32[2,128]{1,0:T(2,128)S(1)} %bitcast.3, ...), custom_call_target="tpu_custom_call" | custom-call | tf_op jit(solution)/shard_map/pallas_call | solution.py:337
  29.0 1.6 %collective-permute-start.11 = (f32[2,128]{1,0:T(2,128)S(1)}, f32[2,128]{1,0:T(2,128)S(1)}, u32[]{:S(2)}, u32[]{:S(2)}) collective-permute-start(f32[2,128]{1,0:T(2,128)S(1)} %get-tuple-element.58), channel_id=1, source_target_pairs={{0,16},{16,0},{1,17},{17,1},{2,18},{18,2},{3,19},{19,3},{4,20},{20... | collective-permute-start | bytes 3080 | tf_op jit(solution)/shard_map/ppermute | solution.py:413
  30.6 0.0 collective-permute-done.10.behind_values_ref
  30.6 1.1 %shard_map.101 = bf16[128,2048]{1,0:T(8,128)(2,1)} custom-call(bf16[16,128,256]{2,1,0:T(8,128)(2,1)S(1)} %get-tuple-element.56.weights_ref, bf16[128,256]{1,0:T(8,128)(2,1)S(1)} %copy-done.2, bf16[128,256]{1,0:T(8,128)(2,1)S(1)} %collective-permute-done.10.behind_values_ref), custom_call_target="tpu_custom_call" | custom-call | flops 134217728 | bytes 1572864 | tf_op jit(solution)/shard_map/pallas_call | solution.py:364
  31.7 0.9 %collective-permute-done.11 = f32[2,128]{1,0:T(2,128)S(1)} collective-permute-done((f32[2,128]{1,0:T(2,128)S(1)}, f32[2,128]{1,0:T(2,128)S(1)}, u32[]{:S(2)}, u32[]{:S(2)}) %collective-permute-start.11) | collective-permute-done | bytes 1056 | tf_op jit(solution)/shard_map/ppermute | solution.py:413
  32.7 0.5 %add_convert_fusion = bf16[2,128]{1,0:T(2,128)(2,1)} fusion(f32[2,128]{1,0:T(2,128)S(1)} %get-tuple-element.57, f32[2,128]{1,0:T(2,128)S(1)} %collective-permute-done.11), kind=kLoop, calls=%fused_computation.1 | loop fusion | flops 512 | bytes 2560 | tf_op jit(solution)/shard_map/convert_element_type | solution.py:414
  (3 shorter events, 0.1 us)
Async XLA Ops:
  1.7 12.9 %collective-permute-start.3 = (bf16[64,2048]{1,0:T(8,128)(2,1)S(1)}, bf16[64,2048]{1,0:T(8,128)(2,1)S(1)}, u32[]{:S(2)}, u32[]{:S(2)}) collective-permute-start(bf16[64,2048]{1,0:T(8,128)(2,1)S(1)} %get-tuple-element.68), channel_id=1, source_target_pairs={{0,16},{16,0},{1,17},{17,1},{2,18},{18,2},{3,19},{19,3},{4,20},{20... | collective-permute-start | bytes 786440 | tf_op jit(solution)/shard_map/ppermute | solution.py:386
  4.7 11.9 %collective-permute-start.4 = (bf16[64,2048]{1,0:T(8,128)(2,1)S(1)}, bf16[64,2048]{1,0:T(8,128)(2,1)S(1)}, u32[]{:S(2)}, u32[]{:S(2)}) collective-permute-start(bf16[64,2048]{1,0:T(8,128)(2,1)S(1)} %get-tuple-element.67), channel_id=1, source_target_pairs={{0,16},{16,0},{1,17},{17,1},{2,18},{18,2},{3,19},{19,3},{4,20},{20... | collective-permute-start | bytes 786440 | tf_op jit(solution)/shard_map/ppermute | solution.py:386
  4.8 9.6 %copy-start.5 = (bf16[8,1024]{1,0:T(8,128)(2,1)S(1)}, bf16[8,1024]{1,0:T(8,128)(2,1)}, u32[]{:S(2)}) copy-start(bf16[8,1024]{1,0:T(8,128)(2,1)} %get-tuple-element.21.gate_out_ref) | copy-start | bytes 49156 | tf_op jit(solution)/shard_map/cond
  7.3 1.5 %collective-permute-start.1 = (f32[112,512]{1,0:T(8,128)S(1)}, f32[112,512]{1,0:T(8,128)S(1)}, u32[]{:S(2)}, u32[]{:S(2)}) collective-permute-start(f32[112,512]{1,0:T(8,128)S(1)} %get-tuple-element.20), channel_id=1, source_target_pairs={{0,4},{4,0},{8,12},{12,8},{1,5},{5,1},{9,13},{13,9},{2,6},{6,2},{1... | collective-permute-start | bytes 688136 | tf_op jit(solution)/shard_map/cond/branch_1_fun/ppermute | solution.py:138
  8.9 5.5 %collective-permute-start.2 = (bf16[112,512]{1,0:T(8,128)(2,1)S(1)}, bf16[112,512]{1,0:T(8,128)(2,1)S(1)}, u32[]{:S(2)}, u32[]{:S(2)}) collective-permute-start(bf16[112,512]{1,0:T(8,128)(2,1)S(1)} %get-tuple-element.63), channel_id=1, source_target_pairs={{0,8},{4,12},{8,0},{12,4},{1,9},{5,13},{9,1},{13,5},{2,10},{6,14},... | collective-permute-start | bytes 344072 | tf_op jit(solution)/shard_map/cond/branch_1_fun/ppermute | solution.py:138
  14.6 6.1 %copy-start.1 = (bf16[128,256]{1,0:T(8,128)(2,1)S(1)}, bf16[128,256]{1,0:T(8,128)(2,1)}, u32[]{:S(2)}) copy-start(bf16[128,256]{1,0:T(8,128)(2,1)} %keys_ref.3) | copy-start | bytes 196612
  14.6 7.6 %copy-start.2 = (bf16[128,256]{1,0:T(8,128)(2,1)S(1)}, bf16[128,256]{1,0:T(8,128)(2,1)}, u32[]{:S(2)}) copy-start(bf16[128,256]{1,0:T(8,128)(2,1)} %values_ref.1) | copy-start | bytes 196612
  14.6 8.1 %copy-start.4 = (bf16[1024,8]{0,1:T(8,128)(2,1)S(1)}, bf16[1024,8]{0,1:T(8,128)(2,1)}, u32[]{:S(2)}) copy-start(bf16[1024,8]{0,1:T(8,128)(2,1)} %param.15) | copy-start | bytes 49156
  14.6 11.6 %copy-start = (bf16[128,2048]{1,0:T(8,128)(2,1)S(1)}, bf16[128,2048]{1,0:T(8,128)(2,1)}, u32[]{:S(2)}) copy-start(bf16[128,2048]{1,0:T(8,128)(2,1)} %queries_ref.1) | copy-start | bytes 1572868
  14.6 11.6 %copy-start.3 = (s32[256]{0:T(256)S(1)}, s32[256]{0:T(256)}, u32[]{:S(2)}) copy-start(s32[256]{0:T(256)} %param.19) | copy-start | bytes 3076
  17.4 1.9 %collective-permute-start.6 = (f32[144,256]{1,0:T(8,128)S(1)}, f32[144,256]{1,0:T(8,128)S(1)}, u32[]{:S(2)}, u32[]{:S(2)}) collective-permute-start(f32[144,256]{1,0:T(8,128)S(1)} %get-tuple-element.53), channel_id=1, source_target_pairs={{0,4},{4,0},{8,12},{12,8},{1,5},{5,1},{9,13},{13,9},{2,6},{6,2},{1... | collective-permute-start | bytes 442376 | tf_op jit(solution)/shard_map/ppermute | solution.py:138
  17.5 5.2 %collective-permute-start.5 = (bf16[144,256]{1,0:T(8,128)(2,1)S(1)}, bf16[144,256]{1,0:T(8,128)(2,1)S(1)}, u32[]{:S(2)}, u32[]{:S(2)}) collective-permute-start(bf16[144,256]{1,0:T(8,128)(2,1)S(1)} %get-tuple-element.52), channel_id=1, source_target_pairs={{0,8},{4,12},{8,0},{12,4},{1,9},{5,13},{9,1},{13,5},{2,10},{6,14},... | collective-permute-start | bytes 221192 | tf_op jit(solution)/shard_map/ppermute | solution.py:138
  19.4 5.0 %collective-permute-start.7 = (bf16[144,256]{1,0:T(8,128)(2,1)S(1)}, bf16[144,256]{1,0:T(8,128)(2,1)S(1)}, u32[]{:S(2)}, u32[]{:S(2)}) collective-permute-start(bf16[144,256]{1,0:T(8,128)(2,1)S(1)} %get-tuple-element.65), channel_id=1, source_target_pairs={{0,8},{4,12},{8,0},{12,4},{1,9},{5,13},{9,1},{13,5},{2,10},{6,14},... | collective-permute-start | bytes 221192 | tf_op jit(solution)/shard_map/ppermute | solution.py:138
  20.7 5.5 %collective-permute-start.9 = (bf16[128,256]{1,0:T(8,128)(2,1)S(1)}, bf16[128,256]{1,0:T(8,128)(2,1)S(1)}, u32[]{:S(2)}, u32[]{:S(2)}) collective-permute-start(bf16[128,256]{1,0:T(8,128)(2,1)S(1)} %copy-done.1), channel_id=1, source_target_pairs={{0,16},{16,0},{1,17},{17,1},{2,18},{18,2},{3,19},{19,3},{4,20},{20... | collective-permute-start | bytes 196616 | tf_op jit(solution)/shard_map/ppermute | solution.py:396
  22.2 8.4 %collective-permute-start.10 = (bf16[128,256]{1,0:T(8,128)(2,1)S(1)}, bf16[128,256]{1,0:T(8,128)(2,1)S(1)}, u32[]{:S(2)}, u32[]{:S(2)}) collective-permute-start(bf16[128,256]{1,0:T(8,128)(2,1)S(1)} %copy-done.2), channel_id=1, source_target_pairs={{0,16},{16,0},{1,17},{17,1},{2,18},{18,2},{3,19},{19,3},{4,20},{20... | collective-permute-start | bytes 196616 | tf_op jit(solution)/shard_map/ppermute | solution.py:397
  22.8 1.4 %collective-permute-start = (f32[144,256]{1,0:T(8,128)S(1)}, f32[144,256]{1,0:T(8,128)S(1)}, u32[]{:S(2)}, u32[]{:S(2)}) collective-permute-start(f32[144,256]{1,0:T(8,128)S(1)} %convert_add_fusion.own_ref), channel_id=1, source_target_pairs={{0,4},{4,0},{8,12},{12,8},{1,5},{5,1},{9,13},{13,9},{2,6},{6,2},{1... | collective-permute-start | bytes 442376 | tf_op jit(solution)/shard_map/cond/branch_1_fun/ppermute | solution.py:138
  24.7 3.7 %collective-permute-start.8 = (f32[2,8,128]{2,1,0:T(8,128)S(1)}, f32[2,8,128]{2,1,0:T(8,128)S(1)}, u32[]{:S(2)}, u32[]{:S(2)}) collective-permute-start(f32[2,8,128]{2,1,0:T(8,128)S(1)} %shard_map.98.share_ref), channel_id=1, source_target_pairs={{0,16},{16,0},{1,17},{17,1},{2,18},{18,2},{3,19},{19,3},{4,20},{20... | collective-permute-start | bytes 24584 | tf_op jit(solution)/shard_map/ppermute | solution.py:405
  29.0 3.6 %collective-permute-start.11 = (f32[2,128]{1,0:T(2,128)S(1)}, f32[2,128]{1,0:T(2,128)S(1)}, u32[]{:S(2)}, u32[]{:S(2)}) collective-permute-start(f32[2,128]{1,0:T(2,128)S(1)} %get-tuple-element.58), channel_id=1, source_target_pairs={{0,16},{16,0},{1,17},{17,1},{2,18},{18,2},{3,19},{19,3},{4,20},{20... | collective-permute-start | bytes 3080 | tf_op jit(solution)/shard_map/ppermute | solution.py:413

commit v11 on v10

--- a/solution.py
+++ b/solution.py
@@ -48,10 +48,9 @@
 
 
 def peer_project_kernel(
-    upper_ref, lower_ref, taps_ref, held_ref, near_ref, far_ref, widened, own_widened
+    peer_ref, taps_ref, held_ref, near_ref, far_ref, widened, own_widened
 ):
-    middle, features = upper_ref.shape
-    rows = middle + lower_ref.shape[0]
+    rows, features = peer_ref.shape
     tile = widened.shape[2]
     first = lax.axis_index("seq") == 0
     half = near_ref.shape[1]
@@ -63,10 +62,9 @@
             features + step * 2 * RIM_ROWS : features + (step + 1) * 2 * RIM_ROWS, :tile
         ]
         own_tail = edges[RIM_ROWS:].astype(jnp.float32)
-        peer_tail = lower_ref[rows - middle - RIM_ROWS :, columns].astype(jnp.float32)
+        peer_tail = peer_ref[rows - RIM_ROWS :, columns].astype(jnp.float32)
         wide[:RIM_ROWS] = jnp.where(first, own_tail, 0.0)
-        wide[RIM_ROWS : RIM_ROWS + middle] = upper_ref[:, columns].astype(jnp.float32)
-        wide[RIM_ROWS + middle :] = lower_ref[:, columns].astype(jnp.float32)
+        wide[RIM_ROWS:] = peer_ref[:, columns].astype(jnp.float32)
         own_wide[:RIM_ROWS] = jnp.where(first, 0.0, peer_tail)
         own_wide[RIM_ROWS:] = edges[:RIM_ROWS].astype(jnp.float32)
         taps = taps_ref[:, columns].astype(jnp.float32)
@@ -101,8 +99,8 @@
     )(activations, conv_taps, gate_in)
 
 
-def peer_project(upper, lower, taps, held):
-    rows, features = upper.shape[0] + lower.shape[0], upper.shape[1]
+def peer_project(peer_rows, taps, held):
+    rows, features = peer_rows.shape
     done = rows + RIM_ROWS
     tile = math.gcd(features, held.shape[1])
     half = held.shape[1] // 2
@@ -118,7 +116,7 @@
         ],
         compiler_params=pltpu.CompilerParams(vmem_limit_bytes=VMEM_BYTES),
         cost_estimate=pl.CostEstimate(flops=1, bytes_accessed=1, transcendentals=0),
-    )(upper, lower, taps, held)
+    )(peer_rows, taps, held)
 
 
 def head_sum(part):
@@ -381,19 +379,18 @@
     segments = segment_ids.reshape(2, rows)
     gate_out = jnp.transpose(gate_out)
 
-    middle = rows // 2
-    peer_rows = [
-        lax.ppermute(block, "seq", swap) for block in (activations[:middle], activations[middle:])
-    ]
+    peer_rows = lax.ppermute(activations, "seq", swap)
 
     def own_work(activations, conv_taps, gate_in, gate_out):
         part, *held = own_project(activations, conv_taps, gate_in)
         return partial_logits(*head_sum(part), gate_out, 0), held
 
     own_share, held = in_one_piece(own_work, activations, conv_taps, gate_in, gate_out)
+    own_share, held, key_vectors = lax.optimization_barrier((own_share, held, key_vectors))
+    behind_keys = lax.ppermute(key_vectors, "seq", swap)
     peer_rows, own_share, held = lax.optimization_barrier((peer_rows, own_share, held))
-    near, far = peer_project(*peer_rows, *held)
-    behind_keys = lax.ppermute(key_vectors, "seq", swap)
+    near, far = peer_project(peer_rows, *held)
+    near, far, behind_keys = lax.optimization_barrier((near, far, behind_keys))
     behind_values = lax.ppermute(value_vectors, "seq", swap)
     near, near_in = head_sum(near)
     far_share = far_logits(far, gate_out)

time: 33.3 us -> 33.1 us (level)
  waiting for transfers between devices: 10.6 us -> 12.6 us
  starting transfers between devices: 13.7 us -> 12.6 us
  local copies, waits for them, and re-layouts: 1.1 us -> 0.03 us
    ppermute x1, starting transfers between devices: 1.49 us -> 0.38 us  [pair_device(): behind_keys = lax.ppermute(key_vectors, 'seq', swap)]
    slice x1 -> x0, local copies, waits for them, and re-layouts: 1.07 us -> none  [pair_device(): activations[middle:]]
    ppermute x1, starting transfers between devices: 0.53 us -> 1.46 us  [pair_device(): behind_values = lax.ppermute(value_vectors, 'seq', swap)]
    ppermute x6, starting transfers between devices: 5.43 us -> 4.67 us  [exchange_heads(): return lax.ppermute(block, 'heads', [(i, i ^ step) for i in range(count)])]
    ppermute x6, waiting for transfers between devices: 6.29 us -> 7.01 us  [exchange_heads(): return lax.ppermute(block, 'heads', [(i, i ^ step) for i in range(count)])]
    ppermute x1, waiting for transfers between devices: 0.01 us -> 0.61 us  [pair_device(): behind_keys = lax.ppermute(key_vectors, 'seq', swap)]
    ppermute x2 -> x1, waiting for transfers between devices: 1.98 us -> 2.55 us  [pair_device(): peer_rows = lax.ppermute(activations, 'seq', swap)]
    ppermute x2 -> x1, starting transfers between devices: 3.08 us -> 3 us  [pair_device(): peer_rows = lax.ppermute(activations, 'seq', swap)]
  transfers between devices with their start and end apart: 12 -> 11, of which waited for: 6 -> 8; matrix products, arithmetic and copies ran while one was open for 0% -> 0% of each run, Pallas kernels for 17% -> 20%
where the time goes in v11:
time: 33.1 us; the launch traced here: 33 us
  starting transfers between devices  12.6 us (38%)
  waiting for transfers between devices  12.6 us (38%)
  Pallas kernels  6.45 us (19%)
  between operations  0.69 us (2%)
  other arithmetic  0.59 us (2%)
    ppermute x6, waiting for transfers between devices, exchange_heads(): return lax.ppermute(block, 'heads', [(i, i ^ step) for i in range(count)])  7.01 us
    ppermute x6, starting transfers between devices, exchange_heads(): return lax.ppermute(block, 'heads', [(i, i ^ step) for i in range(count)])  4.67 us
    ppermute x1, starting transfers between devices, pair_device(): peer_rows = lax.ppermute(activations, 'seq', swap)  3 us
    pallas_call x1, Pallas kernels, own_project(): pl.pallas_call(own_project_kernel, out_shape=(jax.ShapeDtypeStruct((done,...  2.58 us
    ppermute x1, waiting for transfers between devices, pair_device(): peer_rows = lax.ppermute(activations, 'seq', swap)  2.55 us
    ppermute x1, starting transfers between devices, pair_device(): key_mass = own_mass + lax.ppermute(behind_mass, 'seq', swap)  1.6 us
    ppermute x1, starting transfers between devices, pair_device(): lax.ppermute(share, 'seq', swap)  1.51 us
    ppermute x1, starting transfers between devices, pair_device(): behind_values = lax.ppermute(value_vectors, 'seq', swap)  1.46 us
  transfers between devices with their start and end apart: 11, of which 8 were waited for; matrix products, arithmetic and copies ran while one was open for 0% of the time, Pallas kernels for 20%

profile of v11, /device:TPU:0, one launch (start us, length us, event | category | flops | bytes accessed | tf_op | source)
XLA Modules:
  0.0 33.0 jit_solution(914685320338751299)
XLA Ops:
  0.6 3.0 %collective-permute-start.3 = (bf16[128,2048]{1,0:T(8,128)(2,1)}, bf16[128,2048]{1,0:T(8,128)(2,1)S(1)}, u32[]{:S(2)}, u32[]{:S(2)}) collective-permute-start(bf16[128,2048]{1,0:T(8,128)(2,1)} %param.12), channel_id=1, source_target_pairs={{0,16},{16,0},{1,17},{17,1},{2,18},{18,2},{3,19},{19,3},{4,20},{20... | collective-permute-start | bytes 1572872 | tf_op jit(solution)/shard_map/ppermute | solution.py:382
  3.6 0.0 copy-start.1
  3.6 9.6 %conditional.2 = (f32[8,112]{1,0:T(8,128)S(1)}, f32[4,2048]{1,0:T(4,128)S(1)}, bf16[2176,512]{1,0:T(8,128)(2,1)S(1)}) conditional(s32[]{:T(128)} %convert_element_type.19, () %tuple.26, (bf16[128,2048]{1,0:T(8,128)(2,1)}, bf16[4,2048]{1,0:T(4,128)(2,1)}, bf16[2048,512]{1,0:T(8,128)(2,1)}, bf16[8,1024]{1,0:T(8,128)(2,1)}) %tuple.41), branch_computations={%region_0.0_spmd, %region_1.0_spmd} | conditional | flops 114689 | bytes 2264610 | solution.py:141
  3.6 0.0 copy-start.5
  3.6 2.6 %branch_1_fun.3 = (f32[112,512]{1,0:T(8,128)S(1)}, f32[4,2048]{1,0:T(4,128)S(1)}, bf16[2176,512]{1,0:T(8,128)(2,1)S(1)}) custom-call(bf16[128,2048]{1,0:T(8,128)(2,1)} %get-tuple-element.10.rows_ref, bf16[4,2048]{1,0:T(4,128)(2,1)} %get-tuple-element.73.taps_ref, bf16[2048,512]{1,0:T(8,128)(2,1)} %get-tuple-element.74.gate_ref), custom_call_target="tpu_custom_call" | custom-call | flops 1 | bytes 1 | tf_op jit(solution)/shard_map/cond/branch_1_fun/pallas_call | solution.py:87
  6.2 0.1 collective-permute-start.1
  6.3 1.5 %collective-permute-done.1 = f32[112,512]{1,0:T(8,128)S(1)} collective-permute-done((f32[112,512]{1,0:T(8,128)S(1)}, f32[112,512]{1,0:T(8,128)S(1)}, u32[]{:S(2)}, u32[]{:S(2)}) %collective-permute-start.1) | collective-permute-done | bytes 229408 | tf_op jit(solution)/shard_map/cond/branch_1_fun/ppermute | solution.py:136
  7.8 1.6 %collective-permute-start.2 = (bf16[112,512]{1,0:T(8,128)(2,1)S(1)}, bf16[112,512]{1,0:T(8,128)(2,1)S(1)}, u32[]{:S(2)}, u32[]{:S(2)}) collective-permute-start(bf16[112,512]{1,0:T(8,128)(2,1)S(1)} %get-tuple-element.75), channel_id=1, source_target_pairs={{0,8},{4,12},{8,0},{12,4},{1,9},{5,13},{9,1},{13,5},{2,10},{6,14},... | collective-permute-start | bytes 344072 | tf_op jit(solution)/shard_map/cond/branch_1_fun/ppermute | solution.py:136
  9.4 3.7 %collective-permute-done.2.in_ref = bf16[112,512]{1,0:T(8,128)(2,1)S(1)} collective-permute-done((bf16[112,512]{1,0:T(8,128)(2,1)S(1)}, bf16[112,512]{1,0:T(8,128)(2,1)S(1)}, u32[]{:S(2)}, u32[]{:S(2)}) %collective-permute-start.2) | collective-permute-done | bytes 114720 | tf_op jit(solution)/shard_map/cond/branch_1_fun/ppermute | solution.py:136
  13.1 0.0 copy-done.5
  13.1 0.2 branch_1_fun.4
  13.2 0.0 copy-start.2
  13.2 0.0 copy-start.4
  13.3 0.0 copy-start
  13.3 0.0 copy-start.3
  13.3 0.0 copy-done.1
  13.3 0.4 %collective-permute-start.4 = (bf16[128,256]{1,0:T(8,128)(2,1)S(1)}, bf16[128,256]{1,0:T(8,128)(2,1)S(1)}, u32[]{:S(2)}, u32[]{:S(2)}) collective-permute-start(bf16[128,256]{1,0:T(8,128)(2,1)S(1)} %copy-done.1), channel_id=1, source_target_pairs={{0,16},{16,0},{1,17},{17,1},{2,18},{18,2},{3,19},{19,3},{4,20},{20... | collective-permute-start | bytes 196616 | tf_op jit(solution)/shard_map/ppermute | solution.py:390
  13.7 2.5 %collective-permute-done.3.peer_ref = bf16[128,2048]{1,0:T(8,128)(2,1)S(1)} collective-permute-done((bf16[128,2048]{1,0:T(8,128)(2,1)}, bf16[128,2048]{1,0:T(8,128)(2,1)S(1)}, u32[]{:S(2)}, u32[]{:S(2)}) %collective-permute-start.3) | collective-permute-done | bytes 524320 | tf_op jit(solution)/shard_map/ppermute | solution.py:382
  16.2 0.8 %shard_map.97 = (f32[144,256]{1,0:T(8,128)S(1)}, bf16[144,256]{1,0:T(8,128)(2,1)S(1)}) custom-call(bf16[128,2048]{1,0:T(8,128)(2,1)S(1)} %collective-permute-done.3.peer_ref, f32[4,2048]{1,0:T(4,128)S(1)} %get-tuple-element.58.taps_ref, bf16[2176,512]{1,0:T(8,128)(2,1)S(1)} %get-tuple-element.59.held_ref), custom_call_target="tpu_custom_call" | custom-call | flops 1 | bytes 1 | tf_op jit(solution)/shard_map/pallas_call | solution.py:107
  17.0 0.6 %collective-permute-done.4.behind_keys_ref = bf16[128,256]{1,0:T(8,128)(2,1)S(1)} collective-permute-done((bf16[128,256]{1,0:T(8,128)(2,1)S(1)}, bf16[128,256]{1,0:T(8,128)(2,1)S(1)}, u32[]{:S(2)}, u32[]{:S(2)}) %collective-permute-start.4) | collective-permute-done | bytes 65568 | tf_op jit(solution)/shard_map/ppermute | solution.py:390
  17.6 0.0 collective-permute-start.6
  17.6 1.6 %collective-permute-start.5 = (bf16[144,256]{1,0:T(8,128)(2,1)S(1)}, bf16[144,256]{1,0:T(8,128)(2,1)S(1)}, u32[]{:S(2)}, u32[]{:S(2)}) collective-permute-start(bf16[144,256]{1,0:T(8,128)(2,1)S(1)} %get-tuple-element.63), channel_id=1, source_target_pairs={{0,8},{4,12},{8,0},{12,4},{1,9},{5,13},{9,1},{13,5},{2,10},{6,14},... | collective-permute-start | bytes 221192 | tf_op jit(solution)/shard_map/ppermute | solution.py:136
  19.2 0.0 collective-permute-done.6
  19.2 1.4 %collective-permute-start.7 = (bf16[144,256]{1,0:T(8,128)(2,1)S(1)}, bf16[144,256]{1,0:T(8,128)(2,1)S(1)}, u32[]{:S(2)}, u32[]{:S(2)}) collective-permute-start(bf16[144,256]{1,0:T(8,128)(2,1)S(1)} %get-tuple-element.77), channel_id=1, source_target_pairs={{0,8},{4,12},{8,0},{12,4},{1,9},{5,13},{9,1},{13,5},{2,10},{6,14},... | collective-permute-start | bytes 221192 | tf_op jit(solution)/shard_map/ppermute | solution.py:136
  20.6 0.0 copy-done.2
  20.6 1.5 %collective-permute-start.9 = (bf16[128,256]{1,0:T(8,128)(2,1)S(1)}, bf16[128,256]{1,0:T(8,128)(2,1)S(1)}, u32[]{:S(2)}, u32[]{:S(2)}) collective-permute-start(bf16[128,256]{1,0:T(8,128)(2,1)S(1)} %copy-done.2), channel_id=1, source_target_pairs={{0,16},{16,0},{1,17},{17,1},{2,18},{18,2},{3,19},{19,3},{4,20},{20... | collective-permute-start | bytes 196616 | tf_op jit(solution)/shard_map/ppermute | solution.py:394
  22.1 0.5 %collective-permute-done.5 = bf16[144,256]{1,0:T(8,128)(2,1)S(1)} collective-permute-done((bf16[144,256]{1,0:T(8,128)(2,1)S(1)}, bf16[144,256]{1,0:T(8,128)(2,1)S(1)}, u32[]{:S(2)}, u32[]{:S(2)}) %collective-permute-start.5) | collective-permute-done | bytes 73760 | tf_op jit(solution)/shard_map/ppermute | solution.py:136
  22.6 0.0 copy-done.4
  22.6 1.6 %conditional.3 = (f32[8,144]{1,0:T(8,128)S(1)}) conditional(s32[]{:T(128)} %convert_element_type.19, () %tuple.30, (bf16[144,256]{1,0:T(8,128)(2,1)S(1)}, bf16[144,256]{1,0:T(8,128)(2,1)S(1)}, bf16[8,1024]{1,0:T(8,128)(2,1)S(1)}) %tuple.42), branch_computations={%region_2.0_spmd, %region_3.0_spmd} | conditional | flops 110592 | bytes 884784 | solution.py:141
  22.6 0.1 collective-permute-start
  22.7 1.4 %collective-permute-done.in_ref = f32[144,256]{1,0:T(8,128)S(1)} collective-permute-done((f32[144,256]{1,0:T(8,128)S(1)}, f32[144,256]{1,0:T(8,128)S(1)}, u32[]{:S(2)}, u32[]{:S(2)}) %collective-permute-start) | collective-permute-done | bytes 147488 | tf_op jit(solution)/shard_map/cond/branch_1_fun/ppermute | solution.py:136
  24.0 0.2 branch_1_fun.5
  24.2 0.0 collective-permute-done.7.near_in_ref
  24.2 0.3 shard_map.98.share_ref
  24.5 1.5 %collective-permute-start.8 = (f32[2,8,128]{2,1,0:T(8,128)S(1)}, f32[2,8,128]{2,1,0:T(8,128)S(1)}, u32[]{:S(2)}, u32[]{:S(2)}) collective-permute-start(f32[2,8,128]{2,1,0:T(8,128)S(1)} %shard_map.98.share_ref), channel_id=1, source_target_pairs={{0,16},{16,0},{1,17},{17,1},{2,18},{18,2},{3,19},{19,3},{4,20},{20... | collective-permute-start | bytes 24584 | tf_op jit(solution)/shard_map/ppermute | solution.py:402
  26.0 0.0 copy-done
  26.0 0.0 copy-done.3
  26.0 0.7 %shard_map.99.powers_ref = f32[16,128,256]{2,1,0:T(8,128)S(1)} custom-call(s32[2,128]{1,0:T(2,128)S(1)} %bitcast.2, bf16[128,2048]{1,0:T(8,128)(2,1)S(1)} %copy-done, bf16[128,256]{1,0:T(8,128)(2,1)S(1)} %copy-done.1, bf16[128,256]{1,0:T(8,128)(2,1)S(1)} %collective-permute-done.4.behind_keys_ref), custom_call_target="tpu_custom_call" | custom-call | flops 134217728 | bytes 2097152 | tf_op jit(solution)/shard_map/pallas_call | solution.py:261
  26.7 1.5 %collective-permute-done.8.peer_share_ref = f32[2,8,128]{2,1,0:T(8,128)S(1)} collective-permute-done((f32[2,8,128]{2,1,0:T(8,128)S(1)}, f32[2,8,128]{2,1,0:T(8,128)S(1)}, u32[]{:S(2)}, u32[]{:S(2)}) %collective-permute-start.8) | collective-permute-done | bytes 8224 | tf_op jit(solution)/shard_map/ppermute | solution.py:402
  28.2 0.6 %shard_map.100 = (bf16[16,128,256]{2,1,0:T(8,128)(2,1)S(1)}, f32[2,128]{1,0:T(2,128)S(1)}, f32[2,128]{1,0:T(2,128)S(1)}) custom-call(f32[2,8,128]{2,1,0:T(8,128)S(1)} %shard_map.98.share_ref, f32[2,8,128]{2,1,0:T(8,128)S(1)} %collective-permute-done.8.peer_share_ref, f32[16,128,256]{2,1,0:T(8,128)S(1)} %shard_map.99.powers_ref, s32[2,128]{1,0:T(2,128)S(1)} %bitcast.3, ...), custom_call_target="tpu_custom_call" | custom-call | tf_op jit(solution)/shard_map/pallas_call | solution.py:335
  28.8 1.6 %collective-permute-start.10 = (f32[2,128]{1,0:T(2,128)S(1)}, f32[2,128]{1,0:T(2,128)S(1)}, u32[]{:S(2)}, u32[]{:S(2)}) collective-permute-start(f32[2,128]{1,0:T(2,128)S(1)} %get-tuple-element.70), channel_id=1, source_target_pairs={{0,16},{16,0},{1,17},{17,1},{2,18},{18,2},{3,19},{19,3},{4,20},{20... | collective-permute-start | bytes 3080 | tf_op jit(solution)/shard_map/ppermute | solution.py:410
  30.4 0.0 collective-permute-done.9.behind_values_ref
  30.4 1.1 %shard_map.101 = bf16[128,2048]{1,0:T(8,128)(2,1)} custom-call(bf16[16,128,256]{2,1,0:T(8,128)(2,1)S(1)} %get-tuple-element.68.weights_ref, bf16[128,256]{1,0:T(8,128)(2,1)S(1)} %copy-done.2, bf16[128,256]{1,0:T(8,128)(2,1)S(1)} %collective-permute-done.9.behind_values_ref), custom_call_target="tpu_custom_call" | custom-call | flops 134217728 | bytes 1572864 | tf_op jit(solution)/shard_map/pallas_call | solution.py:362
  31.5 0.9 %collective-permute-done.10 = f32[2,128]{1,0:T(2,128)S(1)} collective-permute-done((f32[2,128]{1,0:T(2,128)S(1)}, f32[2,128]{1,0:T(2,128)S(1)}, u32[]{:S(2)}, u32[]{:S(2)}) %collective-permute-start.10) | collective-permute-done | bytes 1056 | tf_op jit(solution)/shard_map/ppermute | solution.py:410
  32.5 0.5 %add_convert_fusion = bf16[2,128]{1,0:T(2,128)(2,1)} fusion(f32[2,128]{1,0:T(2,128)S(1)} %get-tuple-element.69, f32[2,128]{1,0:T(2,128)S(1)} %collective-permute-done.10), kind=kLoop, calls=%fused_computation.1 | loop fusion | flops 512 | bytes 2560 | tf_op jit(solution)/shard_map/convert_element_type | solution.py:411
  (3 shorter events, 0.1 us)
Async XLA Ops:
  0.6 15.6 %collective-permute-start.3 = (bf16[128,2048]{1,0:T(8,128)(2,1)}, bf16[128,2048]{1,0:T(8,128)(2,1)S(1)}, u32[]{:S(2)}, u32[]{:S(2)}) collective-permute-start(bf16[128,2048]{1,0:T(8,128)(2,1)} %param.12), channel_id=1, source_target_pairs={{0,16},{16,0},{1,17},{17,1},{2,18},{18,2},{3,19},{19,3},{4,20},{20... | collective-permute-start | bytes 1572872 | tf_op jit(solution)/shard_map/ppermute | solution.py:382
  3.6 9.6 %copy-start.1 = (bf16[128,256]{1,0:T(8,128)(2,1)S(1)}, bf16[128,256]{1,0:T(8,128)(2,1)}, u32[]{:S(2)}) copy-start(bf16[128,256]{1,0:T(8,128)(2,1)} %keys_ref.1) | copy-start | bytes 196612
  3.6 9.4 %copy-start.5 = (bf16[8,1024]{1,0:T(8,128)(2,1)S(1)}, bf16[8,1024]{1,0:T(8,128)(2,1)}, u32[]{:S(2)}) copy-start(bf16[8,1024]{1,0:T(8,128)(2,1)} %get-tuple-element.21.gate_out_ref) | copy-start | bytes 49156 | tf_op jit(solution)/shard_map/cond
  6.2 1.5 %collective-permute-start.1 = (f32[112,512]{1,0:T(8,128)S(1)}, f32[112,512]{1,0:T(8,128)S(1)}, u32[]{:S(2)}, u32[]{:S(2)}) collective-permute-start(f32[112,512]{1,0:T(8,128)S(1)} %get-tuple-element.20), channel_id=1, source_target_pairs={{0,4},{4,0},{8,12},{12,8},{1,5},{5,1},{9,13},{13,9},{2,6},{6,2},{1... | collective-permute-start | bytes 688136 | tf_op jit(solution)/shard_map/cond/branch_1_fun/ppermute | solution.py:136
  7.8 5.3 %collective-permute-start.2 = (bf16[112,512]{1,0:T(8,128)(2,1)S(1)}, bf16[112,512]{1,0:T(8,128)(2,1)S(1)}, u32[]{:S(2)}, u32[]{:S(2)}) collective-permute-start(bf16[112,512]{1,0:T(8,128)(2,1)S(1)} %get-tuple-element.75), channel_id=1, source_target_pairs={{0,8},{4,12},{8,0},{12,4},{1,9},{5,13},{9,1},{13,5},{2,10},{6,14},... | collective-permute-start | bytes 344072 | tf_op jit(solution)/shard_map/cond/branch_1_fun/ppermute | solution.py:136
  13.2 7.4 %copy-start.2 = (bf16[128,256]{1,0:T(8,128)(2,1)S(1)}, bf16[128,256]{1,0:T(8,128)(2,1)}, u32[]{:S(2)}) copy-start(bf16[128,256]{1,0:T(8,128)(2,1)} %values_ref.1) | copy-start | bytes 196612
  13.2 9.3 %copy-start.4 = (bf16[1024,8]{0,1:T(8,128)(2,1)S(1)}, bf16[1024,8]{0,1:T(8,128)(2,1)}, u32[]{:S(2)}) copy-start(bf16[1024,8]{0,1:T(8,128)(2,1)} %param.15) | copy-start | bytes 49156
  13.3 12.8 %copy-start = (bf16[128,2048]{1,0:T(8,128)(2,1)S(1)}, bf16[128,2048]{1,0:T(8,128)(2,1)}, u32[]{:S(2)}) copy-start(bf16[128,2048]{1,0:T(8,128)(2,1)} %queries_ref.1) | copy-start | bytes 1572868
  13.3 12.8 %copy-start.3 = (s32[256]{0:T(256)S(1)}, s32[256]{0:T(256)}, u32[]{:S(2)}) copy-start(s32[256]{0:T(256)} %param.19) | copy-start | bytes 3076
  13.3 4.3 %collective-permute-start.4 = (bf16[128,256]{1,0:T(8,128)(2,1)S(1)}, bf16[128,256]{1,0:T(8,128)(2,1)S(1)}, u32[]{:S(2)}, u32[]{:S(2)}) collective-permute-start(bf16[128,256]{1,0:T(8,128)(2,1)S(1)} %copy-done.1), channel_id=1, source_target_pairs={{0,16},{16,0},{1,17},{17,1},{2,18},{18,2},{3,19},{19,3},{4,20},{20... | collective-permute-start | bytes 196616 | tf_op jit(solution)/shard_map/ppermute | solution.py:390
  17.6 1.6 %collective-permute-start.6 = (f32[144,256]{1,0:T(8,128)S(1)}, f32[144,256]{1,0:T(8,128)S(1)}, u32[]{:S(2)}, u32[]{:S(2)}) collective-permute-start(f32[144,256]{1,0:T(8,128)S(1)} %get-tuple-element.64), channel_id=1, source_target_pairs={{0,4},{4,0},{8,12},{12,8},{1,5},{5,1},{9,13},{13,9},{2,6},{6,2},{1... | collective-permute-start | bytes 442376 | tf_op jit(solution)/shard_map/ppermute | solution.py:136
  17.6 4.9 %collective-permute-start.5 = (bf16[144,256]{1,0:T(8,128)(2,1)S(1)}, bf16[144,256]{1,0:T(8,128)(2,1)S(1)}, u32[]{:S(2)}, u32[]{:S(2)}) collective-permute-start(bf16[144,256]{1,0:T(8,128)(2,1)S(1)} %get-tuple-element.63), channel_id=1, source_target_pairs={{0,8},{4,12},{8,0},{12,4},{1,9},{5,13},{9,1},{13,5},{2,10},{6,14},... | collective-permute-start | bytes 221192 | tf_op jit(solution)/shard_map/ppermute | solution.py:136
  19.2 5.0 %collective-permute-start.7 = (bf16[144,256]{1,0:T(8,128)(2,1)S(1)}, bf16[144,256]{1,0:T(8,128)(2,1)S(1)}, u32[]{:S(2)}, u32[]{:S(2)}) collective-permute-start(bf16[144,256]{1,0:T(8,128)(2,1)S(1)} %get-tuple-element.77), channel_id=1, source_target_pairs={{0,8},{4,12},{8,0},{12,4},{1,9},{5,13},{9,1},{13,5},{2,10},{6,14},... | collective-permute-start | bytes 221192 | tf_op jit(solution)/shard_map/ppermute | solution.py:136
  20.6 9.8 %collective-permute-start.9 = (bf16[128,256]{1,0:T(8,128)(2,1)S(1)}, bf16[128,256]{1,0:T(8,128)(2,1)S(1)}, u32[]{:S(2)}, u32[]{:S(2)}) collective-permute-start(bf16[128,256]{1,0:T(8,128)(2,1)S(1)} %copy-done.2), channel_id=1, source_target_pairs={{0,16},{16,0},{1,17},{17,1},{2,18},{18,2},{3,19},{19,3},{4,20},{20... | collective-permute-start | bytes 196616 | tf_op jit(solution)/shard_map/ppermute | solution.py:394
  22.6 1.4 %collective-permute-start = (f32[144,256]{1,0:T(8,128)S(1)}, f32[144,256]{1,0:T(8,128)S(1)}, u32[]{:S(2)}, u32[]{:S(2)}) collective-permute-start(f32[144,256]{1,0:T(8,128)S(1)} %convert_add_fusion.own_ref), channel_id=1, source_target_pairs={{0,4},{4,0},{8,12},{12,8},{1,5},{5,1},{9,13},{13,9},{2,6},{6,2},{1... | collective-permute-start | bytes 442376 | tf_op jit(solution)/shard_map/cond/branch_1_fun/ppermute | solution.py:136
  24.5 3.7 %collective-permute-start.8 = (f32[2,8,128]{2,1,0:T(8,128)S(1)}, f32[2,8,128]{2,1,0:T(8,128)S(1)}, u32[]{:S(2)}, u32[]{:S(2)}) collective-permute-start(f32[2,8,128]{2,1,0:T(8,128)S(1)} %shard_map.98.share_ref), channel_id=1, source_target_pairs={{0,16},{16,0},{1,17},{17,1},{2,18},{18,2},{3,19},{19,3},{4,20},{20... | collective-permute-start | bytes 24584 | tf_op jit(solution)/shard_map/ppermute | solution.py:402
  28.8 3.6 %collective-permute-start.10 = (f32[2,128]{1,0:T(2,128)S(1)}, f32[2,128]{1,0:T(2,128)S(1)}, u32[]{:S(2)}, u32[]{:S(2)}) collective-permute-start(f32[2,128]{1,0:T(2,128)S(1)} %get-tuple-element.70), channel_id=1, source_target_pairs={{0,16},{16,0},{1,17},{17,1},{2,18},{18,2},{3,19},{19,3},{4,20},{20... | collective-permute-start | bytes 3080 | tf_op jit(solution)/shard_map/ppermute | solution.py:410

commit v12 on v11

--- a/solution.py
+++ b/solution.py
@@ -386,11 +386,9 @@
         return partial_logits(*head_sum(part), gate_out, 0), held
 
     own_share, held = in_one_piece(own_work, activations, conv_taps, gate_in, gate_out)
-    own_share, held, key_vectors = lax.optimization_barrier((own_share, held, key_vectors))
-    behind_keys = lax.ppermute(key_vectors, "seq", swap)
     peer_rows, own_share, held = lax.optimization_barrier((peer_rows, own_share, held))
     near, far = peer_project(peer_rows, *held)
-    near, far, behind_keys = lax.optimization_barrier((near, far, behind_keys))
+    behind_keys = lax.ppermute(key_vectors, "seq", swap)
     behind_values = lax.ppermute(value_vectors, "seq", swap)
     near, near_in = head_sum(near)
     far_share = far_logits(far, gate_out)

time: 33.1 us -> 32.4 us (0.979)
  waiting for transfers between devices: 12.6 us -> 11.4 us
  starting transfers between devices: 12.6 us -> 13.2 us
    ppermute x1, starting transfers between devices: 0.38 us -> 1.49 us  [pair_device(): behind_keys = lax.ppermute(key_vectors, 'seq', swap)]
    ppermute x1, starting transfers between devices: 1.46 us -> 0.53 us  [pair_device(): behind_values = lax.ppermute(value_vectors, 'seq', swap)]
    ppermute x1, waiting for transfers between devices: 0.61 us -> 0.01 us  [pair_device(): behind_keys = lax.ppermute(key_vectors, 'seq', swap)]
    ppermute x6, waiting for transfers between devices: 7.01 us -> 6.51 us  [exchange_heads(): return lax.ppermute(block, 'heads', [(i, i ^ step) for i in range(count)])]
  transfers between devices with their start and end apart: 11 -> 11, of which waited for: 8 -> 6; matrix products, arithmetic and copies ran while one was open for 0% -> 0% of each run, Pallas kernels for 20% -> 17%
where the time goes in v12:
time: 32.4 us; the launch traced here: 32.3 us
  starting transfers between devices  13.2 us (41%)
  waiting for transfers between devices  11.4 us (35%)
  Pallas kernels  6.41 us (20%)
  between operations  0.7 us (2%)
  other arithmetic  0.59 us (2%)
    ppermute x6, waiting for transfers between devices, exchange_heads(): return lax.ppermute(block, 'heads', [(i, i ^ step) for i in range(count)])  6.51 us
    ppermute x6, starting transfers between devices, exchange_heads(): return lax.ppermute(block, 'heads', [(i, i ^ step) for i in range(count)])  4.97 us
    ppermute x1, starting transfers between devices, pair_device(): peer_rows = lax.ppermute(activations, 'seq', swap)  3 us
    pallas_call x1, Pallas kernels, own_project(): pl.pallas_call(own_project_kernel, out_shape=(jax.ShapeDtypeStruct((done,...  2.55 us
    ppermute x1, waiting for transfers between devices, pair_device(): peer_rows = lax.ppermute(activations, 'seq', swap)  2.51 us
    ppermute x1, starting transfers between devices, pair_device(): key_mass = own_mass + lax.ppermute(behind_mass, 'seq', swap)  1.63 us
    ppermute x1, starting transfers between devices, pair_device(): lax.ppermute(share, 'seq', swap)  1.52 us
    ppermute x1, starting transfers between devices, pair_device(): behind_keys = lax.ppermute(key_vectors, 'seq', swap)  1.49 us
  transfers between devices with their start and end apart: 11, of which 6 were waited for; matrix products, arithmetic and copies ran while one was open for 0% of the time, Pallas kernels for 17%

profile of v12, /device:TPU:0, one launch (start us, length us, event | category | flops | bytes accessed | tf_op | source)
XLA Modules:
  0.0 32.3 jit_solution(15199731706702291080)
XLA Ops:
  0.6 3.0 %collective-permute-start.3 = (bf16[128,2048]{1,0:T(8,128)(2,1)}, bf16[128,2048]{1,0:T(8,128)(2,1)S(1)}, u32[]{:S(2)}, u32[]{:S(2)}) collective-permute-start(bf16[128,2048]{1,0:T(8,128)(2,1)} %param.12), channel_id=1, source_target_pairs={{0,16},{16,0},{1,17},{17,1},{2,18},{18,2},{3,19},{19,3},{4,20},{20... | collective-permute-start | bytes 1572872 | tf_op jit(solution)/shard_map/ppermute | solution.py:382
  3.6 9.6 %conditional.2 = (f32[8,112]{1,0:T(8,128)S(1)}, f32[4,2048]{1,0:T(4,128)S(1)}, bf16[2176,512]{1,0:T(8,128)(2,1)S(1)}) conditional(s32[]{:T(128)} %convert_element_type.19, () %tuple.24, (bf16[128,2048]{1,0:T(8,128)(2,1)}, bf16[4,2048]{1,0:T(4,128)(2,1)}, bf16[2048,512]{1,0:T(8,128)(2,1)}, bf16[8,1024]{1,0:T(8,128)(2,1)}) %tuple.37), branch_computations={%region_0.0_spmd, %region_1.0_spmd} | conditional | flops 114689 | bytes 2264610 | solution.py:141
  3.6 0.0 copy-start.5
  3.6 2.6 %branch_1_fun.3 = (f32[112,512]{1,0:T(8,128)S(1)}, f32[4,2048]{1,0:T(4,128)S(1)}, bf16[2176,512]{1,0:T(8,128)(2,1)S(1)}) custom-call(bf16[128,2048]{1,0:T(8,128)(2,1)} %get-tuple-element.10.rows_ref, bf16[4,2048]{1,0:T(4,128)(2,1)} %get-tuple-element.59.taps_ref, bf16[2048,512]{1,0:T(8,128)(2,1)} %get-tuple-element.60.gate_ref), custom_call_target="tpu_custom_call" | custom-call | flops 1 | bytes 1 | tf_op jit(solution)/shard_map/cond/branch_1_fun/pallas_call | solution.py:87
  6.2 0.1 collective-permute-start.1
  6.3 1.5 %collective-permute-done.1 = f32[112,512]{1,0:T(8,128)S(1)} collective-permute-done((f32[112,512]{1,0:T(8,128)S(1)}, f32[112,512]{1,0:T(8,128)S(1)}, u32[]{:S(2)}, u32[]{:S(2)}) %collective-permute-start.1) | collective-permute-done | bytes 229408 | tf_op jit(solution)/shard_map/cond/branch_1_fun/ppermute | solution.py:136
  7.8 1.6 %collective-permute-start.2 = (bf16[112,512]{1,0:T(8,128)(2,1)S(1)}, bf16[112,512]{1,0:T(8,128)(2,1)S(1)}, u32[]{:S(2)}, u32[]{:S(2)}) collective-permute-start(bf16[112,512]{1,0:T(8,128)(2,1)S(1)} %get-tuple-element.61), channel_id=1, source_target_pairs={{0,8},{4,12},{8,0},{12,4},{1,9},{5,13},{9,1},{13,5},{2,10},{6,14},... | collective-permute-start | bytes 344072 | tf_op jit(solution)/shard_map/cond/branch_1_fun/ppermute | solution.py:136
  9.4 3.7 %collective-permute-done.2.in_ref = bf16[112,512]{1,0:T(8,128)(2,1)S(1)} collective-permute-done((bf16[112,512]{1,0:T(8,128)(2,1)S(1)}, bf16[112,512]{1,0:T(8,128)(2,1)S(1)}, u32[]{:S(2)}, u32[]{:S(2)}) %collective-permute-start.2) | collective-permute-done | bytes 114720 | tf_op jit(solution)/shard_map/cond/branch_1_fun/ppermute | solution.py:136
  13.0 0.0 copy-done.5
  13.0 0.2 branch_1_fun.4
  13.2 0.0 copy-start.1
  13.2 0.0 copy-start.2
  13.2 0.0 copy-start.4
  13.2 0.0 copy-start
  13.2 0.0 copy-start.3
  13.3 2.5 %collective-permute-done.3.peer_ref = bf16[128,2048]{1,0:T(8,128)(2,1)S(1)} collective-permute-done((bf16[128,2048]{1,0:T(8,128)(2,1)}, bf16[128,2048]{1,0:T(8,128)(2,1)S(1)}, u32[]{:S(2)}, u32[]{:S(2)}) %collective-permute-start.3) | collective-permute-done | bytes 524320 | tf_op jit(solution)/shard_map/ppermute | solution.py:382
  15.8 0.8 %shard_map.97 = (f32[144,256]{1,0:T(8,128)S(1)}, bf16[144,256]{1,0:T(8,128)(2,1)S(1)}) custom-call(bf16[128,2048]{1,0:T(8,128)(2,1)S(1)} %collective-permute-done.3.peer_ref, f32[4,2048]{1,0:T(4,128)S(1)} %get-tuple-element.48.taps_ref, bf16[2176,512]{1,0:T(8,128)(2,1)S(1)} %get-tuple-element.49.held_ref), custom_call_target="tpu_custom_call" | custom-call | flops 1 | bytes 1 | tf_op jit(solution)/shard_map/pallas_call | solution.py:107
  16.6 0.1 collective-permute-start.5
  16.6 1.8 %collective-permute-start.4 = (bf16[144,256]{1,0:T(8,128)(2,1)S(1)}, bf16[144,256]{1,0:T(8,128)(2,1)S(1)}, u32[]{:S(2)}, u32[]{:S(2)}) collective-permute-start(bf16[144,256]{1,0:T(8,128)(2,1)S(1)} %get-tuple-element.50), channel_id=1, source_target_pairs={{0,8},{4,12},{8,0},{12,4},{1,9},{5,13},{9,1},{13,5},{2,10},{6,14},... | collective-permute-start | bytes 221192 | tf_op jit(solution)/shard_map/ppermute | solution.py:136
  18.5 0.0 collective-permute-done.5
  18.5 1.4 %collective-permute-start.6 = (bf16[144,256]{1,0:T(8,128)(2,1)S(1)}, bf16[144,256]{1,0:T(8,128)(2,1)S(1)}, u32[]{:S(2)}, u32[]{:S(2)}) collective-permute-start(bf16[144,256]{1,0:T(8,128)(2,1)S(1)} %get-tuple-element.63), channel_id=1, source_target_pairs={{0,8},{4,12},{8,0},{12,4},{1,9},{5,13},{9,1},{13,5},{2,10},{6,14},... | collective-permute-start | bytes 221192 | tf_op jit(solution)/shard_map/ppermute | solution.py:136
  19.8 0.0 copy-done.1
  19.8 1.5 %collective-permute-start.8 = (bf16[128,256]{1,0:T(8,128)(2,1)S(1)}, bf16[128,256]{1,0:T(8,128)(2,1)S(1)}, u32[]{:S(2)}, u32[]{:S(2)}) collective-permute-start(bf16[128,256]{1,0:T(8,128)(2,1)S(1)} %copy-done.1), channel_id=1, source_target_pairs={{0,16},{16,0},{1,17},{17,1},{2,18},{18,2},{3,19},{19,3},{4,20},{20... | collective-permute-start | bytes 196616 | tf_op jit(solution)/shard_map/ppermute | solution.py:391
  21.3 0.0 copy-done.2
  21.3 0.5 %collective-permute-start.9 = (bf16[128,256]{1,0:T(8,128)(2,1)S(1)}, bf16[128,256]{1,0:T(8,128)(2,1)S(1)}, u32[]{:S(2)}, u32[]{:S(2)}) collective-permute-start(bf16[128,256]{1,0:T(8,128)(2,1)S(1)} %copy-done.2), channel_id=1, source_target_pairs={{0,16},{16,0},{1,17},{17,1},{2,18},{18,2},{3,19},{19,3},{4,20},{20... | collective-permute-start | bytes 196616 | tf_op jit(solution)/shard_map/ppermute | solution.py:392
  21.9 0.0 collective-permute-done.4
  21.9 0.0 copy-done.4
  21.9 1.6 %conditional.3 = (f32[8,144]{1,0:T(8,128)S(1)}) conditional(s32[]{:T(128)} %convert_element_type.19, () %tuple.27, (bf16[144,256]{1,0:T(8,128)(2,1)S(1)}, bf16[144,256]{1,0:T(8,128)(2,1)S(1)}, bf16[8,1024]{1,0:T(8,128)(2,1)S(1)}) %tuple.38), branch_computations={%region_2.0_spmd, %region_3.0_spmd} | conditional | flops 110592 | bytes 884784 | solution.py:141
  21.9 0.1 collective-permute-start
  22.0 1.4 %collective-permute-done.in_ref = f32[144,256]{1,0:T(8,128)S(1)} collective-permute-done((f32[144,256]{1,0:T(8,128)S(1)}, f32[144,256]{1,0:T(8,128)S(1)}, u32[]{:S(2)}, u32[]{:S(2)}) %collective-permute-start) | collective-permute-done | bytes 147488 | tf_op jit(solution)/shard_map/cond/branch_1_fun/ppermute | solution.py:136
  23.3 0.2 branch_1_fun.5
  23.5 0.0 collective-permute-done.6.near_in_ref
  23.5 0.3 shard_map.98.share_ref
  23.8 1.5 %collective-permute-start.7 = (f32[2,8,128]{2,1,0:T(8,128)S(1)}, f32[2,8,128]{2,1,0:T(8,128)S(1)}, u32[]{:S(2)}, u32[]{:S(2)}) collective-permute-start(f32[2,8,128]{2,1,0:T(8,128)S(1)} %shard_map.98.share_ref), channel_id=1, source_target_pairs={{0,16},{16,0},{1,17},{17,1},{2,18},{18,2},{3,19},{19,3},{4,20},{20... | collective-permute-start | bytes 24584 | tf_op jit(solution)/shard_map/ppermute | solution.py:400
  25.3 0.0 collective-permute-done.8.behind_keys_ref
  25.3 0.0 copy-done
  25.3 0.0 copy-done.3
  25.3 0.7 %shard_map.99.powers_ref = f32[16,128,256]{2,1,0:T(8,128)S(1)} custom-call(s32[2,128]{1,0:T(2,128)S(1)} %bitcast.2, bf16[128,2048]{1,0:T(8,128)(2,1)S(1)} %copy-done, bf16[128,256]{1,0:T(8,128)(2,1)S(1)} %copy-done.1, bf16[128,256]{1,0:T(8,128)(2,1)S(1)} %collective-permute-done.8.behind_keys_ref), custom_call_target="tpu_custom_call" | custom-call | flops 134217728 | bytes 2097152 | tf_op jit(solution)/shard_map/pallas_call | solution.py:261
  26.0 1.4 %collective-permute-done.7.peer_share_ref = f32[2,8,128]{2,1,0:T(8,128)S(1)} collective-permute-done((f32[2,8,128]{2,1,0:T(8,128)S(1)}, f32[2,8,128]{2,1,0:T(8,128)S(1)}, u32[]{:S(2)}, u32[]{:S(2)}) %collective-permute-start.7) | collective-permute-done | bytes 8224 | tf_op jit(solution)/shard_map/ppermute | solution.py:400
  27.5 0.6 %shard_map.100 = (bf16[16,128,256]{2,1,0:T(8,128)(2,1)S(1)}, f32[2,128]{1,0:T(2,128)S(1)}, f32[2,128]{1,0:T(2,128)S(1)}) custom-call(f32[2,8,128]{2,1,0:T(8,128)S(1)} %shard_map.98.share_ref, f32[2,8,128]{2,1,0:T(8,128)S(1)} %collective-permute-done.7.peer_share_ref, f32[16,128,256]{2,1,0:T(8,128)S(1)} %shard_map.99.powers_ref, s32[2,128]{1,0:T(2,128)S(1)} %bitcast.3, ...), custom_call_target="tpu_custom_call" | custom-call | tf_op jit(solution)/shard_map/pallas_call | solution.py:335
  28.1 1.6 %collective-permute-start.10 = (f32[2,128]{1,0:T(2,128)S(1)}, f32[2,128]{1,0:T(2,128)S(1)}, u32[]{:S(2)}, u32[]{:S(2)}) collective-permute-start(f32[2,128]{1,0:T(2,128)S(1)} %get-tuple-element.56), channel_id=1, source_target_pairs={{0,16},{16,0},{1,17},{17,1},{2,18},{18,2},{3,19},{19,3},{4,20},{20... | collective-permute-start | bytes 3080 | tf_op jit(solution)/shard_map/ppermute | solution.py:408
  29.8 0.0 collective-permute-done.9.behind_values_ref
  29.8 1.1 %shard_map.101 = bf16[128,2048]{1,0:T(8,128)(2,1)} custom-call(bf16[16,128,256]{2,1,0:T(8,128)(2,1)S(1)} %get-tuple-element.54.weights_ref, bf16[128,256]{1,0:T(8,128)(2,1)S(1)} %copy-done.2, bf16[128,256]{1,0:T(8,128)(2,1)S(1)} %collective-permute-done.9.behind_values_ref), custom_call_target="tpu_custom_call" | custom-call | flops 134217728 | bytes 1572864 | tf_op jit(solution)/shard_map/pallas_call | solution.py:362
  30.9 0.9 %collective-permute-done.10 = f32[2,128]{1,0:T(2,128)S(1)} collective-permute-done((f32[2,128]{1,0:T(2,128)S(1)}, f32[2,128]{1,0:T(2,128)S(1)}, u32[]{:S(2)}, u32[]{:S(2)}) %collective-permute-start.10) | collective-permute-done | bytes 1056 | tf_op jit(solution)/shard_map/ppermute | solution.py:408
  31.8 0.5 %add_convert_fusion = bf16[2,128]{1,0:T(2,128)(2,1)} fusion(f32[2,128]{1,0:T(2,128)S(1)} %get-tuple-element.55, f32[2,128]{1,0:T(2,128)S(1)} %collective-permute-done.10), kind=kLoop, calls=%fused_computation.1 | loop fusion | flops 512 | bytes 2560 | tf_op jit(solution)/shard_map/convert_element_type | solution.py:409
  (3 shorter events, 0.1 us)
Async XLA Ops:
  0.6 15.1 %collective-permute-start.3 = (bf16[128,2048]{1,0:T(8,128)(2,1)}, bf16[128,2048]{1,0:T(8,128)(2,1)S(1)}, u32[]{:S(2)}, u32[]{:S(2)}) collective-permute-start(bf16[128,2048]{1,0:T(8,128)(2,1)} %param.12), channel_id=1, source_target_pairs={{0,16},{16,0},{1,17},{17,1},{2,18},{18,2},{3,19},{19,3},{4,20},{20... | collective-permute-start | bytes 1572872 | tf_op jit(solution)/shard_map/ppermute | solution.py:382
  3.6 9.4 %copy-start.5 = (bf16[8,1024]{1,0:T(8,128)(2,1)S(1)}, bf16[8,1024]{1,0:T(8,128)(2,1)}, u32[]{:S(2)}) copy-start(bf16[8,1024]{1,0:T(8,128)(2,1)} %get-tuple-element.21.gate_out_ref) | copy-start | bytes 49156 | tf_op jit(solution)/shard_map/cond
  6.2 1.5 %collective-permute-start.1 = (f32[112,512]{1,0:T(8,128)S(1)}, f32[112,512]{1,0:T(8,128)S(1)}, u32[]{:S(2)}, u32[]{:S(2)}) collective-permute-start(f32[112,512]{1,0:T(8,128)S(1)} %get-tuple-element.20), channel_id=1, source_target_pairs={{0,4},{4,0},{8,12},{12,8},{1,5},{5,1},{9,13},{13,9},{2,6},{6,2},{1... | collective-permute-start | bytes 688136 | tf_op jit(solution)/shard_map/cond/branch_1_fun/ppermute | solution.py:136
  7.8 5.3 %collective-permute-start.2 = (bf16[112,512]{1,0:T(8,128)(2,1)S(1)}, bf16[112,512]{1,0:T(8,128)(2,1)S(1)}, u32[]{:S(2)}, u32[]{:S(2)}) collective-permute-start(bf16[112,512]{1,0:T(8,128)(2,1)S(1)} %get-tuple-element.61), channel_id=1, source_target_pairs={{0,8},{4,12},{8,0},{12,4},{1,9},{5,13},{9,1},{13,5},{2,10},{6,14},... | collective-permute-start | bytes 344072 | tf_op jit(solution)/shard_map/cond/branch_1_fun/ppermute | solution.py:136
  13.2 6.6 %copy-start.1 = (bf16[128,256]{1,0:T(8,128)(2,1)S(1)}, bf16[128,256]{1,0:T(8,128)(2,1)}, u32[]{:S(2)}) copy-start(bf16[128,256]{1,0:T(8,128)(2,1)} %keys_ref.3) | copy-start | bytes 196612
  13.2 8.1 %copy-start.2 = (bf16[128,256]{1,0:T(8,128)(2,1)S(1)}, bf16[128,256]{1,0:T(8,128)(2,1)}, u32[]{:S(2)}) copy-start(bf16[128,256]{1,0:T(8,128)(2,1)} %values_ref.1) | copy-start | bytes 196612
  13.2 8.7 %copy-start.4 = (bf16[1024,8]{0,1:T(8,128)(2,1)S(1)}, bf16[1024,8]{0,1:T(8,128)(2,1)}, u32[]{:S(2)}) copy-start(bf16[1024,8]{0,1:T(8,128)(2,1)} %param.15) | copy-start | bytes 49156
  13.2 12.1 %copy-start = (bf16[128,2048]{1,0:T(8,128)(2,1)S(1)}, bf16[128,2048]{1,0:T(8,128)(2,1)}, u32[]{:S(2)}) copy-start(bf16[128,2048]{1,0:T(8,128)(2,1)} %queries_ref.1) | copy-start | bytes 1572868
  13.2 12.1 %copy-start.3 = (s32[256]{0:T(256)S(1)}, s32[256]{0:T(256)}, u32[]{:S(2)}) copy-start(s32[256]{0:T(256)} %param.19) | copy-start | bytes 3076
  16.6 1.9 %collective-permute-start.5 = (f32[144,256]{1,0:T(8,128)S(1)}, f32[144,256]{1,0:T(8,128)S(1)}, u32[]{:S(2)}, u32[]{:S(2)}) collective-permute-start(f32[144,256]{1,0:T(8,128)S(1)} %get-tuple-element.51), channel_id=1, source_target_pairs={{0,4},{4,0},{8,12},{12,8},{1,5},{5,1},{9,13},{13,9},{2,6},{6,2},{1... | collective-permute-start | bytes 442376 | tf_op jit(solution)/shard_map/ppermute | solution.py:136
  16.6 5.3 %collective-permute-start.4 = (bf16[144,256]{1,0:T(8,128)(2,1)S(1)}, bf16[144,256]{1,0:T(8,128)(2,1)S(1)}, u32[]{:S(2)}, u32[]{:S(2)}) collective-permute-start(bf16[144,256]{1,0:T(8,128)(2,1)S(1)} %get-tuple-element.50), channel_id=1, source_target_pairs={{0,8},{4,12},{8,0},{12,4},{1,9},{5,13},{9,1},{13,5},{2,10},{6,14},... | collective-permute-start | bytes 221192 | tf_op jit(solution)/shard_map/ppermute | solution.py:136
  18.5 5.0 %collective-permute-start.6 = (bf16[144,256]{1,0:T(8,128)(2,1)S(1)}, bf16[144,256]{1,0:T(8,128)(2,1)S(1)}, u32[]{:S(2)}, u32[]{:S(2)}) collective-permute-start(bf16[144,256]{1,0:T(8,128)(2,1)S(1)} %get-tuple-element.63), channel_id=1, source_target_pairs={{0,8},{4,12},{8,0},{12,4},{1,9},{5,13},{9,1},{13,5},{2,10},{6,14},... | collective-permute-start | bytes 221192 | tf_op jit(solution)/shard_map/ppermute | solution.py:136
  19.8 5.5 %collective-permute-start.8 = (bf16[128,256]{1,0:T(8,128)(2,1)S(1)}, bf16[128,256]{1,0:T(8,128)(2,1)S(1)}, u32[]{:S(2)}, u32[]{:S(2)}) collective-permute-start(bf16[128,256]{1,0:T(8,128)(2,1)S(1)} %copy-done.1), channel_id=1, source_target_pairs={{0,16},{16,0},{1,17},{17,1},{2,18},{18,2},{3,19},{19,3},{4,20},{20... | collective-permute-start | bytes 196616 | tf_op jit(solution)/shard_map/ppermute | solution.py:391
  21.3 8.4 %collective-permute-start.9 = (bf16[128,256]{1,0:T(8,128)(2,1)S(1)}, bf16[128,256]{1,0:T(8,128)(2,1)S(1)}, u32[]{:S(2)}, u32[]{:S(2)}) collective-permute-start(bf16[128,256]{1,0:T(8,128)(2,1)S(1)} %copy-done.2), channel_id=1, source_target_pairs={{0,16},{16,0},{1,17},{17,1},{2,18},{18,2},{3,19},{19,3},{4,20},{20... | collective-permute-start | bytes 196616 | tf_op jit(solution)/shard_map/ppermute | solution.py:392
  21.9 1.4 %collective-permute-start = (f32[144,256]{1,0:T(8,128)S(1)}, f32[144,256]{1,0:T(8,128)S(1)}, u32[]{:S(2)}, u32[]{:S(2)}) collective-permute-start(f32[144,256]{1,0:T(8,128)S(1)} %convert_add_fusion.own_ref), channel_id=1, source_target_pairs={{0,4},{4,0},{8,12},{12,8},{1,5},{5,1},{9,13},{13,9},{2,6},{6,2},{1... | collective-permute-start | bytes 442376 | tf_op jit(solution)/shard_map/cond/branch_1_fun/ppermute | solution.py:136
  23.8 3.7 %collective-permute-start.7 = (f32[2,8,128]{2,1,0:T(8,128)S(1)}, f32[2,8,128]{2,1,0:T(8,128)S(1)}, u32[]{:S(2)}, u32[]{:S(2)}) collective-permute-start(f32[2,8,128]{2,1,0:T(8,128)S(1)} %shard_map.98.share_ref), channel_id=1, source_target_pairs={{0,16},{16,0},{1,17},{17,1},{2,18},{18,2},{3,19},{19,3},{4,20},{20... | collective-permute-start | bytes 24584 | tf_op jit(solution)/shard_map/ppermute | solution.py:400
  28.1 3.6 %collective-permute-start.10 = (f32[2,128]{1,0:T(2,128)S(1)}, f32[2,128]{1,0:T(2,128)S(1)}, u32[]{:S(2)}, u32[]{:S(2)}) collective-permute-start(f32[2,128]{1,0:T(2,128)S(1)} %get-tuple-element.56), channel_id=1, source_target_pairs={{0,16},{16,0},{1,17},{17,1},{2,18},{18,2},{3,19},{19,3},{4,20},{20... | collective-permute-start | bytes 3080 | tf_op jit(solution)/shard_map/ppermute | solution.py:408

commit v13 on v12

--- a/solution.py
+++ b/solution.py
@@ -26,12 +26,22 @@
     return summed.astype(jnp.bfloat16)
 
 
-def own_project_kernel(rows_ref, taps_ref, gate_ref, out_ref, held_taps_ref, held_ref, widened):
+def split_by_core(total, kept_ref, given_ref):
+    half = kept_ref.shape[1]
+    low, high = total[:, :half], total[:, half:]
+    even = lax.rem(lax.axis_index("heads"), 2) == 0
+    kept_ref[...] = jnp.where(even, low, high)
+    given_ref[...] = jnp.where(even, high, low)
+
+
+def own_project_kernel(
+    rows_ref, taps_ref, gate_ref, kept_ref, given_ref, held_taps_ref, held_ref, widened
+):
     rows, features = rows_ref.shape
     held_taps_ref[...] = taps_ref[...].astype(jnp.float32)
     held_ref[:features] = gate_ref[...]
     tile = widened.shape[2]
-    total = jnp.zeros(out_ref.shape, jnp.float32)
+    total = jnp.zeros((rows - RIM_ROWS, gate_ref.shape[1]), jnp.float32)
     for step in range(features // tile):
         columns = slice(step * tile, (step + 1) * tile)
         edges = features + step * 2 * RIM_ROWS
@@ -44,17 +54,16 @@
         taps = taps_ref[:, columns].astype(jnp.float32)
         mixed = convolve(wide, taps, RIM_ROWS, rows - RIM_ROWS)
         total = total + jnp.dot(mixed, gate_ref[columns, :], preferred_element_type=jnp.float32)
-    out_ref[...] = total
+    split_by_core(total, kept_ref, given_ref)
 
 
 def peer_project_kernel(
-    peer_ref, taps_ref, held_ref, near_ref, far_ref, widened, own_widened
+    peer_ref, taps_ref, held_ref, kept_ref, given_ref, widened, own_widened
 ):
     rows, features = peer_ref.shape
     tile = widened.shape[2]
     first = lax.axis_index("seq") == 0
-    half = near_ref.shape[1]
-    total = jnp.zeros((near_ref.shape[0], 2 * half), jnp.float32)
+    total = jnp.zeros((kept_ref.shape[0], held_ref.shape[1]), jnp.float32)
     for step in range(features // tile):
         columns = slice(step * tile, (step + 1) * tile)
         wide, own_wide = widened.at[step % 2], own_widened.at[step % 2]
@@ -76,8 +85,7 @@
             axis=0,
         )
         total = total + jnp.dot(mixed, held_ref[columns, :], preferred_element_type=jnp.float32)
-    near_ref[...] = total[:, :half]
-    far_ref[...] = total[:, half:].astype(jnp.bfloat16)
+    split_by_core(total, kept_ref, given_ref)
 
 
 def own_project(activations, conv_taps, gate_in):
@@ -87,7 +95,8 @@
     return pl.pallas_call(
         own_project_kernel,
         out_shape=(
-            jax.ShapeDtypeStruct((done, gate_in.shape[1]), jnp.float32),
+            jax.ShapeDtypeStruct((done, gate_in.shape[1] // 2), jnp.float32),
+            jax.ShapeDtypeStruct((done, gate_in.shape[1] // 2), jnp.float32),
             jax.ShapeDtypeStruct(conv_taps.shape, jnp.float32),
             jax.ShapeDtypeStruct(
                 (features + features // tile * 2 * RIM_ROWS, gate_in.shape[1]), gate_in.dtype
@@ -108,7 +117,7 @@
         peer_project_kernel,
         out_shape=(
             jax.ShapeDtypeStruct((done, half), jnp.float32),
-            jax.ShapeDtypeStruct((done, half), jnp.bfloat16),
+            jax.ShapeDtypeStruct((done, half), jnp.float32),
         ),
         scratch_shapes=[
             pltpu.VMEM((2, rows + RIM_ROWS, tile), jnp.float32),
@@ -119,21 +128,19 @@
     )(peer_rows, taps, held)
 
 
-def head_sum(part):
-    count = lax.axis_size("heads")
-    step = 1
-    received = None
-    while step < count:
-        if received is not None:
-            part = part + received.astype(jnp.float32)
-        received = exchange_heads(part if step == 1 else part.astype(jnp.bfloat16), step)
-        step *= 2
-    return part, received
-
-
 def exchange_heads(block, step):
     count = lax.axis_size("heads")
     return lax.ppermute(block, "heads", [(i, i ^ step) for i in range(count)])
+
+
+def head_sum(kept, given):
+    received = exchange_heads(given, 1)
+    step = 2
+    while step < lax.axis_size("heads"):
+        kept = kept + received.astype(jnp.float32)
+        received = exchange_heads(kept.astype(jnp.bfloat16), step)
+        step *= 2
+    return kept, received
 
 
 def in_one_piece(work, *given):
@@ -146,60 +153,45 @@
     )
 
 
-def far_logits(block, gate_out):
-    step = lax.axis_size("heads") // 2
-    received = exchange_heads(block, step)
-
-    def nearer(block, received, gate_out):
-        distance = step
-        while distance > 1:
-            distance //= 2
-            block = block.astype(jnp.float32) + received.astype(jnp.float32)
-            received = exchange_heads(block, distance)
-        return partial_logits(block, received, gate_out, block.shape[1])
-
-    return in_one_piece(nearer, block, received, gate_out)
-
-
-def share_of_logits(pre_ref, in_ref, gate_out_ref, offset):
-    pre = pre_ref[...] + in_ref[...].astype(jnp.float32)
+def share_of_logits(kept_ref, in_ref, gate_out_ref):
+    pre = kept_ref[...] + in_ref[...].astype(jnp.float32)
     hidden = (pre / (1.0 + jnp.exp(-pre))).astype(jnp.bfloat16)
-    share = gate_out_ref.shape[1] // lax.axis_size("seq")
-    start = pl.multiple_of(lax.axis_index("seq") * share + offset, HEAD_DIM)
-    gate_columns = gate_out_ref[:, pl.ds(start, pre.shape[1])]
+    half = pre.shape[1]
+    part = 2 * lax.axis_index("seq") + lax.rem(lax.axis_index("heads"), 2)
+    gate_columns = gate_out_ref[:, pl.ds(pl.multiple_of(part * half, HEAD_DIM), half)]
     return lax.dot_general(
         gate_columns, hidden, (((1,), (1,)), ((), ())), preferred_element_type=jnp.float32
     )
 
 
-def partial_logits_kernel(offset, own_ref, in_ref, gate_out_ref, out_ref):
-    out_ref[...] = share_of_logits(own_ref, in_ref, gate_out_ref, offset)
-
-
-def partial_logits(part, received, gate_out, offset):
-    return pl.pallas_call(
-        functools.partial(partial_logits_kernel, offset),
-        out_shape=jax.ShapeDtypeStruct((gate_out.shape[0], part.shape[0]), jnp.float32),
-        compiler_params=pltpu.CompilerParams(vmem_limit_bytes=VMEM_BYTES),
-    )(part, received, gate_out)
-
-
-def logits_kernel(own_ref, far_share_ref, near_ref, near_in_ref, gate_out_ref, out_ref):
+def partial_logits_kernel(kept_ref, in_ref, gate_out_ref, out_ref):
+    out_ref[...] = share_of_logits(kept_ref, in_ref, gate_out_ref)
+
+
+def partial_logits(kept, received, gate_out):
+    return pl.pallas_call(
+        partial_logits_kernel,
+        out_shape=jax.ShapeDtypeStruct((gate_out.shape[0], kept.shape[0]), jnp.float32),
+        compiler_params=pltpu.CompilerParams(vmem_limit_bytes=VMEM_BYTES),
+    )(kept, received, gate_out)
+
+
+def logits_kernel(own_ref, kept_ref, in_ref, gate_out_ref, out_ref):
     first = lax.axis_index("seq") == 0
-    share = share_of_logits(near_ref, near_in_ref, gate_out_ref, 0) + far_share_ref[...]
+    share = share_of_logits(kept_ref, in_ref, gate_out_ref)
     own = jnp.concatenate([share[:, :RIM_ROWS], own_ref[...]], axis=1)
     peer = share[:, RIM_ROWS:]
     out_ref[0] = jnp.where(first, own, peer)
     out_ref[1] = jnp.where(first, peer, own)
 
 
-def logits_share(own_share, far_share, near, near_in, gate_out):
+def logits_share(own_share, kept, received, gate_out):
     rows = own_share.shape[1] + RIM_ROWS
     return pl.pallas_call(
         logits_kernel,
         out_shape=jax.ShapeDtypeStruct((2, gate_out.shape[0], rows), jnp.float32),
         compiler_params=pltpu.CompilerParams(vmem_limit_bytes=VMEM_BYTES),
-    )(own_share, far_share, near, near_in, gate_out)
+    )(own_share, kept, received, gate_out)
 
 
 def hide_unseen(seq_rank, segments_ref, rows):
@@ -272,7 +264,9 @@
 
 def weights_kernel(
     share_ref,
+    core_share_ref,
     peer_share_ref,
+    peer_core_share_ref,
     powers_ref,
     segments_ref,
     queries_ref,
@@ -287,7 +281,8 @@
     rows = queries_ref.shape[0]
     kv_local = keys_ref.shape[1] // HEAD_DIM
     group_size = queries_ref.shape[1] // keys_ref.shape[1]
-    logits = share_ref[...] + peer_share_ref[...]
+    logits = share_ref[...] + core_share_ref[...]
+    logits = logits + (peer_share_ref[...] + peer_core_share_ref[...])
     log_gate = jnp.minimum(logits, 0.0) - jnp.log1p(jnp.exp(-jnp.abs(logits)))
     retention[...] = log_gate.astype(jnp.bfloat16).astype(jnp.float32)
     biases = []
@@ -329,15 +324,15 @@
     pl.when(jnp.logical_not(moderate))(lambda: finish(True, by_scores))
 
 
-def weights_of(share, peer_share, powers, segments, queries, keys, behind_keys):
+def weights_of(shares, powers, segments, queries, keys, behind_keys):
     rows = queries.shape[0]
     mass = jax.ShapeDtypeStruct((keys.shape[1] // HEAD_DIM, rows), jnp.float32)
     return pl.pallas_call(
         weights_kernel,
         out_shape=(jax.ShapeDtypeStruct(powers.shape, jnp.bfloat16), mass, mass),
-        scratch_shapes=[pltpu.VMEM(share.shape, jnp.float32)],
-        compiler_params=pltpu.CompilerParams(vmem_limit_bytes=VMEM_BYTES),
-    )(share, peer_share, powers, segments, queries, keys, behind_keys)
+        scratch_shapes=[pltpu.VMEM(shares[0].shape, jnp.float32)],
+        compiler_params=pltpu.CompilerParams(vmem_limit_bytes=VMEM_BYTES),
+    )(*shares, powers, segments, queries, keys, behind_keys)
 
 
 def attend_kernel(weights_ref, values_ref, behind_values_ref, attended_ref):
@@ -382,22 +377,31 @@
     peer_rows = lax.ppermute(activations, "seq", swap)
 
     def own_work(activations, conv_taps, gate_in, gate_out):
-        part, *held = own_project(activations, conv_taps, gate_in)
-        return partial_logits(*head_sum(part), gate_out, 0), held
+        kept, given, *held = own_project(activations, conv_taps, gate_in)
+        return partial_logits(*head_sum(kept, given), gate_out), held
 
     own_share, held = in_one_piece(own_work, activations, conv_taps, gate_in, gate_out)
     peer_rows, own_share, held = lax.optimization_barrier((peer_rows, own_share, held))
-    near, far = peer_project(peer_rows, *held)
+    kept, given = peer_project(peer_rows, *held)
     behind_keys = lax.ppermute(key_vectors, "seq", swap)
     behind_values = lax.ppermute(value_vectors, "seq", swap)
-    near, near_in = head_sum(near)
-    far_share = far_logits(far, gate_out)
-    share = logits_share(own_share, far_share, near, near_in, gate_out)
+    share = logits_share(own_share, *head_sum(kept, given), gate_out)
     share, queries = lax.optimization_barrier((share, queries))
     powers = powers_of(segments, queries, key_vectors, behind_keys)
+    count = lax.axis_size("heads")
+    both = [
+        (seq * count + head, (1 - seq) * count + (head ^ 1))
+        for seq in range(2)
+        for head in range(count)
+    ]
+    shares = (
+        share,
+        exchange_heads(share, 1),
+        lax.ppermute(share, "seq", swap),
+        lax.ppermute(share, ("seq", "heads"), both),
+    )
     weights, own_mass, behind_mass = weights_of(
-        share,
-        lax.ppermute(share, "seq", swap),
+        shares,
         powers,
         segments,
         queries,

time: 32.4 us -> 32.5 us (level)
  waiting for transfers between devices: 11.4 us -> 13.7 us
  starting transfers between devices: 13.2 us -> 11.2 us
    ppermute x6 -> x5, starting transfers between devices: 4.97 us -> 3.55 us  [exchange_heads(): return lax.ppermute(block, 'heads', [(i, i ^ step) for i in range(count)])]
    ppermute x1, waiting for transfers between devices: 2.51 us -> 3.73 us  [pair_device(): peer_rows = lax.ppermute(activations, 'seq', swap)]
    ppermute x0 -> x1, waiting for transfers between devices: none -> 1.17 us  [pair_device(): lax.ppermute(share, ('seq', 'heads'), both)]
    ppermute x1, starting transfers between devices: 1.63 us -> 0.71 us  [pair_device(): key_mass = own_mass + lax.ppermute(behind_mass, 'seq', swap)]
    ppermute x1, waiting for transfers between devices: 0.92 us -> 1.83 us  [pair_device(): key_mass = own_mass + lax.ppermute(behind_mass, 'seq', swap)]
    ppermute x6 -> x5, waiting for transfers between devices: 6.51 us -> 5.88 us  [exchange_heads(): return lax.ppermute(block, 'heads', [(i, i ^ step) for i in range(count)])]
    ppermute x1, waiting for transfers between devices: 1.44 us -> 0.98 us  [pair_device(): lax.ppermute(share, 'seq', swap)]
  transfers between devices with their start and end apart: 11 -> 11, of which waited for: 6 -> 9; matrix products, arithmetic and copies ran while one was open for 0% -> 0% of each run, Pallas kernels for 17% -> 17%
where the time goes in v13:
time: 32.5 us; the launch traced here: 32.3 us
  waiting for transfers between devices  13.7 us (42%)
  starting transfers between devices  11.2 us (34%)
  Pallas kernels  6.19 us (19%)
  between operations  0.69 us (2%)
  other arithmetic  0.56 us (2%)
    ppermute x5, waiting for transfers between devices, exchange_heads(): return lax.ppermute(block, 'heads', [(i, i ^ step) for i in range(count)])  5.88 us
    ppermute x1, waiting for transfers between devices, pair_device(): peer_rows = lax.ppermute(activations, 'seq', swap)  3.73 us
    ppermute x5, starting transfers between devices, exchange_heads(): return lax.ppermute(block, 'heads', [(i, i ^ step) for i in range(count)])  3.55 us
    ppermute x1, starting transfers between devices, pair_device(): peer_rows = lax.ppermute(activations, 'seq', swap)  3 us
    pallas_call x1, Pallas kernels, own_project(): pl.pallas_call(own_project_kernel, out_shape=(jax.ShapeDtypeStruct((done,...  2.55 us
    ppermute x1, waiting for transfers between devices, pair_device(): key_mass = own_mass + lax.ppermute(behind_mass, 'seq', swap)  1.83 us
    ppermute x1, starting transfers between devices, pair_device(): lax.ppermute(share, 'seq', swap)  1.77 us
    ppermute x1, starting transfers between devices, pair_device(): behind_keys = lax.ppermute(key_vectors, 'seq', swap)  1.49 us
  transfers between devices with their start and end apart: 11, of which 9 were waited for; matrix products, arithmetic and copies ran while one was open for 0% of the time, Pallas kernels for 17%

profile of v13, /device:TPU:0, one launch (start us, length us, event | category | flops | bytes accessed | tf_op | source)
XLA Modules:
  0.0 32.3 jit_solution(16434193327441011732)
XLA Ops:
  0.6 3.0 %collective-permute-start.2 = (bf16[128,2048]{1,0:T(8,128)(2,1)}, bf16[128,2048]{1,0:T(8,128)(2,1)S(1)}, u32[]{:S(2)}, u32[]{:S(2)}) collective-permute-start(bf16[128,2048]{1,0:T(8,128)(2,1)} %param.10), channel_id=1, source_target_pairs={{0,16},{16,0},{1,17},{17,1},{2,18},{18,2},{3,19},{19,3},{4,20},{20... | collective-permute-start | bytes 1572872 | tf_op jit(solution)/shard_map/ppermute | solution.py:377
  3.6 8.4 %conditional.1 = (f32[8,112]{1,0:T(8,128)S(1)}, f32[4,2048]{1,0:T(4,128)S(1)}, bf16[2176,512]{1,0:T(8,128)(2,1)S(1)}) conditional(s32[]{:T(128)} %convert_element_type.12, () %tuple.18, (bf16[128,2048]{1,0:T(8,128)(2,1)}, bf16[4,2048]{1,0:T(4,128)(2,1)}, bf16[2048,512]{1,0:T(8,128)(2,1)}, bf16[8,1024]{1,0:T(8,128)(2,1)}) %tuple.27), branch_computations={%region_0.0_spmd, %region_1.0_spmd} | conditional | flops 57345 | bytes 2264610 | solution.py:148
  3.6 0.0 copy-start.5
  3.6 2.6 %branch_1_fun.2 = (f32[112,256]{1,0:T(8,128)S(1)}, f32[112,256]{1,0:T(8,128)S(1)}, f32[4,2048]{1,0:T(4,128)S(1)}, bf16[2176,512]{1,0:T(8,128)(2,1)S(1)}) custom-call(bf16[128,2048]{1,0:T(8,128)(2,1)} %get-tuple-element.8.rows_ref, bf16[4,2048]{1,0:T(4,128)(2,1)} %get-tuple-element.48.taps_ref, bf16[2048,512]{1,0:T(8,128)(2,1)} %get-tuple-element.49.gate_ref), custom_call_target="tpu_custom_call" | custom-call | flops 1 | bytes 1 | tf_op jit(solution)/shard_map/cond/branch_1_fun/pallas_call | solution.py:95
  6.2 0.1 collective-permute-start
  6.3 1.3 %collective-permute-done = f32[112,256]{1,0:T(8,128)S(1)} collective-permute-done((f32[112,256]{1,0:T(8,128)S(1)}, f32[112,256]{1,0:T(8,128)S(1)}, u32[]{:S(2)}, u32[]{:S(2)}) %collective-permute-start) | collective-permute-done | bytes 114720 | tf_op jit(solution)/shard_map/cond/branch_1_fun/ppermute | solution.py:133
  7.6 1.6 %collective-permute-start.1 = (bf16[112,256]{1,0:T(8,128)(2,1)S(1)}, bf16[112,256]{1,0:T(8,128)(2,1)S(1)}, u32[]{:S(2)}, u32[]{:S(2)}) collective-permute-start(bf16[112,256]{1,0:T(8,128)(2,1)S(1)} %get-tuple-element.50), channel_id=1, source_target_pairs={{0,8},{4,12},{8,0},{12,4},{1,9},{5,13},{9,1},{13,5},{2,10},{6,14},... | collective-permute-start | bytes 172040 | tf_op jit(solution)/shard_map/cond/branch_1_fun/ppermute | solution.py:133
  9.2 2.7 %collective-permute-done.1.in_ref = bf16[112,256]{1,0:T(8,128)(2,1)S(1)} collective-permute-done((bf16[112,256]{1,0:T(8,128)(2,1)S(1)}, bf16[112,256]{1,0:T(8,128)(2,1)S(1)}, u32[]{:S(2)}, u32[]{:S(2)}) %collective-permute-start.1) | collective-permute-done | bytes 57376 | tf_op jit(solution)/shard_map/cond/branch_1_fun/ppermute | solution.py:133
  11.8 0.0 copy-done.5
  11.8 0.2 branch_1_fun.3
  12.0 0.0 copy-start.1
  12.0 0.0 copy-start.2
  12.0 0.0 copy-start.4
  12.0 0.0 copy-start
  12.0 0.0 copy-start.3
  12.0 3.7 %collective-permute-done.2.peer_ref = bf16[128,2048]{1,0:T(8,128)(2,1)S(1)} collective-permute-done((bf16[128,2048]{1,0:T(8,128)(2,1)}, bf16[128,2048]{1,0:T(8,128)(2,1)S(1)}, u32[]{:S(2)}, u32[]{:S(2)}) %collective-permute-start.2) | collective-permute-done | bytes 524320 | tf_op jit(solution)/shard_map/ppermute | solution.py:377
  15.8 0.8 %shard_map.97 = (f32[144,256]{1,0:T(8,128)S(1)}, f32[144,256]{1,0:T(8,128)S(1)}) custom-call(bf16[128,2048]{1,0:T(8,128)(2,1)S(1)} %collective-permute-done.2.peer_ref, f32[4,2048]{1,0:T(4,128)S(1)} %get-tuple-element.37.taps_ref, bf16[2176,512]{1,0:T(8,128)(2,1)S(1)} %get-tuple-element.38.held_ref), custom_call_target="tpu_custom_call" | custom-call | flops 1 | bytes 1 | tf_op jit(solution)/shard_map/pallas_call | solution.py:116
  16.5 0.1 collective-permute-start.3
  16.6 1.4 %collective-permute-done.3 = f32[144,256]{1,0:T(8,128)S(1)} collective-permute-done((f32[144,256]{1,0:T(8,128)S(1)}, f32[144,256]{1,0:T(8,128)S(1)}, u32[]{:S(2)}, u32[]{:S(2)}) %collective-permute-start.3) | collective-permute-done | bytes 147488 | tf_op jit(solution)/shard_map/ppermute | solution.py:133
  18.0 1.8 %collective-permute-start.4 = (bf16[144,256]{1,0:T(8,128)(2,1)S(1)}, bf16[144,256]{1,0:T(8,128)(2,1)S(1)}, u32[]{:S(2)}, u32[]{:S(2)}) collective-permute-start(bf16[144,256]{1,0:T(8,128)(2,1)S(1)} %get-tuple-element.52), channel_id=1, source_target_pairs={{0,8},{4,12},{8,0},{12,4},{1,9},{5,13},{9,1},{13,5},{2,10},{6,14},... | collective-permute-start | bytes 221192 | tf_op jit(solution)/shard_map/ppermute | solution.py:133
  19.8 0.0 copy-done.1
  19.8 1.5 %collective-permute-start.8 = (bf16[128,256]{1,0:T(8,128)(2,1)S(1)}, bf16[128,256]{1,0:T(8,128)(2,1)S(1)}, u32[]{:S(2)}, u32[]{:S(2)}) collective-permute-start(bf16[128,256]{1,0:T(8,128)(2,1)S(1)} %copy-done.1), channel_id=1, source_target_pairs={{0,16},{16,0},{1,17},{17,1},{2,18},{18,2},{3,19},{19,3},{4,20},{20... | collective-permute-start | bytes 196616 | tf_op jit(solution)/shard_map/ppermute | solution.py:386
  21.3 0.0 copy-done.2
  21.3 0.5 %collective-permute-start.9 = (bf16[128,256]{1,0:T(8,128)(2,1)S(1)}, bf16[128,256]{1,0:T(8,128)(2,1)S(1)}, u32[]{:S(2)}, u32[]{:S(2)}) collective-permute-start(bf16[128,256]{1,0:T(8,128)(2,1)S(1)} %copy-done.2), channel_id=1, source_target_pairs={{0,16},{16,0},{1,17},{17,1},{2,18},{18,2},{3,19},{19,3},{4,20},{20... | collective-permute-start | bytes 196616 | tf_op jit(solution)/shard_map/ppermute | solution.py:387
  21.9 0.6 %collective-permute-done.4.in_ref = bf16[144,256]{1,0:T(8,128)(2,1)S(1)} collective-permute-done((bf16[144,256]{1,0:T(8,128)(2,1)S(1)}, bf16[144,256]{1,0:T(8,128)(2,1)S(1)}, u32[]{:S(2)}, u32[]{:S(2)}) %collective-permute-start.4) | collective-permute-done | bytes 73760 | tf_op jit(solution)/shard_map/ppermute | solution.py:133
  22.4 0.0 copy-done.4
  22.4 0.3 shard_map.98.share_ref
  22.7 0.0 collective-permute-start.5
  22.7 1.8 %collective-permute-start.6 = (f32[2,8,128]{2,1,0:T(8,128)S(1)}, f32[2,8,128]{2,1,0:T(8,128)S(1)}, u32[]{:S(2)}, u32[]{:S(2)}) collective-permute-start(f32[2,8,128]{2,1,0:T(8,128)S(1)} %shard_map.98.share_ref), channel_id=1, source_target_pairs={{0,16},{16,0},{1,17},{17,1},{2,18},{18,2},{3,19},{19,3},{4,20},{20... | collective-permute-start | bytes 24584 | tf_op jit(solution)/shard_map/ppermute | solution.py:400
  24.5 0.1 collective-permute-start.7
  24.6 0.1 collective-permute-done.8.behind_keys_ref
  24.7 0.0 copy-done
  24.7 0.0 copy-done.3
  24.7 0.7 %shard_map.99.powers_ref = f32[16,128,256]{2,1,0:T(8,128)S(1)} custom-call(s32[2,128]{1,0:T(2,128)S(1)} %bitcast.2, bf16[128,2048]{1,0:T(8,128)(2,1)S(1)} %copy-done, bf16[128,256]{1,0:T(8,128)(2,1)S(1)} %copy-done.1, bf16[128,256]{1,0:T(8,128)(2,1)S(1)} %collective-permute-done.8.behind_keys_ref), custom_call_target="tpu_custom_call" | custom-call | flops 134217728 | bytes 2097152 | tf_op jit(solution)/shard_map/pallas_call | solution.py:253
  25.4 0.0 collective-permute-done.5.core_share_ref
  25.4 1.0 %collective-permute-done.6.peer_share_ref = f32[2,8,128]{2,1,0:T(8,128)S(1)} collective-permute-done((f32[2,8,128]{2,1,0:T(8,128)S(1)}, f32[2,8,128]{2,1,0:T(8,128)S(1)}, u32[]{:S(2)}, u32[]{:S(2)}) %collective-permute-start.6) | collective-permute-done | bytes 8224 | tf_op jit(solution)/shard_map/ppermute | solution.py:400
  26.4 1.2 %collective-permute-done.7.peer_core_share_ref = f32[2,8,128]{2,1,0:T(8,128)S(1)} collective-permute-done((f32[2,8,128]{2,1,0:T(8,128)S(1)}, f32[2,8,128]{2,1,0:T(8,128)S(1)}, u32[]{:S(2)}, u32[]{:S(2)}) %collective-permute-start.7) | collective-permute-done | bytes 8224 | tf_op jit(solution)/shard_map/ppermute | solution.py:401
  27.5 0.6 %shard_map.100 = (bf16[16,128,256]{2,1,0:T(8,128)(2,1)S(1)}, f32[2,128]{1,0:T(2,128)S(1)}, f32[2,128]{1,0:T(2,128)S(1)}) custom-call(f32[2,8,128]{2,1,0:T(8,128)S(1)} %shard_map.98.share_ref, f32[2,8,128]{2,1,0:T(8,128)S(1)} %collective-permute-done.5.core_share_ref, f32[2,8,128]{2,1,0:T(8,128)S(1)} %collective-permute-done.6.peer_share_ref, ...), custom_call_target="tpu_custom_call" | custom-call | tf_op jit(solution)/shard_map/pallas_call | solution.py:330
  28.2 0.7 %collective-permute-start.10 = (f32[2,128]{1,0:T(2,128)S(1)}, f32[2,128]{1,0:T(2,128)S(1)}, u32[]{:S(2)}, u32[]{:S(2)}) collective-permute-start(f32[2,128]{1,0:T(2,128)S(1)} %get-tuple-element.45), channel_id=1, source_target_pairs={{0,16},{16,0},{1,17},{17,1},{2,18},{18,2},{3,19},{19,3},{4,20},{20... | collective-permute-start | bytes 3080 | tf_op jit(solution)/shard_map/ppermute | solution.py:412
  28.9 0.0 collective-permute-done.9.behind_values_ref
  28.9 1.1 %shard_map.101 = bf16[128,2048]{1,0:T(8,128)(2,1)} custom-call(bf16[16,128,256]{2,1,0:T(8,128)(2,1)S(1)} %get-tuple-element.43.weights_ref, bf16[128,256]{1,0:T(8,128)(2,1)S(1)} %copy-done.2, bf16[128,256]{1,0:T(8,128)(2,1)S(1)} %collective-permute-done.9.behind_values_ref), custom_call_target="tpu_custom_call" | custom-call | flops 134217728 | bytes 1572864 | tf_op jit(solution)/shard_map/pallas_call | solution.py:357
  30.0 1.8 %collective-permute-done.10 = f32[2,128]{1,0:T(2,128)S(1)} collective-permute-done((f32[2,128]{1,0:T(2,128)S(1)}, f32[2,128]{1,0:T(2,128)S(1)}, u32[]{:S(2)}, u32[]{:S(2)}) %collective-permute-start.10) | collective-permute-done | bytes 1056 | tf_op jit(solution)/shard_map/ppermute | solution.py:412
  31.8 0.5 %add_convert_fusion = bf16[2,128]{1,0:T(2,128)(2,1)} fusion(f32[2,128]{1,0:T(2,128)S(1)} %get-tuple-element.44, f32[2,128]{1,0:T(2,128)S(1)} %collective-permute-done.10), kind=kLoop, calls=%fused_computation | loop fusion | flops 512 | bytes 2560 | tf_op jit(solution)/shard_map/convert_element_type | solution.py:413
  (2 shorter events, 0.0 us)
Async XLA Ops:
  0.6 15.1 %collective-permute-start.2 = (bf16[128,2048]{1,0:T(8,128)(2,1)}, bf16[128,2048]{1,0:T(8,128)(2,1)S(1)}, u32[]{:S(2)}, u32[]{:S(2)}) collective-permute-start(bf16[128,2048]{1,0:T(8,128)(2,1)} %param.10), channel_id=1, source_target_pairs={{0,16},{16,0},{1,17},{17,1},{2,18},{18,2},{3,19},{19,3},{4,20},{20... | collective-permute-start | bytes 1572872 | tf_op jit(solution)/shard_map/ppermute | solution.py:377
  3.6 8.2 %copy-start.5 = (bf16[8,1024]{1,0:T(8,128)(2,1)S(1)}, bf16[8,1024]{1,0:T(8,128)(2,1)}, u32[]{:S(2)}) copy-start(bf16[8,1024]{1,0:T(8,128)(2,1)} %get-tuple-element.13.gate_out_ref) | copy-start | bytes 49156 | tf_op jit(solution)/shard_map/cond
  6.2 1.4 %collective-permute-start = (f32[112,256]{1,0:T(8,128)S(1)}, f32[112,256]{1,0:T(8,128)S(1)}, u32[]{:S(2)}, u32[]{:S(2)}) collective-permute-start(f32[112,256]{1,0:T(8,128)S(1)} %get-tuple-element.12), channel_id=1, source_target_pairs={{0,4},{4,0},{8,12},{12,8},{1,5},{5,1},{9,13},{13,9},{2,6},{6,2},{1... | collective-permute-start | bytes 344072 | tf_op jit(solution)/shard_map/cond/branch_1_fun/ppermute | solution.py:133
  7.6 4.2 %collective-permute-start.1 = (bf16[112,256]{1,0:T(8,128)(2,1)S(1)}, bf16[112,256]{1,0:T(8,128)(2,1)S(1)}, u32[]{:S(2)}, u32[]{:S(2)}) collective-permute-start(bf16[112,256]{1,0:T(8,128)(2,1)S(1)} %get-tuple-element.50), channel_id=1, source_target_pairs={{0,8},{4,12},{8,0},{12,4},{1,9},{5,13},{9,1},{13,5},{2,10},{6,14},... | collective-permute-start | bytes 172040 | tf_op jit(solution)/shard_map/cond/branch_1_fun/ppermute | solution.py:133
  12.0 7.8 %copy-start.1 = (bf16[128,256]{1,0:T(8,128)(2,1)S(1)}, bf16[128,256]{1,0:T(8,128)(2,1)}, u32[]{:S(2)}) copy-start(bf16[128,256]{1,0:T(8,128)(2,1)} %keys_ref.3) | copy-start | bytes 196612
  12.0 9.3 %copy-start.2 = (bf16[128,256]{1,0:T(8,128)(2,1)S(1)}, bf16[128,256]{1,0:T(8,128)(2,1)}, u32[]{:S(2)}) copy-start(bf16[128,256]{1,0:T(8,128)(2,1)} %values_ref.1) | copy-start | bytes 196612
  12.0 10.4 %copy-start.4 = (bf16[1024,8]{0,1:T(8,128)(2,1)S(1)}, bf16[1024,8]{0,1:T(8,128)(2,1)}, u32[]{:S(2)}) copy-start(bf16[1024,8]{0,1:T(8,128)(2,1)} %param.13) | copy-start | bytes 49156
  12.0 12.7 %copy-start = (bf16[128,2048]{1,0:T(8,128)(2,1)S(1)}, bf16[128,2048]{1,0:T(8,128)(2,1)}, u32[]{:S(2)}) copy-start(bf16[128,2048]{1,0:T(8,128)(2,1)} %queries_ref.1) | copy-start | bytes 1572868
  12.0 12.7 %copy-start.3 = (s32[256]{0:T(256)S(1)}, s32[256]{0:T(256)}, u32[]{:S(2)}) copy-start(s32[256]{0:T(256)} %param.17) | copy-start | bytes 3076
  16.5 1.4 %collective-permute-start.3 = (f32[144,256]{1,0:T(8,128)S(1)}, f32[144,256]{1,0:T(8,128)S(1)}, u32[]{:S(2)}, u32[]{:S(2)}) collective-permute-start(f32[144,256]{1,0:T(8,128)S(1)} %get-tuple-element.40), channel_id=1, source_target_pairs={{0,4},{4,0},{8,12},{12,8},{1,5},{5,1},{9,13},{13,9},{2,6},{6,2},{1... | collective-permute-start | bytes 442376 | tf_op jit(solution)/shard_map/ppermute | solution.py:133
  18.0 4.4 %collective-permute-start.4 = (bf16[144,256]{1,0:T(8,128)(2,1)S(1)}, bf16[144,256]{1,0:T(8,128)(2,1)S(1)}, u32[]{:S(2)}, u32[]{:S(2)}) collective-permute-start(bf16[144,256]{1,0:T(8,128)(2,1)S(1)} %get-tuple-element.52), channel_id=1, source_target_pairs={{0,8},{4,12},{8,0},{12,4},{1,9},{5,13},{9,1},{13,5},{2,10},{6,14},... | collective-permute-start | bytes 221192 | tf_op jit(solution)/shard_map/ppermute | solution.py:133
  19.8 4.9 %collective-permute-start.8 = (bf16[128,256]{1,0:T(8,128)(2,1)S(1)}, bf16[128,256]{1,0:T(8,128)(2,1)S(1)}, u32[]{:S(2)}, u32[]{:S(2)}) collective-permute-start(bf16[128,256]{1,0:T(8,128)(2,1)S(1)} %copy-done.1), channel_id=1, source_target_pairs={{0,16},{16,0},{1,17},{17,1},{2,18},{18,2},{3,19},{19,3},{4,20},{20... | collective-permute-start | bytes 196616 | tf_op jit(solution)/shard_map/ppermute | solution.py:386
  21.3 7.6 %collective-permute-start.9 = (bf16[128,256]{1,0:T(8,128)(2,1)S(1)}, bf16[128,256]{1,0:T(8,128)(2,1)S(1)}, u32[]{:S(2)}, u32[]{:S(2)}) collective-permute-start(bf16[128,256]{1,0:T(8,128)(2,1)S(1)} %copy-done.2), channel_id=1, source_target_pairs={{0,16},{16,0},{1,17},{17,1},{2,18},{18,2},{3,19},{19,3},{4,20},{20... | collective-permute-start | bytes 196616 | tf_op jit(solution)/shard_map/ppermute | solution.py:387
  22.7 2.7 %collective-permute-start.5 = (f32[2,8,128]{2,1,0:T(8,128)S(1)}, f32[2,8,128]{2,1,0:T(8,128)S(1)}, u32[]{:S(2)}, u32[]{:S(2)}) collective-permute-start(f32[2,8,128]{2,1,0:T(8,128)S(1)} %shard_map.98.share_ref), channel_id=1, source_target_pairs={{0,4},{4,0},{8,12},{12,8},{1,5},{5,1},{9,13},{13,9},{2,6},{6,2},{1... | collective-permute-start | bytes 24584 | tf_op jit(solution)/shard_map/ppermute | solution.py:133
  22.7 3.7 %collective-permute-start.6 = (f32[2,8,128]{2,1,0:T(8,128)S(1)}, f32[2,8,128]{2,1,0:T(8,128)S(1)}, u32[]{:S(2)}, u32[]{:S(2)}) collective-permute-start(f32[2,8,128]{2,1,0:T(8,128)S(1)} %shard_map.98.share_ref), channel_id=1, source_target_pairs={{0,16},{16,0},{1,17},{17,1},{2,18},{18,2},{3,19},{19,3},{4,20},{20... | collective-permute-start | bytes 24584 | tf_op jit(solution)/shard_map/ppermute | solution.py:400
  24.5 3.1 %collective-permute-start.7 = (f32[2,8,128]{2,1,0:T(8,128)S(1)}, f32[2,8,128]{2,1,0:T(8,128)S(1)}, u32[]{:S(2)}, u32[]{:S(2)}) collective-permute-start(f32[2,8,128]{2,1,0:T(8,128)S(1)} %shard_map.98.share_ref), channel_id=1, source_target_pairs={{0,20},{4,16},{8,28},{12,24},{16,4},{20,0},{24,12},{28,8},{1,21},{... | collective-permute-start | bytes 24584 | tf_op jit(solution)/shard_map/ppermute | solution.py:401
  28.2 3.6 %collective-permute-start.10 = (f32[2,128]{1,0:T(2,128)S(1)}, f32[2,128]{1,0:T(2,128)S(1)}, u32[]{:S(2)}, u32[]{:S(2)}) collective-permute-start(f32[2,128]{1,0:T(2,128)S(1)} %get-tuple-element.45), channel_id=1, source_target_pairs={{0,16},{16,0},{1,17},{17,1},{2,18},{18,2},{3,19},{19,3},{4,20},{20... | collective-permute-start | bytes 3080 | tf_op jit(solution)/shard_map/ppermute | solution.py:412

commit v14 on v13

--- a/solution.py
+++ b/solution.py
@@ -262,66 +262,82 @@
     )(segments, queries, keys, behind_keys)
 
 
-def weights_kernel(
-    share_ref,
-    core_share_ref,
-    peer_share_ref,
-    peer_core_share_ref,
-    powers_ref,
-    segments_ref,
-    queries_ref,
-    keys_ref,
-    behind_keys_ref,
-    weights_ref,
-    own_mass_ref,
-    behind_mass_ref,
-    retention,
-):
+def read_retention(share_refs, retention):
     seq_rank, head_rank = lax.axis_index("seq"), lax.axis_index("heads")
-    rows = queries_ref.shape[0]
-    kv_local = keys_ref.shape[1] // HEAD_DIM
-    group_size = queries_ref.shape[1] // keys_ref.shape[1]
-    logits = share_ref[...] + core_share_ref[...]
-    logits = logits + (peer_share_ref[...] + peer_core_share_ref[...])
+    logits = share_refs[0][...] + share_refs[1][...]
+    logits = logits + (share_refs[2][...] + share_refs[3][...])
     log_gate = jnp.minimum(logits, 0.0) - jnp.log1p(jnp.exp(-jnp.abs(logits)))
     retention[...] = log_gate.astype(jnp.bfloat16).astype(jnp.float32)
+    kv_local = retention.shape[1] // lax.axis_size("heads")
     biases = []
     for g in range(kv_local):
         at = pl.ds(head_rank * kv_local + g, 1)
         biases.append(jnp.concatenate([retention[0, at, :], retention[seq_rank, at, :]], axis=1))
+    return biases
+
+
+def weigh(whole, biases, powers_ref, segments_ref, queries_ref, keys_ref, behind_keys_ref, use):
+    seq_rank = lax.axis_index("seq")
+    rows = queries_ref.shape[0]
+    group_size = queries_ref.shape[1] // keys_ref.shape[1]
+    start = 0 if whole else rows
     moderate = jnp.min(functools.reduce(jnp.minimum, biases)) >= LEAST_RETENTION
 
-    def finish(whole, terms_of):
-        start = 0 if whole else rows
-        for g in range(kv_local):
+    def finish(terms_of, store_mass):
+        for g in range(len(biases)):
             mass = jnp.zeros((1, 2 * rows - start), jnp.float32)
-            group_terms = terms_of(g, whole, start)
+            group_terms = terms_of(g)
             for head in range(g * group_size, (g + 1) * group_size):
                 weights = group_terms(head)
                 weights = weights * (1.0 / jnp.sum(weights, axis=1, keepdims=True))
                 mass = mass + jnp.sum(weights, axis=0, keepdims=True)
-                weights_ref[head, :, start:] = weights.astype(jnp.bfloat16)
-            mass = mass / group_size
-            own_mass_ref[g : g + 1, :] = mass[:, rows - start :]
-            behind_mass_ref[g : g + 1, :] = mass[:, :rows] if whole else jnp.zeros((1, rows))
-
-    def by_powers(g, whole, start):
+                use(head, weights.astype(jnp.bfloat16))
+            store_mass(g, mass / group_size)
+
+    def by_powers(g):
         factor = jnp.exp(biases[g] - jnp.max(biases[g]))[:, start:]
         return lambda head: powers_ref[head, :, start:] * factor
 
-    def by_scores(g, whole, start):
-        offset = hide_unseen(seq_rank, segments_ref, rows) + biases[g]
+    def by_scores(g):
+        offset = (hide_unseen(seq_rank, segments_ref, rows) + biases[g])[:, start:]
         keys = with_behind(keys_ref, behind_keys_ref, g, whole)
 
         def terms(head):
-            scores = scores_of(queries_ref, keys, offset[:, start:], head)
+            scores = scores_of(queries_ref, keys, offset, head)
             return jnp.exp(scores - jnp.max(scores, axis=1, keepdims=True))
 
         return terms
 
-    pl.when(moderate & (seq_rank > 0))(lambda: finish(True, by_powers))
-    pl.when(moderate & (seq_rank == 0))(lambda: finish(False, by_powers))
-    pl.when(jnp.logical_not(moderate))(lambda: finish(True, by_scores))
+    def run(store_mass):
+        pl.when(moderate)(lambda: finish(by_powers, store_mass))
+        pl.when(jnp.logical_not(moderate))(lambda: finish(by_scores, store_mass))
+
+    return run
+
+
+def weights_kernel(*refs):
+    *share_refs, powers_ref, segments_ref, queries_ref, keys_ref, behind_keys_ref = refs[:9]
+    weights_ref, own_mass_ref, behind_mass_ref, retention = refs[9:]
+    rows = queries_ref.shape[0]
+
+    def whole():
+        def use(head, weights):
+            weights_ref[head] = weights
+
+        def store_mass(g, mass):
+            behind_mass_ref[g : g + 1, :] = mass[:, :rows]
+            own_mass_ref[g : g + 1, :] = mass[:, rows:]
+
+        biases = read_retention(share_refs, retention)
+        weigh(
+            True, biases, powers_ref, segments_ref, queries_ref, keys_ref, behind_keys_ref, use
+        )(store_mass)
+
+    def nothing():
+        behind_mass_ref[...] = jnp.zeros(behind_mass_ref.shape, jnp.float32)
+
+    pl.when(lax.axis_index("seq") > 0)(whole)
+    pl.when(lax.axis_index("seq") == 0)(nothing)
 
 
 def weights_of(shares, powers, segments, queries, keys, behind_keys):
@@ -335,35 +351,55 @@
     )(*shares, powers, segments, queries, keys, behind_keys)
 
 
-def attend_kernel(weights_ref, values_ref, behind_values_ref, attended_ref):
-    seq_rank = lax.axis_index("seq")
-    heads, rows = weights_ref.shape[:2]
+def attend_kernel(*refs):
+    *share_refs, powers_ref, segments_ref, queries_ref, keys_ref, behind_keys_ref = refs[:9]
+    weights_ref, mass_ref, values_ref, behind_values_ref = refs[9:13]
+    attended_ref, own_mass_ref, retention = refs[13:]
     group_size = attended_ref.shape[1] // values_ref.shape[1]
 
-    def fill(whole):
-        start = 0 if whole else rows
-        for head in range(heads):
-            values = with_behind(values_ref, behind_values_ref, head // group_size, whole)
-            attended_ref[:, head_columns(head)] = jnp.dot(
-                weights_ref[head, :, start:], values, preferred_element_type=jnp.float32
-            ).astype(jnp.bfloat16)
-
-    pl.when(seq_rank > 0)(lambda: fill(True))
-    pl.when(seq_rank == 0)(lambda: fill(False))
-
-
-def attend(weights, values, behind_values):
-    heads, rows = weights.shape[:2]
+    def attend_head(head, weights, whole):
+        values = with_behind(values_ref, behind_values_ref, head // group_size, whole)
+        attended_ref[:, head_columns(head)] = jnp.dot(
+            weights, values, preferred_element_type=jnp.float32
+        ).astype(jnp.bfloat16)
+
+    def whole():
+        own_mass_ref[...] = mass_ref[...]
+        for head in range(weights_ref.shape[0]):
+            attend_head(head, weights_ref[head], True)
+
+    def alone():
+        def use(head, weights):
+            attend_head(head, weights, False)
+
+        def store_mass(g, mass):
+            own_mass_ref[g : g + 1, :] = mass
+
+        biases = read_retention(share_refs, retention)
+        weigh(
+            False, biases, powers_ref, segments_ref, queries_ref, keys_ref, behind_keys_ref, use
+        )(store_mass)
+
+    pl.when(lax.axis_index("seq") > 0)(whole)
+    pl.when(lax.axis_index("seq") == 0)(alone)
+
+
+def attend(shares, powers, segments, queries, keys, behind_keys, weights, mass, values, behind):
+    rows = queries.shape[0]
     return pl.pallas_call(
         attend_kernel,
-        out_shape=jax.ShapeDtypeStruct((rows, heads * HEAD_DIM), jnp.bfloat16),
+        out_shape=(
+            jax.ShapeDtypeStruct(queries.shape, jnp.bfloat16),
+            jax.ShapeDtypeStruct(mass.shape, jnp.float32),
+        ),
+        scratch_shapes=[pltpu.VMEM(shares[0].shape, jnp.float32)],
         compiler_params=pltpu.CompilerParams(vmem_limit_bytes=VMEM_BYTES),
         cost_estimate=pl.CostEstimate(
-            flops=4 * rows * rows * heads * HEAD_DIM,
-            bytes_accessed=2 * (weights.size + rows * heads * HEAD_DIM),
+            flops=4 * rows * rows * queries.shape[1],
+            bytes_accessed=2 * (weights.size + queries.size),
             transcendentals=0,
         ),
-    )(weights, values, behind_values)
+    )(*shares, powers, segments, queries, keys, behind_keys, weights, mass, values, behind)
 
 
 def pair_device(
@@ -400,15 +436,9 @@
         lax.ppermute(share, "seq", swap),
         lax.ppermute(share, ("seq", "heads"), both),
     )
-    weights, own_mass, behind_mass = weights_of(
-        shares,
-        powers,
-        segments,
-        queries,
-        key_vectors,
-        behind_keys,
-    )
-    attended = attend(weights, value_vectors, behind_values)
+    given = (shares, powers, segments, queries, key_vectors, behind_keys)
+    weights, own_mass, behind_mass = weights_of(*given)
+    attended, own_mass = attend(*given, weights, own_mass, value_vectors, behind_values)
     key_mass = own_mass + lax.ppermute(behind_mass, "seq", swap)
     return (attended, key_mass.astype(jnp.bfloat16))
 

time: 32.5 us -> 31.8 us (0.978)
  waiting for transfers between devices: 13.7 us -> 12.5 us
  starting transfers between devices: 11.2 us -> 11.9 us
    ppermute x1, waiting for transfers between devices: 1.83 us -> 0.65 us  [pair_device(): key_mass = own_mass + lax.ppermute(behind_mass, 'seq', swap)]
    ppermute x1, starting transfers between devices: 0.71 us -> 1.36 us  [pair_device(): key_mass = own_mass + lax.ppermute(behind_mass, 'seq', swap)]
    pallas_call x1, Pallas kernels: 0.64 us -> 0.01 us  [weights_of(): pl.pallas_call(weights_kernel, out_shape=(jax.ShapeDtypeStruct(powers.sha...]
    pallas_call x1, Pallas kernels: 1.09 us -> 1.56 us  [attend(): pl.pallas_call(attend_kernel, out_shape=(jax.ShapeDtypeStruct(queries.sha...]
where the time goes in v14:
time: 31.8 us; the launch traced here: 31.6 us
  waiting for transfers between devices  12.5 us (39%)
  starting transfers between devices  11.9 us (37%)
  Pallas kernels  6.01 us (19%)
  between operations  0.69 us (2%)
  other arithmetic  0.55 us (2%)
    ppermute x5, waiting for transfers between devices, exchange_heads(): return lax.ppermute(block, 'heads', [(i, i ^ step) for i in range(count)])  5.88 us
    ppermute x1, waiting for transfers between devices, pair_device(): peer_rows = lax.ppermute(activations, 'seq', swap)  3.73 us
    ppermute x5, starting transfers between devices, exchange_heads(): return lax.ppermute(block, 'heads', [(i, i ^ step) for i in range(count)])  3.56 us
    ppermute x1, starting transfers between devices, pair_device(): peer_rows = lax.ppermute(activations, 'seq', swap)  3 us
    pallas_call x1, Pallas kernels, own_project(): pl.pallas_call(own_project_kernel, out_shape=(jax.ShapeDtypeStruct((done,...  2.55 us
    ppermute x1, starting transfers between devices, pair_device(): lax.ppermute(share, 'seq', swap)  1.77 us
    pallas_call x1, Pallas kernels, attend(): pl.pallas_call(attend_kernel, out_shape=(jax.ShapeDtypeStruct(queries.sha...  1.56 us
    ppermute x1, starting transfers between devices, pair_device(): behind_keys = lax.ppermute(key_vectors, 'seq', swap)  1.49 us
  transfers between devices with their start and end apart: 11, of which 9 were waited for; matrix products, arithmetic and copies ran while one was open for 0% of the time, Pallas kernels for 17%

profile of v14, /device:TPU:0, one launch (start us, length us, event | category | flops | bytes accessed | tf_op | source)
XLA Modules:
  0.0 31.6 jit_solution(10967630124161114479)
XLA Ops:
  0.6 3.0 %collective-permute-start.2 = (bf16[128,2048]{1,0:T(8,128)(2,1)}, bf16[128,2048]{1,0:T(8,128)(2,1)S(1)}, u32[]{:S(2)}, u32[]{:S(2)}) collective-permute-start(bf16[128,2048]{1,0:T(8,128)(2,1)} %param.10), channel_id=1, source_target_pairs={{0,16},{16,0},{1,17},{17,1},{2,18},{18,2},{3,19},{19,3},{4,20},{20... | collective-permute-start | bytes 1572872 | tf_op jit(solution)/shard_map/ppermute | solution.py:413
  3.6 8.4 %conditional.1 = (f32[8,112]{1,0:T(8,128)S(1)}, f32[4,2048]{1,0:T(4,128)S(1)}, bf16[2176,512]{1,0:T(8,128)(2,1)S(1)}) conditional(s32[]{:T(128)} %convert_element_type.12, () %tuple.18, (bf16[128,2048]{1,0:T(8,128)(2,1)}, bf16[4,2048]{1,0:T(4,128)(2,1)}, bf16[2048,512]{1,0:T(8,128)(2,1)}, bf16[8,1024]{1,0:T(8,128)(2,1)}) %tuple.27), branch_computations={%region_0.0_spmd, %region_1.0_spmd} | conditional | flops 57345 | bytes 2264610 | solution.py:148
  3.6 0.0 copy-start.5
  3.6 2.6 %branch_1_fun.2 = (f32[112,256]{1,0:T(8,128)S(1)}, f32[112,256]{1,0:T(8,128)S(1)}, f32[4,2048]{1,0:T(4,128)S(1)}, bf16[2176,512]{1,0:T(8,128)(2,1)S(1)}) custom-call(bf16[128,2048]{1,0:T(8,128)(2,1)} %get-tuple-element.8.rows_ref, bf16[4,2048]{1,0:T(4,128)(2,1)} %get-tuple-element.52.taps_ref, bf16[2048,512]{1,0:T(8,128)(2,1)} %get-tuple-element.53.gate_ref), custom_call_target="tpu_custom_call" | custom-call | flops 1 | bytes 1 | tf_op jit(solution)/shard_map/cond/branch_1_fun/pallas_call | solution.py:95
  6.2 0.1 collective-permute-start
  6.3 1.3 %collective-permute-done = f32[112,256]{1,0:T(8,128)S(1)} collective-permute-done((f32[112,256]{1,0:T(8,128)S(1)}, f32[112,256]{1,0:T(8,128)S(1)}, u32[]{:S(2)}, u32[]{:S(2)}) %collective-permute-start) | collective-permute-done | bytes 114720 | tf_op jit(solution)/shard_map/cond/branch_1_fun/ppermute | solution.py:133
  7.6 1.6 %collective-permute-start.1 = (bf16[112,256]{1,0:T(8,128)(2,1)S(1)}, bf16[112,256]{1,0:T(8,128)(2,1)S(1)}, u32[]{:S(2)}, u32[]{:S(2)}) collective-permute-start(bf16[112,256]{1,0:T(8,128)(2,1)S(1)} %get-tuple-element.54), channel_id=1, source_target_pairs={{0,8},{4,12},{8,0},{12,4},{1,9},{5,13},{9,1},{13,5},{2,10},{6,14},... | collective-permute-start | bytes 172040 | tf_op jit(solution)/shard_map/cond/branch_1_fun/ppermute | solution.py:133
  9.2 2.7 %collective-permute-done.1.in_ref = bf16[112,256]{1,0:T(8,128)(2,1)S(1)} collective-permute-done((bf16[112,256]{1,0:T(8,128)(2,1)S(1)}, bf16[112,256]{1,0:T(8,128)(2,1)S(1)}, u32[]{:S(2)}, u32[]{:S(2)}) %collective-permute-start.1) | collective-permute-done | bytes 57376 | tf_op jit(solution)/shard_map/cond/branch_1_fun/ppermute | solution.py:133
  11.8 0.0 copy-done.5
  11.8 0.2 branch_1_fun.3
  12.0 0.0 copy-start.1
  12.0 0.0 copy-start.2
  12.0 0.0 copy-start.4
  12.0 0.0 copy-start
  12.0 0.0 copy-start.3
  12.0 3.7 %collective-permute-done.2.peer_ref = bf16[128,2048]{1,0:T(8,128)(2,1)S(1)} collective-permute-done((bf16[128,2048]{1,0:T(8,128)(2,1)}, bf16[128,2048]{1,0:T(8,128)(2,1)S(1)}, u32[]{:S(2)}, u32[]{:S(2)}) %collective-permute-start.2) | collective-permute-done | bytes 524320 | tf_op jit(solution)/shard_map/ppermute | solution.py:413
  15.8 0.8 %shard_map.97 = (f32[144,256]{1,0:T(8,128)S(1)}, f32[144,256]{1,0:T(8,128)S(1)}) custom-call(bf16[128,2048]{1,0:T(8,128)(2,1)S(1)} %collective-permute-done.2.peer_ref, f32[4,2048]{1,0:T(4,128)S(1)} %get-tuple-element.39.taps_ref, bf16[2176,512]{1,0:T(8,128)(2,1)S(1)} %get-tuple-element.40.held_ref), custom_call_target="tpu_custom_call" | custom-call | flops 1 | bytes 1 | tf_op jit(solution)/shard_map/pallas_call | solution.py:116
  16.5 0.1 collective-permute-start.3
  16.6 1.4 %collective-permute-done.3 = f32[144,256]{1,0:T(8,128)S(1)} collective-permute-done((f32[144,256]{1,0:T(8,128)S(1)}, f32[144,256]{1,0:T(8,128)S(1)}, u32[]{:S(2)}, u32[]{:S(2)}) %collective-permute-start.3) | collective-permute-done | bytes 147488 | tf_op jit(solution)/shard_map/ppermute | solution.py:133
  18.0 1.8 %collective-permute-start.4 = (bf16[144,256]{1,0:T(8,128)(2,1)S(1)}, bf16[144,256]{1,0:T(8,128)(2,1)S(1)}, u32[]{:S(2)}, u32[]{:S(2)}) collective-permute-start(bf16[144,256]{1,0:T(8,128)(2,1)S(1)} %get-tuple-element.56), channel_id=1, source_target_pairs={{0,8},{4,12},{8,0},{12,4},{1,9},{5,13},{9,1},{13,5},{2,10},{6,14},... | collective-permute-start | bytes 221192 | tf_op jit(solution)/shard_map/ppermute | solution.py:133
  19.8 0.0 copy-done.1
  19.8 1.5 %collective-permute-start.8 = (bf16[128,256]{1,0:T(8,128)(2,1)S(1)}, bf16[128,256]{1,0:T(8,128)(2,1)S(1)}, u32[]{:S(2)}, u32[]{:S(2)}) collective-permute-start(bf16[128,256]{1,0:T(8,128)(2,1)S(1)} %copy-done.1), channel_id=1, source_target_pairs={{0,16},{16,0},{1,17},{17,1},{2,18},{18,2},{3,19},{19,3},{4,20},{20... | collective-permute-start | bytes 196616 | tf_op jit(solution)/shard_map/ppermute | solution.py:422
  21.3 0.0 copy-done.2
  21.3 0.5 %collective-permute-start.9 = (bf16[128,256]{1,0:T(8,128)(2,1)S(1)}, bf16[128,256]{1,0:T(8,128)(2,1)S(1)}, u32[]{:S(2)}, u32[]{:S(2)}) collective-permute-start(bf16[128,256]{1,0:T(8,128)(2,1)S(1)} %copy-done.2), channel_id=1, source_target_pairs={{0,16},{16,0},{1,17},{17,1},{2,18},{18,2},{3,19},{19,3},{4,20},{20... | collective-permute-start | bytes 196616 | tf_op jit(solution)/shard_map/ppermute | solution.py:423
  21.9 0.6 %collective-permute-done.4.in_ref = bf16[144,256]{1,0:T(8,128)(2,1)S(1)} collective-permute-done((bf16[144,256]{1,0:T(8,128)(2,1)S(1)}, bf16[144,256]{1,0:T(8,128)(2,1)S(1)}, u32[]{:S(2)}, u32[]{:S(2)}) %collective-permute-start.4) | collective-permute-done | bytes 73760 | tf_op jit(solution)/shard_map/ppermute | solution.py:133
  22.4 0.0 copy-done.4
  22.4 0.3 shard_map.98.refs_0_
  22.7 0.0 collective-permute-start.5
  22.7 1.8 %collective-permute-start.6 = (f32[2,8,128]{2,1,0:T(8,128)S(1)}, f32[2,8,128]{2,1,0:T(8,128)S(1)}, u32[]{:S(2)}, u32[]{:S(2)}) collective-permute-start(f32[2,8,128]{2,1,0:T(8,128)S(1)} %shard_map.98.refs_0_), channel_id=1, source_target_pairs={{0,16},{16,0},{1,17},{17,1},{2,18},{18,2},{3,19},{19,3},{4,20},{20... | collective-permute-start | bytes 24584 | tf_op jit(solution)/shard_map/ppermute | solution.py:436
  24.5 0.1 collective-permute-start.7
  24.6 0.1 collective-permute-done.8.behind_keys_ref.refs_8_
  24.7 0.0 copy-done
  24.7 0.0 copy-done.3
  24.7 0.7 %shard_map.99.refs_4_ = f32[16,128,256]{2,1,0:T(8,128)S(1)} custom-call(s32[2,128]{1,0:T(2,128)S(1)} %bitcast.2, bf16[128,2048]{1,0:T(8,128)(2,1)S(1)} %copy-done, bf16[128,256]{1,0:T(8,128)(2,1)S(1)} %copy-done.1, bf16[128,256]{1,0:T(8,128)(2,1)S(1)} %collective-permute-done.8.behind_keys_ref.refs_8_), custom_call_target="tpu_custom_call" | custom-call | flops 134217728 | bytes 2097152 | tf_op jit(solution)/shard_map/pallas_call | solution.py:253
  25.4 0.0 collective-permute-done.5.refs_1_
  25.4 1.0 %collective-permute-done.6.refs_2_ = f32[2,8,128]{2,1,0:T(8,128)S(1)} collective-permute-done((f32[2,8,128]{2,1,0:T(8,128)S(1)}, f32[2,8,128]{2,1,0:T(8,128)S(1)}, u32[]{:S(2)}, u32[]{:S(2)}) %collective-permute-start.6) | collective-permute-done | bytes 8224 | tf_op jit(solution)/shard_map/ppermute | solution.py:436
  26.4 1.2 %collective-permute-done.7.refs_3_ = f32[2,8,128]{2,1,0:T(8,128)S(1)} collective-permute-done((f32[2,8,128]{2,1,0:T(8,128)S(1)}, f32[2,8,128]{2,1,0:T(8,128)S(1)}, u32[]{:S(2)}, u32[]{:S(2)}) %collective-permute-start.7) | collective-permute-done | bytes 8224 | tf_op jit(solution)/shard_map/ppermute | solution.py:437
  27.5 1.4 %collective-permute-start.10 = (f32[2,128]{1,0:T(2,128)S(1)}, f32[2,128]{1,0:T(2,128)S(1)}, u32[]{:S(2)}, u32[]{:S(2)}) collective-permute-start(f32[2,128]{1,0:T(2,128)S(1)} %get-tuple-element.49), channel_id=1, source_target_pairs={{0,16},{16,0},{1,17},{17,1},{2,18},{18,2},{3,19},{19,3},{4,20},{20... | collective-permute-start | bytes 3080 | tf_op jit(solution)/shard_map/ppermute | solution.py:442
  28.9 0.0 collective-permute-done.9.refs_12_
  28.9 1.6 %shard_map.101 = (bf16[128,2048]{1,0:T(8,128)(2,1)}, f32[2,128]{1,0:T(2,128)S(1)}) custom-call(f32[2,8,128]{2,1,0:T(8,128)S(1)} %shard_map.98.refs_0_, f32[2,8,128]{2,1,0:T(8,128)S(1)} %collective-permute-done.5.refs_1_, f32[2,8,128]{2,1,0:T(8,128)S(1)} %collective-permute-done.6.refs_2_, f32[2,8,128]{2,1,0:T(8,128)S(1)} %collective-permute-done.7.refs_3_, ...), custom_call_target="tpu_custom_call" | custom-call | flops 134217728 | bytes 1572864 | tf_op jit(solution)/shard_map/pallas_call | solution.py:389
  30.5 0.6 %collective-permute-done.10 = f32[2,128]{1,0:T(2,128)S(1)} collective-permute-done((f32[2,128]{1,0:T(2,128)S(1)}, f32[2,128]{1,0:T(2,128)S(1)}, u32[]{:S(2)}, u32[]{:S(2)}) %collective-permute-start.10) | collective-permute-done | bytes 1056 | tf_op jit(solution)/shard_map/ppermute | solution.py:442
  31.1 0.5 %add_convert_fusion = bf16[2,128]{1,0:T(2,128)(2,1)} fusion(f32[2,128]{1,0:T(2,128)S(1)} %get-tuple-element.48, f32[2,128]{1,0:T(2,128)S(1)} %collective-permute-done.10), kind=kLoop, calls=%fused_computation | loop fusion | flops 512 | bytes 2560 | tf_op jit(solution)/shard_map/convert_element_type | solution.py:443
  (3 shorter events, 0.0 us)
Async XLA Ops:
  0.6 15.1 %collective-permute-start.2 = (bf16[128,2048]{1,0:T(8,128)(2,1)}, bf16[128,2048]{1,0:T(8,128)(2,1)S(1)}, u32[]{:S(2)}, u32[]{:S(2)}) collective-permute-start(bf16[128,2048]{1,0:T(8,128)(2,1)} %param.10), channel_id=1, source_target_pairs={{0,16},{16,0},{1,17},{17,1},{2,18},{18,2},{3,19},{19,3},{4,20},{20... | collective-permute-start | bytes 1572872 | tf_op jit(solution)/shard_map/ppermute | solution.py:413
  3.6 8.2 %copy-start.5 = (bf16[8,1024]{1,0:T(8,128)(2,1)S(1)}, bf16[8,1024]{1,0:T(8,128)(2,1)}, u32[]{:S(2)}) copy-start(bf16[8,1024]{1,0:T(8,128)(2,1)} %get-tuple-element.13.gate_out_ref) | copy-start | bytes 49156 | tf_op jit(solution)/shard_map/cond
  6.2 1.4 %collective-permute-start = (f32[112,256]{1,0:T(8,128)S(1)}, f32[112,256]{1,0:T(8,128)S(1)}, u32[]{:S(2)}, u32[]{:S(2)}) collective-permute-start(f32[112,256]{1,0:T(8,128)S(1)} %get-tuple-element.12), channel_id=1, source_target_pairs={{0,4},{4,0},{8,12},{12,8},{1,5},{5,1},{9,13},{13,9},{2,6},{6,2},{1... | collective-permute-start | bytes 344072 | tf_op jit(solution)/shard_map/cond/branch_1_fun/ppermute | solution.py:133
  7.6 4.2 %collective-permute-start.1 = (bf16[112,256]{1,0:T(8,128)(2,1)S(1)}, bf16[112,256]{1,0:T(8,128)(2,1)S(1)}, u32[]{:S(2)}, u32[]{:S(2)}) collective-permute-start(bf16[112,256]{1,0:T(8,128)(2,1)S(1)} %get-tuple-element.54), channel_id=1, source_target_pairs={{0,8},{4,12},{8,0},{12,4},{1,9},{5,13},{9,1},{13,5},{2,10},{6,14},... | collective-permute-start | bytes 172040 | tf_op jit(solution)/shard_map/cond/branch_1_fun/ppermute | solution.py:133
  12.0 7.8 %copy-start.1 = (bf16[128,256]{1,0:T(8,128)(2,1)S(1)}, bf16[128,256]{1,0:T(8,128)(2,1)}, u32[]{:S(2)}) copy-start(bf16[128,256]{1,0:T(8,128)(2,1)} %refs_7_.3) | copy-start | bytes 196612
  12.0 9.3 %copy-start.2 = (bf16[128,256]{1,0:T(8,128)(2,1)S(1)}, bf16[128,256]{1,0:T(8,128)(2,1)}, u32[]{:S(2)}) copy-start(bf16[128,256]{1,0:T(8,128)(2,1)} %refs_11_.1) | copy-start | bytes 196612
  12.0 10.4 %copy-start.4 = (bf16[1024,8]{0,1:T(8,128)(2,1)S(1)}, bf16[1024,8]{0,1:T(8,128)(2,1)}, u32[]{:S(2)}) copy-start(bf16[1024,8]{0,1:T(8,128)(2,1)} %param.13) | copy-start | bytes 49156
  12.0 12.7 %copy-start = (bf16[128,2048]{1,0:T(8,128)(2,1)S(1)}, bf16[128,2048]{1,0:T(8,128)(2,1)}, u32[]{:S(2)}) copy-start(bf16[128,2048]{1,0:T(8,128)(2,1)} %refs_6_.1) | copy-start | bytes 1572868
  12.0 12.7 %copy-start.3 = (s32[256]{0:T(256)S(1)}, s32[256]{0:T(256)}, u32[]{:S(2)}) copy-start(s32[256]{0:T(256)} %param.17) | copy-start | bytes 3076
  16.5 1.4 %collective-permute-start.3 = (f32[144,256]{1,0:T(8,128)S(1)}, f32[144,256]{1,0:T(8,128)S(1)}, u32[]{:S(2)}, u32[]{:S(2)}) collective-permute-start(f32[144,256]{1,0:T(8,128)S(1)} %get-tuple-element.42), channel_id=1, source_target_pairs={{0,4},{4,0},{8,12},{12,8},{1,5},{5,1},{9,13},{13,9},{2,6},{6,2},{1... | collective-permute-start | bytes 442376 | tf_op jit(solution)/shard_map/ppermute | solution.py:133
  18.0 4.4 %collective-permute-start.4 = (bf16[144,256]{1,0:T(8,128)(2,1)S(1)}, bf16[144,256]{1,0:T(8,128)(2,1)S(1)}, u32[]{:S(2)}, u32[]{:S(2)}) collective-permute-start(bf16[144,256]{1,0:T(8,128)(2,1)S(1)} %get-tuple-element.56), channel_id=1, source_target_pairs={{0,8},{4,12},{8,0},{12,4},{1,9},{5,13},{9,1},{13,5},{2,10},{6,14},... | collective-permute-start | bytes 221192 | tf_op jit(solution)/shard_map/ppermute | solution.py:133
  19.8 4.9 %collective-permute-start.8 = (bf16[128,256]{1,0:T(8,128)(2,1)S(1)}, bf16[128,256]{1,0:T(8,128)(2,1)S(1)}, u32[]{:S(2)}, u32[]{:S(2)}) collective-permute-start(bf16[128,256]{1,0:T(8,128)(2,1)S(1)} %copy-done.1), channel_id=1, source_target_pairs={{0,16},{16,0},{1,17},{17,1},{2,18},{18,2},{3,19},{19,3},{4,20},{20... | collective-permute-start | bytes 196616 | tf_op jit(solution)/shard_map/ppermute | solution.py:422
  21.3 7.6 %collective-permute-start.9 = (bf16[128,256]{1,0:T(8,128)(2,1)S(1)}, bf16[128,256]{1,0:T(8,128)(2,1)S(1)}, u32[]{:S(2)}, u32[]{:S(2)}) collective-permute-start(bf16[128,256]{1,0:T(8,128)(2,1)S(1)} %copy-done.2), channel_id=1, source_target_pairs={{0,16},{16,0},{1,17},{17,1},{2,18},{18,2},{3,19},{19,3},{4,20},{20... | collective-permute-start | bytes 196616 | tf_op jit(solution)/shard_map/ppermute | solution.py:423
  22.7 2.7 %collective-permute-start.5 = (f32[2,8,128]{2,1,0:T(8,128)S(1)}, f32[2,8,128]{2,1,0:T(8,128)S(1)}, u32[]{:S(2)}, u32[]{:S(2)}) collective-permute-start(f32[2,8,128]{2,1,0:T(8,128)S(1)} %shard_map.98.refs_0_), channel_id=1, source_target_pairs={{0,4},{4,0},{8,12},{12,8},{1,5},{5,1},{9,13},{13,9},{2,6},{6,2},{1... | collective-permute-start | bytes 24584 | tf_op jit(solution)/shard_map/ppermute | solution.py:133
  22.7 3.7 %collective-permute-start.6 = (f32[2,8,128]{2,1,0:T(8,128)S(1)}, f32[2,8,128]{2,1,0:T(8,128)S(1)}, u32[]{:S(2)}, u32[]{:S(2)}) collective-permute-start(f32[2,8,128]{2,1,0:T(8,128)S(1)} %shard_map.98.refs_0_), channel_id=1, source_target_pairs={{0,16},{16,0},{1,17},{17,1},{2,18},{18,2},{3,19},{19,3},{4,20},{20... | collective-permute-start | bytes 24584 | tf_op jit(solution)/shard_map/ppermute | solution.py:436
  24.5 3.1 %collective-permute-start.7 = (f32[2,8,128]{2,1,0:T(8,128)S(1)}, f32[2,8,128]{2,1,0:T(8,128)S(1)}, u32[]{:S(2)}, u32[]{:S(2)}) collective-permute-start(f32[2,8,128]{2,1,0:T(8,128)S(1)} %shard_map.98.refs_0_), channel_id=1, source_target_pairs={{0,20},{4,16},{8,28},{12,24},{16,4},{20,0},{24,12},{28,8},{1,21},{... | collective-permute-start | bytes 24584 | tf_op jit(solution)/shard_map/ppermute | solution.py:437
  27.5 3.6 %collective-permute-start.10 = (f32[2,128]{1,0:T(2,128)S(1)}, f32[2,128]{1,0:T(2,128)S(1)}, u32[]{:S(2)}, u32[]{:S(2)}) collective-permute-start(f32[2,128]{1,0:T(2,128)S(1)} %get-tuple-element.49), channel_id=1, source_target_pairs={{0,16},{16,0},{1,17},{17,1},{2,18},{18,2},{3,19},{19,3},{4,20},{20... | collective-permute-start | bytes 3080 | tf_op jit(solution)/shard_map/ppermute | solution.py:442

commit v15 on v14

--- a/solution.py
+++ b/solution.py
@@ -26,22 +26,12 @@
     return summed.astype(jnp.bfloat16)
 
 
-def split_by_core(total, kept_ref, given_ref):
-    half = kept_ref.shape[1]
-    low, high = total[:, :half], total[:, half:]
-    even = lax.rem(lax.axis_index("heads"), 2) == 0
-    kept_ref[...] = jnp.where(even, low, high)
-    given_ref[...] = jnp.where(even, high, low)
-
-
-def own_project_kernel(
-    rows_ref, taps_ref, gate_ref, kept_ref, given_ref, held_taps_ref, held_ref, widened
-):
+def own_project_kernel(rows_ref, taps_ref, gate_ref, out_ref, held_taps_ref, held_ref, widened):
     rows, features = rows_ref.shape
     held_taps_ref[...] = taps_ref[...].astype(jnp.float32)
     held_ref[:features] = gate_ref[...]
     tile = widened.shape[2]
-    total = jnp.zeros((rows - RIM_ROWS, gate_ref.shape[1]), jnp.float32)
+    total = jnp.zeros(out_ref.shape, jnp.float32)
     for step in range(features // tile):
         columns = slice(step * tile, (step + 1) * tile)
         edges = features + step * 2 * RIM_ROWS
@@ -54,16 +44,17 @@
         taps = taps_ref[:, columns].astype(jnp.float32)
         mixed = convolve(wide, taps, RIM_ROWS, rows - RIM_ROWS)
         total = total + jnp.dot(mixed, gate_ref[columns, :], preferred_element_type=jnp.float32)
-    split_by_core(total, kept_ref, given_ref)
+    out_ref[...] = total
 
 
 def peer_project_kernel(
-    peer_ref, taps_ref, held_ref, kept_ref, given_ref, widened, own_widened
+    peer_ref, taps_ref, held_ref, near_ref, far_ref, widened, own_widened
 ):
     rows, features = peer_ref.shape
     tile = widened.shape[2]
     first = lax.axis_index("seq") == 0
-    total = jnp.zeros((kept_ref.shape[0], held_ref.shape[1]), jnp.float32)
+    half = near_ref.shape[1]
+    total = jnp.zeros((near_ref.shape[0], 2 * half), jnp.float32)
     for step in range(features // tile):
         columns = slice(step * tile, (step + 1) * tile)
         wide, own_wide = widened.at[step % 2], own_widened.at[step % 2]
@@ -85,7 +76,8 @@
             axis=0,
         )
         total = total + jnp.dot(mixed, held_ref[columns, :], preferred_element_type=jnp.float32)
-    split_by_core(total, kept_ref, given_ref)
+    near_ref[...] = total[:, :half]
+    far_ref[...] = total[:, half:].astype(jnp.bfloat16)
 
 
 def own_project(activations, conv_taps, gate_in):
@@ -95,8 +87,7 @@
     return pl.pallas_call(
         own_project_kernel,
         out_shape=(
-            jax.ShapeDtypeStruct((done, gate_in.shape[1] // 2), jnp.float32),
-            jax.ShapeDtypeStruct((done, gate_in.shape[1] // 2), jnp.float32),
+            jax.ShapeDtypeStruct((done, gate_in.shape[1]), jnp.float32),
             jax.ShapeDtypeStruct(conv_taps.shape, jnp.float32),
             jax.ShapeDtypeStruct(
                 (features + features // tile * 2 * RIM_ROWS, gate_in.shape[1]), gate_in.dtype
@@ -117,7 +108,7 @@
         peer_project_kernel,
         out_shape=(
             jax.ShapeDtypeStruct((done, half), jnp.float32),
-            jax.ShapeDtypeStruct((done, half), jnp.float32),
+            jax.ShapeDtypeStruct((done, half), jnp.bfloat16),
         ),
         scratch_shapes=[
             pltpu.VMEM((2, rows + RIM_ROWS, tile), jnp.float32),
@@ -128,19 +119,21 @@
     )(peer_rows, taps, held)
 
 
+def head_sum(part):
+    count = lax.axis_size("heads")
+    step = 1
+    received = None
+    while step < count:
+        if received is not None:
+            part = part + received.astype(jnp.float32)
+        received = exchange_heads(part if step == 1 else part.astype(jnp.bfloat16), step)
+        step *= 2
+    return part, received
+
+
 def exchange_heads(block, step):
     count = lax.axis_size("heads")
     return lax.ppermute(block, "heads", [(i, i ^ step) for i in range(count)])
-
-
-def head_sum(kept, given):
-    received = exchange_heads(given, 1)
-    step = 2
-    while step < lax.axis_size("heads"):
-        kept = kept + received.astype(jnp.float32)
-        received = exchange_heads(kept.astype(jnp.bfloat16), step)
-        step *= 2
-    return kept, received
 
 
 def in_one_piece(work, *given):
@@ -153,45 +146,60 @@
     )
 
 
-def share_of_logits(kept_ref, in_ref, gate_out_ref):
-    pre = kept_ref[...] + in_ref[...].astype(jnp.float32)
+def far_logits(block, gate_out):
+    step = lax.axis_size("heads") // 2
+    received = exchange_heads(block, step)
+
+    def nearer(block, received, gate_out):
+        distance = step
+        while distance > 1:
+            distance //= 2
+            block = block.astype(jnp.float32) + received.astype(jnp.float32)
+            received = exchange_heads(block, distance)
+        return partial_logits(block, received, gate_out, block.shape[1])
+
+    return in_one_piece(nearer, block, received, gate_out)
+
+
+def share_of_logits(pre_ref, in_ref, gate_out_ref, offset):
+    pre = pre_ref[...] + in_ref[...].astype(jnp.float32)
     hidden = (pre / (1.0 + jnp.exp(-pre))).astype(jnp.bfloat16)
-    half = pre.shape[1]
-    part = 2 * lax.axis_index("seq") + lax.rem(lax.axis_index("heads"), 2)
-    gate_columns = gate_out_ref[:, pl.ds(pl.multiple_of(part * half, HEAD_DIM), half)]
+    share = gate_out_ref.shape[1] // lax.axis_size("seq")
+    start = pl.multiple_of(lax.axis_index("seq") * share + offset, HEAD_DIM)
+    gate_columns = gate_out_ref[:, pl.ds(start, pre.shape[1])]
     return lax.dot_general(
         gate_columns, hidden, (((1,), (1,)), ((), ())), preferred_element_type=jnp.float32
     )
 
 
-def partial_logits_kernel(kept_ref, in_ref, gate_out_ref, out_ref):
-    out_ref[...] = share_of_logits(kept_ref, in_ref, gate_out_ref)
-
-
-def partial_logits(kept, received, gate_out):
+def partial_logits_kernel(offset, own_ref, in_ref, gate_out_ref, out_ref):
+    out_ref[...] = share_of_logits(own_ref, in_ref, gate_out_ref, offset)
+
+
+def partial_logits(part, received, gate_out, offset):
     return pl.pallas_call(
-        partial_logits_kernel,
-        out_shape=jax.ShapeDtypeStruct((gate_out.shape[0], kept.shape[0]), jnp.float32),
+        functools.partial(partial_logits_kernel, offset),
+        out_shape=jax.ShapeDtypeStruct((gate_out.shape[0], part.shape[0]), jnp.float32),
         compiler_params=pltpu.CompilerParams(vmem_limit_bytes=VMEM_BYTES),
-    )(kept, received, gate_out)
-
-
-def logits_kernel(own_ref, kept_ref, in_ref, gate_out_ref, out_ref):
+    )(part, received, gate_out)
+
+
+def logits_kernel(own_ref, far_share_ref, near_ref, near_in_ref, gate_out_ref, out_ref):
     first = lax.axis_index("seq") == 0
-    share = share_of_logits(kept_ref, in_ref, gate_out_ref)
+    share = share_of_logits(near_ref, near_in_ref, gate_out_ref, 0) + far_share_ref[...]
     own = jnp.concatenate([share[:, :RIM_ROWS], own_ref[...]], axis=1)
     peer = share[:, RIM_ROWS:]
     out_ref[0] = jnp.where(first, own, peer)
     out_ref[1] = jnp.where(first, peer, own)
 
 
-def logits_share(own_share, kept, received, gate_out):
+def logits_share(own_share, far_share, near, near_in, gate_out):
     rows = own_share.shape[1] + RIM_ROWS
     return pl.pallas_call(
         logits_kernel,
         out_shape=jax.ShapeDtypeStruct((2, gate_out.shape[0], rows), jnp.float32),
         compiler_params=pltpu.CompilerParams(vmem_limit_bytes=VMEM_BYTES),
-    )(own_share, kept, received, gate_out)
+    )(own_share, far_share, near, near_in, gate_out)
 
 
 def hide_unseen(seq_rank, segments_ref, rows):
@@ -265,7 +273,6 @@
 def read_retention(share_refs, retention):
     seq_rank, head_rank = lax.axis_index("seq"), lax.axis_index("heads")
     logits = share_refs[0][...] + share_refs[1][...]
-    logits = logits + (share_refs[2][...] + share_refs[3][...])
     log_gate = jnp.minimum(logits, 0.0) - jnp.log1p(jnp.exp(-jnp.abs(logits)))
     retention[...] = log_gate.astype(jnp.bfloat16).astype(jnp.float32)
     kv_local = retention.shape[1] // lax.axis_size("heads")
@@ -316,8 +323,8 @@
 
 
 def weights_kernel(*refs):
-    *share_refs, powers_ref, segments_ref, queries_ref, keys_ref, behind_keys_ref = refs[:9]
-    weights_ref, own_mass_ref, behind_mass_ref, retention = refs[9:]
+    *share_refs, powers_ref, segments_ref, queries_ref, keys_ref, behind_keys_ref = refs[:7]
+    weights_ref, own_mass_ref, behind_mass_ref, retention = refs[7:]
     rows = queries_ref.shape[0]
 
     def whole():
@@ -352,9 +359,9 @@
 
 
 def attend_kernel(*refs):
-    *share_refs, powers_ref, segments_ref, queries_ref, keys_ref, behind_keys_ref = refs[:9]
-    weights_ref, mass_ref, values_ref, behind_values_ref = refs[9:13]
-    attended_ref, own_mass_ref, retention = refs[13:]
+    *share_refs, powers_ref, segments_ref, queries_ref, keys_ref, behind_keys_ref = refs[:7]
+    weights_ref, mass_ref, values_ref, behind_values_ref = refs[7:11]
+    attended_ref, own_mass_ref, retention = refs[11:]
     group_size = attended_ref.shape[1] // values_ref.shape[1]
 
     def attend_head(head, weights, whole):
@@ -413,29 +420,26 @@
     peer_rows = lax.ppermute(activations, "seq", swap)
 
     def own_work(activations, conv_taps, gate_in, gate_out):
-        kept, given, *held = own_project(activations, conv_taps, gate_in)
-        return partial_logits(*head_sum(kept, given), gate_out), held
+        part, *held = own_project(activations, conv_taps, gate_in)
+        return partial_logits(*head_sum(part), gate_out, 0), held
 
     own_share, held = in_one_piece(own_work, activations, conv_taps, gate_in, gate_out)
     peer_rows, own_share, held = lax.optimization_barrier((peer_rows, own_share, held))
-    kept, given = peer_project(peer_rows, *held)
+    near, far = peer_project(peer_rows, *held)
     behind_keys = lax.ppermute(key_vectors, "seq", swap)
     behind_values = lax.ppermute(value_vectors, "seq", swap)
-    share = logits_share(own_share, *head_sum(kept, given), gate_out)
+    near, near_in = head_sum(near)
+    far_share = far_logits(far, gate_out)
+    share = logits_share(own_share, far_share, near, near_in, gate_out)
     share, queries = lax.optimization_barrier((share, queries))
     powers = powers_of(segments, queries, key_vectors, behind_keys)
     count = lax.axis_size("heads")
-    both = [
+    across = [
         (seq * count + head, (1 - seq) * count + (head ^ 1))
         for seq in range(2)
         for head in range(count)
     ]
-    shares = (
-        share,
-        exchange_heads(share, 1),
-        lax.ppermute(share, "seq", swap),
-        lax.ppermute(share, ("seq", "heads"), both),
-    )
+    shares = (share, lax.ppermute(share, ("seq", "heads"), across))
     given = (shares, powers, segments, queries, key_vectors, behind_keys)
     weights, own_mass, behind_mass = weights_of(*given)
     attended, own_mass = attend(*given, weights, own_mass, value_vectors, behind_values)

time: 31.8 us -> 31.4 us (0.987)
  waiting for transfers between devices: 12.5 us -> 10.1 us
  starting transfers between devices: 11.9 us -> 13.5 us
    ppermute x5 -> x6, starting transfers between devices: 3.56 us -> 4.97 us  [exchange_heads(): return lax.ppermute(block, 'heads', [(i, i ^ step) for i in range(count)])]
    ppermute x1, waiting for transfers between devices: 3.73 us -> 2.51 us  [pair_device(): peer_rows = lax.ppermute(activations, 'seq', swap)]
    ppermute x2 -> x1, waiting for transfers between devices: 2.15 us -> 1.12 us  [pair_device(): shares = (share, lax.ppermute(share, ('seq', 'heads'), across))]
    ppermute x1, starting transfers between devices: 1.36 us -> 2.26 us  [pair_device(): key_mass = own_mass + lax.ppermute(behind_mass, 'seq', swap)]
    ppermute x1, waiting for transfers between devices: 0.65 us -> 0.01 us  [pair_device(): key_mass = own_mass + lax.ppermute(behind_mass, 'seq', swap)]
    ppermute x2 -> x1, starting transfers between devices: 1.91 us -> 1.27 us  [pair_device(): shares = (share, lax.ppermute(share, ('seq', 'heads'), across))]
    ppermute x5 -> x6, waiting for transfers between devices: 5.88 us -> 6.51 us  [exchange_heads(): return lax.ppermute(block, 'heads', [(i, i ^ step) for i in range(count)])]
  transfers between devices with their start and end apart: 11 -> 11, of which waited for: 9 -> 5; matrix products, arithmetic and copies ran while one was open for 0% -> 0% of each run, Pallas kernels for 17% -> 17%
where the time goes in v15:
time: 31.4 us; the launch traced here: 31.2 us
  starting transfers between devices  13.5 us (43%)
  waiting for transfers between devices  10.1 us (32%)
  Pallas kernels  6.23 us (20%)
  between operations  0.69 us (2%)
  other arithmetic  0.59 us (2%)
    ppermute x6, waiting for transfers between devices, exchange_heads(): return lax.ppermute(block, 'heads', [(i, i ^ step) for i in range(count)])  6.51 us
    ppermute x6, starting transfers between devices, exchange_heads(): return lax.ppermute(block, 'heads', [(i, i ^ step) for i in range(count)])  4.97 us
    ppermute x1, starting transfers between devices, pair_device(): peer_rows = lax.ppermute(activations, 'seq', swap)  3 us
    pallas_call x1, Pallas kernels, own_project(): pl.pallas_call(own_project_kernel, out_shape=(jax.ShapeDtypeStruct((done,...  2.55 us
    ppermute x1, waiting for transfers between devices, pair_device(): peer_rows = lax.ppermute(activations, 'seq', swap)  2.51 us
    ppermute x1, starting transfers between devices, pair_device(): key_mass = own_mass + lax.ppermute(behind_mass, 'seq', swap)  2.26 us
    pallas_call x1, Pallas kernels, attend(): pl.pallas_call(attend_kernel, out_shape=(jax.ShapeDtypeStruct(queries.sha...  1.55 us
    ppermute x1, starting transfers between devices, pair_device(): behind_keys = lax.ppermute(key_vectors, 'seq', swap)  1.49 us
  transfers between devices with their start and end apart: 11, of which 5 were waited for; matrix products, arithmetic and copies ran while one was open for 0% of the time, Pallas kernels for 17%

profile of v15, /device:TPU:0, one launch (start us, length us, event | category | flops | bytes accessed | tf_op | source)
XLA Modules:
  0.0 31.2 jit_solution(10594437189689299662)
XLA Ops:
  0.6 3.0 %collective-permute-start.3 = (bf16[128,2048]{1,0:T(8,128)(2,1)}, bf16[128,2048]{1,0:T(8,128)(2,1)S(1)}, u32[]{:S(2)}, u32[]{:S(2)}) collective-permute-start(bf16[128,2048]{1,0:T(8,128)(2,1)} %param.12), channel_id=1, source_target_pairs={{0,16},{16,0},{1,17},{17,1},{2,18},{18,2},{3,19},{19,3},{4,20},{20... | collective-permute-start | bytes 1572872 | tf_op jit(solution)/shard_map/ppermute | solution.py:420
  3.6 9.6 %conditional.2 = (f32[8,112]{1,0:T(8,128)S(1)}, f32[4,2048]{1,0:T(4,128)S(1)}, bf16[2176,512]{1,0:T(8,128)(2,1)S(1)}) conditional(s32[]{:T(128)} %convert_element_type.19, () %tuple.24, (bf16[128,2048]{1,0:T(8,128)(2,1)}, bf16[4,2048]{1,0:T(4,128)(2,1)}, bf16[2048,512]{1,0:T(8,128)(2,1)}, bf16[8,1024]{1,0:T(8,128)(2,1)}) %tuple.37), branch_computations={%region_0.0_spmd, %region_1.0_spmd} | conditional | flops 114689 | bytes 2264610 | solution.py:141
  3.6 0.0 copy-start.5
  3.6 2.6 %branch_1_fun.3 = (f32[112,512]{1,0:T(8,128)S(1)}, f32[4,2048]{1,0:T(4,128)S(1)}, bf16[2176,512]{1,0:T(8,128)(2,1)S(1)}) custom-call(bf16[128,2048]{1,0:T(8,128)(2,1)} %get-tuple-element.10.rows_ref, bf16[4,2048]{1,0:T(4,128)(2,1)} %get-tuple-element.63.taps_ref, bf16[2048,512]{1,0:T(8,128)(2,1)} %get-tuple-element.64.gate_ref), custom_call_target="tpu_custom_call" | custom-call | flops 1 | bytes 1 | tf_op jit(solution)/shard_map/cond/branch_1_fun/pallas_call | solution.py:87
  6.2 0.1 collective-permute-start.1
  6.3 1.5 %collective-permute-done.1 = f32[112,512]{1,0:T(8,128)S(1)} collective-permute-done((f32[112,512]{1,0:T(8,128)S(1)}, f32[112,512]{1,0:T(8,128)S(1)}, u32[]{:S(2)}, u32[]{:S(2)}) %collective-permute-start.1) | collective-permute-done | bytes 229408 | tf_op jit(solution)/shard_map/cond/branch_1_fun/ppermute | solution.py:136
  7.8 1.6 %collective-permute-start.2 = (bf16[112,512]{1,0:T(8,128)(2,1)S(1)}, bf16[112,512]{1,0:T(8,128)(2,1)S(1)}, u32[]{:S(2)}, u32[]{:S(2)}) collective-permute-start(bf16[112,512]{1,0:T(8,128)(2,1)S(1)} %get-tuple-element.65), channel_id=1, source_target_pairs={{0,8},{4,12},{8,0},{12,4},{1,9},{5,13},{9,1},{13,5},{2,10},{6,14},... | collective-permute-start | bytes 344072 | tf_op jit(solution)/shard_map/cond/branch_1_fun/ppermute | solution.py:136
  9.4 3.7 %collective-permute-done.2.in_ref = bf16[112,512]{1,0:T(8,128)(2,1)S(1)} collective-permute-done((bf16[112,512]{1,0:T(8,128)(2,1)S(1)}, bf16[112,512]{1,0:T(8,128)(2,1)S(1)}, u32[]{:S(2)}, u32[]{:S(2)}) %collective-permute-start.2) | collective-permute-done | bytes 114720 | tf_op jit(solution)/shard_map/cond/branch_1_fun/ppermute | solution.py:136
  13.0 0.0 copy-done.5
  13.0 0.2 branch_1_fun.4
  13.2 0.0 copy-start.1
  13.2 0.0 copy-start.2
  13.2 0.0 copy-start.4
  13.2 0.0 copy-start
  13.2 0.0 copy-start.3
  13.3 2.5 %collective-permute-done.3.peer_ref = bf16[128,2048]{1,0:T(8,128)(2,1)S(1)} collective-permute-done((bf16[128,2048]{1,0:T(8,128)(2,1)}, bf16[128,2048]{1,0:T(8,128)(2,1)S(1)}, u32[]{:S(2)}, u32[]{:S(2)}) %collective-permute-start.3) | collective-permute-done | bytes 524320 | tf_op jit(solution)/shard_map/ppermute | solution.py:420
  15.8 0.8 %shard_map.97 = (f32[144,256]{1,0:T(8,128)S(1)}, bf16[144,256]{1,0:T(8,128)(2,1)S(1)}) custom-call(bf16[128,2048]{1,0:T(8,128)(2,1)S(1)} %collective-permute-done.3.peer_ref, f32[4,2048]{1,0:T(4,128)S(1)} %get-tuple-element.50.taps_ref, bf16[2176,512]{1,0:T(8,128)(2,1)S(1)} %get-tuple-element.51.held_ref), custom_call_target="tpu_custom_call" | custom-call | flops 1 | bytes 1 | tf_op jit(solution)/shard_map/pallas_call | solution.py:107
  16.6 0.1 collective-permute-start.5
  16.6 1.8 %collective-permute-start.4 = (bf16[144,256]{1,0:T(8,128)(2,1)S(1)}, bf16[144,256]{1,0:T(8,128)(2,1)S(1)}, u32[]{:S(2)}, u32[]{:S(2)}) collective-permute-start(bf16[144,256]{1,0:T(8,128)(2,1)S(1)} %get-tuple-element.52), channel_id=1, source_target_pairs={{0,8},{4,12},{8,0},{12,4},{1,9},{5,13},{9,1},{13,5},{2,10},{6,14},... | collective-permute-start | bytes 221192 | tf_op jit(solution)/shard_map/ppermute | solution.py:136
  18.5 0.0 collective-permute-done.5
  18.5 1.4 %collective-permute-start.6 = (bf16[144,256]{1,0:T(8,128)(2,1)S(1)}, bf16[144,256]{1,0:T(8,128)(2,1)S(1)}, u32[]{:S(2)}, u32[]{:S(2)}) collective-permute-start(bf16[144,256]{1,0:T(8,128)(2,1)S(1)} %get-tuple-element.67), channel_id=1, source_target_pairs={{0,8},{4,12},{8,0},{12,4},{1,9},{5,13},{9,1},{13,5},{2,10},{6,14},... | collective-permute-start | bytes 221192 | tf_op jit(solution)/shard_map/ppermute | solution.py:136
  19.8 0.0 copy-done.1
  19.8 1.5 %collective-permute-start.8 = (bf16[128,256]{1,0:T(8,128)(2,1)S(1)}, bf16[128,256]{1,0:T(8,128)(2,1)S(1)}, u32[]{:S(2)}, u32[]{:S(2)}) collective-permute-start(bf16[128,256]{1,0:T(8,128)(2,1)S(1)} %copy-done.1), channel_id=1, source_target_pairs={{0,16},{16,0},{1,17},{17,1},{2,18},{18,2},{3,19},{19,3},{4,20},{20... | collective-permute-start | bytes 196616 | tf_op jit(solution)/shard_map/ppermute | solution.py:429
  21.3 0.0 copy-done.2
  21.3 0.5 %collective-permute-start.9 = (bf16[128,256]{1,0:T(8,128)(2,1)S(1)}, bf16[128,256]{1,0:T(8,128)(2,1)S(1)}, u32[]{:S(2)}, u32[]{:S(2)}) collective-permute-start(bf16[128,256]{1,0:T(8,128)(2,1)S(1)} %copy-done.2), channel_id=1, source_target_pairs={{0,16},{16,0},{1,17},{17,1},{2,18},{18,2},{3,19},{19,3},{4,20},{20... | collective-permute-start | bytes 196616 | tf_op jit(solution)/shard_map/ppermute | solution.py:430
  21.9 0.0 collective-permute-done.4
  21.9 0.0 copy-done.4
  21.9 1.6 %conditional.3 = (f32[8,144]{1,0:T(8,128)S(1)}) conditional(s32[]{:T(128)} %convert_element_type.19, () %tuple.27, (bf16[144,256]{1,0:T(8,128)(2,1)S(1)}, bf16[144,256]{1,0:T(8,128)(2,1)S(1)}, bf16[8,1024]{1,0:T(8,128)(2,1)S(1)}) %tuple.38), branch_computations={%region_2.0_spmd, %region_3.0_spmd} | conditional | flops 110592 | bytes 884784 | solution.py:141
  21.9 0.1 collective-permute-start
  22.0 1.4 %collective-permute-done.in_ref = f32[144,256]{1,0:T(8,128)S(1)} collective-permute-done((f32[144,256]{1,0:T(8,128)S(1)}, f32[144,256]{1,0:T(8,128)S(1)}, u32[]{:S(2)}, u32[]{:S(2)}) %collective-permute-start) | collective-permute-done | bytes 147488 | tf_op jit(solution)/shard_map/cond/branch_1_fun/ppermute | solution.py:136
  23.3 0.2 branch_1_fun.5
  23.5 0.0 collective-permute-done.6.near_in_ref
  23.5 0.3 shard_map.98.refs_0_
  23.8 1.3 %collective-permute-start.7 = (f32[2,8,128]{2,1,0:T(8,128)S(1)}, f32[2,8,128]{2,1,0:T(8,128)S(1)}, u32[]{:S(2)}, u32[]{:S(2)}) collective-permute-start(f32[2,8,128]{2,1,0:T(8,128)S(1)} %shard_map.98.refs_0_), channel_id=1, source_target_pairs={{0,20},{4,16},{8,28},{12,24},{16,4},{20,0},{24,12},{28,8},{1,21},{... | collective-permute-start | bytes 24584 | tf_op jit(solution)/shard_map/ppermute | solution.py:442
  25.1 0.0 collective-permute-done.8.behind_keys_ref.refs_6_
  25.1 0.0 copy-done
  25.1 0.0 copy-done.3
  25.1 0.7 %shard_map.99.refs_2_ = f32[16,128,256]{2,1,0:T(8,128)S(1)} custom-call(s32[2,128]{1,0:T(2,128)S(1)} %bitcast.2, bf16[128,2048]{1,0:T(8,128)(2,1)S(1)} %copy-done, bf16[128,256]{1,0:T(8,128)(2,1)S(1)} %copy-done.1, bf16[128,256]{1,0:T(8,128)(2,1)S(1)} %collective-permute-done.8.behind_keys_ref.refs_6_), custom_call_target="tpu_custom_call" | custom-call | flops 134217728 | bytes 2097152 | tf_op jit(solution)/shard_map/pallas_call | solution.py:261
  25.8 1.1 %collective-permute-done.7.refs_1_ = f32[2,8,128]{2,1,0:T(8,128)S(1)} collective-permute-done((f32[2,8,128]{2,1,0:T(8,128)S(1)}, f32[2,8,128]{2,1,0:T(8,128)S(1)}, u32[]{:S(2)}, u32[]{:S(2)}) %collective-permute-start.7) | collective-permute-done | bytes 8224 | tf_op jit(solution)/shard_map/ppermute | solution.py:442
  26.9 2.3 %collective-permute-start.10 = (f32[2,128]{1,0:T(2,128)S(1)}, f32[2,128]{1,0:T(2,128)S(1)}, u32[]{:S(2)}, u32[]{:S(2)}) collective-permute-start(f32[2,128]{1,0:T(2,128)S(1)} %get-tuple-element.60), channel_id=1, source_target_pairs={{0,16},{16,0},{1,17},{17,1},{2,18},{18,2},{3,19},{19,3},{4,20},{20... | collective-permute-start | bytes 3080 | tf_op jit(solution)/shard_map/ppermute | solution.py:446
  29.2 0.0 collective-permute-done.9.refs_10_
  29.2 1.5 %shard_map.101 = (bf16[128,2048]{1,0:T(8,128)(2,1)}, f32[2,128]{1,0:T(2,128)S(1)}) custom-call(f32[2,8,128]{2,1,0:T(8,128)S(1)} %shard_map.98.refs_0_, f32[2,8,128]{2,1,0:T(8,128)S(1)} %collective-permute-done.7.refs_1_, f32[16,128,256]{2,1,0:T(8,128)S(1)} %shard_map.99.refs_2_, s32[2,128]{1,0:T(2,128)S(1)} %bitcast.4, bf16[128,2048]{1,0:T(8,128)(2,1)S(1)} %copy-done, ...), custom_call_target="tpu_custom_call" | custom-call | flops 134217728 | bytes 1572864 | tf_op jit(solution)/shard_map/pallas_call | solution.py:396
  30.7 0.0 collective-permute-done.10
  30.7 0.5 %add_convert_fusion = bf16[2,128]{1,0:T(2,128)(2,1)} fusion(f32[2,128]{1,0:T(2,128)S(1)} %get-tuple-element.59, f32[2,128]{1,0:T(2,128)S(1)} %collective-permute-done.10), kind=kLoop, calls=%fused_computation.1 | loop fusion | flops 512 | bytes 2560 | tf_op jit(solution)/shard_map/convert_element_type | solution.py:447
  (4 shorter events, 0.1 us)
Async XLA Ops:
  0.6 15.1 %collective-permute-start.3 = (bf16[128,2048]{1,0:T(8,128)(2,1)}, bf16[128,2048]{1,0:T(8,128)(2,1)S(1)}, u32[]{:S(2)}, u32[]{:S(2)}) collective-permute-start(bf16[128,2048]{1,0:T(8,128)(2,1)} %param.12), channel_id=1, source_target_pairs={{0,16},{16,0},{1,17},{17,1},{2,18},{18,2},{3,19},{19,3},{4,20},{20... | collective-permute-start | bytes 1572872 | tf_op jit(solution)/shard_map/ppermute | solution.py:420
  3.6 9.4 %copy-start.5 = (bf16[8,1024]{1,0:T(8,128)(2,1)S(1)}, bf16[8,1024]{1,0:T(8,128)(2,1)}, u32[]{:S(2)}) copy-start(bf16[8,1024]{1,0:T(8,128)(2,1)} %get-tuple-element.21.gate_out_ref) | copy-start | bytes 49156 | tf_op jit(solution)/shard_map/cond
  6.2 1.5 %collective-permute-start.1 = (f32[112,512]{1,0:T(8,128)S(1)}, f32[112,512]{1,0:T(8,128)S(1)}, u32[]{:S(2)}, u32[]{:S(2)}) collective-permute-start(f32[112,512]{1,0:T(8,128)S(1)} %get-tuple-element.20), channel_id=1, source_target_pairs={{0,4},{4,0},{8,12},{12,8},{1,5},{5,1},{9,13},{13,9},{2,6},{6,2},{1... | collective-permute-start | bytes 688136 | tf_op jit(solution)/shard_map/cond/branch_1_fun/ppermute | solution.py:136
  7.8 5.3 %collective-permute-start.2 = (bf16[112,512]{1,0:T(8,128)(2,1)S(1)}, bf16[112,512]{1,0:T(8,128)(2,1)S(1)}, u32[]{:S(2)}, u32[]{:S(2)}) collective-permute-start(bf16[112,512]{1,0:T(8,128)(2,1)S(1)} %get-tuple-element.65), channel_id=1, source_target_pairs={{0,8},{4,12},{8,0},{12,4},{1,9},{5,13},{9,1},{13,5},{2,10},{6,14},... | collective-permute-start | bytes 344072 | tf_op jit(solution)/shard_map/cond/branch_1_fun/ppermute | solution.py:136
  13.2 6.6 %copy-start.1 = (bf16[128,256]{1,0:T(8,128)(2,1)S(1)}, bf16[128,256]{1,0:T(8,128)(2,1)}, u32[]{:S(2)}) copy-start(bf16[128,256]{1,0:T(8,128)(2,1)} %refs_5_.3) | copy-start | bytes 196612
  13.2 8.1 %copy-start.2 = (bf16[128,256]{1,0:T(8,128)(2,1)S(1)}, bf16[128,256]{1,0:T(8,128)(2,1)}, u32[]{:S(2)}) copy-start(bf16[128,256]{1,0:T(8,128)(2,1)} %refs_9_.1) | copy-start | bytes 196612
  13.2 8.7 %copy-start.4 = (bf16[1024,8]{0,1:T(8,128)(2,1)S(1)}, bf16[1024,8]{0,1:T(8,128)(2,1)}, u32[]{:S(2)}) copy-start(bf16[1024,8]{0,1:T(8,128)(2,1)} %param.15) | copy-start | bytes 49156
  13.2 11.9 %copy-start = (bf16[128,2048]{1,0:T(8,128)(2,1)S(1)}, bf16[128,2048]{1,0:T(8,128)(2,1)}, u32[]{:S(2)}) copy-start(bf16[128,2048]{1,0:T(8,128)(2,1)} %refs_4_.1) | copy-start | bytes 1572868
  13.2 11.8 %copy-start.3 = (s32[256]{0:T(256)S(1)}, s32[256]{0:T(256)}, u32[]{:S(2)}) copy-start(s32[256]{0:T(256)} %param.19) | copy-start | bytes 3076
  16.6 1.9 %collective-permute-start.5 = (f32[144,256]{1,0:T(8,128)S(1)}, f32[144,256]{1,0:T(8,128)S(1)}, u32[]{:S(2)}, u32[]{:S(2)}) collective-permute-start(f32[144,256]{1,0:T(8,128)S(1)} %get-tuple-element.53), channel_id=1, source_target_pairs={{0,4},{4,0},{8,12},{12,8},{1,5},{5,1},{9,13},{13,9},{2,6},{6,2},{1... | collective-permute-start | bytes 442376 | tf_op jit(solution)/shard_map/ppermute | solution.py:136
  16.6 5.3 %collective-permute-start.4 = (bf16[144,256]{1,0:T(8,128)(2,1)S(1)}, bf16[144,256]{1,0:T(8,128)(2,1)S(1)}, u32[]{:S(2)}, u32[]{:S(2)}) collective-permute-start(bf16[144,256]{1,0:T(8,128)(2,1)S(1)} %get-tuple-element.52), channel_id=1, source_target_pairs={{0,8},{4,12},{8,0},{12,4},{1,9},{5,13},{9,1},{13,5},{2,10},{6,14},... | collective-permute-start | bytes 221192 | tf_op jit(solution)/shard_map/ppermute | solution.py:136
  18.5 5.0 %collective-permute-start.6 = (bf16[144,256]{1,0:T(8,128)(2,1)S(1)}, bf16[144,256]{1,0:T(8,128)(2,1)S(1)}, u32[]{:S(2)}, u32[]{:S(2)}) collective-permute-start(bf16[144,256]{1,0:T(8,128)(2,1)S(1)} %get-tuple-element.67), channel_id=1, source_target_pairs={{0,8},{4,12},{8,0},{12,4},{1,9},{5,13},{9,1},{13,5},{2,10},{6,14},... | collective-permute-start | bytes 221192 | tf_op jit(solution)/shard_map/ppermute | solution.py:136
  19.8 5.2 %collective-permute-start.8 = (bf16[128,256]{1,0:T(8,128)(2,1)S(1)}, bf16[128,256]{1,0:T(8,128)(2,1)S(1)}, u32[]{:S(2)}, u32[]{:S(2)}) collective-permute-start(bf16[128,256]{1,0:T(8,128)(2,1)S(1)} %copy-done.1), channel_id=1, source_target_pairs={{0,16},{16,0},{1,17},{17,1},{2,18},{18,2},{3,19},{19,3},{4,20},{20... | collective-permute-start | bytes 196616 | tf_op jit(solution)/shard_map/ppermute | solution.py:429
  21.3 7.8 %collective-permute-start.9 = (bf16[128,256]{1,0:T(8,128)(2,1)S(1)}, bf16[128,256]{1,0:T(8,128)(2,1)S(1)}, u32[]{:S(2)}, u32[]{:S(2)}) collective-permute-start(bf16[128,256]{1,0:T(8,128)(2,1)S(1)} %copy-done.2), channel_id=1, source_target_pairs={{0,16},{16,0},{1,17},{17,1},{2,18},{18,2},{3,19},{19,3},{4,20},{20... | collective-permute-start | bytes 196616 | tf_op jit(solution)/shard_map/ppermute | solution.py:430
  21.9 1.4 %collective-permute-start = (f32[144,256]{1,0:T(8,128)S(1)}, f32[144,256]{1,0:T(8,128)S(1)}, u32[]{:S(2)}, u32[]{:S(2)}) collective-permute-start(f32[144,256]{1,0:T(8,128)S(1)} %convert_add_fusion.own_ref), channel_id=1, source_target_pairs={{0,4},{4,0},{8,12},{12,8},{1,5},{5,1},{9,13},{13,9},{2,6},{6,2},{1... | collective-permute-start | bytes 442376 | tf_op jit(solution)/shard_map/cond/branch_1_fun/ppermute | solution.py:136
  23.8 3.1 %collective-permute-start.7 = (f32[2,8,128]{2,1,0:T(8,128)S(1)}, f32[2,8,128]{2,1,0:T(8,128)S(1)}, u32[]{:S(2)}, u32[]{:S(2)}) collective-permute-start(f32[2,8,128]{2,1,0:T(8,128)S(1)} %shard_map.98.refs_0_), channel_id=1, source_target_pairs={{0,20},{4,16},{8,28},{12,24},{16,4},{20,0},{24,12},{28,8},{1,21},{... | collective-permute-start | bytes 24584 | tf_op jit(solution)/shard_map/ppermute | solution.py:442
  26.9 3.8 %collective-permute-start.10 = (f32[2,128]{1,0:T(2,128)S(1)}, f32[2,128]{1,0:T(2,128)S(1)}, u32[]{:S(2)}, u32[]{:S(2)}) collective-permute-start(f32[2,128]{1,0:T(2,128)S(1)} %get-tuple-element.60), channel_id=1, source_target_pairs={{0,16},{16,0},{1,17},{17,1},{2,18},{18,2},{3,19},{19,3},{4,20},{20... | collective-permute-start | bytes 3080 | tf_op jit(solution)/shard_map/ppermute | solution.py:446

commit v16 on v15

--- a/solution.py
+++ b/solution.py
@@ -283,30 +283,20 @@
     return biases
 
 
-def weigh(whole, biases, powers_ref, segments_ref, queries_ref, keys_ref, behind_keys_ref, use):
-    seq_rank = lax.axis_index("seq")
+def by_group(
+    whole, biases, powers_ref, segments_ref, queries_ref, keys_ref, behind_keys_ref, group
+):
     rows = queries_ref.shape[0]
-    group_size = queries_ref.shape[1] // keys_ref.shape[1]
     start = 0 if whole else rows
     moderate = jnp.min(functools.reduce(jnp.minimum, biases)) >= LEAST_RETENTION
-
-    def finish(terms_of, store_mass):
-        for g in range(len(biases)):
-            mass = jnp.zeros((1, 2 * rows - start), jnp.float32)
-            group_terms = terms_of(g)
-            for head in range(g * group_size, (g + 1) * group_size):
-                weights = group_terms(head)
-                weights = weights * (1.0 / jnp.sum(weights, axis=1, keepdims=True))
-                mass = mass + jnp.sum(weights, axis=0, keepdims=True)
-                use(head, weights.astype(jnp.bfloat16))
-            store_mass(g, mass / group_size)
 
     def by_powers(g):
         factor = jnp.exp(biases[g] - jnp.max(biases[g]))[:, start:]
         return lambda head: powers_ref[head, :, start:] * factor
 
     def by_scores(g):
-        offset = (hide_unseen(seq_rank, segments_ref, rows) + biases[g])[:, start:]
+        hide = hide_unseen(lax.axis_index("seq"), segments_ref, rows)
+        offset = (hide + biases[g])[:, start:]
         keys = with_behind(keys_ref, behind_keys_ref, g, whole)
 
         def terms(head):
@@ -315,44 +305,47 @@
 
         return terms
 
-    def run(store_mass):
-        pl.when(moderate)(lambda: finish(by_powers, store_mass))
-        pl.when(jnp.logical_not(moderate))(lambda: finish(by_scores, store_mass))
-
-    return run
-
-
-def weights_kernel(*refs):
+    def run(terms_of):
+        for g in range(len(biases)):
+            group(g, terms_of(g))
+
+    pl.when(moderate)(lambda: run(by_powers))
+    pl.when(jnp.logical_not(moderate))(lambda: run(by_scores))
+
+
+def behind_mass_kernel(*refs):
     *share_refs, powers_ref, segments_ref, queries_ref, keys_ref, behind_keys_ref = refs[:7]
-    weights_ref, own_mass_ref, behind_mass_ref, retention = refs[7:]
+    mass_ref, retention = refs[7:]
     rows = queries_ref.shape[0]
-
-    def whole():
-        def use(head, weights):
-            weights_ref[head] = weights
-
-        def store_mass(g, mass):
-            behind_mass_ref[g : g + 1, :] = mass[:, :rows]
-            own_mass_ref[g : g + 1, :] = mass[:, rows:]
-
+    group_size = queries_ref.shape[1] // keys_ref.shape[1]
+
+    def group(g, terms_of):
+        mass = jnp.zeros((1, rows), jnp.float32)
+        for head in range(g * group_size, (g + 1) * group_size):
+            terms = terms_of(head)
+            weights = terms[:, :rows] * (1.0 / jnp.sum(terms, axis=1, keepdims=True))
+            mass = mass + jnp.sum(weights, axis=0, keepdims=True)
+        mass_ref[g : g + 1, :] = mass / group_size
+
+    def fill():
         biases = read_retention(share_refs, retention)
-        weigh(
-            True, biases, powers_ref, segments_ref, queries_ref, keys_ref, behind_keys_ref, use
-        )(store_mass)
-
-    def nothing():
-        behind_mass_ref[...] = jnp.zeros(behind_mass_ref.shape, jnp.float32)
-
-    pl.when(lax.axis_index("seq") > 0)(whole)
-    pl.when(lax.axis_index("seq") == 0)(nothing)
-
-
-def weights_of(shares, powers, segments, queries, keys, behind_keys):
-    rows = queries.shape[0]
-    mass = jax.ShapeDtypeStruct((keys.shape[1] // HEAD_DIM, rows), jnp.float32)
+        by_group(
+            True, biases, powers_ref, segments_ref, queries_ref, keys_ref, behind_keys_ref, group
+        )
+
+    def clear():
+        mass_ref[...] = jnp.zeros(mass_ref.shape, jnp.float32)
+
+    pl.when(lax.axis_index("seq") > 0)(fill)
+    pl.when(lax.axis_index("seq") == 0)(clear)
+
+
+def behind_mass_of(shares, powers, segments, queries, keys, behind_keys):
     return pl.pallas_call(
-        weights_kernel,
-        out_shape=(jax.ShapeDtypeStruct(powers.shape, jnp.bfloat16), mass, mass),
+        behind_mass_kernel,
+        out_shape=jax.ShapeDtypeStruct(
+            (keys.shape[1] // HEAD_DIM, queries.shape[0]), jnp.float32
+        ),
         scratch_shapes=[pltpu.VMEM(shares[0].shape, jnp.float32)],
         compiler_params=pltpu.CompilerParams(vmem_limit_bytes=VMEM_BYTES),
     )(*shares, powers, segments, queries, keys, behind_keys)
@@ -360,53 +353,51 @@
 
 def attend_kernel(*refs):
     *share_refs, powers_ref, segments_ref, queries_ref, keys_ref, behind_keys_ref = refs[:7]
-    weights_ref, mass_ref, values_ref, behind_values_ref = refs[7:11]
-    attended_ref, own_mass_ref, retention = refs[11:]
-    group_size = attended_ref.shape[1] // values_ref.shape[1]
-
-    def attend_head(head, weights, whole):
-        values = with_behind(values_ref, behind_values_ref, head // group_size, whole)
-        attended_ref[:, head_columns(head)] = jnp.dot(
-            weights, values, preferred_element_type=jnp.float32
-        ).astype(jnp.bfloat16)
-
-    def whole():
-        own_mass_ref[...] = mass_ref[...]
-        for head in range(weights_ref.shape[0]):
-            attend_head(head, weights_ref[head], True)
-
-    def alone():
-        def use(head, weights):
-            attend_head(head, weights, False)
-
-        def store_mass(g, mass):
-            own_mass_ref[g : g + 1, :] = mass
+    values_ref, behind_values_ref, attended_ref, mass_ref, retention = refs[7:]
+    rows = queries_ref.shape[0]
+    group_size = queries_ref.shape[1] // keys_ref.shape[1]
+
+    def fill(whole):
+        def group(g, terms_of):
+            values = with_behind(values_ref, behind_values_ref, g, whole)
+            own = values.shape[0] - rows
+            mass = jnp.zeros((1, rows), jnp.float32)
+            for head in range(g * group_size, (g + 1) * group_size):
+                terms = terms_of(head)
+                weights = terms * (1.0 / jnp.sum(terms, axis=1, keepdims=True))
+                mass = mass + jnp.sum(weights[:, own:], axis=0, keepdims=True)
+                attended_ref[:, head_columns(head)] = jnp.dot(
+                    weights.astype(jnp.bfloat16), values, preferred_element_type=jnp.float32
+                ).astype(jnp.bfloat16)
+            mass_ref[g : g + 1, :] = mass / group_size
 
         biases = read_retention(share_refs, retention)
-        weigh(
-            False, biases, powers_ref, segments_ref, queries_ref, keys_ref, behind_keys_ref, use
-        )(store_mass)
-
-    pl.when(lax.axis_index("seq") > 0)(whole)
-    pl.when(lax.axis_index("seq") == 0)(alone)
-
-
-def attend(shares, powers, segments, queries, keys, behind_keys, weights, mass, values, behind):
+        by_group(
+            whole, biases, powers_ref, segments_ref, queries_ref, keys_ref, behind_keys_ref, group
+        )
+
+    pl.when(lax.axis_index("seq") > 0)(lambda: fill(True))
+    pl.when(lax.axis_index("seq") == 0)(lambda: fill(False))
+
+
+def attend(shares, powers, segments, queries, keys, behind_keys, values, behind_values, sent):
     rows = queries.shape[0]
-    return pl.pallas_call(
+    shares, powers, sent = lax.optimization_barrier((shares, powers, sent))
+    attended, mass = pl.pallas_call(
         attend_kernel,
         out_shape=(
             jax.ShapeDtypeStruct(queries.shape, jnp.bfloat16),
-            jax.ShapeDtypeStruct(mass.shape, jnp.float32),
+            jax.ShapeDtypeStruct((keys.shape[1] // HEAD_DIM, rows), jnp.float32),
         ),
         scratch_shapes=[pltpu.VMEM(shares[0].shape, jnp.float32)],
         compiler_params=pltpu.CompilerParams(vmem_limit_bytes=VMEM_BYTES),
         cost_estimate=pl.CostEstimate(
             flops=4 * rows * rows * queries.shape[1],
-            bytes_accessed=2 * (weights.size + queries.size),
+            bytes_accessed=4 * queries.size,
             transcendentals=0,
         ),
-    )(*shares, powers, segments, queries, keys, behind_keys, weights, mass, values, behind)
+    )(*shares, powers, segments, queries, keys, behind_keys, values, behind_values)
+    return attended, mass, sent
 
 
 def pair_device(
@@ -441,9 +432,9 @@
     ]
     shares = (share, lax.ppermute(share, ("seq", "heads"), across))
     given = (shares, powers, segments, queries, key_vectors, behind_keys)
-    weights, own_mass, behind_mass = weights_of(*given)
-    attended, own_mass = attend(*given, weights, own_mass, value_vectors, behind_values)
-    key_mass = own_mass + lax.ppermute(behind_mass, "seq", swap)
+    sent = behind_mass_of(*given)
+    attended, own_mass, sent = attend(*given, value_vectors, behind_values, sent)
+    key_mass = own_mass + lax.ppermute(sent, "seq", swap)
     return (attended, key_mass.astype(jnp.bfloat16))
 
 

time: 31.4 us -> 31.4 us (level)
  no operation moved by 1% of the time
where the time goes in v16:
time: 31.4 us; the launch traced here: 31.2 us
  starting transfers between devices  13.5 us (43%)
  waiting for transfers between devices  10.1 us (32%)
  Pallas kernels  6.26 us (20%)
  between operations  0.69 us (2%)
  other arithmetic  0.58 us (2%)
    ppermute x6, waiting for transfers between devices, exchange_heads(): return lax.ppermute(block, 'heads', [(i, i ^ step) for i in range(count)])  6.51 us
    ppermute x6, starting transfers between devices, exchange_heads(): return lax.ppermute(block, 'heads', [(i, i ^ step) for i in range(count)])  4.97 us
    ppermute x1, starting transfers between devices, pair_device(): peer_rows = lax.ppermute(activations, 'seq', swap)  3 us
    pallas_call x1, Pallas kernels, own_project(): pl.pallas_call(own_project_kernel, out_shape=(jax.ShapeDtypeStruct((done,...  2.55 us
    ppermute x1, waiting for transfers between devices, pair_device(): peer_rows = lax.ppermute(activations, 'seq', swap)  2.51 us
    ppermute x1, starting transfers between devices, pair_device(): key_mass = own_mass + lax.ppermute(sent, 'seq', swap)  2.22 us
    pallas_call x1, Pallas kernels, attend(): pl.pallas_call(attend_kernel, out_shape=(jax.ShapeDtypeStruct(queries.sha...  1.55 us
    ppermute x1, starting transfers between devices, pair_device(): behind_keys = lax.ppermute(key_vectors, 'seq', swap)  1.49 us
  transfers between devices with their start and end apart: 11, of which 5 were waited for; matrix products, arithmetic and copies ran while one was open for 0% of the time, Pallas kernels for 17%

profile of v16, /device:TPU:0, one launch (start us, length us, event | category | flops | bytes accessed | tf_op | source)
XLA Modules:
  0.0 31.2 jit_solution(9394201035573969874)
XLA Ops:
  0.6 3.0 %collective-permute-start.3 = (bf16[128,2048]{1,0:T(8,128)(2,1)}, bf16[128,2048]{1,0:T(8,128)(2,1)S(1)}, u32[]{:S(2)}, u32[]{:S(2)}) collective-permute-start(bf16[128,2048]{1,0:T(8,128)(2,1)} %param.12), channel_id=1, source_target_pairs={{0,16},{16,0},{1,17},{17,1},{2,18},{18,2},{3,19},{19,3},{4,20},{20... | collective-permute-start | bytes 1572872 | tf_op jit(solution)/shard_map/ppermute | solution.py:411
  3.6 9.6 %conditional.2 = (f32[8,112]{1,0:T(8,128)S(1)}, f32[4,2048]{1,0:T(4,128)S(1)}, bf16[2176,512]{1,0:T(8,128)(2,1)S(1)}) conditional(s32[]{:T(128)} %convert_element_type.19, () %tuple.25, (bf16[128,2048]{1,0:T(8,128)(2,1)}, bf16[4,2048]{1,0:T(4,128)(2,1)}, bf16[2048,512]{1,0:T(8,128)(2,1)}, bf16[8,1024]{1,0:T(8,128)(2,1)}) %tuple.39), branch_computations={%region_0.0_spmd, %region_1.0_spmd} | conditional | flops 114689 | bytes 2264610 | solution.py:141
  3.6 0.0 copy-start.5
  3.6 2.6 %branch_1_fun.3 = (f32[112,512]{1,0:T(8,128)S(1)}, f32[4,2048]{1,0:T(4,128)S(1)}, bf16[2176,512]{1,0:T(8,128)(2,1)S(1)}) custom-call(bf16[128,2048]{1,0:T(8,128)(2,1)} %get-tuple-element.10.rows_ref, bf16[4,2048]{1,0:T(4,128)(2,1)} %get-tuple-element.65.taps_ref, bf16[2048,512]{1,0:T(8,128)(2,1)} %get-tuple-element.66.gate_ref), custom_call_target="tpu_custom_call" | custom-call | flops 1 | bytes 1 | tf_op jit(solution)/shard_map/cond/branch_1_fun/pallas_call | solution.py:87
  6.2 0.1 collective-permute-start.1
  6.3 1.5 %collective-permute-done.1 = f32[112,512]{1,0:T(8,128)S(1)} collective-permute-done((f32[112,512]{1,0:T(8,128)S(1)}, f32[112,512]{1,0:T(8,128)S(1)}, u32[]{:S(2)}, u32[]{:S(2)}) %collective-permute-start.1) | collective-permute-done | bytes 229408 | tf_op jit(solution)/shard_map/cond/branch_1_fun/ppermute | solution.py:136
  7.8 1.6 %collective-permute-start.2 = (bf16[112,512]{1,0:T(8,128)(2,1)S(1)}, bf16[112,512]{1,0:T(8,128)(2,1)S(1)}, u32[]{:S(2)}, u32[]{:S(2)}) collective-permute-start(bf16[112,512]{1,0:T(8,128)(2,1)S(1)} %get-tuple-element.67), channel_id=1, source_target_pairs={{0,8},{4,12},{8,0},{12,4},{1,9},{5,13},{9,1},{13,5},{2,10},{6,14},... | collective-permute-start | bytes 344072 | tf_op jit(solution)/shard_map/cond/branch_1_fun/ppermute | solution.py:136
  9.4 3.7 %collective-permute-done.2.in_ref = bf16[112,512]{1,0:T(8,128)(2,1)S(1)} collective-permute-done((bf16[112,512]{1,0:T(8,128)(2,1)S(1)}, bf16[112,512]{1,0:T(8,128)(2,1)S(1)}, u32[]{:S(2)}, u32[]{:S(2)}) %collective-permute-start.2) | collective-permute-done | bytes 114720 | tf_op jit(solution)/shard_map/cond/branch_1_fun/ppermute | solution.py:136
  13.0 0.0 copy-done.5
  13.0 0.2 branch_1_fun.4
  13.2 0.0 copy-start.1
  13.2 0.0 copy-start.2
  13.2 0.0 copy-start.4
  13.2 0.0 copy-start
  13.2 0.0 copy-start.3
  13.3 2.5 %collective-permute-done.3.peer_ref = bf16[128,2048]{1,0:T(8,128)(2,1)S(1)} collective-permute-done((bf16[128,2048]{1,0:T(8,128)(2,1)}, bf16[128,2048]{1,0:T(8,128)(2,1)S(1)}, u32[]{:S(2)}, u32[]{:S(2)}) %collective-permute-start.3) | collective-permute-done | bytes 524320 | tf_op jit(solution)/shard_map/ppermute | solution.py:411
  15.8 0.8 %shard_map.97 = (f32[144,256]{1,0:T(8,128)S(1)}, bf16[144,256]{1,0:T(8,128)(2,1)S(1)}) custom-call(bf16[128,2048]{1,0:T(8,128)(2,1)S(1)} %collective-permute-done.3.peer_ref, f32[4,2048]{1,0:T(4,128)S(1)} %get-tuple-element.51.taps_ref, bf16[2176,512]{1,0:T(8,128)(2,1)S(1)} %get-tuple-element.52.held_ref), custom_call_target="tpu_custom_call" | custom-call | flops 1 | bytes 1 | tf_op jit(solution)/shard_map/pallas_call | solution.py:107
  16.6 0.1 collective-permute-start.5
  16.6 1.8 %collective-permute-start.4 = (bf16[144,256]{1,0:T(8,128)(2,1)S(1)}, bf16[144,256]{1,0:T(8,128)(2,1)S(1)}, u32[]{:S(2)}, u32[]{:S(2)}) collective-permute-start(bf16[144,256]{1,0:T(8,128)(2,1)S(1)} %get-tuple-element.53), channel_id=1, source_target_pairs={{0,8},{4,12},{8,0},{12,4},{1,9},{5,13},{9,1},{13,5},{2,10},{6,14},... | collective-permute-start | bytes 221192 | tf_op jit(solution)/shard_map/ppermute | solution.py:136
  18.5 0.0 collective-permute-done.5
  18.5 1.4 %collective-permute-start.6 = (bf16[144,256]{1,0:T(8,128)(2,1)S(1)}, bf16[144,256]{1,0:T(8,128)(2,1)S(1)}, u32[]{:S(2)}, u32[]{:S(2)}) collective-permute-start(bf16[144,256]{1,0:T(8,128)(2,1)S(1)} %get-tuple-element.69), channel_id=1, source_target_pairs={{0,8},{4,12},{8,0},{12,4},{1,9},{5,13},{9,1},{13,5},{2,10},{6,14},... | collective-permute-start | bytes 221192 | tf_op jit(solution)/shard_map/ppermute | solution.py:136
  19.9 0.0 copy-done.1
  19.9 1.5 %collective-permute-start.8 = (bf16[128,256]{1,0:T(8,128)(2,1)S(1)}, bf16[128,256]{1,0:T(8,128)(2,1)S(1)}, u32[]{:S(2)}, u32[]{:S(2)}) collective-permute-start(bf16[128,256]{1,0:T(8,128)(2,1)S(1)} %copy-done.1), channel_id=1, source_target_pairs={{0,16},{16,0},{1,17},{17,1},{2,18},{18,2},{3,19},{19,3},{4,20},{20... | collective-permute-start | bytes 196616 | tf_op jit(solution)/shard_map/ppermute | solution.py:420
  21.4 0.0 copy-done.2
  21.4 0.5 %collective-permute-start.9 = (bf16[128,256]{1,0:T(8,128)(2,1)S(1)}, bf16[128,256]{1,0:T(8,128)(2,1)S(1)}, u32[]{:S(2)}, u32[]{:S(2)}) collective-permute-start(bf16[128,256]{1,0:T(8,128)(2,1)S(1)} %copy-done.2), channel_id=1, source_target_pairs={{0,16},{16,0},{1,17},{17,1},{2,18},{18,2},{3,19},{19,3},{4,20},{20... | collective-permute-start | bytes 196616 | tf_op jit(solution)/shard_map/ppermute | solution.py:421
  21.9 0.0 collective-permute-done.4
  21.9 0.0 copy-done.4
  21.9 1.6 %conditional.3 = (f32[8,144]{1,0:T(8,128)S(1)}) conditional(s32[]{:T(128)} %convert_element_type.19, () %tuple.28, (bf16[144,256]{1,0:T(8,128)(2,1)S(1)}, bf16[144,256]{1,0:T(8,128)(2,1)S(1)}, bf16[8,1024]{1,0:T(8,128)(2,1)S(1)}) %tuple.40), branch_computations={%region_2.0_spmd, %region_3.0_spmd} | conditional | flops 110592 | bytes 884784 | solution.py:141
  21.9 0.1 collective-permute-start
  22.0 1.4 %collective-permute-done.in_ref = f32[144,256]{1,0:T(8,128)S(1)} collective-permute-done((f32[144,256]{1,0:T(8,128)S(1)}, f32[144,256]{1,0:T(8,128)S(1)}, u32[]{:S(2)}, u32[]{:S(2)}) %collective-permute-start) | collective-permute-done | bytes 147488 | tf_op jit(solution)/shard_map/cond/branch_1_fun/ppermute | solution.py:136
  23.4 0.2 branch_1_fun.5
  23.5 0.0 collective-permute-done.6.near_in_ref
  23.5 0.3 shard_map.98.refs_0_
  23.8 1.3 %collective-permute-start.7 = (f32[2,8,128]{2,1,0:T(8,128)S(1)}, f32[2,8,128]{2,1,0:T(8,128)S(1)}, u32[]{:S(2)}, u32[]{:S(2)}) collective-permute-start(f32[2,8,128]{2,1,0:T(8,128)S(1)} %shard_map.98.refs_0_), channel_id=1, source_target_pairs={{0,20},{4,16},{8,28},{12,24},{16,4},{20,0},{24,12},{28,8},{1,21},{... | collective-permute-start | bytes 24584 | tf_op jit(solution)/shard_map/ppermute | solution.py:433
  25.1 0.0 collective-permute-done.8.behind_keys_ref.refs_6_
  25.1 0.0 copy-done
  25.1 0.0 copy-done.3
  25.1 0.7 %shard_map.99.refs_2_ = f32[16,128,256]{2,1,0:T(8,128)S(1)} custom-call(s32[2,128]{1,0:T(2,128)S(1)} %bitcast.2, bf16[128,2048]{1,0:T(8,128)(2,1)S(1)} %copy-done, bf16[128,256]{1,0:T(8,128)(2,1)S(1)} %copy-done.1, bf16[128,256]{1,0:T(8,128)(2,1)S(1)} %collective-permute-done.8.behind_keys_ref.refs_6_), custom_call_target="tpu_custom_call" | custom-call | flops 134217728 | bytes 2097152 | tf_op jit(solution)/shard_map/pallas_call | solution.py:261
  25.8 1.1 %collective-permute-done.7.refs_1_ = f32[2,8,128]{2,1,0:T(8,128)S(1)} collective-permute-done((f32[2,8,128]{2,1,0:T(8,128)S(1)}, f32[2,8,128]{2,1,0:T(8,128)S(1)}, u32[]{:S(2)}, u32[]{:S(2)}) %collective-permute-start.7) | collective-permute-done | bytes 8224 | tf_op jit(solution)/shard_map/ppermute | solution.py:433
  26.9 2.2 %collective-permute-start.10 = (f32[2,128]{1,0:T(2,128)S(1)}, f32[2,128]{1,0:T(2,128)S(1)}, u32[]{:S(2)}, u32[]{:S(2)}) collective-permute-start(f32[2,128]{1,0:T(2,128)S(1)} %shard_map.100), channel_id=1, source_target_pairs={{0,16},{16,0},{1,17},{17,1},{2,18},{18,2},{3,19},{19,3},{4,20},{20... | collective-permute-start | bytes 3080 | tf_op jit(solution)/shard_map/ppermute | solution.py:437
  29.1 0.0 collective-permute-done.9.refs_8_
  29.2 1.6 %shard_map.101 = (bf16[128,2048]{1,0:T(8,128)(2,1)}, f32[2,128]{1,0:T(2,128)S(1)}) custom-call(f32[2,8,128]{2,1,0:T(8,128)S(1)} %shard_map.98.refs_0_, f32[2,8,128]{2,1,0:T(8,128)S(1)} %collective-permute-done.7.refs_1_, f32[16,128,256]{2,1,0:T(8,128)S(1)} %shard_map.99.refs_2_, s32[2,128]{1,0:T(2,128)S(1)} %bitcast.4, bf16[128,2048]{1,0:T(8,128)(2,1)S(1)} %copy-done, ...), custom_call_target="tpu_custom_call" | custom-call | flops 134217728 | bytes 1048576 | tf_op jit(solution)/shard_map/pallas_call | solution.py:386
  30.7 0.0 collective-permute-done.10
  30.7 0.5 %add_convert_fusion = bf16[2,128]{1,0:T(2,128)(2,1)} fusion(f32[2,128]{1,0:T(2,128)S(1)} %get-tuple-element.61, f32[2,128]{1,0:T(2,128)S(1)} %collective-permute-done.10), kind=kLoop, calls=%fused_computation.1 | loop fusion | flops 512 | bytes 2560 | tf_op jit(solution)/shard_map/convert_element_type | solution.py:438
  (4 shorter events, 0.1 us)
Async XLA Ops:
  0.6 15.1 %collective-permute-start.3 = (bf16[128,2048]{1,0:T(8,128)(2,1)}, bf16[128,2048]{1,0:T(8,128)(2,1)S(1)}, u32[]{:S(2)}, u32[]{:S(2)}) collective-permute-start(bf16[128,2048]{1,0:T(8,128)(2,1)} %param.12), channel_id=1, source_target_pairs={{0,16},{16,0},{1,17},{17,1},{2,18},{18,2},{3,19},{19,3},{4,20},{20... | collective-permute-start | bytes 1572872 | tf_op jit(solution)/shard_map/ppermute | solution.py:411
  3.6 9.4 %copy-start.5 = (bf16[8,1024]{1,0:T(8,128)(2,1)S(1)}, bf16[8,1024]{1,0:T(8,128)(2,1)}, u32[]{:S(2)}) copy-start(bf16[8,1024]{1,0:T(8,128)(2,1)} %get-tuple-element.21.gate_out_ref) | copy-start | bytes 49156 | tf_op jit(solution)/shard_map/cond
  6.2 1.5 %collective-permute-start.1 = (f32[112,512]{1,0:T(8,128)S(1)}, f32[112,512]{1,0:T(8,128)S(1)}, u32[]{:S(2)}, u32[]{:S(2)}) collective-permute-start(f32[112,512]{1,0:T(8,128)S(1)} %get-tuple-element.20), channel_id=1, source_target_pairs={{0,4},{4,0},{8,12},{12,8},{1,5},{5,1},{9,13},{13,9},{2,6},{6,2},{1... | collective-permute-start | bytes 688136 | tf_op jit(solution)/shard_map/cond/branch_1_fun/ppermute | solution.py:136
  7.8 5.3 %collective-permute-start.2 = (bf16[112,512]{1,0:T(8,128)(2,1)S(1)}, bf16[112,512]{1,0:T(8,128)(2,1)S(1)}, u32[]{:S(2)}, u32[]{:S(2)}) collective-permute-start(bf16[112,512]{1,0:T(8,128)(2,1)S(1)} %get-tuple-element.67), channel_id=1, source_target_pairs={{0,8},{4,12},{8,0},{12,4},{1,9},{5,13},{9,1},{13,5},{2,10},{6,14},... | collective-permute-start | bytes 344072 | tf_op jit(solution)/shard_map/cond/branch_1_fun/ppermute | solution.py:136
  13.2 6.6 %copy-start.1 = (bf16[128,256]{1,0:T(8,128)(2,1)S(1)}, bf16[128,256]{1,0:T(8,128)(2,1)}, u32[]{:S(2)}) copy-start(bf16[128,256]{1,0:T(8,128)(2,1)} %refs_5_.3) | copy-start | bytes 196612
  13.2 8.1 %copy-start.2 = (bf16[128,256]{1,0:T(8,128)(2,1)S(1)}, bf16[128,256]{1,0:T(8,128)(2,1)}, u32[]{:S(2)}) copy-start(bf16[128,256]{1,0:T(8,128)(2,1)} %refs_7_.1) | copy-start | bytes 196612
  13.2 8.7 %copy-start.4 = (bf16[1024,8]{0,1:T(8,128)(2,1)S(1)}, bf16[1024,8]{0,1:T(8,128)(2,1)}, u32[]{:S(2)}) copy-start(bf16[1024,8]{0,1:T(8,128)(2,1)} %param.15) | copy-start | bytes 49156
  13.2 11.9 %copy-start = (bf16[128,2048]{1,0:T(8,128)(2,1)S(1)}, bf16[128,2048]{1,0:T(8,128)(2,1)}, u32[]{:S(2)}) copy-start(bf16[128,2048]{1,0:T(8,128)(2,1)} %refs_4_.1) | copy-start | bytes 1572868
  13.2 11.9 %copy-start.3 = (s32[256]{0:T(256)S(1)}, s32[256]{0:T(256)}, u32[]{:S(2)}) copy-start(s32[256]{0:T(256)} %param.19) | copy-start | bytes 3076
  16.6 1.9 %collective-permute-start.5 = (f32[144,256]{1,0:T(8,128)S(1)}, f32[144,256]{1,0:T(8,128)S(1)}, u32[]{:S(2)}, u32[]{:S(2)}) collective-permute-start(f32[144,256]{1,0:T(8,128)S(1)} %get-tuple-element.54), channel_id=1, source_target_pairs={{0,4},{4,0},{8,12},{12,8},{1,5},{5,1},{9,13},{13,9},{2,6},{6,2},{1... | collective-permute-start | bytes 442376 | tf_op jit(solution)/shard_map/ppermute | solution.py:136
  16.6 5.3 %collective-permute-start.4 = (bf16[144,256]{1,0:T(8,128)(2,1)S(1)}, bf16[144,256]{1,0:T(8,128)(2,1)S(1)}, u32[]{:S(2)}, u32[]{:S(2)}) collective-permute-start(bf16[144,256]{1,0:T(8,128)(2,1)S(1)} %get-tuple-element.53), channel_id=1, source_target_pairs={{0,8},{4,12},{8,0},{12,4},{1,9},{5,13},{9,1},{13,5},{2,10},{6,14},... | collective-permute-start | bytes 221192 | tf_op jit(solution)/shard_map/ppermute | solution.py:136
  18.5 5.0 %collective-permute-start.6 = (bf16[144,256]{1,0:T(8,128)(2,1)S(1)}, bf16[144,256]{1,0:T(8,128)(2,1)S(1)}, u32[]{:S(2)}, u32[]{:S(2)}) collective-permute-start(bf16[144,256]{1,0:T(8,128)(2,1)S(1)} %get-tuple-element.69), channel_id=1, source_target_pairs={{0,8},{4,12},{8,0},{12,4},{1,9},{5,13},{9,1},{13,5},{2,10},{6,14},... | collective-permute-start | bytes 221192 | tf_op jit(solution)/shard_map/ppermute | solution.py:136
  19.9 5.2 %collective-permute-start.8 = (bf16[128,256]{1,0:T(8,128)(2,1)S(1)}, bf16[128,256]{1,0:T(8,128)(2,1)S(1)}, u32[]{:S(2)}, u32[]{:S(2)}) collective-permute-start(bf16[128,256]{1,0:T(8,128)(2,1)S(1)} %copy-done.1), channel_id=1, source_target_pairs={{0,16},{16,0},{1,17},{17,1},{2,18},{18,2},{3,19},{19,3},{4,20},{20... | collective-permute-start | bytes 196616 | tf_op jit(solution)/shard_map/ppermute | solution.py:420
  21.4 7.8 %collective-permute-start.9 = (bf16[128,256]{1,0:T(8,128)(2,1)S(1)}, bf16[128,256]{1,0:T(8,128)(2,1)S(1)}, u32[]{:S(2)}, u32[]{:S(2)}) collective-permute-start(bf16[128,256]{1,0:T(8,128)(2,1)S(1)} %copy-done.2), channel_id=1, source_target_pairs={{0,16},{16,0},{1,17},{17,1},{2,18},{18,2},{3,19},{19,3},{4,20},{20... | collective-permute-start | bytes 196616 | tf_op jit(solution)/shard_map/ppermute | solution.py:421
  21.9 1.4 %collective-permute-start = (f32[144,256]{1,0:T(8,128)S(1)}, f32[144,256]{1,0:T(8,128)S(1)}, u32[]{:S(2)}, u32[]{:S(2)}) collective-permute-start(f32[144,256]{1,0:T(8,128)S(1)} %convert_add_fusion.own_ref), channel_id=1, source_target_pairs={{0,4},{4,0},{8,12},{12,8},{1,5},{5,1},{9,13},{13,9},{2,6},{6,2},{1... | collective-permute-start | bytes 442376 | tf_op jit(solution)/shard_map/cond/branch_1_fun/ppermute | solution.py:136
  23.8 3.1 %collective-permute-start.7 = (f32[2,8,128]{2,1,0:T(8,128)S(1)}, f32[2,8,128]{2,1,0:T(8,128)S(1)}, u32[]{:S(2)}, u32[]{:S(2)}) collective-permute-start(f32[2,8,128]{2,1,0:T(8,128)S(1)} %shard_map.98.refs_0_), channel_id=1, source_target_pairs={{0,20},{4,16},{8,28},{12,24},{16,4},{20,0},{24,12},{28,8},{1,21},{... | collective-permute-start | bytes 24584 | tf_op jit(solution)/shard_map/ppermute | solution.py:433
  26.9 3.8 %collective-permute-start.10 = (f32[2,128]{1,0:T(2,128)S(1)}, f32[2,128]{1,0:T(2,128)S(1)}, u32[]{:S(2)}, u32[]{:S(2)}) collective-permute-start(f32[2,128]{1,0:T(2,128)S(1)} %shard_map.100), channel_id=1, source_target_pairs={{0,16},{16,0},{1,17},{17,1},{2,18},{18,2},{3,19},{19,3},{4,20},{20... | collective-permute-start | bytes 3080 | tf_op jit(solution)/shard_map/ppermute | solution.py:437

commit v17 on v16

--- a/solution.py
+++ b/solution.py
@@ -15,6 +15,7 @@
 
 NEG_FILL = -1e30
 RIM_ROWS = 16
+PIECE_HEADS = 4
 LEAST_RETENTION = -40.0
 VMEM_BYTES = 16 * 1024 * 1024
 
@@ -155,7 +156,7 @@
         while distance > 1:
             distance //= 2
             block = block.astype(jnp.float32) + received.astype(jnp.float32)
-            received = exchange_heads(block, distance)
+            received = exchange_heads(block.astype(jnp.bfloat16), distance)
         return partial_logits(block, received, gate_out, block.shape[1])
 
     return in_one_piece(nearer, block, received, gate_out)
@@ -284,7 +285,15 @@
 
 
 def by_group(
-    whole, biases, powers_ref, segments_ref, queries_ref, keys_ref, behind_keys_ref, group
+    whole,
+    biases,
+    powers_ref,
+    segments_ref,
+    queries_ref,
+    keys_ref,
+    behind_keys_ref,
+    group,
+    finish=None,
 ):
     rows = queries_ref.shape[0]
     start = 0 if whole else rows
@@ -308,6 +317,9 @@
     def run(terms_of):
         for g in range(len(biases)):
             group(g, terms_of(g))
+
+        if finish is not None:
+            finish()
 
     pl.when(moderate)(lambda: run(by_powers))
     pl.when(jnp.logical_not(moderate))(lambda: run(by_scores))
@@ -353,9 +365,19 @@
 
 def attend_kernel(*refs):
     *share_refs, powers_ref, segments_ref, queries_ref, keys_ref, behind_keys_ref = refs[:7]
-    values_ref, behind_values_ref, attended_ref, mass_ref, retention = refs[7:]
+    values_ref, behind_values_ref, attended_hbm, mass_ref, retention, attended_ref, done = refs[7:]
     rows = queries_ref.shape[0]
     group_size = queries_ref.shape[1] // keys_ref.shape[1]
+
+    def copy_out(piece):
+        columns = slice(piece * PIECE_HEADS * HEAD_DIM, (piece + 1) * PIECE_HEADS * HEAD_DIM)
+        return pltpu.make_async_copy(
+            attended_ref.at[:, columns], attended_hbm.at[:, columns], done.at[piece]
+        )
+
+    def finish():
+        for piece in range(done.shape[0]):
+            copy_out(piece).wait()
 
     def fill(whole):
         def group(g, terms_of):
@@ -369,11 +391,21 @@
                 attended_ref[:, head_columns(head)] = jnp.dot(
                     weights.astype(jnp.bfloat16), values, preferred_element_type=jnp.float32
                 ).astype(jnp.bfloat16)
+                if (head + 1) % PIECE_HEADS == 0:
+                    copy_out(head // PIECE_HEADS).start()
             mass_ref[g : g + 1, :] = mass / group_size
 
         biases = read_retention(share_refs, retention)
         by_group(
-            whole, biases, powers_ref, segments_ref, queries_ref, keys_ref, behind_keys_ref, group
+            whole,
+            biases,
+            powers_ref,
+            segments_ref,
+            queries_ref,
+            keys_ref,
+            behind_keys_ref,
+            group,
+            finish,
         )
 
     pl.when(lax.axis_index("seq") > 0)(lambda: fill(True))
@@ -385,11 +417,19 @@
     shares, powers, sent = lax.optimization_barrier((shares, powers, sent))
     attended, mass = pl.pallas_call(
         attend_kernel,
+        out_specs=(
+            pl.BlockSpec(memory_space=pl.ANY),
+            pl.BlockSpec(memory_space=pltpu.VMEM),
+        ),
         out_shape=(
             jax.ShapeDtypeStruct(queries.shape, jnp.bfloat16),
             jax.ShapeDtypeStruct((keys.shape[1] // HEAD_DIM, rows), jnp.float32),
         ),
-        scratch_shapes=[pltpu.VMEM(shares[0].shape, jnp.float32)],
+        scratch_shapes=[
+            pltpu.VMEM(shares[0].shape, jnp.float32),
+            pltpu.VMEM(queries.shape, jnp.bfloat16),
+            pltpu.SemaphoreType.DMA((queries.shape[1] // HEAD_DIM // PIECE_HEADS,)),
+        ],
         compiler_params=pltpu.CompilerParams(vmem_limit_bytes=VMEM_BYTES),
         cost_estimate=pl.CostEstimate(
             flops=4 * rows * rows * queries.shape[1],

time: 31.4 us -> 31.3 us (level)
  transfers between devices with their start and end apart: 11 -> 11, of which waited for: 5 -> 6; matrix products, arithmetic and copies ran while one was open for 0% -> 0% of each run, Pallas kernels for 17% -> 17%
where the time goes in v17:
time: 31.3 us; the launch traced here: 31.1 us
  starting transfers between devices  13.5 us (43%)
  waiting for transfers between devices  10.1 us (32%)
  Pallas kernels  6.15 us (20%)
  between operations  0.7 us (2%)
  other arithmetic  0.59 us (2%)
    ppermute x6, waiting for transfers between devices, exchange_heads(): return lax.ppermute(block, 'heads', [(i, i ^ step) for i in range(count)])  6.4 us
    ppermute x6, starting transfers between devices, exchange_heads(): return lax.ppermute(block, 'heads', [(i, i ^ step) for i in range(count)])  4.97 us
    ppermute x1, starting transfers between devices, pair_device(): peer_rows = lax.ppermute(activations, 'seq', swap)  3 us
    pallas_call x1, Pallas kernels, own_project(): pl.pallas_call(own_project_kernel, out_shape=(jax.ShapeDtypeStruct((done,...  2.55 us
    ppermute x1, waiting for transfers between devices, pair_device(): peer_rows = lax.ppermute(activations, 'seq', swap)  2.51 us
    ppermute x1, starting transfers between devices, pair_device(): key_mass = own_mass + lax.ppermute(sent, 'seq', swap)  2.22 us
    ppermute x1, starting transfers between devices, pair_device(): behind_keys = lax.ppermute(key_vectors, 'seq', swap)  1.49 us
    pallas_call x1, Pallas kernels, attend(): pl.pallas_call(attend_kernel, out_specs=(pl.BlockSpec(memory_space=pl.ANY...  1.45 us
  transfers between devices with their start and end apart: 11, of which 6 were waited for; matrix products, arithmetic and copies ran while one was open for 0% of the time, Pallas kernels for 17%

profile of v17, /device:TPU:0, one launch (start us, length us, event | category | flops | bytes accessed | tf_op | source)
XLA Modules:
  0.0 31.1 jit_solution(11654172791464431439)
XLA Ops:
  0.6 3.0 %collective-permute-start.3 = (bf16[128,2048]{1,0:T(8,128)(2,1)}, bf16[128,2048]{1,0:T(8,128)(2,1)S(1)}, u32[]{:S(2)}, u32[]{:S(2)}) collective-permute-start(bf16[128,2048]{1,0:T(8,128)(2,1)} %param.12), channel_id=1, source_target_pairs={{0,16},{16,0},{1,17},{17,1},{2,18},{18,2},{3,19},{19,3},{4,20},{20... | collective-permute-start | bytes 1572872 | tf_op jit(solution)/shard_map/ppermute | solution.py:451
  3.6 9.6 %conditional.2 = (f32[8,112]{1,0:T(8,128)S(1)}, f32[4,2048]{1,0:T(4,128)S(1)}, bf16[2176,512]{1,0:T(8,128)(2,1)S(1)}) conditional(s32[]{:T(128)} %convert_element_type.22, () %tuple.25, (bf16[128,2048]{1,0:T(8,128)(2,1)}, bf16[4,2048]{1,0:T(4,128)(2,1)}, bf16[2048,512]{1,0:T(8,128)(2,1)}, bf16[8,1024]{1,0:T(8,128)(2,1)}) %tuple.40), branch_computations={%region_0.0_spmd, %region_1.0_spmd} | conditional | flops 114689 | bytes 2264610 | solution.py:142
  3.6 0.0 copy-start.5
  3.6 2.6 %branch_1_fun.3 = (f32[112,512]{1,0:T(8,128)S(1)}, f32[4,2048]{1,0:T(4,128)S(1)}, bf16[2176,512]{1,0:T(8,128)(2,1)S(1)}) custom-call(bf16[128,2048]{1,0:T(8,128)(2,1)} %get-tuple-element.10.rows_ref, bf16[4,2048]{1,0:T(4,128)(2,1)} %get-tuple-element.65.taps_ref, bf16[2048,512]{1,0:T(8,128)(2,1)} %get-tuple-element.66.gate_ref), custom_call_target="tpu_custom_call" | custom-call | flops 1 | bytes 1 | tf_op jit(solution)/shard_map/cond/branch_1_fun/pallas_call | solution.py:88
  6.2 0.1 collective-permute-start.1
  6.3 1.5 %collective-permute-done.1 = f32[112,512]{1,0:T(8,128)S(1)} collective-permute-done((f32[112,512]{1,0:T(8,128)S(1)}, f32[112,512]{1,0:T(8,128)S(1)}, u32[]{:S(2)}, u32[]{:S(2)}) %collective-permute-start.1) | collective-permute-done | bytes 229408 | tf_op jit(solution)/shard_map/cond/branch_1_fun/ppermute | solution.py:137
  7.8 1.6 %collective-permute-start.2 = (bf16[112,512]{1,0:T(8,128)(2,1)S(1)}, bf16[112,512]{1,0:T(8,128)(2,1)S(1)}, u32[]{:S(2)}, u32[]{:S(2)}) collective-permute-start(bf16[112,512]{1,0:T(8,128)(2,1)S(1)} %get-tuple-element.67), channel_id=1, source_target_pairs={{0,8},{4,12},{8,0},{12,4},{1,9},{5,13},{9,1},{13,5},{2,10},{6,14},... | collective-permute-start | bytes 344072 | tf_op jit(solution)/shard_map/cond/branch_1_fun/ppermute | solution.py:137
  9.4 3.7 %collective-permute-done.2.in_ref = bf16[112,512]{1,0:T(8,128)(2,1)S(1)} collective-permute-done((bf16[112,512]{1,0:T(8,128)(2,1)S(1)}, bf16[112,512]{1,0:T(8,128)(2,1)S(1)}, u32[]{:S(2)}, u32[]{:S(2)}) %collective-permute-start.2) | collective-permute-done | bytes 114720 | tf_op jit(solution)/shard_map/cond/branch_1_fun/ppermute | solution.py:137
  13.0 0.0 copy-done.5
  13.0 0.2 branch_1_fun.4
  13.2 0.0 copy-start.1
  13.2 0.0 copy-start.2
  13.2 0.0 copy-start.4
  13.2 0.0 copy-start
  13.2 0.0 copy-start.3
  13.3 2.5 %collective-permute-done.3.peer_ref = bf16[128,2048]{1,0:T(8,128)(2,1)S(1)} collective-permute-done((bf16[128,2048]{1,0:T(8,128)(2,1)}, bf16[128,2048]{1,0:T(8,128)(2,1)S(1)}, u32[]{:S(2)}, u32[]{:S(2)}) %collective-permute-start.3) | collective-permute-done | bytes 524320 | tf_op jit(solution)/shard_map/ppermute | solution.py:451
  15.8 0.8 %shard_map.97 = (f32[144,256]{1,0:T(8,128)S(1)}, bf16[144,256]{1,0:T(8,128)(2,1)S(1)}) custom-call(bf16[128,2048]{1,0:T(8,128)(2,1)S(1)} %collective-permute-done.3.peer_ref, f32[4,2048]{1,0:T(4,128)S(1)} %get-tuple-element.51.taps_ref, bf16[2176,512]{1,0:T(8,128)(2,1)S(1)} %get-tuple-element.52.held_ref), custom_call_target="tpu_custom_call" | custom-call | flops 1 | bytes 1 | tf_op jit(solution)/shard_map/pallas_call | solution.py:108
  16.6 0.1 collective-permute-start.5
  16.6 1.8 %collective-permute-start.4 = (bf16[144,256]{1,0:T(8,128)(2,1)S(1)}, bf16[144,256]{1,0:T(8,128)(2,1)S(1)}, u32[]{:S(2)}, u32[]{:S(2)}) collective-permute-start(bf16[144,256]{1,0:T(8,128)(2,1)S(1)} %get-tuple-element.53), channel_id=1, source_target_pairs={{0,8},{4,12},{8,0},{12,4},{1,9},{5,13},{9,1},{13,5},{2,10},{6,14},... | collective-permute-start | bytes 221192 | tf_op jit(solution)/shard_map/ppermute | solution.py:137
  18.5 0.0 collective-permute-done.5
  18.5 1.4 %collective-permute-start.6 = (bf16[144,256]{1,0:T(8,128)(2,1)S(1)}, bf16[144,256]{1,0:T(8,128)(2,1)S(1)}, u32[]{:S(2)}, u32[]{:S(2)}) collective-permute-start(bf16[144,256]{1,0:T(8,128)(2,1)S(1)} %get-tuple-element.69), channel_id=1, source_target_pairs={{0,8},{4,12},{8,0},{12,4},{1,9},{5,13},{9,1},{13,5},{2,10},{6,14},... | collective-permute-start | bytes 221192 | tf_op jit(solution)/shard_map/ppermute | solution.py:137
  19.9 0.0 copy-done.1
  19.9 1.5 %collective-permute-start.8 = (bf16[128,256]{1,0:T(8,128)(2,1)S(1)}, bf16[128,256]{1,0:T(8,128)(2,1)S(1)}, u32[]{:S(2)}, u32[]{:S(2)}) collective-permute-start(bf16[128,256]{1,0:T(8,128)(2,1)S(1)} %copy-done.1), channel_id=1, source_target_pairs={{0,16},{16,0},{1,17},{17,1},{2,18},{18,2},{3,19},{19,3},{4,20},{20... | collective-permute-start | bytes 196616 | tf_op jit(solution)/shard_map/ppermute | solution.py:460
  21.4 0.0 copy-done.2
  21.4 0.5 %collective-permute-start.9 = (bf16[128,256]{1,0:T(8,128)(2,1)S(1)}, bf16[128,256]{1,0:T(8,128)(2,1)S(1)}, u32[]{:S(2)}, u32[]{:S(2)}) collective-permute-start(bf16[128,256]{1,0:T(8,128)(2,1)S(1)} %copy-done.2), channel_id=1, source_target_pairs={{0,16},{16,0},{1,17},{17,1},{2,18},{18,2},{3,19},{19,3},{4,20},{20... | collective-permute-start | bytes 196616 | tf_op jit(solution)/shard_map/ppermute | solution.py:461
  21.9 0.0 collective-permute-done.4
  21.9 0.0 copy-done.4
  21.9 1.5 %conditional.3 = (f32[8,144]{1,0:T(8,128)S(1)}) conditional(s32[]{:T(128)} %convert_element_type.22, () %tuple.28, (bf16[144,256]{1,0:T(8,128)(2,1)S(1)}, bf16[144,256]{1,0:T(8,128)(2,1)S(1)}, bf16[8,1024]{1,0:T(8,128)(2,1)S(1)}) %tuple.41), branch_computations={%region_2.0_spmd, %region_3.0_spmd} | conditional | flops 147456 | bytes 663600 | solution.py:142
  21.9 0.1 collective-permute-start
  22.0 1.3 %collective-permute-done.in_ref = bf16[144,256]{1,0:T(8,128)(2,1)S(1)} collective-permute-done((bf16[144,256]{1,0:T(8,128)(2,1)S(1)}, bf16[144,256]{1,0:T(8,128)(2,1)S(1)}, u32[]{:S(2)}, u32[]{:S(2)}) %collective-permute-start) | collective-permute-done | bytes 73760 | tf_op jit(solution)/shard_map/cond/branch_1_fun/ppermute | solution.py:137
  23.3 0.2 branch_1_fun.5
  23.4 0.0 collective-permute-done.6.near_in_ref
  23.4 0.3 shard_map.98.refs_0_
  23.7 1.3 %collective-permute-start.7 = (f32[2,8,128]{2,1,0:T(8,128)S(1)}, f32[2,8,128]{2,1,0:T(8,128)S(1)}, u32[]{:S(2)}, u32[]{:S(2)}) collective-permute-start(f32[2,8,128]{2,1,0:T(8,128)S(1)} %shard_map.98.refs_0_), channel_id=1, source_target_pairs={{0,20},{4,16},{8,28},{12,24},{16,4},{20,0},{24,12},{28,8},{1,21},{... | collective-permute-start | bytes 24584 | tf_op jit(solution)/shard_map/ppermute | solution.py:473
  25.0 0.0 collective-permute-done.8.behind_keys_ref.refs_6_
  25.0 0.0 copy-done
  25.0 0.0 copy-done.3
  25.0 0.7 %shard_map.99.refs_2_ = f32[16,128,256]{2,1,0:T(8,128)S(1)} custom-call(s32[2,128]{1,0:T(2,128)S(1)} %bitcast.2, bf16[128,2048]{1,0:T(8,128)(2,1)S(1)} %copy-done, bf16[128,256]{1,0:T(8,128)(2,1)S(1)} %copy-done.1, bf16[128,256]{1,0:T(8,128)(2,1)S(1)} %collective-permute-done.8.behind_keys_ref.refs_6_), custom_call_target="tpu_custom_call" | custom-call | flops 134217728 | bytes 2097152 | tf_op jit(solution)/shard_map/pallas_call | solution.py:262
  25.7 1.1 %collective-permute-done.7.refs_1_ = f32[2,8,128]{2,1,0:T(8,128)S(1)} collective-permute-done((f32[2,8,128]{2,1,0:T(8,128)S(1)}, f32[2,8,128]{2,1,0:T(8,128)S(1)}, u32[]{:S(2)}, u32[]{:S(2)}) %collective-permute-start.7) | collective-permute-done | bytes 8224 | tf_op jit(solution)/shard_map/ppermute | solution.py:473
  26.8 2.2 %collective-permute-start.10 = (f32[2,128]{1,0:T(2,128)S(1)}, f32[2,128]{1,0:T(2,128)S(1)}, u32[]{:S(2)}, u32[]{:S(2)}) collective-permute-start(f32[2,128]{1,0:T(2,128)S(1)} %shard_map.100), channel_id=1, source_target_pairs={{0,16},{16,0},{1,17},{17,1},{2,18},{18,2},{3,19},{19,3},{4,20},{20... | collective-permute-start | bytes 3080 | tf_op jit(solution)/shard_map/ppermute | solution.py:477
  29.0 0.0 collective-permute-done.9.refs_8_
  29.1 1.4 %shard_map.101 = (bf16[128,2048]{1,0:T(8,128)(2,1)}, f32[2,128]{1,0:T(2,128)S(1)}) custom-call(f32[2,8,128]{2,1,0:T(8,128)S(1)} %shard_map.98.refs_0_, f32[2,8,128]{2,1,0:T(8,128)S(1)} %collective-permute-done.7.refs_1_, f32[16,128,256]{2,1,0:T(8,128)S(1)} %shard_map.99.refs_2_, s32[2,128]{1,0:T(2,128)S(1)} %bitcast.4, bf16[128,2048]{1,0:T(8,128)(2,1)S(1)} %copy-done, ...), custom_call_target="tpu_custom_call" | custom-call | flops 134217728 | bytes 1048576 | tf_op jit(solution)/shard_map/pallas_call | solution.py:418
  30.5 0.1 collective-permute-done.10
  30.6 0.5 %add_convert_fusion = bf16[2,128]{1,0:T(2,128)(2,1)} fusion(f32[2,128]{1,0:T(2,128)S(1)} %get-tuple-element.61, f32[2,128]{1,0:T(2,128)S(1)} %collective-permute-done.10), kind=kLoop, calls=%fused_computation.2 | loop fusion | flops 512 | bytes 2560 | tf_op jit(solution)/shard_map/convert_element_type | solution.py:478
  (4 shorter events, 0.1 us)
Async XLA Ops:
  0.6 15.1 %collective-permute-start.3 = (bf16[128,2048]{1,0:T(8,128)(2,1)}, bf16[128,2048]{1,0:T(8,128)(2,1)S(1)}, u32[]{:S(2)}, u32[]{:S(2)}) collective-permute-start(bf16[128,2048]{1,0:T(8,128)(2,1)} %param.12), channel_id=1, source_target_pairs={{0,16},{16,0},{1,17},{17,1},{2,18},{18,2},{3,19},{19,3},{4,20},{20... | collective-permute-start | bytes 1572872 | tf_op jit(solution)/shard_map/ppermute | solution.py:451
  3.6 9.4 %copy-start.5 = (bf16[8,1024]{1,0:T(8,128)(2,1)S(1)}, bf16[8,1024]{1,0:T(8,128)(2,1)}, u32[]{:S(2)}) copy-start(bf16[8,1024]{1,0:T(8,128)(2,1)} %get-tuple-element.21.gate_out_ref) | copy-start | bytes 49156 | tf_op jit(solution)/shard_map/cond
  6.2 1.5 %collective-permute-start.1 = (f32[112,512]{1,0:T(8,128)S(1)}, f32[112,512]{1,0:T(8,128)S(1)}, u32[]{:S(2)}, u32[]{:S(2)}) collective-permute-start(f32[112,512]{1,0:T(8,128)S(1)} %get-tuple-element.20), channel_id=1, source_target_pairs={{0,4},{4,0},{8,12},{12,8},{1,5},{5,1},{9,13},{13,9},{2,6},{6,2},{1... | collective-permute-start | bytes 688136 | tf_op jit(solution)/shard_map/cond/branch_1_fun/ppermute | solution.py:137
  7.8 5.3 %collective-permute-start.2 = (bf16[112,512]{1,0:T(8,128)(2,1)S(1)}, bf16[112,512]{1,0:T(8,128)(2,1)S(1)}, u32[]{:S(2)}, u32[]{:S(2)}) collective-permute-start(bf16[112,512]{1,0:T(8,128)(2,1)S(1)} %get-tuple-element.67), channel_id=1, source_target_pairs={{0,8},{4,12},{8,0},{12,4},{1,9},{5,13},{9,1},{13,5},{2,10},{6,14},... | collective-permute-start | bytes 344072 | tf_op jit(solution)/shard_map/cond/branch_1_fun/ppermute | solution.py:137
  13.2 6.6 %copy-start.1 = (bf16[128,256]{1,0:T(8,128)(2,1)S(1)}, bf16[128,256]{1,0:T(8,128)(2,1)}, u32[]{:S(2)}) copy-start(bf16[128,256]{1,0:T(8,128)(2,1)} %refs_5_.3) | copy-start | bytes 196612
  13.2 8.1 %copy-start.2 = (bf16[128,256]{1,0:T(8,128)(2,1)S(1)}, bf16[128,256]{1,0:T(8,128)(2,1)}, u32[]{:S(2)}) copy-start(bf16[128,256]{1,0:T(8,128)(2,1)} %refs_7_.1) | copy-start | bytes 196612
  13.2 8.7 %copy-start.4 = (bf16[1024,8]{0,1:T(8,128)(2,1)S(1)}, bf16[1024,8]{0,1:T(8,128)(2,1)}, u32[]{:S(2)}) copy-start(bf16[1024,8]{0,1:T(8,128)(2,1)} %param.15) | copy-start | bytes 49156
  13.2 11.8 %copy-start = (bf16[128,2048]{1,0:T(8,128)(2,1)S(1)}, bf16[128,2048]{1,0:T(8,128)(2,1)}, u32[]{:S(2)}) copy-start(bf16[128,2048]{1,0:T(8,128)(2,1)} %refs_4_.1) | copy-start | bytes 1572868
  13.2 11.8 %copy-start.3 = (s32[256]{0:T(256)S(1)}, s32[256]{0:T(256)}, u32[]{:S(2)}) copy-start(s32[256]{0:T(256)} %param.19) | copy-start | bytes 3076
  16.6 1.9 %collective-permute-start.5 = (f32[144,256]{1,0:T(8,128)S(1)}, f32[144,256]{1,0:T(8,128)S(1)}, u32[]{:S(2)}, u32[]{:S(2)}) collective-permute-start(f32[144,256]{1,0:T(8,128)S(1)} %get-tuple-element.54), channel_id=1, source_target_pairs={{0,4},{4,0},{8,12},{12,8},{1,5},{5,1},{9,13},{13,9},{2,6},{6,2},{1... | collective-permute-start | bytes 442376 | tf_op jit(solution)/shard_map/ppermute | solution.py:137
  16.6 5.3 %collective-permute-start.4 = (bf16[144,256]{1,0:T(8,128)(2,1)S(1)}, bf16[144,256]{1,0:T(8,128)(2,1)S(1)}, u32[]{:S(2)}, u32[]{:S(2)}) collective-permute-start(bf16[144,256]{1,0:T(8,128)(2,1)S(1)} %get-tuple-element.53), channel_id=1, source_target_pairs={{0,8},{4,12},{8,0},{12,4},{1,9},{5,13},{9,1},{13,5},{2,10},{6,14},... | collective-permute-start | bytes 221192 | tf_op jit(solution)/shard_map/ppermute | solution.py:137
  18.5 4.9 %collective-permute-start.6 = (bf16[144,256]{1,0:T(8,128)(2,1)S(1)}, bf16[144,256]{1,0:T(8,128)(2,1)S(1)}, u32[]{:S(2)}, u32[]{:S(2)}) collective-permute-start(bf16[144,256]{1,0:T(8,128)(2,1)S(1)} %get-tuple-element.69), channel_id=1, source_target_pairs={{0,8},{4,12},{8,0},{12,4},{1,9},{5,13},{9,1},{13,5},{2,10},{6,14},... | collective-permute-start | bytes 221192 | tf_op jit(solution)/shard_map/ppermute | solution.py:137
  19.9 5.1 %collective-permute-start.8 = (bf16[128,256]{1,0:T(8,128)(2,1)S(1)}, bf16[128,256]{1,0:T(8,128)(2,1)S(1)}, u32[]{:S(2)}, u32[]{:S(2)}) collective-permute-start(bf16[128,256]{1,0:T(8,128)(2,1)S(1)} %copy-done.1), channel_id=1, source_target_pairs={{0,16},{16,0},{1,17},{17,1},{2,18},{18,2},{3,19},{19,3},{4,20},{20... | collective-permute-start | bytes 196616 | tf_op jit(solution)/shard_map/ppermute | solution.py:460
  21.4 7.7 %collective-permute-start.9 = (bf16[128,256]{1,0:T(8,128)(2,1)S(1)}, bf16[128,256]{1,0:T(8,128)(2,1)S(1)}, u32[]{:S(2)}, u32[]{:S(2)}) collective-permute-start(bf16[128,256]{1,0:T(8,128)(2,1)S(1)} %copy-done.2), channel_id=1, source_target_pairs={{0,16},{16,0},{1,17},{17,1},{2,18},{18,2},{3,19},{19,3},{4,20},{20... | collective-permute-start | bytes 196616 | tf_op jit(solution)/shard_map/ppermute | solution.py:461
  21.9 1.3 %collective-permute-start = (bf16[144,256]{1,0:T(8,128)(2,1)S(1)}, bf16[144,256]{1,0:T(8,128)(2,1)S(1)}, u32[]{:S(2)}, u32[]{:S(2)}) collective-permute-start(bf16[144,256]{1,0:T(8,128)(2,1)S(1)} %get-tuple-element.71), channel_id=1, source_target_pairs={{0,4},{4,0},{8,12},{12,8},{1,5},{5,1},{9,13},{13,9},{2,6},{6,2},{1... | collective-permute-start | bytes 221192 | tf_op jit(solution)/shard_map/cond/branch_1_fun/ppermute | solution.py:137
  23.7 3.1 %collective-permute-start.7 = (f32[2,8,128]{2,1,0:T(8,128)S(1)}, f32[2,8,128]{2,1,0:T(8,128)S(1)}, u32[]{:S(2)}, u32[]{:S(2)}) collective-permute-start(f32[2,8,128]{2,1,0:T(8,128)S(1)} %shard_map.98.refs_0_), channel_id=1, source_target_pairs={{0,20},{4,16},{8,28},{12,24},{16,4},{20,0},{24,12},{28,8},{1,21},{... | collective-permute-start | bytes 24584 | tf_op jit(solution)/shard_map/ppermute | solution.py:473
  26.8 3.8 %collective-permute-start.10 = (f32[2,128]{1,0:T(2,128)S(1)}, f32[2,128]{1,0:T(2,128)S(1)}, u32[]{:S(2)}, u32[]{:S(2)}) collective-permute-start(f32[2,128]{1,0:T(2,128)S(1)} %shard_map.100), channel_id=1, source_target_pairs={{0,16},{16,0},{1,17},{17,1},{2,18},{18,2},{3,19},{19,3},{4,20},{20... | collective-permute-start | bytes 3080 | tf_op jit(solution)/shard_map/ppermute | solution.py:477

commit v18 on v17

--- a/solution.py
+++ b/solution.py
@@ -29,7 +29,7 @@
 
 def own_project_kernel(rows_ref, taps_ref, gate_ref, out_ref, held_taps_ref, held_ref, widened):
     rows, features = rows_ref.shape
-    held_taps_ref[...] = taps_ref[...].astype(jnp.float32)
+    held_taps_ref[...] = taps_ref[...]
     held_ref[:features] = gate_ref[...]
     tile = widened.shape[2]
     total = jnp.zeros(out_ref.shape, jnp.float32)
@@ -42,7 +42,7 @@
         ]
         wide = widened.at[step % 2]
         wide[...] = rows_ref[:, columns].astype(jnp.float32)
-        taps = taps_ref[:, columns].astype(jnp.float32)
+        taps = taps_ref[:, columns]
         mixed = convolve(wide, taps, RIM_ROWS, rows - RIM_ROWS)
         total = total + jnp.dot(mixed, gate_ref[columns, :], preferred_element_type=jnp.float32)
     out_ref[...] = total
@@ -68,7 +68,7 @@
         wide[RIM_ROWS:] = peer_ref[:, columns].astype(jnp.float32)
         own_wide[:RIM_ROWS] = jnp.where(first, 0.0, peer_tail)
         own_wide[RIM_ROWS:] = edges[:RIM_ROWS].astype(jnp.float32)
-        taps = taps_ref[:, columns].astype(jnp.float32)
+        taps = taps_ref[:, columns]
         mixed = jnp.concatenate(
             [
                 convolve(own_wide, taps, RIM_ROWS, RIM_ROWS),
@@ -167,7 +167,7 @@
     hidden = (pre / (1.0 + jnp.exp(-pre))).astype(jnp.bfloat16)
     share = gate_out_ref.shape[1] // lax.axis_size("seq")
     start = pl.multiple_of(lax.axis_index("seq") * share + offset, HEAD_DIM)
-    gate_columns = gate_out_ref[:, pl.ds(start, pre.shape[1])]
+    gate_columns = gate_out_ref[:, pl.ds(start, pre.shape[1])].astype(jnp.bfloat16)
     return lax.dot_general(
         gate_columns, hidden, (((1,), (1,)), ((), ())), preferred_element_type=jnp.float32
     )
@@ -446,7 +446,8 @@
     rows = activations.shape[0]
     swap = [(0, 1), (1, 0)]
     segments = segment_ids.reshape(2, rows)
-    gate_out = jnp.transpose(gate_out)
+    gate_out = jnp.transpose(gate_out).astype(jnp.float32)
+    conv_taps = conv_taps.astype(jnp.float32)
 
     peer_rows = lax.ppermute(activations, "seq", swap)
 

time: 31.3 us -> 31.5 us (level)
  other arithmetic: 0.59 us -> 2.03 us
  waiting for transfers between devices: 10.1 us -> 8.71 us
    convert_element_type x0 -> x2, other arithmetic: none -> 1.44 us  [the longest x1 0.72 us: pair_device(): conv_taps = conv_taps.astype(jnp.float32)]
    ppermute x1, waiting for transfers between devices: 2.51 us -> 1.11 us  [pair_device(): peer_rows = lax.ppermute(activations, 'seq', swap)]
  transfers between devices with their start and end apart: 11 -> 11, of which waited for: 6 -> 6; matrix products, arithmetic and copies ran while one was open for 0% -> 5% of each run, Pallas kernels for 17% -> 17%
where the time goes in v18:
time: 31.5 us; the launch traced here: 31.1 us
  starting transfers between devices  13.5 us (43%)
  waiting for transfers between devices  8.71 us (28%)
  Pallas kernels  6.13 us (19%)
  other arithmetic  2.03 us (6%)
  between operations  0.69 us (2%)
    ppermute x6, waiting for transfers between devices, exchange_heads(): return lax.ppermute(block, 'heads', [(i, i ^ step) for i in range(count)])  6.4 us
    ppermute x6, starting transfers between devices, exchange_heads(): return lax.ppermute(block, 'heads', [(i, i ^ step) for i in range(count)])  4.97 us
    ppermute x1, starting transfers between devices, pair_device(): peer_rows = lax.ppermute(activations, 'seq', swap)  3 us
    pallas_call x1, Pallas kernels, own_project(): pl.pallas_call(own_project_kernel, out_shape=(jax.ShapeDtypeStruct((done,...  2.53 us
    ppermute x1, starting transfers between devices, pair_device(): key_mass = own_mass + lax.ppermute(sent, 'seq', swap)  2.22 us
    ppermute x1, starting transfers between devices, pair_device(): behind_keys = lax.ppermute(key_vectors, 'seq', swap)  1.49 us
    pallas_call x1, Pallas kernels, attend(): pl.pallas_call(attend_kernel, out_specs=(pl.BlockSpec(memory_space=pl.ANY...  1.45 us
    ppermute x1, starting transfers between devices, pair_device(): shares = (share, lax.ppermute(share, ('seq', 'heads'), across))  1.28 us
  transfers between devices with their start and end apart: 11, of which 6 were waited for; matrix products, arithmetic and copies ran while one was open for 5% of the time, Pallas kernels for 17%

profile of v18, /device:TPU:0, one launch (start us, length us, event | category | flops | bytes accessed | tf_op | source)
XLA Modules:
  0.0 31.1 jit_solution(12445134997389811595)
XLA Ops:
  0.6 3.0 %collective-permute-start.3 = (bf16[128,2048]{1,0:T(8,128)(2,1)}, bf16[128,2048]{1,0:T(8,128)(2,1)S(1)}, u32[]{:S(2)}, u32[]{:S(2)}) collective-permute-start(bf16[128,2048]{1,0:T(8,128)(2,1)} %param.12), channel_id=1, source_target_pairs={{0,16},{16,0},{1,17},{17,1},{2,18},{18,2},{3,19},{19,3},{4,20},{20... | collective-permute-start | bytes 1572872 | tf_op jit(solution)/shard_map/ppermute | solution.py:452
  3.6 0.7 %convert_element_type.31 = f32[4,2048]{1,0:T(4,128)S(1)} convert(bf16[4,2048]{1,0:T(4,128)(2,1)} %param.13) | non-fusion elementwise | flops 8192 | bytes 49152 | tf_op jit(solution)/shard_map/convert_element_type | solution.py:450
  4.4 0.7 %convert_bitcast_fusion.gate_out_ref = f32[8,1024]{1,0:T(8,128)S(1)} fusion(bf16[1024,8]{0,1:T(8,128)(2,1)} %param.15), kind=kLoop, calls=%fused_computation.2 | loop fusion | flops 8192 | bytes 49152 | tf_op jit(solution)/shard_map/convert_element_type | solution.py:449
  5.1 9.6 %conditional.2 = (f32[8,112]{1,0:T(8,128)S(1)}, f32[4,2048]{1,0:T(4,128)S(1)}, bf16[2176,512]{1,0:T(8,128)(2,1)S(1)}) conditional(s32[]{:T(128)} %convert_element_type.30, () %tuple.25, (bf16[128,2048]{1,0:T(8,128)(2,1)}, f32[4,2048]{1,0:T(4,128)S(1)}, bf16[2048,512]{1,0:T(8,128)(2,1)}, f32[8,1024]{1,0:T(8,128)S(1)}) %tuple.26), branch_computations={%region_0.0_spmd, %region_1.0_spmd} | conditional | flops 114689 | bytes 2264610 | solution.py:142
  5.1 2.5 %branch_1_fun.3 = (f32[112,512]{1,0:T(8,128)S(1)}, f32[4,2048]{1,0:T(4,128)S(1)}, bf16[2176,512]{1,0:T(8,128)(2,1)S(1)}) custom-call(bf16[128,2048]{1,0:T(8,128)(2,1)} %get-tuple-element.10.rows_ref, f32[4,2048]{1,0:T(4,128)S(1)} %get-tuple-element.18.taps_ref, bf16[2048,512]{1,0:T(8,128)(2,1)} %get-tuple-element.64.gate_ref), custom_call_target="tpu_custom_call" | custom-call | flops 1 | bytes 1 | tf_op jit(solution)/shard_map/cond/branch_1_fun/pallas_call | solution.py:88
  7.6 0.1 collective-permute-start.1
  7.7 1.5 %collective-permute-done.1 = f32[112,512]{1,0:T(8,128)S(1)} collective-permute-done((f32[112,512]{1,0:T(8,128)S(1)}, f32[112,512]{1,0:T(8,128)S(1)}, u32[]{:S(2)}, u32[]{:S(2)}) %collective-permute-start.1) | collective-permute-done | bytes 229408 | tf_op jit(solution)/shard_map/cond/branch_1_fun/ppermute | solution.py:137
  9.2 1.6 %collective-permute-start.2 = (bf16[112,512]{1,0:T(8,128)(2,1)S(1)}, bf16[112,512]{1,0:T(8,128)(2,1)S(1)}, u32[]{:S(2)}, u32[]{:S(2)}) collective-permute-start(bf16[112,512]{1,0:T(8,128)(2,1)S(1)} %get-tuple-element.65), channel_id=1, source_target_pairs={{0,8},{4,12},{8,0},{12,4},{1,9},{5,13},{9,1},{13,5},{2,10},{6,14},... | collective-permute-start | bytes 344072 | tf_op jit(solution)/shard_map/cond/branch_1_fun/ppermute | solution.py:137
  10.8 3.7 %collective-permute-done.2.in_ref = bf16[112,512]{1,0:T(8,128)(2,1)S(1)} collective-permute-done((bf16[112,512]{1,0:T(8,128)(2,1)S(1)}, bf16[112,512]{1,0:T(8,128)(2,1)S(1)}, u32[]{:S(2)}, u32[]{:S(2)}) %collective-permute-start.2) | collective-permute-done | bytes 114720 | tf_op jit(solution)/shard_map/cond/branch_1_fun/ppermute | solution.py:137
  14.4 0.2 branch_1_fun.4
  14.6 0.0 copy-start.1
  14.6 0.0 copy-start.2
  14.6 0.0 copy-start
  14.6 0.0 copy-start.3
  14.7 1.1 %collective-permute-done.3.peer_ref = bf16[128,2048]{1,0:T(8,128)(2,1)S(1)} collective-permute-done((bf16[128,2048]{1,0:T(8,128)(2,1)}, bf16[128,2048]{1,0:T(8,128)(2,1)S(1)}, u32[]{:S(2)}, u32[]{:S(2)}) %collective-permute-start.3) | collective-permute-done | bytes 524320 | tf_op jit(solution)/shard_map/ppermute | solution.py:452
  15.8 0.8 %shard_map.96 = (f32[144,256]{1,0:T(8,128)S(1)}, bf16[144,256]{1,0:T(8,128)(2,1)S(1)}) custom-call(bf16[128,2048]{1,0:T(8,128)(2,1)S(1)} %collective-permute-done.3.peer_ref, f32[4,2048]{1,0:T(4,128)S(1)} %get-tuple-element.51.taps_ref, bf16[2176,512]{1,0:T(8,128)(2,1)S(1)} %get-tuple-element.52.held_ref), custom_call_target="tpu_custom_call" | custom-call | flops 1 | bytes 1 | tf_op jit(solution)/shard_map/pallas_call | solution.py:108
  16.6 0.1 collective-permute-start.5
  16.6 1.8 %collective-permute-start.4 = (bf16[144,256]{1,0:T(8,128)(2,1)S(1)}, bf16[144,256]{1,0:T(8,128)(2,1)S(1)}, u32[]{:S(2)}, u32[]{:S(2)}) collective-permute-start(bf16[144,256]{1,0:T(8,128)(2,1)S(1)} %get-tuple-element.53), channel_id=1, source_target_pairs={{0,8},{4,12},{8,0},{12,4},{1,9},{5,13},{9,1},{13,5},{2,10},{6,14},... | collective-permute-start | bytes 221192 | tf_op jit(solution)/shard_map/ppermute | solution.py:137
  18.5 0.0 collective-permute-done.5
  18.5 1.4 %collective-permute-start.6 = (bf16[144,256]{1,0:T(8,128)(2,1)S(1)}, bf16[144,256]{1,0:T(8,128)(2,1)S(1)}, u32[]{:S(2)}, u32[]{:S(2)}) collective-permute-start(bf16[144,256]{1,0:T(8,128)(2,1)S(1)} %get-tuple-element.67), channel_id=1, source_target_pairs={{0,8},{4,12},{8,0},{12,4},{1,9},{5,13},{9,1},{13,5},{2,10},{6,14},... | collective-permute-start | bytes 221192 | tf_op jit(solution)/shard_map/ppermute | solution.py:137
  19.9 0.0 copy-done.1
  19.9 1.5 %collective-permute-start.8 = (bf16[128,256]{1,0:T(8,128)(2,1)S(1)}, bf16[128,256]{1,0:T(8,128)(2,1)S(1)}, u32[]{:S(2)}, u32[]{:S(2)}) collective-permute-start(bf16[128,256]{1,0:T(8,128)(2,1)S(1)} %copy-done.1), channel_id=1, source_target_pairs={{0,16},{16,0},{1,17},{17,1},{2,18},{18,2},{3,19},{19,3},{4,20},{20... | collective-permute-start | bytes 196616 | tf_op jit(solution)/shard_map/ppermute | solution.py:461
  21.4 0.0 copy-done.2
  21.4 0.5 %collective-permute-start.9 = (bf16[128,256]{1,0:T(8,128)(2,1)S(1)}, bf16[128,256]{1,0:T(8,128)(2,1)S(1)}, u32[]{:S(2)}, u32[]{:S(2)}) collective-permute-start(bf16[128,256]{1,0:T(8,128)(2,1)S(1)} %copy-done.2), channel_id=1, source_target_pairs={{0,16},{16,0},{1,17},{17,1},{2,18},{18,2},{3,19},{19,3},{4,20},{20... | collective-permute-start | bytes 196616 | tf_op jit(solution)/shard_map/ppermute | solution.py:462
  21.9 0.0 collective-permute-done.4
  21.9 1.5 %conditional.3 = (f32[8,144]{1,0:T(8,128)S(1)}) conditional(s32[]{:T(128)} %convert_element_type.30, () %tuple.28, (bf16[144,256]{1,0:T(8,128)(2,1)S(1)}, bf16[144,256]{1,0:T(8,128)(2,1)S(1)}, f32[8,1024]{1,0:T(8,128)S(1)}) %tuple.29), branch_computations={%region_2.0_spmd, %region_3.0_spmd} | conditional | flops 147456 | bytes 663600 | solution.py:142
  21.9 0.1 collective-permute-start
  22.0 1.3 %collective-permute-done.in_ref = bf16[144,256]{1,0:T(8,128)(2,1)S(1)} collective-permute-done((bf16[144,256]{1,0:T(8,128)(2,1)S(1)}, bf16[144,256]{1,0:T(8,128)(2,1)S(1)}, u32[]{:S(2)}, u32[]{:S(2)}) %collective-permute-start) | collective-permute-done | bytes 73760 | tf_op jit(solution)/shard_map/cond/branch_1_fun/ppermute | solution.py:137
  23.2 0.2 branch_1_fun.5
  23.4 0.0 collective-permute-done.6.near_in_ref
  23.4 0.3 shard_map.97.refs_0_
  23.7 1.3 %collective-permute-start.7 = (f32[2,8,128]{2,1,0:T(8,128)S(1)}, f32[2,8,128]{2,1,0:T(8,128)S(1)}, u32[]{:S(2)}, u32[]{:S(2)}) collective-permute-start(f32[2,8,128]{2,1,0:T(8,128)S(1)} %shard_map.97.refs_0_), channel_id=1, source_target_pairs={{0,20},{4,16},{8,28},{12,24},{16,4},{20,0},{24,12},{28,8},{1,21},{... | collective-permute-start | bytes 24584 | tf_op jit(solution)/shard_map/ppermute | solution.py:474
  25.0 0.0 collective-permute-done.8.behind_keys_ref.refs_6_
  25.0 0.0 copy-done
  25.0 0.0 copy-done.3
  25.0 0.7 %shard_map.98.refs_2_ = f32[16,128,256]{2,1,0:T(8,128)S(1)} custom-call(s32[2,128]{1,0:T(2,128)S(1)} %bitcast.3, bf16[128,2048]{1,0:T(8,128)(2,1)S(1)} %copy-done, bf16[128,256]{1,0:T(8,128)(2,1)S(1)} %copy-done.1, bf16[128,256]{1,0:T(8,128)(2,1)S(1)} %collective-permute-done.8.behind_keys_ref.refs_6_), custom_call_target="tpu_custom_call" | custom-call | flops 134217728 | bytes 2097152 | tf_op jit(solution)/shard_map/pallas_call | solution.py:262
  25.7 1.1 %collective-permute-done.7.refs_1_ = f32[2,8,128]{2,1,0:T(8,128)S(1)} collective-permute-done((f32[2,8,128]{2,1,0:T(8,128)S(1)}, f32[2,8,128]{2,1,0:T(8,128)S(1)}, u32[]{:S(2)}, u32[]{:S(2)}) %collective-permute-start.7) | collective-permute-done | bytes 8224 | tf_op jit(solution)/shard_map/ppermute | solution.py:474
  26.8 2.2 %collective-permute-start.10 = (f32[2,128]{1,0:T(2,128)S(1)}, f32[2,128]{1,0:T(2,128)S(1)}, u32[]{:S(2)}, u32[]{:S(2)}) collective-permute-start(f32[2,128]{1,0:T(2,128)S(1)} %shard_map.99), channel_id=1, source_target_pairs={{0,16},{16,0},{1,17},{17,1},{2,18},{18,2},{3,19},{19,3},{4,20},{20... | collective-permute-start | bytes 3080 | tf_op jit(solution)/shard_map/ppermute | solution.py:478
  29.0 0.0 collective-permute-done.9.refs_8_
  29.0 1.4 %shard_map.100 = (bf16[128,2048]{1,0:T(8,128)(2,1)}, f32[2,128]{1,0:T(2,128)S(1)}) custom-call(f32[2,8,128]{2,1,0:T(8,128)S(1)} %shard_map.97.refs_0_, f32[2,8,128]{2,1,0:T(8,128)S(1)} %collective-permute-done.7.refs_1_, f32[16,128,256]{2,1,0:T(8,128)S(1)} %shard_map.98.refs_2_, s32[2,128]{1,0:T(2,128)S(1)} %bitcast.5, bf16[128,2048]{1,0:T(8,128)(2,1)S(1)} %copy-done, ...), custom_call_target="tpu_custom_call" | custom-call | flops 134217728 | bytes 1048576 | tf_op jit(solution)/shard_map/pallas_call | solution.py:418
  30.5 0.1 collective-permute-done.10
  30.6 0.5 %add_convert_fusion = bf16[2,128]{1,0:T(2,128)(2,1)} fusion(f32[2,128]{1,0:T(2,128)S(1)} %get-tuple-element.61, f32[2,128]{1,0:T(2,128)S(1)} %collective-permute-done.10), kind=kLoop, calls=%fused_computation.3 | loop fusion | flops 512 | bytes 2560 | tf_op jit(solution)/shard_map/convert_element_type | solution.py:479
  (4 shorter events, 0.1 us)
Async XLA Ops:
  0.6 15.1 %collective-permute-start.3 = (bf16[128,2048]{1,0:T(8,128)(2,1)}, bf16[128,2048]{1,0:T(8,128)(2,1)S(1)}, u32[]{:S(2)}, u32[]{:S(2)}) collective-permute-start(bf16[128,2048]{1,0:T(8,128)(2,1)} %param.12), channel_id=1, source_target_pairs={{0,16},{16,0},{1,17},{17,1},{2,18},{18,2},{3,19},{19,3},{4,20},{20... | collective-permute-start | bytes 1572872 | tf_op jit(solution)/shard_map/ppermute | solution.py:452
  7.6 1.5 %collective-permute-start.1 = (f32[112,512]{1,0:T(8,128)S(1)}, f32[112,512]{1,0:T(8,128)S(1)}, u32[]{:S(2)}, u32[]{:S(2)}) collective-permute-start(f32[112,512]{1,0:T(8,128)S(1)} %get-tuple-element.20), channel_id=1, source_target_pairs={{0,4},{4,0},{8,12},{12,8},{1,5},{5,1},{9,13},{13,9},{2,6},{6,2},{1... | collective-permute-start | bytes 688136 | tf_op jit(solution)/shard_map/cond/branch_1_fun/ppermute | solution.py:137
  9.2 5.3 %collective-permute-start.2 = (bf16[112,512]{1,0:T(8,128)(2,1)S(1)}, bf16[112,512]{1,0:T(8,128)(2,1)S(1)}, u32[]{:S(2)}, u32[]{:S(2)}) collective-permute-start(bf16[112,512]{1,0:T(8,128)(2,1)S(1)} %get-tuple-element.65), channel_id=1, source_target_pairs={{0,8},{4,12},{8,0},{12,4},{1,9},{5,13},{9,1},{13,5},{2,10},{6,14},... | collective-permute-start | bytes 344072 | tf_op jit(solution)/shard_map/cond/branch_1_fun/ppermute | solution.py:137
  14.6 5.2 %copy-start.1 = (bf16[128,256]{1,0:T(8,128)(2,1)S(1)}, bf16[128,256]{1,0:T(8,128)(2,1)}, u32[]{:S(2)}) copy-start(bf16[128,256]{1,0:T(8,128)(2,1)} %refs_5_.3) | copy-start | bytes 196612
  14.6 6.7 %copy-start.2 = (bf16[128,256]{1,0:T(8,128)(2,1)S(1)}, bf16[128,256]{1,0:T(8,128)(2,1)}, u32[]{:S(2)}) copy-start(bf16[128,256]{1,0:T(8,128)(2,1)} %refs_7_.1) | copy-start | bytes 196612
  14.6 10.4 %copy-start = (bf16[128,2048]{1,0:T(8,128)(2,1)S(1)}, bf16[128,2048]{1,0:T(8,128)(2,1)}, u32[]{:S(2)}) copy-start(bf16[128,2048]{1,0:T(8,128)(2,1)} %refs_4_.1) | copy-start | bytes 1572868
  14.6 10.4 %copy-start.3 = (s32[256]{0:T(256)S(1)}, s32[256]{0:T(256)}, u32[]{:S(2)}) copy-start(s32[256]{0:T(256)} %param.19) | copy-start | bytes 3076
  16.6 1.9 %collective-permute-start.5 = (f32[144,256]{1,0:T(8,128)S(1)}, f32[144,256]{1,0:T(8,128)S(1)}, u32[]{:S(2)}, u32[]{:S(2)}) collective-permute-start(f32[144,256]{1,0:T(8,128)S(1)} %get-tuple-element.54), channel_id=1, source_target_pairs={{0,4},{4,0},{8,12},{12,8},{1,5},{5,1},{9,13},{13,9},{2,6},{6,2},{1... | collective-permute-start | bytes 442376 | tf_op jit(solution)/shard_map/ppermute | solution.py:137
  16.6 5.2 %collective-permute-start.4 = (bf16[144,256]{1,0:T(8,128)(2,1)S(1)}, bf16[144,256]{1,0:T(8,128)(2,1)S(1)}, u32[]{:S(2)}, u32[]{:S(2)}) collective-permute-start(bf16[144,256]{1,0:T(8,128)(2,1)S(1)} %get-tuple-element.53), channel_id=1, source_target_pairs={{0,8},{4,12},{8,0},{12,4},{1,9},{5,13},{9,1},{13,5},{2,10},{6,14},... | collective-permute-start | bytes 221192 | tf_op jit(solution)/shard_map/ppermute | solution.py:137
  18.5 4.9 %collective-permute-start.6 = (bf16[144,256]{1,0:T(8,128)(2,1)S(1)}, bf16[144,256]{1,0:T(8,128)(2,1)S(1)}, u32[]{:S(2)}, u32[]{:S(2)}) collective-permute-start(bf16[144,256]{1,0:T(8,128)(2,1)S(1)} %get-tuple-element.67), channel_id=1, source_target_pairs={{0,8},{4,12},{8,0},{12,4},{1,9},{5,13},{9,1},{13,5},{2,10},{6,14},... | collective-permute-start | bytes 221192 | tf_op jit(solution)/shard_map/ppermute | solution.py:137
  19.9 5.1 %collective-permute-start.8 = (bf16[128,256]{1,0:T(8,128)(2,1)S(1)}, bf16[128,256]{1,0:T(8,128)(2,1)S(1)}, u32[]{:S(2)}, u32[]{:S(2)}) collective-permute-start(bf16[128,256]{1,0:T(8,128)(2,1)S(1)} %copy-done.1), channel_id=1, source_target_pairs={{0,16},{16,0},{1,17},{17,1},{2,18},{18,2},{3,19},{19,3},{4,20},{20... | collective-permute-start | bytes 196616 | tf_op jit(solution)/shard_map/ppermute | solution.py:461
  21.4 7.7 %collective-permute-start.9 = (bf16[128,256]{1,0:T(8,128)(2,1)S(1)}, bf16[128,256]{1,0:T(8,128)(2,1)S(1)}, u32[]{:S(2)}, u32[]{:S(2)}) collective-permute-start(bf16[128,256]{1,0:T(8,128)(2,1)S(1)} %copy-done.2), channel_id=1, source_target_pairs={{0,16},{16,0},{1,17},{17,1},{2,18},{18,2},{3,19},{19,3},{4,20},{20... | collective-permute-start | bytes 196616 | tf_op jit(solution)/shard_map/ppermute | solution.py:462
  21.9 1.3 %collective-permute-start = (bf16[144,256]{1,0:T(8,128)(2,1)S(1)}, bf16[144,256]{1,0:T(8,128)(2,1)S(1)}, u32[]{:S(2)}, u32[]{:S(2)}) collective-permute-start(bf16[144,256]{1,0:T(8,128)(2,1)S(1)} %get-tuple-element.69), channel_id=1, source_target_pairs={{0,4},{4,0},{8,12},{12,8},{1,5},{5,1},{9,13},{13,9},{2,6},{6,2},{1... | collective-permute-start | bytes 221192 | tf_op jit(solution)/shard_map/cond/branch_1_fun/ppermute | solution.py:137
  23.7 3.1 %collective-permute-start.7 = (f32[2,8,128]{2,1,0:T(8,128)S(1)}, f32[2,8,128]{2,1,0:T(8,128)S(1)}, u32[]{:S(2)}, u32[]{:S(2)}) collective-permute-start(f32[2,8,128]{2,1,0:T(8,128)S(1)} %shard_map.97.refs_0_), channel_id=1, source_target_pairs={{0,20},{4,16},{8,28},{12,24},{16,4},{20,0},{24,12},{28,8},{1,21},{... | collective-permute-start | bytes 24584 | tf_op jit(solution)/shard_map/ppermute | solution.py:474
  26.8 3.8 %collective-permute-start.10 = (f32[2,128]{1,0:T(2,128)S(1)}, f32[2,128]{1,0:T(2,128)S(1)}, u32[]{:S(2)}, u32[]{:S(2)}) collective-permute-start(f32[2,128]{1,0:T(2,128)S(1)} %shard_map.99), channel_id=1, source_target_pairs={{0,16},{16,0},{1,17},{17,1},{2,18},{18,2},{3,19},{19,3},{4,20},{20... | collective-permute-start | bytes 3080 | tf_op jit(solution)/shard_map/ppermute | solution.py:478

commit v19 on v17

--- a/solution.py
+++ b/solution.py
@@ -15,7 +15,7 @@
 
 NEG_FILL = -1e30
 RIM_ROWS = 16
-PIECE_HEADS = 4
+PIECE_HEADS = 2
 LEAST_RETENTION = -40.0
 VMEM_BYTES = 16 * 1024 * 1024
 

time: 31.3 us -> 31.3 us (level)
  no operation moved by 1% of the time
where the time goes in v19:
time: 31.3 us; the launch traced here: 31.1 us
  starting transfers between devices  13.5 us (43%)
  waiting for transfers between devices  10.1 us (32%)
  Pallas kernels  6.16 us (20%)
  between operations  0.7 us (2%)
  other arithmetic  0.59 us (2%)
    ppermute x6, waiting for transfers between devices, exchange_heads(): return lax.ppermute(block, 'heads', [(i, i ^ step) for i in range(count)])  6.4 us
    ppermute x6, starting transfers between devices, exchange_heads(): return lax.ppermute(block, 'heads', [(i, i ^ step) for i in range(count)])  4.97 us
    ppermute x1, starting transfers between devices, pair_device(): peer_rows = lax.ppermute(activations, 'seq', swap)  3 us
    pallas_call x1, Pallas kernels, own_project(): pl.pallas_call(own_project_kernel, out_shape=(jax.ShapeDtypeStruct((done,...  2.55 us
    ppermute x1, waiting for transfers between devices, pair_device(): peer_rows = lax.ppermute(activations, 'seq', swap)  2.51 us
    ppermute x1, starting transfers between devices, pair_device(): key_mass = own_mass + lax.ppermute(sent, 'seq', swap)  2.22 us
    ppermute x1, starting transfers between devices, pair_device(): behind_keys = lax.ppermute(key_vectors, 'seq', swap)  1.49 us
    pallas_call x1, Pallas kernels, attend(): pl.pallas_call(attend_kernel, out_specs=(pl.BlockSpec(memory_space=pl.ANY...  1.46 us
  transfers between devices with their start and end apart: 11, of which 6 were waited for; matrix products, arithmetic and copies ran while one was open for 0% of the time, Pallas kernels for 17%

profile of v19, /device:TPU:0, one launch (start us, length us, event | category | flops | bytes accessed | tf_op | source)
XLA Modules:
  0.0 31.1 jit_solution(8816033607919760219)
XLA Ops:
  0.6 3.0 %collective-permute-start.3 = (bf16[128,2048]{1,0:T(8,128)(2,1)}, bf16[128,2048]{1,0:T(8,128)(2,1)S(1)}, u32[]{:S(2)}, u32[]{:S(2)}) collective-permute-start(bf16[128,2048]{1,0:T(8,128)(2,1)} %param.12), channel_id=1, source_target_pairs={{0,16},{16,0},{1,17},{17,1},{2,18},{18,2},{3,19},{19,3},{4,20},{20... | collective-permute-start | bytes 1572872 | tf_op jit(solution)/shard_map/ppermute | solution.py:451
  3.6 9.6 %conditional.2 = (f32[8,112]{1,0:T(8,128)S(1)}, f32[4,2048]{1,0:T(4,128)S(1)}, bf16[2176,512]{1,0:T(8,128)(2,1)S(1)}) conditional(s32[]{:T(128)} %convert_element_type.22, () %tuple.25, (bf16[128,2048]{1,0:T(8,128)(2,1)}, bf16[4,2048]{1,0:T(4,128)(2,1)}, bf16[2048,512]{1,0:T(8,128)(2,1)}, bf16[8,1024]{1,0:T(8,128)(2,1)}) %tuple.40), branch_computations={%region_0.0_spmd, %region_1.0_spmd} | conditional | flops 114689 | bytes 2264610 | solution.py:142
  3.6 0.0 copy-start.5
  3.6 2.6 %branch_1_fun.3 = (f32[112,512]{1,0:T(8,128)S(1)}, f32[4,2048]{1,0:T(4,128)S(1)}, bf16[2176,512]{1,0:T(8,128)(2,1)S(1)}) custom-call(bf16[128,2048]{1,0:T(8,128)(2,1)} %get-tuple-element.10.rows_ref, bf16[4,2048]{1,0:T(4,128)(2,1)} %get-tuple-element.65.taps_ref, bf16[2048,512]{1,0:T(8,128)(2,1)} %get-tuple-element.66.gate_ref), custom_call_target="tpu_custom_call" | custom-call | flops 1 | bytes 1 | tf_op jit(solution)/shard_map/cond/branch_1_fun/pallas_call | solution.py:88
  6.2 0.1 collective-permute-start.1
  6.3 1.5 %collective-permute-done.1 = f32[112,512]{1,0:T(8,128)S(1)} collective-permute-done((f32[112,512]{1,0:T(8,128)S(1)}, f32[112,512]{1,0:T(8,128)S(1)}, u32[]{:S(2)}, u32[]{:S(2)}) %collective-permute-start.1) | collective-permute-done | bytes 229408 | tf_op jit(solution)/shard_map/cond/branch_1_fun/ppermute | solution.py:137
  7.8 1.6 %collective-permute-start.2 = (bf16[112,512]{1,0:T(8,128)(2,1)S(1)}, bf16[112,512]{1,0:T(8,128)(2,1)S(1)}, u32[]{:S(2)}, u32[]{:S(2)}) collective-permute-start(bf16[112,512]{1,0:T(8,128)(2,1)S(1)} %get-tuple-element.67), channel_id=1, source_target_pairs={{0,8},{4,12},{8,0},{12,4},{1,9},{5,13},{9,1},{13,5},{2,10},{6,14},... | collective-permute-start | bytes 344072 | tf_op jit(solution)/shard_map/cond/branch_1_fun/ppermute | solution.py:137
  9.4 3.7 %collective-permute-done.2.in_ref = bf16[112,512]{1,0:T(8,128)(2,1)S(1)} collective-permute-done((bf16[112,512]{1,0:T(8,128)(2,1)S(1)}, bf16[112,512]{1,0:T(8,128)(2,1)S(1)}, u32[]{:S(2)}, u32[]{:S(2)}) %collective-permute-start.2) | collective-permute-done | bytes 114720 | tf_op jit(solution)/shard_map/cond/branch_1_fun/ppermute | solution.py:137
  13.0 0.0 copy-done.5
  13.0 0.2 branch_1_fun.4
  13.2 0.0 copy-start.1
  13.2 0.0 copy-start.2
  13.2 0.0 copy-start.4
  13.2 0.0 copy-start
  13.2 0.0 copy-start.3
  13.3 2.5 %collective-permute-done.3.peer_ref = bf16[128,2048]{1,0:T(8,128)(2,1)S(1)} collective-permute-done((bf16[128,2048]{1,0:T(8,128)(2,1)}, bf16[128,2048]{1,0:T(8,128)(2,1)S(1)}, u32[]{:S(2)}, u32[]{:S(2)}) %collective-permute-start.3) | collective-permute-done | bytes 524320 | tf_op jit(solution)/shard_map/ppermute | solution.py:451
  15.8 0.8 %shard_map.97 = (f32[144,256]{1,0:T(8,128)S(1)}, bf16[144,256]{1,0:T(8,128)(2,1)S(1)}) custom-call(bf16[128,2048]{1,0:T(8,128)(2,1)S(1)} %collective-permute-done.3.peer_ref, f32[4,2048]{1,0:T(4,128)S(1)} %get-tuple-element.51.taps_ref, bf16[2176,512]{1,0:T(8,128)(2,1)S(1)} %get-tuple-element.52.held_ref), custom_call_target="tpu_custom_call" | custom-call | flops 1 | bytes 1 | tf_op jit(solution)/shard_map/pallas_call | solution.py:108
  16.6 0.1 collective-permute-start.5
  16.6 1.8 %collective-permute-start.4 = (bf16[144,256]{1,0:T(8,128)(2,1)S(1)}, bf16[144,256]{1,0:T(8,128)(2,1)S(1)}, u32[]{:S(2)}, u32[]{:S(2)}) collective-permute-start(bf16[144,256]{1,0:T(8,128)(2,1)S(1)} %get-tuple-element.53), channel_id=1, source_target_pairs={{0,8},{4,12},{8,0},{12,4},{1,9},{5,13},{9,1},{13,5},{2,10},{6,14},... | collective-permute-start | bytes 221192 | tf_op jit(solution)/shard_map/ppermute | solution.py:137
  18.5 0.0 collective-permute-done.5
  18.5 1.4 %collective-permute-start.6 = (bf16[144,256]{1,0:T(8,128)(2,1)S(1)}, bf16[144,256]{1,0:T(8,128)(2,1)S(1)}, u32[]{:S(2)}, u32[]{:S(2)}) collective-permute-start(bf16[144,256]{1,0:T(8,128)(2,1)S(1)} %get-tuple-element.69), channel_id=1, source_target_pairs={{0,8},{4,12},{8,0},{12,4},{1,9},{5,13},{9,1},{13,5},{2,10},{6,14},... | collective-permute-start | bytes 221192 | tf_op jit(solution)/shard_map/ppermute | solution.py:137
  19.9 0.0 copy-done.1
  19.9 1.5 %collective-permute-start.8 = (bf16[128,256]{1,0:T(8,128)(2,1)S(1)}, bf16[128,256]{1,0:T(8,128)(2,1)S(1)}, u32[]{:S(2)}, u32[]{:S(2)}) collective-permute-start(bf16[128,256]{1,0:T(8,128)(2,1)S(1)} %copy-done.1), channel_id=1, source_target_pairs={{0,16},{16,0},{1,17},{17,1},{2,18},{18,2},{3,19},{19,3},{4,20},{20... | collective-permute-start | bytes 196616 | tf_op jit(solution)/shard_map/ppermute | solution.py:460
  21.4 0.0 copy-done.2
  21.4 0.5 %collective-permute-start.9 = (bf16[128,256]{1,0:T(8,128)(2,1)S(1)}, bf16[128,256]{1,0:T(8,128)(2,1)S(1)}, u32[]{:S(2)}, u32[]{:S(2)}) collective-permute-start(bf16[128,256]{1,0:T(8,128)(2,1)S(1)} %copy-done.2), channel_id=1, source_target_pairs={{0,16},{16,0},{1,17},{17,1},{2,18},{18,2},{3,19},{19,3},{4,20},{20... | collective-permute-start | bytes 196616 | tf_op jit(solution)/shard_map/ppermute | solution.py:461
  21.9 0.0 collective-permute-done.4
  21.9 0.0 copy-done.4
  21.9 1.5 %conditional.3 = (f32[8,144]{1,0:T(8,128)S(1)}) conditional(s32[]{:T(128)} %convert_element_type.22, () %tuple.28, (bf16[144,256]{1,0:T(8,128)(2,1)S(1)}, bf16[144,256]{1,0:T(8,128)(2,1)S(1)}, bf16[8,1024]{1,0:T(8,128)(2,1)S(1)}) %tuple.41), branch_computations={%region_2.0_spmd, %region_3.0_spmd} | conditional | flops 147456 | bytes 663600 | solution.py:142
  21.9 0.1 collective-permute-start
  22.0 1.3 %collective-permute-done.in_ref = bf16[144,256]{1,0:T(8,128)(2,1)S(1)} collective-permute-done((bf16[144,256]{1,0:T(8,128)(2,1)S(1)}, bf16[144,256]{1,0:T(8,128)(2,1)S(1)}, u32[]{:S(2)}, u32[]{:S(2)}) %collective-permute-start) | collective-permute-done | bytes 73760 | tf_op jit(solution)/shard_map/cond/branch_1_fun/ppermute | solution.py:137
  23.3 0.2 branch_1_fun.5
  23.4 0.0 collective-permute-done.6.near_in_ref
  23.4 0.3 shard_map.98.refs_0_
  23.7 1.3 %collective-permute-start.7 = (f32[2,8,128]{2,1,0:T(8,128)S(1)}, f32[2,8,128]{2,1,0:T(8,128)S(1)}, u32[]{:S(2)}, u32[]{:S(2)}) collective-permute-start(f32[2,8,128]{2,1,0:T(8,128)S(1)} %shard_map.98.refs_0_), channel_id=1, source_target_pairs={{0,20},{4,16},{8,28},{12,24},{16,4},{20,0},{24,12},{28,8},{1,21},{... | collective-permute-start | bytes 24584 | tf_op jit(solution)/shard_map/ppermute | solution.py:473
  25.0 0.0 collective-permute-done.8.behind_keys_ref.refs_6_
  25.0 0.0 copy-done
  25.0 0.0 copy-done.3
  25.0 0.7 %shard_map.99.refs_2_ = f32[16,128,256]{2,1,0:T(8,128)S(1)} custom-call(s32[2,128]{1,0:T(2,128)S(1)} %bitcast.2, bf16[128,2048]{1,0:T(8,128)(2,1)S(1)} %copy-done, bf16[128,256]{1,0:T(8,128)(2,1)S(1)} %copy-done.1, bf16[128,256]{1,0:T(8,128)(2,1)S(1)} %collective-permute-done.8.behind_keys_ref.refs_6_), custom_call_target="tpu_custom_call" | custom-call | flops 134217728 | bytes 2097152 | tf_op jit(solution)/shard_map/pallas_call | solution.py:262
  25.7 1.1 %collective-permute-done.7.refs_1_ = f32[2,8,128]{2,1,0:T(8,128)S(1)} collective-permute-done((f32[2,8,128]{2,1,0:T(8,128)S(1)}, f32[2,8,128]{2,1,0:T(8,128)S(1)}, u32[]{:S(2)}, u32[]{:S(2)}) %collective-permute-start.7) | collective-permute-done | bytes 8224 | tf_op jit(solution)/shard_map/ppermute | solution.py:473
  26.8 2.2 %collective-permute-start.10 = (f32[2,128]{1,0:T(2,128)S(1)}, f32[2,128]{1,0:T(2,128)S(1)}, u32[]{:S(2)}, u32[]{:S(2)}) collective-permute-start(f32[2,128]{1,0:T(2,128)S(1)} %shard_map.100), channel_id=1, source_target_pairs={{0,16},{16,0},{1,17},{17,1},{2,18},{18,2},{3,19},{19,3},{4,20},{20... | collective-permute-start | bytes 3080 | tf_op jit(solution)/shard_map/ppermute | solution.py:477
  29.0 0.0 collective-permute-done.9.refs_8_
  29.1 1.5 %shard_map.101 = (bf16[128,2048]{1,0:T(8,128)(2,1)}, f32[2,128]{1,0:T(2,128)S(1)}) custom-call(f32[2,8,128]{2,1,0:T(8,128)S(1)} %shard_map.98.refs_0_, f32[2,8,128]{2,1,0:T(8,128)S(1)} %collective-permute-done.7.refs_1_, f32[16,128,256]{2,1,0:T(8,128)S(1)} %shard_map.99.refs_2_, s32[2,128]{1,0:T(2,128)S(1)} %bitcast.4, bf16[128,2048]{1,0:T(8,128)(2,1)S(1)} %copy-done, ...), custom_call_target="tpu_custom_call" | custom-call | flops 134217728 | bytes 1048576 | tf_op jit(solution)/shard_map/pallas_call | solution.py:418
  30.5 0.1 collective-permute-done.10
  30.6 0.5 %add_convert_fusion = bf16[2,128]{1,0:T(2,128)(2,1)} fusion(f32[2,128]{1,0:T(2,128)S(1)} %get-tuple-element.61, f32[2,128]{1,0:T(2,128)S(1)} %collective-permute-done.10), kind=kLoop, calls=%fused_computation.2 | loop fusion | flops 512 | bytes 2560 | tf_op jit(solution)/shard_map/convert_element_type | solution.py:478
  (4 shorter events, 0.1 us)
Async XLA Ops:
  0.6 15.1 %collective-permute-start.3 = (bf16[128,2048]{1,0:T(8,128)(2,1)}, bf16[128,2048]{1,0:T(8,128)(2,1)S(1)}, u32[]{:S(2)}, u32[]{:S(2)}) collective-permute-start(bf16[128,2048]{1,0:T(8,128)(2,1)} %param.12), channel_id=1, source_target_pairs={{0,16},{16,0},{1,17},{17,1},{2,18},{18,2},{3,19},{19,3},{4,20},{20... | collective-permute-start | bytes 1572872 | tf_op jit(solution)/shard_map/ppermute | solution.py:451
  3.6 9.4 %copy-start.5 = (bf16[8,1024]{1,0:T(8,128)(2,1)S(1)}, bf16[8,1024]{1,0:T(8,128)(2,1)}, u32[]{:S(2)}) copy-start(bf16[8,1024]{1,0:T(8,128)(2,1)} %get-tuple-element.21.gate_out_ref) | copy-start | bytes 49156 | tf_op jit(solution)/shard_map/cond
  6.2 1.5 %collective-permute-start.1 = (f32[112,512]{1,0:T(8,128)S(1)}, f32[112,512]{1,0:T(8,128)S(1)}, u32[]{:S(2)}, u32[]{:S(2)}) collective-permute-start(f32[112,512]{1,0:T(8,128)S(1)} %get-tuple-element.20), channel_id=1, source_target_pairs={{0,4},{4,0},{8,12},{12,8},{1,5},{5,1},{9,13},{13,9},{2,6},{6,2},{1... | collective-permute-start | bytes 688136 | tf_op jit(solution)/shard_map/cond/branch_1_fun/ppermute | solution.py:137
  7.8 5.3 %collective-permute-start.2 = (bf16[112,512]{1,0:T(8,128)(2,1)S(1)}, bf16[112,512]{1,0:T(8,128)(2,1)S(1)}, u32[]{:S(2)}, u32[]{:S(2)}) collective-permute-start(bf16[112,512]{1,0:T(8,128)(2,1)S(1)} %get-tuple-element.67), channel_id=1, source_target_pairs={{0,8},{4,12},{8,0},{12,4},{1,9},{5,13},{9,1},{13,5},{2,10},{6,14},... | collective-permute-start | bytes 344072 | tf_op jit(solution)/shard_map/cond/branch_1_fun/ppermute | solution.py:137
  13.2 6.6 %copy-start.1 = (bf16[128,256]{1,0:T(8,128)(2,1)S(1)}, bf16[128,256]{1,0:T(8,128)(2,1)}, u32[]{:S(2)}) copy-start(bf16[128,256]{1,0:T(8,128)(2,1)} %refs_5_.3) | copy-start | bytes 196612
  13.2 8.1 %copy-start.2 = (bf16[128,256]{1,0:T(8,128)(2,1)S(1)}, bf16[128,256]{1,0:T(8,128)(2,1)}, u32[]{:S(2)}) copy-start(bf16[128,256]{1,0:T(8,128)(2,1)} %refs_7_.1) | copy-start | bytes 196612
  13.2 8.7 %copy-start.4 = (bf16[1024,8]{0,1:T(8,128)(2,1)S(1)}, bf16[1024,8]{0,1:T(8,128)(2,1)}, u32[]{:S(2)}) copy-start(bf16[1024,8]{0,1:T(8,128)(2,1)} %param.15) | copy-start | bytes 49156
  13.2 11.8 %copy-start = (bf16[128,2048]{1,0:T(8,128)(2,1)S(1)}, bf16[128,2048]{1,0:T(8,128)(2,1)}, u32[]{:S(2)}) copy-start(bf16[128,2048]{1,0:T(8,128)(2,1)} %refs_4_.1) | copy-start | bytes 1572868
  13.2 11.8 %copy-start.3 = (s32[256]{0:T(256)S(1)}, s32[256]{0:T(256)}, u32[]{:S(2)}) copy-start(s32[256]{0:T(256)} %param.19) | copy-start | bytes 3076
  16.6 1.9 %collective-permute-start.5 = (f32[144,256]{1,0:T(8,128)S(1)}, f32[144,256]{1,0:T(8,128)S(1)}, u32[]{:S(2)}, u32[]{:S(2)}) collective-permute-start(f32[144,256]{1,0:T(8,128)S(1)} %get-tuple-element.54), channel_id=1, source_target_pairs={{0,4},{4,0},{8,12},{12,8},{1,5},{5,1},{9,13},{13,9},{2,6},{6,2},{1... | collective-permute-start | bytes 442376 | tf_op jit(solution)/shard_map/ppermute | solution.py:137
  16.6 5.3 %collective-permute-start.4 = (bf16[144,256]{1,0:T(8,128)(2,1)S(1)}, bf16[144,256]{1,0:T(8,128)(2,1)S(1)}, u32[]{:S(2)}, u32[]{:S(2)}) collective-permute-start(bf16[144,256]{1,0:T(8,128)(2,1)S(1)} %get-tuple-element.53), channel_id=1, source_target_pairs={{0,8},{4,12},{8,0},{12,4},{1,9},{5,13},{9,1},{13,5},{2,10},{6,14},... | collective-permute-start | bytes 221192 | tf_op jit(solution)/shard_map/ppermute | solution.py:137
  18.5 4.9 %collective-permute-start.6 = (bf16[144,256]{1,0:T(8,128)(2,1)S(1)}, bf16[144,256]{1,0:T(8,128)(2,1)S(1)}, u32[]{:S(2)}, u32[]{:S(2)}) collective-permute-start(bf16[144,256]{1,0:T(8,128)(2,1)S(1)} %get-tuple-element.69), channel_id=1, source_target_pairs={{0,8},{4,12},{8,0},{12,4},{1,9},{5,13},{9,1},{13,5},{2,10},{6,14},... | collective-permute-start | bytes 221192 | tf_op jit(solution)/shard_map/ppermute | solution.py:137
  19.9 5.1 %collective-permute-start.8 = (bf16[128,256]{1,0:T(8,128)(2,1)S(1)}, bf16[128,256]{1,0:T(8,128)(2,1)S(1)}, u32[]{:S(2)}, u32[]{:S(2)}) collective-permute-start(bf16[128,256]{1,0:T(8,128)(2,1)S(1)} %copy-done.1), channel_id=1, source_target_pairs={{0,16},{16,0},{1,17},{17,1},{2,18},{18,2},{3,19},{19,3},{4,20},{20... | collective-permute-start | bytes 196616 | tf_op jit(solution)/shard_map/ppermute | solution.py:460
  21.4 7.7 %collective-permute-start.9 = (bf16[128,256]{1,0:T(8,128)(2,1)S(1)}, bf16[128,256]{1,0:T(8,128)(2,1)S(1)}, u32[]{:S(2)}, u32[]{:S(2)}) collective-permute-start(bf16[128,256]{1,0:T(8,128)(2,1)S(1)} %copy-done.2), channel_id=1, source_target_pairs={{0,16},{16,0},{1,17},{17,1},{2,18},{18,2},{3,19},{19,3},{4,20},{20... | collective-permute-start | bytes 196616 | tf_op jit(solution)/shard_map/ppermute | solution.py:461
  21.9 1.3 %collective-permute-start = (bf16[144,256]{1,0:T(8,128)(2,1)S(1)}, bf16[144,256]{1,0:T(8,128)(2,1)S(1)}, u32[]{:S(2)}, u32[]{:S(2)}) collective-permute-start(bf16[144,256]{1,0:T(8,128)(2,1)S(1)} %get-tuple-element.71), channel_id=1, source_target_pairs={{0,4},{4,0},{8,12},{12,8},{1,5},{5,1},{9,13},{13,9},{2,6},{6,2},{1... | collective-permute-start | bytes 221192 | tf_op jit(solution)/shard_map/cond/branch_1_fun/ppermute | solution.py:137
  23.7 3.1 %collective-permute-start.7 = (f32[2,8,128]{2,1,0:T(8,128)S(1)}, f32[2,8,128]{2,1,0:T(8,128)S(1)}, u32[]{:S(2)}, u32[]{:S(2)}) collective-permute-start(f32[2,8,128]{2,1,0:T(8,128)S(1)} %shard_map.98.refs_0_), channel_id=1, source_target_pairs={{0,20},{4,16},{8,28},{12,24},{16,4},{20,0},{24,12},{28,8},{1,21},{... | collective-permute-start | bytes 24584 | tf_op jit(solution)/shard_map/ppermute | solution.py:473
  26.8 3.8 %collective-permute-start.10 = (f32[2,128]{1,0:T(2,128)S(1)}, f32[2,128]{1,0:T(2,128)S(1)}, u32[]{:S(2)}, u32[]{:S(2)}) collective-permute-start(f32[2,128]{1,0:T(2,128)S(1)} %shard_map.100), channel_id=1, source_target_pairs={{0,16},{16,0},{1,17},{17,1},{2,18},{18,2},{3,19},{19,3},{4,20},{20... | collective-permute-start | bytes 3080 | tf_op jit(solution)/shard_map/ppermute | solution.py:477
